TPU v7x, 256 devices: a whole 4x4x8 slice. The times are simulated.
256 devices in a mesh: role: 2 (over y_hi), fsdp: 64 (over x, z, core), seq: 2 (over y_lo).
Axes of the slice: x: 4, y: 4 (y_hi: 2, y_lo: 2; y = y_hi * 2 + y_lo), z: 8, core: 2. Of those that a mesh axis runs over, the one named last changes fastest.
Arguments:
- base_latents: bfloat16 [2, 64, 256, 64], P('role', 'fsdp', 'seq'), may hold values from -6 to 6
- noise_latents: bfloat16 [2, 64, 256, 64], P('role', 'fsdp', 'seq'), may hold values from -6 to 6
- noise_levels: float32 [2, 64], P('role', 'fsdp'), may hold values from 0.1 to 0.95
- replay_latents: bfloat16 [2, 64, 256, 64], P('role', 'fsdp', 'seq'), may hold values from -6 to 6
- replay_levels: float32 [2, 64], P('role', 'fsdp'), may hold values from 0.1 to 0.95
- cotangent: bfloat16 [2, 64, 256, 64], P('role', 'fsdp', 'seq'), may hold values from -6 to 6
- embed_weight: bfloat16 [2, 64, 3072], P('role'), may hold values from -0.75 to 0.75
- qkv_weight: bfloat16 [2, 3072, 4608], P('role', 'fsdp', 'seq'), as said below
- output_weight: bfloat16 [2, 1536, 64], P('role', 'seq'), may hold values from -0.15625 to 0.15625
- modulation: float32 [2, 2, 2, 3072], P('role'), may hold values from -3 to 3
Outputs:
- crossed: bfloat16 [2, 64, 256, 64], P('role', 'fsdp', 'seq')
- mod_grads: float32 [2, 2, 3072], P('role')
Inputs may be any that keep to these rules, and one draw needn't show every extreme that they name: `qkv_weight`: each head's query, key and value columns stand in that order, head after head.
All inputs are finite; a program needn't handle non-finite values.
Results may differ from a plain program's by a relative error of at most 0.0076.
Values may be sent and summed in bfloat16 or wider, within the bound.
No kernel may reach another device: no remote copies, remote signals or barrier semaphores. Data moves between devices by JAX's collectives and lax.ppermute only.
A program may use at most 128 MiB of HBM per device.

v0:
```python
from functools import partial
import math

import jax
import jax.numpy as jnp
from jax import lax
from jax.sharding import PartitionSpec as P

HEAD_DIM = 128


EPSILON = 1e-06


def partner(value, axis, stride):
    mask = 2**stride
    pairs = [(source, source ^ mask) for source in range(lax.axis_size(axis))]
    return lax.ppermute(value, axis, pairs)


def embed_normed(latents, embed_weight):
    embedded = jnp.dot(latents, embed_weight, preferred_element_type=jnp.float32)
    return embedded * lax.rsqrt(jnp.mean(embedded * embedded, axis=-1, keepdims=True) + EPSILON)


def attend_heads(qkv_rows, head_count):
    tokens = qkv_rows.shape[0]
    split = qkv_rows.reshape(tokens, head_count, 3, HEAD_DIM).astype(jnp.float32)
    scores = jnp.einsum("shd,thd->hst", split[:, :, 0], split[:, :, 1]) / math.sqrt(HEAD_DIM)
    weights = jax.nn.softmax(scores, axis=-1)
    rounded = lax.optimization_barrier(weights.astype(jnp.bfloat16)).astype(jnp.float32)
    mixed = jnp.einsum("hst,thd->shd", rounded, split[:, :, 2])
    return (mixed.astype(jnp.bfloat16).reshape(tokens, head_count * HEAD_DIM), weights)


def attend_back(qkv_rows, weights, grad_mixed, head_count):
    tokens = qkv_rows.shape[0]
    split = qkv_rows.reshape(tokens, head_count, 3, HEAD_DIM).astype(jnp.float32)
    grad_heads = grad_mixed.reshape(tokens, head_count, HEAD_DIM).astype(jnp.float32)
    rounded = lax.optimization_barrier(weights.astype(jnp.bfloat16)).astype(jnp.float32)
    grad_value = jnp.einsum("hst,shd->thd", rounded, grad_heads).astype(jnp.bfloat16)
    grad_weights = jnp.einsum("shd,thd->hst", grad_heads, split[:, :, 2])
    grad_scores = (
        weights
        * (grad_weights - jnp.sum(grad_weights * weights, axis=-1, keepdims=True))
        / math.sqrt(HEAD_DIM)
    )
    grad_rounded = lax.optimization_barrier(grad_scores.astype(jnp.bfloat16)).astype(jnp.float32)
    grad_query = jnp.einsum("hst,thd->shd", grad_rounded, split[:, :, 1]).astype(jnp.bfloat16)
    grad_key = jnp.einsum("hst,shd->thd", grad_rounded, split[:, :, 0]).astype(jnp.bfloat16)
    return jnp.stack([grad_query, grad_key, grad_value], axis=2).reshape(tokens, -1)


def cross_over(payload):
    return partner(payload, "role", 0)


def per_device(
    base_latents,
    noise_latents,
    noise_levels,
    replay_latents,
    replay_levels,
    cotangent,
    embed_weight,
    qkv_weight,
    output_weight,
    modulation,
):
    is_critic = lax.axis_index("role") == 1
    sample_count = base_latents.shape[1]
    head_local = output_weight.shape[1] // HEAD_DIM
    base_f = base_latents[0].astype(jnp.float32)
    noise_f = noise_latents[0].astype(jnp.float32)
    level_one = noise_levels[0]
    level_col = level_one[:, None, None]
    input_a = ((1.0 - level_col) * base_f + level_col * noise_f).astype(jnp.bfloat16)
    input_b = jnp.where(is_critic, input_a, replay_latents[0])
    level_two = jnp.where(is_critic, level_one, replay_levels[0])
    level_two_col = level_two[:, None, None]
    mod_one = modulation[0, 0]
    mod_two = jnp.where(is_critic, modulation[0, 1], modulation[0, 0])
    gathered = lax.all_gather(
        jnp.concatenate([input_a, input_b], axis=0), "seq", axis=1, tiled=True
    )
    length = gathered.shape[1]
    normed = embed_normed(gathered.reshape(-1, gathered.shape[2]), embed_weight[0]).reshape(
        2 * sample_count, length, -1
    )
    hidden_one = normed[:sample_count] * (1.0 + level_col * mod_one[0]) + level_col * mod_one[1]
    hidden_two = (
        normed[sample_count:] * (1.0 + level_two_col * mod_two[0]) + level_two_col * mod_two[1]
    )
    hidden = (
        jnp.concatenate([hidden_one, hidden_two], axis=0)
        .astype(jnp.bfloat16)
        .reshape(2 * sample_count * length, -1)
    )
    weight_shard = qkv_weight[0]
    qkv_flat = jnp.dot(
        hidden,
        lax.all_gather(weight_shard, "fsdp", axis=0, tiled=True),
        preferred_element_type=jnp.float32,
    )
    qkv_rows = qkv_flat.astype(jnp.bfloat16).reshape(2 * sample_count, length, -1)
    mixed, weights = jax.vmap(partial(attend_heads, head_count=head_local))(qkv_rows)
    partial_vel = jnp.dot(
        mixed.reshape(2 * sample_count * length, -1),
        output_weight[0],
        preferred_element_type=jnp.float32,
    )
    velocity = lax.psum_scatter(
        partial_vel.reshape(2 * sample_count, length, -1), "seq", scatter_dimension=1, tiled=True
    )
    vel_one = velocity[:sample_count]
    vel_two = velocity[sample_count:]
    payload = jnp.where(
        is_critic, vel_two - vel_one, input_a.astype(jnp.float32) - level_col * vel_one
    ).astype(jnp.bfloat16)
    grad_own = jnp.where(is_critic, vel_two - (noise_f - base_f), cotangent[0].astype(jnp.float32))
    grad_all = lax.all_gather(grad_own.astype(jnp.bfloat16), "seq", axis=1, tiled=True).astype(
        grad_own.dtype
    )
    out_float = output_weight[0].astype(jnp.float32)
    grad_mixed = jnp.dot(
        grad_all.reshape(sample_count * length, -1), out_float.T, preferred_element_type=jnp.float32
    ).astype(jnp.bfloat16)
    grad_qkv = jax.vmap(partial(attend_back, head_count=head_local))(
        qkv_rows[sample_count:],
        weights[sample_count:],
        grad_mixed.reshape(sample_count, length, -1),
    )
    grad_qkv = grad_qkv.reshape(sample_count * length, -1)
    grad_hidden = lax.dot_general(
        grad_qkv,
        lax.all_gather(weight_shard, "fsdp", axis=0, tiled=True),
        (((1,), (1,)), ((), ())),
        preferred_element_type=jnp.float32,
    )
    grad_hidden = grad_hidden.reshape(sample_count, length, -1) * level_two_col
    grad_scale = jnp.sum(grad_hidden * normed[sample_count:], axis=(0, 1))
    grad_shift = jnp.sum(grad_hidden, axis=(0, 1))
    total_scale, total_shift = lax.psum((grad_scale, grad_shift), ("fsdp", "seq"))
    factor = 1.0 / (sample_count * lax.axis_size("fsdp") * length)
    mod_grads = jnp.stack([total_scale, total_shift])[None] * factor
    crossed = cross_over(payload)
    return (crossed[None], mod_grads)


def solution(mesh):
    return jax.shard_map(
        per_device,
        mesh=mesh,
        in_specs=(
            P("role", "fsdp", "seq", None),
            P("role", "fsdp", "seq", None),
            P("role", "fsdp"),
            P("role", "fsdp", "seq", None),
            P("role", "fsdp"),
            P("role", "fsdp", "seq", None),
            P("role", None, None),
            P("role", "fsdp", "seq"),
            P("role", "seq", None),
            P("role", None, None, None),
        ),
        out_specs=(P("role", "fsdp", "seq", None), P("role", None, None)),
        check_vma=False,
    )
```

profile of v0, /device:TPU:1, one launch (start us, length us, event | category | flops | bytes accessed | tf_op | source)
XLA Modules:
  0.0 736.2 jit_solution(5812914632337217622)
XLA Ops:
  7.2 0.0 copy-start
  7.2 0.0 all-gather.3.cloned.1.call-start
  7.2 0.7 all-gather.3.cloned.1.call-update
  7.9 0.0 reduce-scatter.2.cloned.1.call-start
  9.3 0.8 bitcast_select_fusion
  10.0 4.1 all_gather.10
  14.2 0.0 copy-done
  14.2 0.0 copy-start.9
  14.2 1.1 multiply_reduce_fusion
  15.3 0.0 copy-done.9
  15.4 0.9 broadcast_multiply_fusion
  16.3 0.0 copy-start.2
  16.3 0.8 fusion.17
  17.1 1.7 copy-done.2
  18.9 2.0 pad_maximum_fusion
  20.8 87.5 %all-gather.3.cloned.1.call-done = bf16[1,3072,2304]{2,1,0:T(8,128)(2,1)} async-done(((bf16[1,48,2304]{2,1,0:T(8,128)(2,1)}), bf16[1,3072,2304]{2,1,0:T(8,128)(2,1)}) %all-gather.3.cloned.1.call-update) | async-done | bytes 14155792 | tf_op jit(solution)/shard_map/all_gather | solution.py:102
  108.3 12.4 %fusion.5 = bf16[512,2304]{1,0:T(8,128)(2,1)S(1)} fusion(bf16[512,3072]{1,0:T(8,128)(2,1)} %bitcast.149, bf16[1,3072,2304]{2,1,0:T(8,128)(2,1)} %all-gather.3.cloned.1.call-done), kind=kOutput, calls=%fused_computation.6 | convolution fusion | flops 7248936960 | bytes 19660800 | tf_op jit(solution)/shard_map/dot_general | solution.py:100
  120.7 0.0 copy-start.4
  120.7 1.4 copy-done.4
  122.2 2.5 copy.26
  124.6 5.0 reshape_reshape.4
  129.6 2.7 fusion.49
  132.3 2.3 copy.50
  134.6 0.7 copy.49
  135.3 0.6 fusion.28
  135.9 2.5 fusion.50
  138.4 0.0 copy-start.7
  138.4 0.5 fusion.47
  138.9 0.0 copy-start.3
  138.9 0.0 copy-start.8
  138.9 0.6 copy-done.7
  139.5 0.4 convolution_convert_fusion
  139.9 0.0 copy-done.8
  139.9 0.9 fusion.34
  140.8 0.0 reduce-scatter.2.cloned.1.call-update
  140.9 0.0 copy-start.10
  140.9 0.0 copy-start.11
  140.9 0.0 copy-start.12
  140.9 2.4 slice.92
  143.3 2.4 copy.32
  145.7 1.0 slice.128
  146.7 6.4 reduce-scatter.2.cloned.1.call-done
  153.1 0.0 copy-done.10
  153.1 1.4 fusion.42
  154.5 3.5 all_gather.12
  158.0 1.1 convolution_convert_fusion.4
  159.0 1.2 copy.34
  160.2 1.5 fusion.20
  161.7 0.0 copy-start.13
  161.8 0.0 slice-start
  161.8 1.8 fusion.19
  163.6 0.4 fusion.23
  164.0 0.0 slice-start.1
  164.0 0.3 fusion.22
  164.3 2.5 collective-permute-start
  166.9 0.4 fusion.24
  167.3 0.1 pad_maximum_fusion.1
  167.4 1.1 copy.41
  168.5 0.0 slice-done.1
  168.5 10.1 %multiply_reduce_fusion.1 = (f32[3072]{0:T(1024)}, f32[3072]{0:T(1024)}) fusion(f32[512,3072]{1,0:T(8,128)S(1)} %bitcast.143, f32[]{:T(128)} %bitcast.11, bf16[256,2304]{0,1:T(8,128)(2,1)} %bitcast.151, bf16[1,3072,2304]{2,1,0:T(8,128)(2,1)} %all-gather.3.cloned.1.call-done), kind=kOutput, calls=%fused_computation.12 | convolution fusion | flops 3627018240 | bytes 18505732 | tf_op jit(solution)/shard_map/dot_general | solution.py:134
  178.6 549.5 %all-reduce = (f32[1,1,3072]{2,1,0:T(1,128)S(1)}, f32[1,1,3072]{2,1,0:T(1,128)S(1)}) all-reduce(f32[1,1,3072]{2,1,0:T(1,128)} %bitcast.160, f32[1,1,3072]{2,1,0:T(1,128)} %bitcast.159), channel_id=1, replica_groups=mesh['role'=2,'fsdp'=64,'seq'=2] {'fsdp','seq'}, use_global_device_ids=true, to_apply=%region_8.9 | all-reduce | flops 6144 | bytes 49152 | tf_op jit(solution)/shard_map/psum | solution.py:143
  728.2 0.6 maximum_multiply_fusion
  728.8 0.0 collective-permute-done
  728.8 0.6 copy.60
  (18 shorter events, 0.1 us)
Async XLA Ops:
  7.2 7.0 copy-start
  7.2 101.1 %all-gather.3.cloned.1.call-start = ((), (), s32[]{:S(2)}) async-start(), calls=%async_computation.2 | async-start | bytes 14376960 | tf_op jit(solution)/shard_map/all_gather | solution.py:102
  7.9 145.2 %reduce-scatter.2.cloned.1.call-start = ((), (), s32[]{:S(2)}) async-start(), calls=%async_computation.1 | async-start | bytes 196608 | tf_op jit(solution)/shard_map/reduce_scatter | solution.py:112
  14.2 1.1 copy-start.9
  16.3 2.6 copy-start.2
  120.7 1.5 copy-start.4
  138.4 1.1 copy-start.7
  138.9 21.3 %copy-start.3 = (f32[2,6,256,256]{2,3,1,0:T(8,128)}, f32[2,6,256,256]{2,3,1,0:T(8,128)S(1)}, u32[]{:S(2)}) copy-start(f32[2,6,256,256]{2,3,1,0:T(8,128)S(1)} %get-tuple-element.7) | copy-start | bytes 9437188
  138.9 1.0 copy-start.8
  140.9 12.2 %copy-start.10 = (bf16[1,1,128,64]{2,3,1,0:T(8,128)(2,1)S(1)}, bf16[1,1,128,64]{2,3,1,0:T(8,128)(2,1)}, u32[]{:S(2)}) copy-start(bf16[1,1,128,64]{2,3,1,0:T(8,128)(2,1)} %param.10) | copy-start | bytes 49156
  140.9 12.2 %copy-start.11 = (bf16[1,1,128,64]{2,3,1,0:T(8,128)(2,1)S(1)}, bf16[1,1,128,64]{2,3,1,0:T(8,128)(2,1)}, u32[]{:S(2)}) copy-start(bf16[1,1,128,64]{2,3,1,0:T(8,128)(2,1)} %param.11) | copy-start | bytes 49156
  140.9 12.2 %copy-start.12 = (bf16[1,1,128,64]{2,3,1,0:T(8,128)(2,1)S(1)}, bf16[1,1,128,64]{2,3,1,0:T(8,128)(2,1)}, u32[]{:S(2)}) copy-start(bf16[1,1,128,64]{2,3,1,0:T(8,128)(2,1)} %param.15) | copy-start | bytes 49156
  160.2 3.4 copy-start.5
  161.7 2.6 copy-start.13
  161.8 5.1 copy-start.6
  161.8 6.8 slice-start
  164.0 4.5 slice-start.1
  164.3 564.5 %collective-permute-start = (bf16[1,128,64]{1,2,0:T(8,128)(2,1)S(1)}, bf16[1,128,64]{1,2,0:T(8,128)(2,1)S(1)}, u32[]{:S(2)}, u32[]{:S(2)}) collective-permute-start(bf16[1,128,64]{1,2,0:T(8,128)(2,1)S(1)} %copy-done.13), channel_id=1, source_target_pairs={{0,128},{128,0},{1,129},{129,1},{2,130},{130,2},{3,131},{131,3},{4... | collective-permute-start | bytes 49160 | tf_op jit(solution)/shard_map/ppermute | solution.py:18
  168.5 560.9 %copy-start.1 = (bf16[1,64,3072]{2,1,0:T(8,128)(2,1)S(1)}, bf16[1,64,3072]{2,1,0:T(8,128)(2,1)}, u32[]{:S(2)}) copy-start(bf16[1,64,3072]{2,1,0:T(8,128)(2,1)} %param.16) | copy-start | bytes 1179652
Sparse Core Ops, SparseCore 0:
  10.8 97.5 all-gather.2
  141.0 12.0 reduce-scatter.1
where the time goes:
time: 738 us; the launch traced here: 736 us
  blocking collectives  557 us (75%)
  waiting for transfers between devices  94.6 us (13%)
  matrix products  29 us (4%)
  local copies, waits for them, and re-layouts  25.7 us (3%)
  between operations  15.7 us (2%)
  other arithmetic  11.5 us (2%)
    psum x1, blocking collectives, per_device(): lax.psum((grad_scale, grad_shift), ('fsdp', 'seq'))  550 us
    all_gather x1, waiting for transfers between devices, per_device(): lax.all_gather(weight_shard, 'fsdp', axis=0, tiled=True)  87.5 us
  transfers between devices with their start and end apart: 3, of which 2 were waited for; matrix products, arithmetic and copies ran while one was open for 3% of the time, Pallas kernels for 0%

commit v1 on v0

v1 whole, which is shorter than its diff:
```python
import functools

import jax
import jax.numpy as jnp
from jax import lax
from jax.experimental import pallas as pl
from jax.experimental.pallas import tpu as pltpu
from jax.sharding import PartitionSpec as P

HEAD_DIM = 128
CHANNELS = 64
EPSILON = 1e-06
F32 = jnp.float32
BF16 = jnp.bfloat16
NT = (((1,), (1,)), ((), ()))
NN = (((1,), (0,)), ((), ()))
TN = (((0,), (0,)), ((), ()))


def dot(a, b, dims=NN):
    return lax.dot_general(a, b, dims, preferred_element_type=F32)


def round_up(value, step):
    return (value + step - 1) // step * step


def rounded(value):
    return value.astype(BF16).astype(F32)


def three_parts(value):
    high = rounded(value)
    middle = rounded(value - high)
    return high, middle, rounded(value - high - middle)


def lane_index(shape):
    return lax.broadcasted_iota(jnp.int32, shape, len(shape) - 1)


def row_index(shape):
    return lax.broadcasted_iota(jnp.int32, shape, len(shape) - 2)


def pack_kernel(flags, levels, base, noise, replay, cotangent, embed, pack):
    critic = flags[1] == 1
    level = levels[0]
    base_f = base[...].astype(F32)
    noise_f = noise[...].astype(F32)
    input_a = rounded((1.0 - level) * base_f + level * noise_f)
    input_b = jnp.where(critic, input_a, replay[...].astype(F32))
    known = jnp.where(critic, noise_f - base_f, cotangent[...].astype(F32))
    known_high = rounded(known)
    tokens = input_a.shape[0]
    rows = jnp.concatenate([input_a, input_b], axis=0).astype(BF16)
    total = jnp.zeros((2 * tokens, 1), F32)
    width = embed.shape[1]
    for start in range(0, width, 512):
        embedded = dot(rows, embed[:, start : start + 512])
        total = total + jnp.sum(embedded * embedded, axis=-1, keepdims=True)
    scale = lax.rsqrt(total / width + EPSILON)
    lane = lane_index((tokens, 128))
    tail = jnp.zeros((tokens, 128), F32)
    for which in range(2):
        column = scale[which * tokens : (which + 1) * tokens]
        for part, value in enumerate(three_parts(column)):
            tail = jnp.where(lane == which * 3 + part, value, tail)
    pack[:, 0:64] = input_a.astype(BF16)
    pack[:, 64:128] = input_b.astype(BF16)
    pack[:, 128:192] = known_high.astype(BF16)
    pack[:, 192:256] = (known - known_high).astype(BF16)
    pack[:, 256:384] = tail.astype(BF16)


def weight_kernel(chips, flags, levels, weight, received, out, turned):
    first = flags[0] == 0
    rows, columns = received.shape
    own = jnp.where(first, weight[:, 0:columns].astype(F32), weight[:, columns:].astype(F32))
    other = received[...].astype(F32)
    both = [jnp.where(first, own, other), jnp.where(first, other, own)]
    padded = out.shape[2]
    if padded > 2 * rows:
        both.append(jnp.zeros((padded - 2 * rows, columns), F32))
    whole = jnp.concatenate(both, axis=0)
    turned[0:columns, :] = whole.T
    turned[columns:, :] = jnp.zeros((turned.shape[0] - columns, padded), F32)
    block = columns // chips
    height = out.shape[1]
    lane = lane_index((1, padded))
    value = jnp.where(
        lane % 4 == 0,
        levels[0],
        jnp.where(lane % 4 == 1, levels[1], jnp.where(lane % 4 == 2, levels[2], levels[3])),
    )
    parts = three_parts(value)
    line = jnp.zeros((1, padded), F32)
    for index in range(3):
        line = jnp.where(lane // 4 == index, parts[index], line)
    row = row_index((height, padded))
    for chip in range(chips):
        piece = turned[chip * block : chip * block + height, :]
        piece = jnp.where(row < block, piece, jnp.where(row == block, line, 0.0))
        out[chip] = piece.astype(BF16)


def product_kernel(block, taken, embed, modulation_a, modulation_b, out, columns_out, lines):
    chips, height, padded = taken.shape
    width = embed.shape[1]
    depth = width // chips
    row = row_index((height, 1))
    group = 1 if depth % 128 == 0 else 128 // (depth & -depth)
    for start in range(0, chips, group):
        pieces = []
        for chip in range(start, start + group):
            piece = taken[chip].astype(F32)
            lines[chip : chip + 1, :] = piece[block : block + 1, 0:128]
            pieces.append(jnp.where(row < block, piece, 0.0)[:, 0:depth])
        joined = jnp.concatenate(pieces, axis=1) if group > 1 else pieces[0]
        columns_out[:, start * depth : (start + group) * depth] = joined.astype(BF16)
    weight = columns_out[...]
    embed_b = embed[...]
    embed_f = embed_b.astype(F32)
    plain = dot(weight, embed_b, NT)
    scaled_a = dot(weight, (embed_f * modulation_a[0:1, :]).astype(BF16), NT)
    scaled_b = dot(weight, (embed_f * modulation_b[0:1, :]).astype(BF16), NT)
    shifts = []
    for modulation in (modulation_a, modulation_b):
        shift = modulation[1:2, :]
        high = rounded(shift)
        shifts += [high, shift - high]
    shifts.append(jnp.zeros((4, width), F32))
    offsets = dot(jnp.concatenate(shifts, axis=0).astype(BF16), weight, NT)
    offset_a = offsets[0:1] + offsets[1:2]
    offset_b = offsets[2:3] + offsets[3:4]
    high_a = rounded(offset_a)
    high_b = rounded(offset_b)
    offset_rows = (high_a, offset_a - high_a, high_b, offset_b - high_b)
    pick_shape = (128, 4 * CHANNELS)
    source = row_index(pick_shape)
    pick = jnp.where((source < 12) & (source % 4 == lane_index(pick_shape) // CHANNELS), 1.0, 0.0)
    level = dot(lines[...].astype(BF16), pick.astype(BF16))
    plain_all = jnp.concatenate([plain, plain, plain, plain], axis=1)
    scaled_all = jnp.concatenate([scaled_a, scaled_b, scaled_a, scaled_b], axis=1)
    pad = jnp.zeros((1, 4 * CHANNELS - height), F32)
    row_all = row_index((height, 4 * CHANNELS))
    tail = jnp.zeros((height, 4 * CHANNELS), F32)
    for index, line in enumerate(offset_rows):
        wide = jnp.concatenate([line, pad], axis=1) if 4 * CHANNELS > height else line[:, : 4 * CHANNELS]
        tail = jnp.where(row_all == block + index, wide, tail)
    for chip in range(chips):
        matrix = plain_all + level[chip : chip + 1] * scaled_all
        out[chip] = jnp.where(row_all < block, matrix, tail).astype(BF16)


def token_rows(first, second, start, stop):
    return jnp.concatenate([first[:, start:stop], second[:, start:stop]], axis=0)


def inverse_norms(pack_one, pack_two, which):
    tail = token_rows(pack_one, pack_two, 256, 384).astype(F32)
    at = 3 * which
    return tail[:, at : at + 1] + tail[:, at + 1 : at + 2] + tail[:, at + 2 : at + 3]


def forward(which, levels, packs, matrices, offsets, output_weight, keep, velocity):
    heads = output_weight.shape[0] // HEAD_DIM
    offset = offsets[2 * which : 2 * which + 1, :] + offsets[2 * which + 1 : 2 * which + 2, :]
    lane = lane_index((1, 128))
    chosen = lane // CHANNELS == which
    for sample in range(2):
        one, two = packs[2 * sample], packs[2 * sample + 1]
        rows = jnp.where(chosen, token_rows(one, two, 0, 128).astype(F32), 0.0).astype(BF16)
        scale = inverse_norms(one, two, which)
        shift = offset * levels[2 * sample + which]
        total = jnp.zeros((rows.shape[0], CHANNELS), F32)
        for head in range(heads):
            at = head * 3 * HEAD_DIM
            matrix = matrices[at : at + 3 * HEAD_DIM, sample * 128 : (sample + 1) * 128]
            qkv = dot(rows, matrix, NT) * scale + shift[:, at : at + 3 * HEAD_DIM]
            qkv = qkv.astype(BF16)
            if keep is not None:
                keep[sample, :, at : at + 3 * HEAD_DIM] = qkv
            query = qkv[:, 0:HEAD_DIM]
            key = qkv[:, HEAD_DIM : 2 * HEAD_DIM]
            value = qkv[:, 2 * HEAD_DIM :]
            scores = dot(query, key, NT) * (HEAD_DIM**-0.5)
            top = jnp.max(scores, axis=-1, keepdims=True)
            powers = jnp.exp(scores - top)
            probs = powers / jnp.sum(powers, axis=-1, keepdims=True)
            mixed = dot(probs.astype(BF16), value).astype(BF16)
            total = total + dot(mixed, output_weight[head * HEAD_DIM : (head + 1) * HEAD_DIM, :])
        velocity[:, sample * CHANNELS : (sample + 1) * CHANNELS] = total


def second_pass_kernel(
    block, levels, taken, own, seq, core, both, output_weight, matrices, offsets, keep, velocity, stacked
):
    chips = taken.shape[0]
    lines = []
    for chip in range(chips):
        piece = taken[chip].astype(F32)
        stacked[chip * block : (chip + 1) * block, :] = piece[0:block]
        lines.append(piece[block : block + 4, 0:block] if block <= 256 else None)
    matrices[...] = stacked[...].astype(BF16)
    offsets[...] = jnp.concatenate([jnp.concatenate(lines, axis=1), jnp.zeros((4, offsets.shape[1]), F32)], axis=0)
    forward(1, levels, (own, seq, core, both), matrices, offsets, output_weight, keep, velocity)


def first_pass_kernel(levels, matrices, offsets, own, seq, core, both, output_weight, velocity):
    forward(0, levels, (own, seq, core, both), matrices, offsets, output_weight, None, velocity)


def swap_tokens(value):
    half = value.shape[0] // 2
    return jnp.concatenate([value[half:], value[:half]], axis=0)


def backward_kernel(
    block, flags, levels, kept, own, seq, core, both, vel_own, vel_seq, vel_core, vel_both, output_weight, out, gathered
):
    critic = flags[1] == 1
    packs = (own, seq, core, both)
    heads = output_weight.shape[0] // HEAD_DIM
    velocity = vel_own[...] + swap_tokens(vel_seq[...])
    crossing = vel_core[...] + swap_tokens(vel_both[...])
    lane = lane_index((1, 128))
    grads, rows = [], []
    for sample in range(2):
        one, two = packs[2 * sample], packs[2 * sample + 1]
        known = token_rows(one, two, 128, 256).astype(F32)
        known = known[:, 0:CHANNELS] + known[:, CHANNELS:]
        at = sample * CHANNELS
        back = (1 - sample) * CHANNELS
        total = velocity[:, at : at + CHANNELS] + crossing[:, back : back + CHANNELS]
        grads.append(jnp.where(critic, total - known, known).astype(BF16))
        level = levels[2 * sample + 1]
        scaled = token_rows(one, two, 0, 128).astype(F32) * (inverse_norms(one, two, 1) * level)
        level_line = jnp.full((1, 128), level, F32)
        high = rounded(level_line)
        ends = jnp.where(lane == 0, high, jnp.where(lane == 1, level_line - high, 0.0))
        scaled = jnp.where(lane < CHANNELS, ends, scaled)
        rows.append(scaled.T.astype(BF16))
    for head in range(heads):
        at = head * 3 * HEAD_DIM
        total = None
        for sample in range(2):
            qkv = kept[sample, :, at : at + 3 * HEAD_DIM]
            query = qkv[:, 0:HEAD_DIM]
            key = qkv[:, HEAD_DIM : 2 * HEAD_DIM]
            value = qkv[:, 2 * HEAD_DIM :]
            grad_mixed = dot(grads[sample], output_weight[head * HEAD_DIM : (head + 1) * HEAD_DIM, :], NT).astype(BF16)
            scores = dot(key, query, NT) * (HEAD_DIM**-0.5)
            top = jnp.max(scores, axis=0, keepdims=True)
            powers = jnp.exp(scores - top)
            probs = powers / jnp.sum(powers, axis=0, keepdims=True)
            grad_value = dot(probs.astype(BF16), grad_mixed)
            grad_probs = dot(value, grad_mixed, NT)
            inner = jnp.sum(grad_probs * probs, axis=0, keepdims=True)
            grad_scores = (probs * (grad_probs - inner) * (HEAD_DIM**-0.5)).astype(BF16)
            grad_key = dot(grad_scores, query)
            grad_query = dot(grad_scores, key, TN)
            grad = jnp.concatenate([grad_query, grad_key, grad_value], axis=1).astype(BF16)
            term = dot(rows[sample], grad)
            total = term if total is None else total + term
        gathered[at : at + 3 * HEAD_DIM, :] = total.T
    columns = heads * 3 * HEAD_DIM
    gathered[columns:, :] = jnp.zeros((gathered.shape[0] - columns, 128), F32)
    chips, height = out.shape[0], out.shape[1]
    row = row_index((height, 128))
    for chip in range(chips):
        piece = gathered[chip * block : chip * block + height, :]
        out[chip] = jnp.where(row < block, piece, 0.0).astype(BF16)


def closing_kernel(factor, flags, taken, weight, embed, kept, sent):
    first = flags[0] == 0
    total = taken[0].astype(F32)
    for chip in range(1, taken.shape[0]):
        total = total + taken[chip].astype(F32)
    turned = total.T
    high = turned.astype(BF16)
    low = (turned - high.astype(F32)).astype(BF16)
    half = embed.shape[1] // 2
    step = half // 3
    halves = []
    for start in range(0, 2 * half, step):
        columns = weight[:, start : start + step]
        product = dot(high, columns) + dot(low, columns)
        scale = jnp.sum(product[CHANNELS:] * embed[:, start : start + step].astype(F32), axis=0, keepdims=True)
        shift = product[0:1] + product[1:2]
        halves.append(jnp.concatenate([scale, shift], axis=0) * factor)
    left = jnp.concatenate(halves[:3], axis=1)
    right = jnp.concatenate(halves[3:], axis=1)
    kept[...] = jnp.where(first, left, right)
    sent[...] = jnp.where(first, right, left)


def call(kernel, out_shapes, inputs, scalars, scratch=(), flops=0, moved=0):
    specs = [pl.BlockSpec(memory_space=pltpu.SMEM)] * scalars
    specs += [pl.BlockSpec(memory_space=pltpu.VMEM)] * (len(inputs) - scalars)
    return pl.pallas_call(
        kernel,
        out_shape=out_shapes,
        in_specs=specs,
        out_specs=jax.tree.map(lambda _: pl.BlockSpec(memory_space=pltpu.VMEM), out_shapes),
        scratch_shapes=list(scratch),
        compiler_params=pltpu.CompilerParams(vmem_limit_bytes=28 * 2**20),
        cost_estimate=pl.CostEstimate(flops=flops, bytes_accessed=moved, transcendentals=0),
    )(*inputs)


def struct(shape, dtype):
    return jax.ShapeDtypeStruct(shape, dtype)


def other_core(value):
    return lax.ppermute(value, "fsdp", [(i, i ^ 1) for i in range(lax.axis_size("fsdp"))])


def other_half(value):
    return lax.ppermute(value, "seq", [(0, 1), (1, 0)])


def other_both(value):
    count = lax.axis_size("fsdp") * 2
    return lax.ppermute(value, ("fsdp", "seq"), [(i, i ^ 3) for i in range(count)])


def between_chips(value):
    count = lax.axis_size("fsdp")
    groups = [list(range(core, count, 2)) for core in range(2)]
    return lax.all_to_all(value, "fsdp", 0, 0, tiled=True, axis_index_groups=groups)


def per_device(
    base_latents,
    noise_latents,
    noise_levels,
    replay_latents,
    replay_levels,
    cotangent,
    embed_weight,
    qkv_weight,
    output_weight,
    modulation,
):
    is_critic = lax.axis_index("role") == 1
    core = lax.rem(lax.axis_index("fsdp"), 2)
    devices = lax.axis_size("fsdp")
    chips = devices // 2
    embed = embed_weight[0]
    weight = qkv_weight[0]
    width = embed.shape[1]
    columns = weight.shape[1] // 2
    block = columns // chips
    height = round_up(block + 4, 8)
    padded = round_up(2 * weight.shape[0], 128)
    tokens = base_latents.shape[2]
    out_rows = output_weight.shape[1] // 2
    out_half = jnp.where(core == 0, output_weight[0, :out_rows], output_weight[0, out_rows:])

    received = other_core(jnp.where(core == 0, weight[:, columns:], weight[:, :columns]))
    level_two = jnp.where(is_critic, noise_levels[0, 0], replay_levels[0, 0])
    own_levels = jnp.stack([noise_levels[0, 0], level_two])
    levels = jnp.concatenate([own_levels, other_core(own_levels)])
    flags = jnp.stack([core.astype(jnp.int32), is_critic.astype(jnp.int32)])
    modulation_a = modulation[0, 0]
    modulation_b = jnp.where(is_critic, modulation[0, 1], modulation[0, 0])

    own = call(
        pack_kernel,
        struct((tokens, 384), BF16),
        (flags, own_levels, base_latents[0, 0], noise_latents[0, 0], replay_latents[0, 0], cotangent[0, 0], embed),
        2,
    )
    seq, near, both = other_half(own), other_core(own), other_both(own)

    turned = call(
        functools.partial(weight_kernel, chips),
        struct((chips, height, padded), BF16),
        (flags, levels, weight, received),
        2,
        [pltpu.VMEM((columns + height - block, padded), F32)],
    )
    taken = between_chips(turned)
    matrices, own_columns = call(
        functools.partial(product_kernel, block),
        (struct((chips, height, 4 * CHANNELS), BF16), struct((height, width), BF16)),
        (taken, embed, modulation_a, modulation_b),
        0,
        [pltpu.VMEM((chips, 128), F32)],
    )
    taken = between_chips(matrices)

    packs = (own, seq, near, both)
    whole, offsets, kept, vel_b = call(
        functools.partial(second_pass_kernel, block),
        (
            struct((columns, 4 * CHANNELS), BF16),
            struct((8, columns), F32),
            struct((2, 2 * tokens, columns), BF16),
            struct((2 * tokens, 2 * CHANNELS), F32),
        ),
        (levels, taken) + packs + (out_half,),
        1,
        [pltpu.VMEM((columns, 4 * CHANNELS), F32)],
    )
    vel_seq, vel_near, vel_both = other_half(vel_b), other_core(vel_b), other_both(vel_b)
    vel_a = call(
        first_pass_kernel,
        struct((2 * tokens, 2 * CHANNELS), F32),
        (levels, whole, offsets) + packs + (out_half,),
        1,
    )
    products = call(
        functools.partial(backward_kernel, block),
        struct((chips, height, 128), BF16),
        (flags, levels, kept) + packs + (vel_b, vel_seq, vel_near, vel_both, out_half),
        2,
        [pltpu.VMEM((columns + height - block, 128), F32)],
    )

    own_a = vel_a[:tokens, :CHANNELS] + other_half(vel_a[tokens:, :CHANNELS])
    own_a = own_a + other_core(vel_a[:tokens, CHANNELS:]) + other_both(vel_a[tokens:, CHANNELS:])
    own_b = vel_b[:tokens, :CHANNELS] + vel_seq[tokens:, :CHANNELS]
    own_b = own_b + vel_near[:tokens, CHANNELS:] + vel_both[tokens:, CHANNELS:]
    payload = jnp.where(is_critic, own_b - own_a, own[:, :CHANNELS].astype(F32) - own_levels[0] * own_a)
    crossed = lax.ppermute(payload.astype(BF16), "role", [(0, 1), (1, 0)])

    samples = devices * base_latents.shape[1]
    kept_half, sent_half = call(
        functools.partial(closing_kernel, 1.0 / (samples * 2 * tokens)),
        (struct((2, width // 2), F32), struct((2, width // 2), F32)),
        (flags, between_chips(products), own_columns, embed),
        1,
    )
    total = kept_half + other_core(sent_half)
    total = total + other_half(total)
    spread = between_chips(jnp.broadcast_to(total[None], (chips,) + total.shape))
    total = jnp.sum(spread, axis=0)
    near_total = other_core(total)
    mod_grads = jnp.where(
        core == 0,
        jnp.concatenate([total, near_total], axis=1),
        jnp.concatenate([near_total, total], axis=1),
    )
    return (crossed[None, None], mod_grads[None])


def solution(mesh):
    return jax.shard_map(
        per_device,
        mesh=mesh,
        in_specs=(
            P("role", "fsdp", "seq", None),
            P("role", "fsdp", "seq", None),
            P("role", "fsdp"),
            P("role", "fsdp", "seq", None),
            P("role", "fsdp"),
            P("role", "fsdp", "seq", None),
            P("role", None, None),
            P("role", "fsdp", "seq"),
            P("role", "seq", None),
            P("role", None, None, None),
        ),
        out_specs=(P("role", "fsdp", "seq", None), P("role", None, None)),
        check_vma=False,
    )
```

time: 738 us -> 124 us (0.17)
  blocking collectives: 557 us -> 14.5 us
  waiting for transfers between devices: 94.6 us -> 36.4 us
  starting transfers between devices: 2.62 us -> 46.2 us
  matrix products: 29 us -> 0 us
  local copies, waits for them, and re-layouts: 25.7 us -> 3.35 us
  Pallas kernels: 0 us -> 17.9 us
  between operations: 15.7 us -> 2.2 us
  other arithmetic: 11.5 us -> 2.86 us
    psum x1 -> x0, blocking collectives: 550 us -> none  [per_device(): lax.psum((grad_scale, grad_shift), ('fsdp', 'seq'))]
    all_gather x1 -> x0, waiting for transfers between devices: 87.5 us -> none  [per_device(): lax.all_gather(weight_shard, 'fsdp', axis=0, tiled=True)]
    dot_general x11 -> x0, matrix products: 29 us -> none  [the longest x1 12.4 us: per_device(): jnp.dot(hidden, lax.all_gather(weight_shard, 'fsdp', axis=0, tiled=True),...]
    ppermute x1 -> x15, starting transfers between devices: 2.54 us -> 25 us  [the longest x3 11.6 us: other_both(): lax.ppermute(value, ('fsdp', 'seq'), [(i, i ^ 3) for i in range(count)])]
    all_to_all x0 -> x3, starting transfers between devices: none -> 21.1 us  [between_chips(): lax.all_to_all(value, 'fsdp', 0, 0, tiled=True, axis_index_groups=groups)]
    ppermute x1 -> x15, waiting for transfers between devices: 0.01 us -> 18.7 us  [the longest x3 10.6 us: other_both(): lax.ppermute(value, ('fsdp', 'seq'), [(i, i ^ 3) for i in range(count)])]
    pallas_call x0 -> x7, Pallas kernels: none -> 17.9 us  [call(): pl.pallas_call(kernel, out_shape=out_shapes, in_specs=specs, out_specs=ja...]
    all_to_all x0 -> x3, waiting for transfers between devices: none -> 17.6 us  [between_chips(): lax.all_to_all(value, 'fsdp', 0, 0, tiled=True, axis_index_groups=groups)]
  transfers between devices with their start and end apart: 3 -> 18, of which waited for: 2 -> 11; matrix products, arithmetic and copies ran while one was open for 3% -> 3% of each run, Pallas kernels for 0% -> 4%
where the time goes in v1:
time: 124 us; the launch traced here: 123 us
  starting transfers between devices  46.2 us (37%)
  waiting for transfers between devices  36.4 us (29%)
  Pallas kernels  17.9 us (14%)
  blocking collectives  14.5 us (12%)
  local copies, waits for them, and re-layouts  3.35 us (3%)
  other arithmetic  2.86 us (2%)
  between operations  2.2 us (2%)
    all_to_all x3, starting transfers between devices, between_chips(): lax.all_to_all(value, 'fsdp', 0, 0, tiled=True, axis_index_groups=groups)  21.1 us
    pallas_call x7, Pallas kernels, call(): pl.pallas_call(kernel, out_shape=out_shapes, in_specs=specs, out_specs=ja...  17.9 us
    all_to_all x3, waiting for transfers between devices, between_chips(): lax.all_to_all(value, 'fsdp', 0, 0, tiled=True, axis_index_groups=groups)  17.6 us
    all_to_all x1, blocking collectives, between_chips(): lax.all_to_all(value, 'fsdp', 0, 0, tiled=True, axis_index_groups=groups)  14.5 us
    ppermute x3, starting transfers between devices, other_both(): lax.ppermute(value, ('fsdp', 'seq'), [(i, i ^ 3) for i in range(count)])  11.6 us
    ppermute x3, waiting for transfers between devices, other_both(): lax.ppermute(value, ('fsdp', 'seq'), [(i, i ^ 3) for i in range(count)])  10.6 us
    ppermute x7, starting transfers between devices, other_core(): lax.ppermute(value, 'fsdp', [(i, i ^ 1) for i in range(lax.axis_size('fsd...  9.14 us
    ppermute x4, waiting for transfers between devices, other_half(): return lax.ppermute(value, 'seq', [(0, 1), (1, 0)])  6.73 us
  transfers between devices with their start and end apart: 18, of which 11 were waited for; matrix products, arithmetic and copies ran while one was open for 3% of the time, Pallas kernels for 4%

profile of v1, /device:TPU:1, one launch (start us, length us, event | category | flops | bytes accessed | tf_op | source)
XLA Modules:
  0.0 123.4 jit_solution(9583312856476325163)
XLA Ops:
  0.6 0.0 copy-start.2
  2.0 0.1 pad_maximum_fusion.levels
  2.1 3.3 %collective-permute-start = (f32[2]{0:T(128)S(1)}, f32[2]{0:T(128)S(1)}, u32[]{:S(2)}, u32[]{:S(2)}) collective-permute-start(f32[2]{0:T(128)S(1)} %pad_maximum_fusion.levels), channel_id=1, source_target_pairs={{0,2},{2,0},{4,6},{6,4},{8,10},{10,8},{12,14},{14,12},{16,18},{18,... | collective-permute-start | bytes 32 | tf_op jit(solution)/shard_map/ppermute | solution.py:318
  5.3 1.0 slice_select_fusion
  6.3 0.1 collective-permute-start.1
  6.4 0.8 bitcast_select_fusion.modulation_b
  7.2 0.1 pad_add_fusion.flags
  7.3 0.0 collective-permute-done
  7.3 0.1 pad_maximum_fusion.1.levels
  7.4 0.4 collective-permute-done.1.received
  7.7 0.9 copy-done.1
  8.7 1.5 %shard_map.113 = bf16[32,40,128]{2,1,0:T(8,128)(2,1)} custom-call(s32[2]{0:T(128)S(1)} %pad_add_fusion.flags, f32[4]{0:T(128)S(1)} %pad_maximum_fusion.1.levels, bf16[48,2304]{1,0:T(8,128)(2,1)S(1)} %bitcast.32, bf16[48,1152]{1,0:T(8,128)(2,1)S(1)} %collective-permute-done.1.received), custom_call_target="tpu_custom_call" | custom-call | tf_op jit(solution)/shard_map/pallas_call | solution.py:302
  10.2 9.3 %all-to-all-start = ((bf16[32,40,128]{2,1,0:T(8,128)(2,1)}), bf16[32,40,128]{2,1,0:T(8,128)(2,1)S(1)}, u32[]{:S(2)}, u32[]{:S(2)}) async-start(bf16[32,40,128]{2,1,0:T(8,128)(2,1)} %shard_map.113), calls=%async_computation | async-start | bytes 655360 | tf_op jit(solution)/shard_map/all_to_all | solution.py:333
  19.5 0.0 copy-start.4
  19.5 0.0 copy-start.5
  19.5 0.0 copy-start.6
  19.5 0.0 copy-start.7
  19.5 10.7 %all-to-all-done.taken = bf16[32,40,128]{2,1,0:T(8,128)(2,1)S(1)} async-done(((bf16[32,40,128]{2,1,0:T(8,128)(2,1)}), bf16[32,40,128]{2,1,0:T(8,128)(2,1)S(1)}, u32[]{:S(2)}, u32[]{:S(2)}) %all-to-all-start) | async-done | bytes 327712 | tf_op jit(solution)/shard_map/all_to_all | solution.py:333
  30.2 1.7 %shard_map.114 = (bf16[32,40,256]{2,1,0:T(8,128)(2,1)}, bf16[40,3072]{1,0:T(8,128)(2,1)S(1)}) custom-call(bf16[32,40,128]{2,1,0:T(8,128)(2,1)S(1)} %all-to-all-done.taken, bf16[64,3072]{1,0:T(8,128)(2,1)S(1)} %bitcast.28, f32[2,3072]{1,0:T(2,128)S(1)} %slice_bitcast_fusion.modulation_a, f32[2,3072]{1,0:T(2,128)S(1)} %bitcast_select_fusion.modulation_b), custom_call_target="tpu_custom_call" | custom-call | tf_op jit(solution)/shard_map/pallas_call | solution.py:302
  31.9 7.4 %all-to-all-start.1 = ((bf16[32,40,256]{2,1,0:T(8,128)(2,1)}), bf16[32,40,256]{2,1,0:T(8,128)(2,1)S(1)}, u32[]{:S(2)}, u32[]{:S(2)}) async-start(bf16[32,40,256]{2,1,0:T(8,128)(2,1)} %get-tuple-element.10), calls=%async_computation.1 | async-start | bytes 1310720 | tf_op jit(solution)/shard_map/all_to_all | solution.py:333
  39.3 0.1 copy.26
  39.4 0.1 copy.27
  39.5 0.1 copy.28
  39.7 0.1 copy.29
  39.8 1.2 shard_map.115.own
  41.0 2.5 %collective-permute-start.4 = (bf16[128,384]{1,0:T(8,128)(2,1)S(1)}, bf16[128,384]{1,0:T(8,128)(2,1)S(1)}, u32[]{:S(2)}, u32[]{:S(2)}) collective-permute-start(bf16[128,384]{1,0:T(8,128)(2,1)S(1)} %shard_map.115.own), channel_id=1, source_target_pairs={{0,3},{1,2},{2,1},{3,0},{4,7},{5,6},{6,5},{7,4},{8,11},{9,10},{10,... | collective-permute-start | bytes 294920 | tf_op jit(solution)/shard_map/ppermute | solution.py:327
  43.5 0.2 collective-permute-start.2
  43.7 0.1 copy.36
  43.8 0.1 copy.35
  44.0 3.1 %collective-permute-done.4.both = bf16[128,384]{1,0:T(8,128)(2,1)S(1)} collective-permute-done((bf16[128,384]{1,0:T(8,128)(2,1)S(1)}, bf16[128,384]{1,0:T(8,128)(2,1)S(1)}, u32[]{:S(2)}, u32[]{:S(2)}) %collective-permute-start.4) | collective-permute-done | bytes 98336 | tf_op jit(solution)/shard_map/ppermute | solution.py:327
  47.1 0.0 collective-permute-done.3.core
  47.1 1.7 %collective-permute-done.2.seq = bf16[128,384]{1,0:T(8,128)(2,1)S(1)} collective-permute-done((bf16[128,384]{1,0:T(8,128)(2,1)S(1)}, bf16[128,384]{1,0:T(8,128)(2,1)S(1)}, u32[]{:S(2)}, u32[]{:S(2)}) %collective-permute-start.2) | collective-permute-done | bytes 98336 | tf_op jit(solution)/shard_map/ppermute | solution.py:322
  48.9 7.0 %all-to-all-done.1.taken = bf16[32,40,256]{2,1,0:T(8,128)(2,1)S(1)} async-done(((bf16[32,40,256]{2,1,0:T(8,128)(2,1)}), bf16[32,40,256]{2,1,0:T(8,128)(2,1)S(1)}, u32[]{:S(2)}, u32[]{:S(2)}) %all-to-all-start.1) | async-done | bytes 655392 | tf_op jit(solution)/shard_map/all_to_all | solution.py:333
  55.8 4.0 %shard_map.116 = (bf16[1152,256]{1,0:T(8,128)(2,1)S(1)}, f32[8,1152]{1,0:T(8,128)S(1)}, bf16[2,256,1152]{2,1,0:T(8,128)(2,1)S(1)}, f32[256,128]{1,0:T(8,128)S(1)}) custom-call(f32[4]{0:T(128)S(1)} %pad_maximum_fusion.1.levels, bf16[32,40,256]{2,1,0:T(8,128)(2,1)S(1)} %all-to-all-done.1.taken, bf16[128,384]{1,0:T(8,128)(2,1)S(1)} %shard_map.115.own, ...), custom_call_target="tpu_custom_call" | custom-call | tf_op jit(solution)/shard_map/pallas_call | solution.py:302
  59.8 6.3 %collective-permute-start.7 = (f32[256,128]{1,0:T(8,128)S(1)}, f32[256,128]{1,0:T(8,128)S(1)}, u32[]{:S(2)}, u32[]{:S(2)}) collective-permute-start(f32[256,128]{1,0:T(8,128)S(1)} %get-tuple-element.11.vel_own), channel_id=1, source_target_pairs={{0,3},{1,2},{2,1},{3,0},{4,7},{5,6},{6,5},{7,4},{8,11},{9,10},{10,... | collective-permute-start | bytes 393224 | tf_op jit(solution)/shard_map/ppermute | solution.py:327
  66.1 0.0 collective-permute-start.6
  66.1 0.2 collective-permute-start.5
  66.3 3.9 %collective-permute-done.7.vel_both = f32[256,128]{1,0:T(8,128)S(1)} collective-permute-done((f32[256,128]{1,0:T(8,128)S(1)}, f32[256,128]{1,0:T(8,128)S(1)}, u32[]{:S(2)}, u32[]{:S(2)}) %collective-permute-start.7) | collective-permute-done | bytes 131104 | tf_op jit(solution)/shard_map/ppermute | solution.py:327
  70.1 0.0 collective-permute-done.6.vel_core
  70.2 2.8 %collective-permute-done.5.vel_seq = f32[256,128]{1,0:T(8,128)S(1)} collective-permute-done((f32[256,128]{1,0:T(8,128)S(1)}, f32[256,128]{1,0:T(8,128)S(1)}, u32[]{:S(2)}, u32[]{:S(2)}) %collective-permute-start.5) | collective-permute-done | bytes 131104 | tf_op jit(solution)/shard_map/ppermute | solution.py:322
  73.0 4.5 %shard_map.118 = bf16[32,40,128]{2,1,0:T(8,128)(2,1)S(1)} custom-call(s32[2]{0:T(128)S(1)} %pad_add_fusion.flags, f32[4]{0:T(128)S(1)} %pad_maximum_fusion.1.levels, bf16[2,256,1152]{2,1,0:T(8,128)(2,1)S(1)} %get-tuple-element.14.kept, bf16[128,384]{1,0:T(8,128)(2,1)S(1)} %shard_map.115.own, bf16[128,384]{1,0:T(8,128)(2,1)S(1)} %collective-permute-done.2.seq, ...), custom_call_target="tpu_custom_call" | custom-call | tf_op jit(solution)/shard_map/pallas_call | solution.py:302
  77.4 14.5 %all_to_all.20.taken = bf16[32,40,128]{2,1,0:T(8,128)(2,1)S(1)} all-to-all(bf16[32,40,128]{2,1,0:T(8,128)(2,1)S(1)} %shard_map.118), channel_id=1, replica_groups={{0,4,8,12,16,20,24,28,32,36,40,44,48,52,56,60,64,68,72,76,80,84,88,92,9..., dimensions={0} | all-to-all | bytes 655360 | tf_op jit(solution)/shard_map/all_to_all | solution.py:333
  91.9 1.2 shard_map.119
  93.1 4.3 %collective-permute-start.12 = (f32[2,1536]{1,0:T(2,128)S(1)}, f32[2,1536]{1,0:T(2,128)S(1)}, u32[]{:S(2)}, u32[]{:S(2)}) collective-permute-start(f32[2,1536]{1,0:T(2,128)S(1)} %get-tuple-element.17), channel_id=1, source_target_pairs={{0,2},{2,0},{4,6},{6,4},{8,10},{10,8},{12,14},{14,12},{16,18},{18,... | collective-permute-start | bytes 36872 | tf_op jit(solution)/shard_map/ppermute | solution.py:318
  97.4 0.8 collective-permute-done.12
  98.3 0.5 collective-permute-start.13
  98.7 2.2 %collective-permute-done.13 = f32[2,1536]{1,0:T(2,128)S(1)} collective-permute-done((f32[2,1536]{1,0:T(2,128)S(1)}, f32[2,1536]{1,0:T(2,128)S(1)}, u32[]{:S(2)}, u32[]{:S(2)}) %collective-permute-start.13) | collective-permute-done | bytes 12320 | tf_op jit(solution)/shard_map/ppermute | solution.py:322
  100.9 0.9 broadcast_in_dim.5
  101.8 4.4 %all-to-all-start.3 = ((f32[32,2,1536]{2,1,0:T(2,128)}), f32[32,2,1536]{2,1,0:T(2,128)S(1)}, u32[]{:S(2)}, u32[]{:S(2)}) async-start(f32[32,2,1536]{2,1,0:T(2,128)} %broadcast_in_dim.5), calls=%async_computation.3 | async-start | bytes 786432 | tf_op jit(solution)/shard_map/all_to_all | solution.py:333
  106.2 3.9 %shard_map.117 = f32[256,128]{1,0:T(8,128)S(1)} custom-call(f32[4]{0:T(128)S(1)} %pad_maximum_fusion.1.levels, bf16[1152,256]{1,0:T(8,128)(2,1)S(1)} %get-tuple-element.12.matrices, f32[8,1152]{1,0:T(8,128)S(1)} %get-tuple-element.13.offsets, bf16[128,384]{1,0:T(8,128)(2,1)S(1)} %shard_map.115.own, bf16[128,384]{1,0:T(8,128)(2,1)S(1)} %collective-permute-done.2.seq, ...), custom_call_target="tpu_custom_call" | custom-call | tf_op jit(solution)/shard_map/pallas_call | solution.py:302
  110.1 0.1 fusion.5
  110.2 0.6 collective-permute-start.8
  110.8 2.9 %collective-permute-start.10 = (f32[128,64]{1,0:T(8,128)S(1)}, f32[128,64]{1,0:T(8,128)S(1)}, u32[]{:S(2)}, u32[]{:S(2)}) collective-permute-start(f32[128,64]{1,0:T(8,128)S(1)} %get-tuple-element.25), channel_id=1, source_target_pairs={{0,3},{1,2},{2,1},{3,0},{4,7},{5,6},{6,5},{7,4},{8,11},{9,10},{10,... | collective-permute-start | bytes 98312 | tf_op jit(solution)/shard_map/ppermute | solution.py:327
  113.7 0.0 collective-permute-start.9
  113.8 0.0 collective-permute-done.8
  113.8 3.6 %collective-permute-done.10 = f32[128,64]{1,0:T(8,128)S(1)} collective-permute-done((f32[128,64]{1,0:T(8,128)S(1)}, f32[128,64]{1,0:T(8,128)S(1)}, u32[]{:S(2)}, u32[]{:S(2)}) %collective-permute-start.10) | collective-permute-done | bytes 32800 | tf_op jit(solution)/shard_map/ppermute | solution.py:327
  117.4 0.0 collective-permute-done.9
  117.4 0.1 fusion.4
  117.5 2.8 %collective-permute-start.11 = (bf16[128,64]{1,0:T(8,128)(2,1)S(1)}, bf16[128,64]{1,0:T(8,128)(2,1)S(1)}, u32[]{:S(2)}, u32[]{:S(2)}) collective-permute-start(bf16[128,64]{1,0:T(8,128)(2,1)S(1)} %fusion.4), channel_id=1, source_target_pairs={{0,128},{128,0},{1,129},{129,1},{2,130},{130,2},{3,131},{131,3},{4... | collective-permute-start | bytes 49160 | tf_op jit(solution)/shard_map/ppermute | solution.py:429
  120.3 0.1 reduce_sum.9
  120.4 1.5 %collective-permute-start.14 = (f32[2,1536]{1,0:T(2,128)S(1)}, f32[2,1536]{1,0:T(2,128)S(1)}, u32[]{:S(2)}, u32[]{:S(2)}) collective-permute-start(f32[2,1536]{1,0:T(2,128)S(1)} %reduce_sum.9), channel_id=1, source_target_pairs={{0,2},{2,0},{4,6},{6,4},{8,10},{10,8},{12,14},{14,12},{16,18},{18,... | collective-permute-start | bytes 36872 | tf_op jit(solution)/shard_map/ppermute | solution.py:318
  121.9 0.7 copy.33
  122.6 0.1 collective-permute-done.14
  122.7 0.6 maximum_select_fusion
  (18 shorter events, 0.1 us)
Async XLA Ops:
  0.6 18.8 %copy-start.2 = (f32[1,2,2,3072]{3,2,1,0:T(2,128)S(1)}, f32[1,2,2,3072]{3,2,1,0:T(2,128)}, u32[]{:S(2)}) copy-start(f32[1,2,2,3072]{3,2,1,0:T(2,128)} %param.19) | copy-start | bytes 147460
  0.6 29.6 %copy-start = (bf16[1,64,3072]{2,1,0:T(8,128)(2,1)S(1)}, bf16[1,64,3072]{2,1,0:T(8,128)(2,1)}, u32[]{:S(2)}) copy-start(bf16[1,64,3072]{2,1,0:T(8,128)(2,1)} %param.16) | copy-start | bytes 1179652
  2.1 5.2 %collective-permute-start = (f32[2]{0:T(128)S(1)}, f32[2]{0:T(128)S(1)}, u32[]{:S(2)}, u32[]{:S(2)}) collective-permute-start(f32[2]{0:T(128)S(1)} %pad_maximum_fusion.levels), channel_id=1, source_target_pairs={{0,2},{2,0},{4,6},{6,4},{8,10},{10,8},{12,14},{14,12},{16,18},{18,... | collective-permute-start | bytes 32 | tf_op jit(solution)/shard_map/ppermute | solution.py:318
  6.3 1.4 %collective-permute-start.1 = (bf16[48,1152]{1,0:T(8,128)(2,1)S(1)}, bf16[48,1152]{1,0:T(8,128)(2,1)S(1)}, u32[]{:S(2)}, u32[]{:S(2)}) collective-permute-start(bf16[48,1152]{1,0:T(8,128)(2,1)S(1)} %slice_select_fusion), channel_id=1, source_target_pairs={{0,2},{2,0},{4,6},{6,4},{8,10},{10,8},{12,14},{14,12},{16,18},{18,... | collective-permute-start | bytes 331784 | tf_op jit(solution)/shard_map/ppermute | solution.py:318
  7.7 0.9 copy-start.1
  10.2 20.1 %all-to-all-start = ((bf16[32,40,128]{2,1,0:T(8,128)(2,1)}), bf16[32,40,128]{2,1,0:T(8,128)(2,1)S(1)}, u32[]{:S(2)}, u32[]{:S(2)}) async-start(bf16[32,40,128]{2,1,0:T(8,128)(2,1)} %shard_map.113), calls=%async_computation | async-start | bytes 655360 | tf_op jit(solution)/shard_map/all_to_all | solution.py:333
  19.5 19.8 %copy-start.4 = (bf16[1,1,128,64]{2,3,1,0:T(8,128)(2,1)S(1)}, bf16[1,1,128,64]{2,3,1,0:T(8,128)(2,1)}, u32[]{:S(2)}) copy-start(bf16[1,1,128,64]{2,3,1,0:T(8,128)(2,1)} %param.10) | copy-start | bytes 49156
  19.5 19.9 %copy-start.5 = (bf16[1,1,128,64]{2,3,1,0:T(8,128)(2,1)S(1)}, bf16[1,1,128,64]{2,3,1,0:T(8,128)(2,1)}, u32[]{:S(2)}) copy-start(bf16[1,1,128,64]{2,3,1,0:T(8,128)(2,1)} %param.11) | copy-start | bytes 49156
  19.5 20.0 %copy-start.6 = (bf16[1,1,128,64]{2,3,1,0:T(8,128)(2,1)S(1)}, bf16[1,1,128,64]{2,3,1,0:T(8,128)(2,1)}, u32[]{:S(2)}) copy-start(bf16[1,1,128,64]{2,3,1,0:T(8,128)(2,1)} %param.13) | copy-start | bytes 49156
  19.5 20.2 %copy-start.7 = (bf16[1,1,128,64]{2,3,1,0:T(8,128)(2,1)S(1)}, bf16[1,1,128,64]{2,3,1,0:T(8,128)(2,1)}, u32[]{:S(2)}) copy-start(bf16[1,1,128,64]{2,3,1,0:T(8,128)(2,1)} %param.15) | copy-start | bytes 49156
  31.9 11.8 %copy-start.3 = (bf16[1,768,64]{1,2,0:T(8,128)(2,1)S(1)}, bf16[1,768,64]{1,2,0:T(8,128)(2,1)}, u32[]{:S(2)}) copy-start(bf16[1,768,64]{1,2,0:T(8,128)(2,1)} %param.18) | copy-start | bytes 294916
  31.9 24.0 %all-to-all-start.1 = ((bf16[32,40,256]{2,1,0:T(8,128)(2,1)}), bf16[32,40,256]{2,1,0:T(8,128)(2,1)S(1)}, u32[]{:S(2)}, u32[]{:S(2)}) async-start(bf16[32,40,256]{2,1,0:T(8,128)(2,1)} %get-tuple-element.10), calls=%async_computation.1 | async-start | bytes 1310720 | tf_op jit(solution)/shard_map/all_to_all | solution.py:333
  41.0 6.1 %collective-permute-start.4 = (bf16[128,384]{1,0:T(8,128)(2,1)S(1)}, bf16[128,384]{1,0:T(8,128)(2,1)S(1)}, u32[]{:S(2)}, u32[]{:S(2)}) collective-permute-start(bf16[128,384]{1,0:T(8,128)(2,1)S(1)} %shard_map.115.own), channel_id=1, source_target_pairs={{0,3},{1,2},{2,1},{3,0},{4,7},{5,6},{6,5},{7,4},{8,11},{9,10},{10,... | collective-permute-start | bytes 294920 | tf_op jit(solution)/shard_map/ppermute | solution.py:327
  43.5 3.6 %collective-permute-start.3 = (bf16[128,384]{1,0:T(8,128)(2,1)S(1)}, bf16[128,384]{1,0:T(8,128)(2,1)S(1)}, u32[]{:S(2)}, u32[]{:S(2)}) collective-permute-start(bf16[128,384]{1,0:T(8,128)(2,1)S(1)} %shard_map.115.own), channel_id=1, source_target_pairs={{0,2},{2,0},{4,6},{6,4},{8,10},{10,8},{12,14},{14,12},{16,18},{18,... | collective-permute-start | bytes 294920 | tf_op jit(solution)/shard_map/ppermute | solution.py:318
  43.5 5.4 %collective-permute-start.2 = (bf16[128,384]{1,0:T(8,128)(2,1)S(1)}, bf16[128,384]{1,0:T(8,128)(2,1)S(1)}, u32[]{:S(2)}, u32[]{:S(2)}) collective-permute-start(bf16[128,384]{1,0:T(8,128)(2,1)S(1)} %shard_map.115.own), channel_id=1, source_target_pairs={{0,1},{1,0},{2,3},{3,2},{4,5},{5,4},{6,7},{7,6},{8,9},{9,8},{10,11... | collective-permute-start | bytes 294920 | tf_op jit(solution)/shard_map/ppermute | solution.py:322
  59.8 10.3 %collective-permute-start.7 = (f32[256,128]{1,0:T(8,128)S(1)}, f32[256,128]{1,0:T(8,128)S(1)}, u32[]{:S(2)}, u32[]{:S(2)}) collective-permute-start(f32[256,128]{1,0:T(8,128)S(1)} %get-tuple-element.11.vel_own), channel_id=1, source_target_pairs={{0,3},{1,2},{2,1},{3,0},{4,7},{5,6},{6,5},{7,4},{8,11},{9,10},{10,... | collective-permute-start | bytes 393224 | tf_op jit(solution)/shard_map/ppermute | solution.py:327
  66.1 4.1 %collective-permute-start.6 = (f32[256,128]{1,0:T(8,128)S(1)}, f32[256,128]{1,0:T(8,128)S(1)}, u32[]{:S(2)}, u32[]{:S(2)}) collective-permute-start(f32[256,128]{1,0:T(8,128)S(1)} %get-tuple-element.11.vel_own), channel_id=1, source_target_pairs={{0,2},{2,0},{4,6},{6,4},{8,10},{10,8},{12,14},{14,12},{16,18},{18,... | collective-permute-start | bytes 393224 | tf_op jit(solution)/shard_map/ppermute | solution.py:318
  66.1 6.9 %collective-permute-start.5 = (f32[256,128]{1,0:T(8,128)S(1)}, f32[256,128]{1,0:T(8,128)S(1)}, u32[]{:S(2)}, u32[]{:S(2)}) collective-permute-start(f32[256,128]{1,0:T(8,128)S(1)} %get-tuple-element.11.vel_own), channel_id=1, source_target_pairs={{0,1},{1,0},{2,3},{3,2},{4,5},{5,4},{6,7},{7,6},{8,9},{9,8},{10,11... | collective-permute-start | bytes 393224 | tf_op jit(solution)/shard_map/ppermute | solution.py:322
  93.1 5.1 %collective-permute-start.12 = (f32[2,1536]{1,0:T(2,128)S(1)}, f32[2,1536]{1,0:T(2,128)S(1)}, u32[]{:S(2)}, u32[]{:S(2)}) collective-permute-start(f32[2,1536]{1,0:T(2,128)S(1)} %get-tuple-element.17), channel_id=1, source_target_pairs={{0,2},{2,0},{4,6},{6,4},{8,10},{10,8},{12,14},{14,12},{16,18},{18,... | collective-permute-start | bytes 36872 | tf_op jit(solution)/shard_map/ppermute | solution.py:318
  98.3 2.6 %collective-permute-start.13 = (f32[2,1536]{1,0:T(2,128)S(1)}, f32[2,1536]{1,0:T(2,128)S(1)}, u32[]{:S(2)}, u32[]{:S(2)}) collective-permute-start(f32[2,1536]{1,0:T(2,128)S(1)} %add.30), channel_id=1, source_target_pairs={{0,1},{1,0},{2,3},{3,2},{4,5},{5,4},{6,7},{7,6},{8,9},{9,8},{10,11... | collective-permute-start | bytes 36872 | tf_op jit(solution)/shard_map/ppermute | solution.py:322
  101.8 18.5 %all-to-all-start.3 = ((f32[32,2,1536]{2,1,0:T(2,128)}), f32[32,2,1536]{2,1,0:T(2,128)S(1)}, u32[]{:S(2)}, u32[]{:S(2)}) async-start(f32[32,2,1536]{2,1,0:T(2,128)} %broadcast_in_dim.5), calls=%async_computation.3 | async-start | bytes 786432 | tf_op jit(solution)/shard_map/all_to_all | solution.py:333
  110.2 3.5 %collective-permute-start.8 = (f32[128,64]{1,0:T(8,128)S(1)}, f32[128,64]{1,0:T(8,128)S(1)}, u32[]{:S(2)}, u32[]{:S(2)}) collective-permute-start(f32[128,64]{1,0:T(8,128)S(1)} %get-tuple-element.24), channel_id=1, source_target_pairs={{0,1},{1,0},{2,3},{3,2},{4,5},{5,4},{6,7},{7,6},{8,9},{9,8},{10,11... | collective-permute-start | bytes 98312 | tf_op jit(solution)/shard_map/ppermute | solution.py:322
  110.8 6.5 %collective-permute-start.10 = (f32[128,64]{1,0:T(8,128)S(1)}, f32[128,64]{1,0:T(8,128)S(1)}, u32[]{:S(2)}, u32[]{:S(2)}) collective-permute-start(f32[128,64]{1,0:T(8,128)S(1)} %get-tuple-element.25), channel_id=1, source_target_pairs={{0,3},{1,2},{2,1},{3,0},{4,7},{5,6},{6,5},{7,4},{8,11},{9,10},{10,... | collective-permute-start | bytes 98312 | tf_op jit(solution)/shard_map/ppermute | solution.py:327
  113.7 3.6 %collective-permute-start.9 = (f32[128,64]{1,0:T(8,128)S(1)}, f32[128,64]{1,0:T(8,128)S(1)}, u32[]{:S(2)}, u32[]{:S(2)}) collective-permute-start(f32[128,64]{1,0:T(8,128)S(1)} %get-tuple-element.26), channel_id=1, source_target_pairs={{0,2},{2,0},{4,6},{6,4},{8,10},{10,8},{12,14},{14,12},{16,18},{18,... | collective-permute-start | bytes 98312 | tf_op jit(solution)/shard_map/ppermute | solution.py:318
  117.5 4.4 %collective-permute-start.11 = (bf16[128,64]{1,0:T(8,128)(2,1)S(1)}, bf16[128,64]{1,0:T(8,128)(2,1)S(1)}, u32[]{:S(2)}, u32[]{:S(2)}) collective-permute-start(bf16[128,64]{1,0:T(8,128)(2,1)S(1)} %fusion.4), channel_id=1, source_target_pairs={{0,128},{128,0},{1,129},{129,1},{2,130},{130,2},{3,131},{131,3},{4... | collective-permute-start | bytes 49160 | tf_op jit(solution)/shard_map/ppermute | solution.py:429
  120.4 2.3 %collective-permute-start.14 = (f32[2,1536]{1,0:T(2,128)S(1)}, f32[2,1536]{1,0:T(2,128)S(1)}, u32[]{:S(2)}, u32[]{:S(2)}) collective-permute-start(f32[2,1536]{1,0:T(2,128)S(1)} %reduce_sum.9), channel_id=1, source_target_pairs={{0,2},{2,0},{4,6},{6,4},{8,10},{10,8},{12,14},{14,12},{16,18},{18,... | collective-permute-start | bytes 36872 | tf_op jit(solution)/shard_map/ppermute | solution.py:318

commit v2 on v1

--- a/solution.py
+++ b/solution.py
@@ -75,9 +75,9 @@
 
 def weight_kernel(chips, flags, levels, weight, received, out, turned):
     first = flags[0] == 0
-    rows, columns = received.shape
+    rows, columns = received.shape[0], received.shape[1] // 2
     own = jnp.where(first, weight[:, 0:columns].astype(F32), weight[:, columns:].astype(F32))
-    other = received[...].astype(F32)
+    other = jnp.where(first, received[:, 0:columns].astype(F32), received[:, columns:].astype(F32))
     both = [jnp.where(first, own, other), jnp.where(first, other, own)]
     padded = out.shape[2]
     if padded > 2 * rows:
@@ -104,8 +104,12 @@
         out[chip] = piece.astype(BF16)
 
 
-def product_kernel(block, taken, embed, modulation_a, modulation_b, out, columns_out, lines):
+def product_kernel(block, flags, taken, embed, modulation, out, halves_out, columns_out, lines):
+    critic = flags[1] == 1
     chips, height, padded = taken.shape
+    half = block // 2
+    stride = halves_out.shape[0] // 2
+    row_half = row_index((stride, 1))
     width = embed.shape[1]
     depth = width // chips
     row = row_index((height, 1))
@@ -117,16 +121,23 @@
             lines[chip : chip + 1, :] = piece[block : block + 1, 0:128]
             pieces.append(jnp.where(row < block, piece, 0.0)[:, 0:depth])
         joined = jnp.concatenate(pieces, axis=1) if group > 1 else pieces[0]
-        columns_out[:, start * depth : (start + group) * depth] = joined.astype(BF16)
+        span = slice(start * depth, (start + group) * depth)
+        columns_out[:, span] = joined.astype(BF16)
+        longer = jnp.concatenate([joined, jnp.zeros((stride, joined.shape[1]), F32)], axis=0)
+        low = jnp.where(row_half < half, longer[0:stride], 0.0)
+        high = jnp.where(row_half < half, longer[half : half + stride], 0.0)
+        halves_out[:, span] = jnp.concatenate([low, high], axis=0).astype(BF16)
     weight = columns_out[...]
     embed_b = embed[...]
     embed_f = embed_b.astype(F32)
+    modulation_a = modulation[0]
+    modulation_b = jnp.where(critic, modulation[1], modulation_a)
     plain = dot(weight, embed_b, NT)
     scaled_a = dot(weight, (embed_f * modulation_a[0:1, :]).astype(BF16), NT)
     scaled_b = dot(weight, (embed_f * modulation_b[0:1, :]).astype(BF16), NT)
     shifts = []
-    for modulation in (modulation_a, modulation_b):
-        shift = modulation[1:2, :]
+    for pair in (modulation_a, modulation_b):
+        shift = pair[1:2, :]
         high = rounded(shift)
         shifts += [high, shift - high]
     shifts.append(jnp.zeros((4, width), F32))
@@ -153,12 +164,13 @@
         out[chip] = jnp.where(row_all < block, matrix, tail).astype(BF16)
 
 
-def token_rows(first, second, start, stop):
-    return jnp.concatenate([first[:, start:stop], second[:, start:stop]], axis=0)
-
-
-def inverse_norms(pack_one, pack_two, which):
-    tail = token_rows(pack_one, pack_two, 256, 384).astype(F32)
+def token_rows(packs, sample, start, stop):
+    tokens = packs[0].shape[1]
+    return jnp.concatenate([pack[sample, :, start:stop] for pack in packs], axis=0).reshape(2 * tokens, stop - start)
+
+
+def inverse_norms(packs, sample, which):
+    tail = token_rows(packs, sample, 256, 384).astype(F32)
     at = 3 * which
     return tail[:, at : at + 1] + tail[:, at + 1 : at + 2] + tail[:, at + 2 : at + 3]
 
@@ -169,9 +181,8 @@
     lane = lane_index((1, 128))
     chosen = lane // CHANNELS == which
     for sample in range(2):
-        one, two = packs[2 * sample], packs[2 * sample + 1]
-        rows = jnp.where(chosen, token_rows(one, two, 0, 128).astype(F32), 0.0).astype(BF16)
-        scale = inverse_norms(one, two, which)
+        rows = jnp.where(chosen, token_rows(packs, sample, 0, 128).astype(F32), 0.0).astype(BF16)
+        scale = inverse_norms(packs, sample, which)
         shift = offset * levels[2 * sample + which]
         total = jnp.zeros((rows.shape[0], CHANNELS), F32)
         for head in range(heads):
@@ -194,7 +205,7 @@
 
 
 def second_pass_kernel(
-    block, levels, taken, own, seq, core, both, output_weight, matrices, offsets, keep, velocity, stacked
+    block, levels, taken, here, there, output_weight, matrices, offsets, keep, velocity, crossing, stacked
 ):
     chips = taken.shape[0]
     lines = []
@@ -204,11 +215,12 @@
         lines.append(piece[block : block + 4, 0:block] if block <= 256 else None)
     matrices[...] = stacked[...].astype(BF16)
     offsets[...] = jnp.concatenate([jnp.concatenate(lines, axis=1), jnp.zeros((4, offsets.shape[1]), F32)], axis=0)
-    forward(1, levels, (own, seq, core, both), matrices, offsets, output_weight, keep, velocity)
-
-
-def first_pass_kernel(levels, matrices, offsets, own, seq, core, both, output_weight, velocity):
-    forward(0, levels, (own, seq, core, both), matrices, offsets, output_weight, None, velocity)
+    forward(1, levels, (here, there), matrices, offsets, output_weight, keep, velocity)
+    crossing[...] = pltpu.roll(velocity[...], CHANNELS, 1)
+
+
+def first_pass_kernel(levels, matrices, offsets, here, there, output_weight, velocity):
+    forward(0, levels, (here, there), matrices, offsets, output_weight, None, velocity)
 
 
 def swap_tokens(value):
@@ -216,34 +228,25 @@
     return jnp.concatenate([value[half:], value[:half]], axis=0)
 
 
-def backward_kernel(
-    block, flags, levels, kept, own, seq, core, both, vel_own, vel_seq, vel_core, vel_both, output_weight, out, gathered
-):
+def backward_kernel(block, flags, levels, kept, here, there, vel_here, vel_there, output_weight, out, gathered, summed):
     critic = flags[1] == 1
-    packs = (own, seq, core, both)
+    packs = (here, there)
     heads = output_weight.shape[0] // HEAD_DIM
-    velocity = vel_own[...] + swap_tokens(vel_seq[...])
-    crossing = vel_core[...] + swap_tokens(vel_both[...])
+    velocity = vel_here[...] + swap_tokens(vel_there[...])
     lane = lane_index((1, 128))
     grads, rows = [], []
     for sample in range(2):
-        one, two = packs[2 * sample], packs[2 * sample + 1]
-        known = token_rows(one, two, 128, 256).astype(F32)
+        known = token_rows(packs, sample, 128, 256).astype(F32)
         known = known[:, 0:CHANNELS] + known[:, CHANNELS:]
-        at = sample * CHANNELS
-        back = (1 - sample) * CHANNELS
-        total = velocity[:, at : at + CHANNELS] + crossing[:, back : back + CHANNELS]
+        total = velocity[:, sample * CHANNELS : (sample + 1) * CHANNELS]
         grads.append(jnp.where(critic, total - known, known).astype(BF16))
-        level = levels[2 * sample + 1]
-        scaled = token_rows(one, two, 0, 128).astype(F32) * (inverse_norms(one, two, 1) * level)
-        level_line = jnp.full((1, 128), level, F32)
-        high = rounded(level_line)
-        ends = jnp.where(lane == 0, high, jnp.where(lane == 1, level_line - high, 0.0))
-        scaled = jnp.where(lane < CHANNELS, ends, scaled)
+        inputs = token_rows(packs, sample, 0, 128).astype(F32)
+        inputs = jnp.where(lane < CHANNELS, pltpu.roll(inputs, CHANNELS, 1), inputs)
+        scaled = inputs * (inverse_norms(packs, sample, 1) * levels[2 * sample + 1])
         rows.append(scaled.T.astype(BF16))
     for head in range(heads):
         at = head * 3 * HEAD_DIM
-        total = None
+        total, ends = None, None
         for sample in range(2):
             qkv = kept[sample, :, at : at + 3 * HEAD_DIM]
             query = qkv[:, 0:HEAD_DIM]
@@ -262,36 +265,58 @@
             grad_query = dot(grad_scores, key, TN)
             grad = jnp.concatenate([grad_query, grad_key, grad_value], axis=1).astype(BF16)
             term = dot(rows[sample], grad)
+            end = jnp.sum(grad.astype(F32), axis=0, keepdims=True) * levels[2 * sample + 1]
             total = term if total is None else total + term
+            ends = end if ends is None else ends + end
         gathered[at : at + 3 * HEAD_DIM, :] = total.T
+        summed[:, at : at + 3 * HEAD_DIM] = ends
     columns = heads * 3 * HEAD_DIM
     gathered[columns:, :] = jnp.zeros((gathered.shape[0] - columns, 128), F32)
     chips, height = out.shape[0], out.shape[1]
+    half = block // 2
     row = row_index((height, 128))
+    low_lanes = lane_index((height, 128)) < CHANNELS
+    pad = jnp.zeros((1, 128 - block), F32) if block < 128 else None
     for chip in range(chips):
-        piece = gathered[chip * block : chip * block + height, :]
-        out[chip] = jnp.where(row < block, piece, 0.0).astype(BF16)
-
-
-def closing_kernel(factor, flags, taken, weight, embed, kept, sent):
+        at = chip * block
+        piece = jnp.where(low_lanes, gathered[at : at + height, :], gathered[at + half : at + half + height, :])
+        line = summed[:, at : at + block]
+        high = rounded(line)
+        pair = [high, line - high]
+        if pad is not None:
+            pair = [jnp.concatenate([part, pad], axis=1) for part in pair]
+        piece = jnp.where(row < half, piece, jnp.where(row == half, pair[0], jnp.where(row == half + 1, pair[1], 0.0)))
+        out[chip] = piece.astype(BF16)
+
+
+def closing_kernel(block, factor, flags, taken, weight, embed, kept, sent):
     first = flags[0] == 0
     total = taken[0].astype(F32)
     for chip in range(1, taken.shape[0]):
         total = total + taken[chip].astype(F32)
-    turned = total.T
-    high = turned.astype(BF16)
-    low = (turned - high.astype(F32)).astype(BF16)
-    half = embed.shape[1] // 2
-    step = half // 3
-    halves = []
-    for start in range(0, 2 * half, step):
+    half = block // 2
+    height = total.shape[0]
+    row = row_index((height, 128))
+    ends = total[half : half + 1] + total[half + 1 : half + 2]
+    turned = jnp.where(row < half, total, 0.0).T
+    lane = lane_index((1, 128))
+    ends_low = jnp.where(lane < half, ends, 0.0)[:, 0:height]
+    ends_high = jnp.where(lane < half, pltpu.roll(ends, 128 - half, 1), 0.0)[:, 0:height]
+    lower = jnp.concatenate([turned[0:CHANNELS], ends_low, jnp.zeros((7, height), F32)], axis=0)
+    upper = jnp.concatenate([turned[CHANNELS:], ends_high, jnp.zeros((7, height), F32)], axis=0)
+    joined = jnp.concatenate([lower, upper], axis=1)
+    high = joined.astype(BF16)
+    low = (joined - high.astype(F32)).astype(BF16)
+    middle = embed.shape[1] // 2
+    step = middle // 3
+    parts = []
+    for start in range(0, 2 * middle, step):
         columns = weight[:, start : start + step]
         product = dot(high, columns) + dot(low, columns)
-        scale = jnp.sum(product[CHANNELS:] * embed[:, start : start + step].astype(F32), axis=0, keepdims=True)
-        shift = product[0:1] + product[1:2]
-        halves.append(jnp.concatenate([scale, shift], axis=0) * factor)
-    left = jnp.concatenate(halves[:3], axis=1)
-    right = jnp.concatenate(halves[3:], axis=1)
+        scale = jnp.sum(product[:CHANNELS] * embed[:, start : start + step].astype(F32), axis=0, keepdims=True)
+        parts.append(jnp.concatenate([scale, product[CHANNELS : CHANNELS + 1]], axis=0) * factor)
+    left = jnp.concatenate(parts[:3], axis=1)
+    right = jnp.concatenate(parts[3:], axis=1)
     kept[...] = jnp.where(first, left, right)
     sent[...] = jnp.where(first, right, left)
 
@@ -320,11 +345,6 @@
 
 def other_half(value):
     return lax.ppermute(value, "seq", [(0, 1), (1, 0)])
-
-
-def other_both(value):
-    count = lax.axis_size("fsdp") * 2
-    return lax.ppermute(value, ("fsdp", "seq"), [(i, i ^ 3) for i in range(count)])
 
 
 def between_chips(value):
@@ -360,21 +380,19 @@
     out_rows = output_weight.shape[1] // 2
     out_half = jnp.where(core == 0, output_weight[0, :out_rows], output_weight[0, out_rows:])
 
-    received = other_core(jnp.where(core == 0, weight[:, columns:], weight[:, :columns]))
+    received = other_core(weight)
     level_two = jnp.where(is_critic, noise_levels[0, 0], replay_levels[0, 0])
     own_levels = jnp.stack([noise_levels[0, 0], level_two])
     levels = jnp.concatenate([own_levels, other_core(own_levels)])
     flags = jnp.stack([core.astype(jnp.int32), is_critic.astype(jnp.int32)])
-    modulation_a = modulation[0, 0]
-    modulation_b = jnp.where(is_critic, modulation[0, 1], modulation[0, 0])
-
     own = call(
         pack_kernel,
         struct((tokens, 384), BF16),
         (flags, own_levels, base_latents[0, 0], noise_latents[0, 0], replay_latents[0, 0], cotangent[0, 0], embed),
         2,
     )
-    seq, near, both = other_half(own), other_core(own), other_both(own)
+    here = jnp.stack([own, other_core(own)])
+    there = other_half(here)
 
     turned = call(
         functools.partial(weight_kernel, chips),
@@ -384,55 +402,61 @@
         [pltpu.VMEM((columns + height - block, padded), F32)],
     )
     taken = between_chips(turned)
+    packed = round_up(block // 2 + 2, 8)
     matrices, own_columns = call(
         functools.partial(product_kernel, block),
-        (struct((chips, height, 4 * CHANNELS), BF16), struct((height, width), BF16)),
-        (taken, embed, modulation_a, modulation_b),
-        0,
-        [pltpu.VMEM((chips, 128), F32)],
+        (struct((chips, height, 4 * CHANNELS), BF16), struct((2 * packed, width), BF16)),
+        (flags, taken, embed, modulation[0]),
+        1,
+        [pltpu.VMEM((height, width), BF16), pltpu.VMEM((chips, 128), F32)],
     )
     taken = between_chips(matrices)
 
-    packs = (own, seq, near, both)
-    whole, offsets, kept, vel_b = call(
+    whole, offsets, kept, vel_b, vel_crossing = call(
         functools.partial(second_pass_kernel, block),
         (
             struct((columns, 4 * CHANNELS), BF16),
             struct((8, columns), F32),
             struct((2, 2 * tokens, columns), BF16),
             struct((2 * tokens, 2 * CHANNELS), F32),
+            struct((2 * tokens, 2 * CHANNELS), F32),
         ),
-        (levels, taken) + packs + (out_half,),
+        (levels, taken, here, there, out_half),
         1,
         [pltpu.VMEM((columns, 4 * CHANNELS), F32)],
     )
-    vel_seq, vel_near, vel_both = other_half(vel_b), other_core(vel_b), other_both(vel_b)
+    vel_here = vel_b + other_core(vel_crossing)
+    vel_there = other_half(vel_here)
     vel_a = call(
         first_pass_kernel,
         struct((2 * tokens, 2 * CHANNELS), F32),
-        (levels, whole, offsets) + packs + (out_half,),
+        (levels, whole, offsets, here, there, out_half),
         1,
-    )
+        flops=4 * 10**9,
+    )
+    vel_there, vel_a = lax.optimization_barrier((vel_there, vel_a))
     products = call(
         functools.partial(backward_kernel, block),
-        struct((chips, height, 128), BF16),
-        (flags, levels, kept) + packs + (vel_b, vel_seq, vel_near, vel_both, out_half),
+        struct((chips, packed, 128), BF16),
+        (flags, levels, kept, here, there, vel_here, vel_there, out_half),
         2,
-        [pltpu.VMEM((columns + height - block, 128), F32)],
-    )
-
-    own_a = vel_a[:tokens, :CHANNELS] + other_half(vel_a[tokens:, :CHANNELS])
-    own_a = own_a + other_core(vel_a[:tokens, CHANNELS:]) + other_both(vel_a[tokens:, CHANNELS:])
-    own_b = vel_b[:tokens, :CHANNELS] + vel_seq[tokens:, :CHANNELS]
-    own_b = own_b + vel_near[:tokens, CHANNELS:] + vel_both[tokens:, CHANNELS:]
+        [pltpu.VMEM((columns + 2 * packed, 128), F32), pltpu.VMEM((1, columns), F32)],
+    )
+    gathered = between_chips(products)
+
+    own_a = vel_a[:, :CHANNELS] + other_core(vel_a[:, CHANNELS:])
+    own_a = own_a[:tokens] + other_half(own_a[tokens:])
+    own_b = vel_here[:tokens, :CHANNELS] + vel_there[tokens:, :CHANNELS]
     payload = jnp.where(is_critic, own_b - own_a, own[:, :CHANNELS].astype(F32) - own_levels[0] * own_a)
-    crossed = lax.ppermute(payload.astype(BF16), "role", [(0, 1), (1, 0)])
+    payload = payload.astype(BF16)
+    gathered, payload = lax.optimization_barrier((gathered, payload))
+    crossed = lax.ppermute(payload, "role", [(0, 1), (1, 0)])
 
     samples = devices * base_latents.shape[1]
     kept_half, sent_half = call(
-        functools.partial(closing_kernel, 1.0 / (samples * 2 * tokens)),
+        functools.partial(closing_kernel, block, 1.0 / (samples * 2 * tokens)),
         (struct((2, width // 2), F32), struct((2, width // 2), F32)),
-        (flags, between_chips(products), own_columns, embed),
+        (flags, gathered, own_columns, embed),
         1,
     )
     total = kept_half + other_core(sent_half)

time: 124 us -> 120 us (0.968)
  blocking collectives: 14.5 us -> 19.9 us
  waiting for transfers between devices: 36.4 us -> 32.3 us
  starting transfers between devices: 46.2 us -> 42.5 us
  other arithmetic: 2.86 us -> 1.09 us
    ppermute x4 -> x1, starting transfers between devices: 14.4 us -> 3 us  [per_device(): crossed = lax.ppermute(payload, 'role', [(0, 1), (1, 0)])]
    ppermute x4 -> x1, waiting for transfers between devices: 10.6 us -> 0.01 us  [per_device(): crossed = lax.ppermute(payload, 'role', [(0, 1), (1, 0)])]
    ppermute x7, starting transfers between devices: 9.14 us -> 18.3 us  [other_core(): lax.ppermute(value, 'fsdp', [(i, i ^ 1) for i in range(lax.axis_size('fsd...]
    all_to_all x3, starting transfers between devices: 21.1 us -> 15.7 us  [between_chips(): lax.all_to_all(value, 'fsdp', 0, 0, tiled=True, axis_index_groups=groups)]
    all_to_all x1, blocking collectives: 14.5 us -> 19.9 us  [between_chips(): lax.all_to_all(value, 'fsdp', 0, 0, tiled=True, axis_index_groups=groups)]
    ppermute x4, starting transfers between devices: 1.48 us -> 5.53 us  [other_half(): return lax.ppermute(value, 'seq', [(0, 1), (1, 0)])]
    ppermute x7, waiting for transfers between devices: 1.34 us -> 4.06 us  [other_core(): lax.ppermute(value, 'fsdp', [(i, i ^ 1) for i in range(lax.axis_size('fsd...]
    all_to_all x3, waiting for transfers between devices: 17.6 us -> 20.2 us  [between_chips(): lax.all_to_all(value, 'fsdp', 0, 0, tiled=True, axis_index_groups=groups)]
  transfers between devices with their start and end apart: 18 -> 15, of which waited for: 11 -> 12; matrix products, arithmetic and copies ran while one was open for 3% -> 1% of each run, Pallas kernels for 4% -> 9%
where the time goes in v2:
time: 120 us
  starting transfers between devices  42.5 us (35%)
  waiting for transfers between devices  32.3 us (27%)
  blocking collectives  19.9 us (17%)
  Pallas kernels  18.4 us (15%)
  local copies, waits for them, and re-layouts  3.32 us (3%)
  between operations  2.18 us (2%)
    all_to_all x3, waiting for transfers between devices, between_chips(): lax.all_to_all(value, 'fsdp', 0, 0, tiled=True, axis_index_groups=groups)  20.2 us
    all_to_all x1, blocking collectives, between_chips(): lax.all_to_all(value, 'fsdp', 0, 0, tiled=True, axis_index_groups=groups)  19.9 us
    pallas_call x7, Pallas kernels, call(): pl.pallas_call(kernel, out_shape=out_shapes, in_specs=specs, out_specs=ja...  18.4 us
    ppermute x7, starting transfers between devices, other_core(): lax.ppermute(value, 'fsdp', [(i, i ^ 1) for i in range(lax.axis_size('fsd...  18.3 us
    all_to_all x3, starting transfers between devices, between_chips(): lax.all_to_all(value, 'fsdp', 0, 0, tiled=True, axis_index_groups=groups)  15.7 us
    ppermute x4, waiting for transfers between devices, other_half(): return lax.ppermute(value, 'seq', [(0, 1), (1, 0)])  8.03 us
    ppermute x4, starting transfers between devices, other_half(): return lax.ppermute(value, 'seq', [(0, 1), (1, 0)])  5.53 us
    ppermute x7, waiting for transfers between devices, other_core(): lax.ppermute(value, 'fsdp', [(i, i ^ 1) for i in range(lax.axis_size('fsd...  4.06 us
  transfers between devices with their start and end apart: 15, of which 12 were waited for; matrix products, arithmetic and copies ran while one was open for 1% of the time, Pallas kernels for 9%

profile of v2, /device:TPU:1, one launch (start us, length us, event | category | flops | bytes accessed | tf_op | source)
XLA Modules:
  0.0 119.7 jit_solution(11827120552943767902)
XLA Ops:
  0.6 0.0 copy-start
  2.0 0.1 pad_maximum_fusion.1.levels
  2.1 3.3 %collective-permute-start = (f32[2]{0:T(128)S(1)}, f32[2]{0:T(128)S(1)}, u32[]{:S(2)}, u32[]{:S(2)}) collective-permute-start(f32[2]{0:T(128)S(1)} %pad_maximum_fusion.1.levels), channel_id=1, source_target_pairs={{0,2},{2,0},{4,6},{6,4},{8,10},{10,8},{12,14},{14,12},{16,18},{18,... | collective-permute-start | bytes 32 | tf_op jit(solution)/shard_map/ppermute | solution.py:343
  5.3 0.1 collective-permute-start.1
  5.4 0.1 pad_add_fusion.flags
  5.5 0.6 collective-permute-done
  6.2 0.1 pad_maximum_fusion.2.levels
  6.2 0.8 collective-permute-done.1.received
  7.0 0.0 copy-start.1
  7.0 0.9 copy-done.1
  8.0 0.0 copy-start.2
  8.0 0.8 shard_map.113
  8.7 19.9 %all_to_all.20.taken = bf16[32,40,128]{2,1,0:T(8,128)(2,1)S(1)} all-to-all(bf16[32,40,128]{2,1,0:T(8,128)(2,1)S(1)} %shard_map.113), channel_id=1, replica_groups={{0,4,8,12,16,20,24,28,32,36,40,44,48,52,56,60,64,68,72,76,80,84,88,92,9..., dimensions={0} | all-to-all | bytes 655360 | tf_op jit(solution)/shard_map/all_to_all | solution.py:353
  28.6 0.0 copy-start.4
  28.6 0.0 copy-done
  28.6 0.0 copy-done.2
  28.6 2.2 %shard_map.114 = (bf16[32,40,256]{2,1,0:T(8,128)(2,1)}, bf16[48,3072]{1,0:T(8,128)(2,1)S(1)}) custom-call(s32[2]{0:T(128)S(1)} %pad_add_fusion.flags, bf16[32,40,128]{2,1,0:T(8,128)(2,1)S(1)} %all_to_all.20.taken, bf16[64,3072]{1,0:T(8,128)(2,1)S(1)} %bitcast.25, f32[2,2,3072]{2,1,0:T(2,128)S(1)} %bitcast.35), custom_call_target="tpu_custom_call" | custom-call | tf_op jit(solution)/shard_map/pallas_call | solution.py:327
  30.9 7.4 %all-to-all-start.1 = ((bf16[32,40,256]{2,1,0:T(8,128)(2,1)}), bf16[32,40,256]{2,1,0:T(8,128)(2,1)S(1)}, u32[]{:S(2)}, u32[]{:S(2)}) async-start(bf16[32,40,256]{2,1,0:T(8,128)(2,1)} %get-tuple-element.15), calls=%async_computation.1 | async-start | bytes 1310720 | tf_op jit(solution)/shard_map/all_to_all | solution.py:353
  38.2 0.0 copy-done.4
  38.2 0.1 copy.26
  38.4 0.0 copy-done.5
  38.4 0.1 copy.27
  38.5 0.0 copy-done.6
  38.5 0.1 copy.28
  38.6 0.0 copy-done.7
  38.6 0.1 copy.29
  38.8 1.2 %shard_map.115 = bf16[128,384]{1,0:T(8,128)(2,1)S(1)} custom-call(s32[2]{0:T(128)S(1)} %pad_add_fusion.flags, f32[2]{0:T(128)S(1)} %pad_maximum_fusion.1.levels, bf16[128,64]{1,0:T(8,128)(2,1)S(1)} %bitcast.31, bf16[128,64]{1,0:T(8,128)(2,1)S(1)} %bitcast.32, bf16[128,64]{1,0:T(8,128)(2,1)S(1)} %bitcast.33, bf16[128,64]{1,0:T(8,128)(2,1)S(1)} %bitcast.34, ...), custom_call_target="tpu_custom_call" | custom-call | tf_op jit(solution)/shard_map/pallas_call | solution.py:327
  40.0 1.3 %collective-permute-start.2 = (bf16[128,384]{1,0:T(8,128)(2,1)S(1)}, bf16[128,384]{1,0:T(8,128)(2,1)S(1)}, u32[]{:S(2)}, u32[]{:S(2)}) collective-permute-start(bf16[128,384]{1,0:T(8,128)(2,1)S(1)} %shard_map.115), channel_id=1, source_target_pairs={{0,2},{2,0},{4,6},{6,4},{8,10},{10,8},{12,14},{14,12},{16,18},{18,... | collective-permute-start | bytes 294920 | tf_op jit(solution)/shard_map/ppermute | solution.py:343
  41.3 0.0 copy-done.3
  41.3 0.1 copy.36
  41.4 0.1 copy.35
  41.5 0.7 collective-permute-done.2
  42.2 1.4 %collective-permute-start.3 = (bf16[2,128,384]{2,1,0:T(8,128)(2,1)S(1)}, bf16[2,128,384]{2,1,0:T(8,128)(2,1)S(1)}, u32[]{:S(2)}, u32[]{:S(2)}) collective-permute-start(bf16[2,128,384]{2,1,0:T(8,128)(2,1)S(1)} %pad_maximum_fusion.here), channel_id=1, source_target_pairs={{0,1},{1,0},{2,3},{3,2},{4,5},{5,4},{6,7},{7,6},{8,9},{9,8},{10,11... | collective-permute-start | bytes 589832 | tf_op jit(solution)/shard_map/ppermute | solution.py:347
  43.6 4.8 %collective-permute-done.3.there = bf16[2,128,384]{2,1,0:T(8,128)(2,1)S(1)} collective-permute-done((bf16[2,128,384]{2,1,0:T(8,128)(2,1)S(1)}, bf16[2,128,384]{2,1,0:T(8,128)(2,1)S(1)}, u32[]{:S(2)}, u32[]{:S(2)}) %collective-permute-start.3) | collective-permute-done | bytes 196640 | tf_op jit(solution)/shard_map/ppermute | solution.py:347
  48.4 6.3 %all-to-all-done.1.taken = bf16[32,40,256]{2,1,0:T(8,128)(2,1)S(1)} async-done(((bf16[32,40,256]{2,1,0:T(8,128)(2,1)}), bf16[32,40,256]{2,1,0:T(8,128)(2,1)S(1)}, u32[]{:S(2)}, u32[]{:S(2)}) %all-to-all-start.1) | async-done | bytes 655392 | tf_op jit(solution)/shard_map/all_to_all | solution.py:353
  54.8 4.1 %shard_map.116 = (bf16[1152,256]{1,0:T(8,128)(2,1)S(1)}, f32[8,1152]{1,0:T(8,128)S(1)}, bf16[2,256,1152]{2,1,0:T(8,128)(2,1)S(1)}, f32[256,128]{1,0:T(8,128)S(1)}, f32[256,128]{1,0:T(8,128)S(1)}) custom-call(f32[4]{0:T(128)S(1)} %pad_maximum_fusion.2.levels, bf16[32,40,256]{2,1,0:T(8,128)(2,1)S(1)} %all-to-all-done.1.taken, ...), custom_call_target="tpu_custom_call" | custom-call | tf_op jit(solution)/shard_map/pallas_call | solution.py:327
  58.9 5.1 %collective-permute-start.4 = (f32[256,128]{1,0:T(8,128)S(1)}, f32[256,128]{1,0:T(8,128)S(1)}, u32[]{:S(2)}, u32[]{:S(2)}) collective-permute-start(f32[256,128]{1,0:T(8,128)S(1)} %get-tuple-element.18), channel_id=1, source_target_pairs={{0,2},{2,0},{4,6},{6,4},{8,10},{10,8},{12,14},{14,12},{16,18},{18,... | collective-permute-start | bytes 393224 | tf_op jit(solution)/shard_map/ppermute | solution.py:343
  63.9 1.0 collective-permute-done.4
  64.9 1.4 %collective-permute-start.5 = (f32[256,128]{1,0:T(8,128)S(1)}, f32[256,128]{1,0:T(8,128)S(1)}, u32[]{:S(2)}, u32[]{:S(2)}) collective-permute-start(f32[256,128]{1,0:T(8,128)S(1)} %add.18.vel_here), channel_id=1, source_target_pairs={{0,1},{1,0},{2,3},{3,2},{4,5},{5,4},{6,7},{7,6},{8,9},{9,8},{10,11... | collective-permute-start | bytes 393224 | tf_op jit(solution)/shard_map/ppermute | solution.py:347
  66.3 3.9 %shard_map.117 = f32[256,128]{1,0:T(8,128)S(1)} custom-call(f32[4]{0:T(128)S(1)} %pad_maximum_fusion.2.levels, bf16[1152,256]{1,0:T(8,128)(2,1)S(1)} %get-tuple-element.19.matrices, f32[8,1152]{1,0:T(8,128)S(1)} %get-tuple-element.20.offsets, bf16[2,128,384]{2,1,0:T(8,128)(2,1)S(1)} %pad_maximum_fusion.here, ...), custom_call_target="tpu_custom_call" | custom-call | flops 4000000000 | tf_op jit(solution)/shard_map/pallas_call | solution.py:327
  70.2 0.0 collective-permute-done.5.vel_there
  70.2 0.1 slice.32
  70.3 1.0 collective-permute-start.6
  71.3 5.1 %shard_map.118 = bf16[32,24,128]{2,1,0:T(8,128)(2,1)} custom-call(s32[2]{0:T(128)S(1)} %pad_add_fusion.flags, f32[4]{0:T(128)S(1)} %pad_maximum_fusion.2.levels, bf16[2,256,1152]{2,1,0:T(8,128)(2,1)S(1)} %get-tuple-element.16.kept, bf16[2,128,384]{2,1,0:T(8,128)(2,1)S(1)} %pad_maximum_fusion.here, bf16[2,128,384]{2,1,0:T(8,128)(2,1)S(1)} %collective-permute-done.3.there, ...), custom_call_target="tpu_custom_call" | custom-call | tf_op jit(solution)/shard_map/pallas_call | solution.py:327
  76.4 4.4 %all-to-all-start.2 = ((bf16[32,24,128]{2,1,0:T(8,128)(2,1)}), bf16[32,24,128]{2,1,0:T(8,128)(2,1)S(1)}, u32[]{:S(2)}, u32[]{:S(2)}) async-start(bf16[32,24,128]{2,1,0:T(8,128)(2,1)} %shard_map.118), calls=%async_computation.2 | async-start | bytes 393216 | tf_op jit(solution)/shard_map/all_to_all | solution.py:353
  80.8 0.0 collective-permute-done.6
  80.9 1.4 %collective-permute-start.7 = (f32[128,64]{1,0:T(8,128)S(1)}, f32[128,64]{1,0:T(8,128)S(1)}, u32[]{:S(2)}, u32[]{:S(2)}) collective-permute-start(f32[128,64]{1,0:T(8,128)S(1)} %slice.38), channel_id=1, source_target_pairs={{0,1},{1,0},{2,3},{3,2},{4,5},{5,4},{6,7},{7,6},{8,9},{9,8},{10,11... | collective-permute-start | bytes 98312 | tf_op jit(solution)/shard_map/ppermute | solution.py:347
  82.2 2.0 %collective-permute-done.7 = f32[128,64]{1,0:T(8,128)S(1)} collective-permute-done((f32[128,64]{1,0:T(8,128)S(1)}, f32[128,64]{1,0:T(8,128)S(1)}, u32[]{:S(2)}, u32[]{:S(2)}) %collective-permute-start.7) | collective-permute-done | bytes 32800 | tf_op jit(solution)/shard_map/ppermute | solution.py:347
  84.2 6.3 %all-to-all-done.2.taken = bf16[32,24,128]{2,1,0:T(8,128)(2,1)S(1)} async-done(((bf16[32,24,128]{2,1,0:T(8,128)(2,1)}), bf16[32,24,128]{2,1,0:T(8,128)(2,1)S(1)}, u32[]{:S(2)}, u32[]{:S(2)}) %all-to-all-start.2) | async-done | bytes 196640 | tf_op jit(solution)/shard_map/all_to_all | solution.py:353
  90.5 1.1 shard_map.119
  91.7 2.6 %collective-permute-start.9 = (f32[2,1536]{1,0:T(2,128)S(1)}, f32[2,1536]{1,0:T(2,128)S(1)}, u32[]{:S(2)}, u32[]{:S(2)}) collective-permute-start(f32[2,1536]{1,0:T(2,128)S(1)} %get-tuple-element.27), channel_id=1, source_target_pairs={{0,2},{2,0},{4,6},{6,4},{8,10},{10,8},{12,14},{14,12},{16,18},{18,... | collective-permute-start | bytes 36872 | tf_op jit(solution)/shard_map/ppermute | solution.py:343
  94.3 0.8 collective-permute-done.9
  95.2 1.4 %collective-permute-start.10 = (f32[2,1536]{1,0:T(2,128)S(1)}, f32[2,1536]{1,0:T(2,128)S(1)}, u32[]{:S(2)}, u32[]{:S(2)}) collective-permute-start(f32[2,1536]{1,0:T(2,128)S(1)} %add.22), channel_id=1, source_target_pairs={{0,1},{1,0},{2,3},{3,2},{4,5},{5,4},{6,7},{7,6},{8,9},{9,8},{10,11... | collective-permute-start | bytes 36872 | tf_op jit(solution)/shard_map/ppermute | solution.py:347
  96.5 1.2 %collective-permute-done.10 = f32[2,1536]{1,0:T(2,128)S(1)} collective-permute-done((f32[2,1536]{1,0:T(2,128)S(1)}, f32[2,1536]{1,0:T(2,128)S(1)}, u32[]{:S(2)}, u32[]{:S(2)}) %collective-permute-start.10) | collective-permute-done | bytes 12320 | tf_op jit(solution)/shard_map/ppermute | solution.py:347
  97.8 0.8 broadcast_in_dim.5
  98.7 3.9 %all-to-all-start.3 = ((f32[32,2,1536]{2,1,0:T(2,128)}), f32[32,2,1536]{2,1,0:T(2,128)S(1)}, u32[]{:S(2)}, u32[]{:S(2)}) async-start(f32[32,2,1536]{2,1,0:T(2,128)} %broadcast_in_dim.5), calls=%async_computation.3 | async-start | bytes 786432 | tf_op jit(solution)/shard_map/all_to_all | solution.py:353
  102.5 3.0 %collective-permute-start.8 = (bf16[128,64]{1,0:T(8,128)(2,1)S(1)}, bf16[128,64]{1,0:T(8,128)(2,1)S(1)}, u32[]{:S(2)}, u32[]{:S(2)}) collective-permute-start(bf16[128,64]{1,0:T(8,128)(2,1)S(1)} %fusion.2), channel_id=1, source_target_pairs={{0,128},{128,0},{1,129},{129,1},{2,130},{130,2},{3,131},{131,3},{4... | collective-permute-start | bytes 49160 | tf_op jit(solution)/shard_map/ppermute | solution.py:453
  105.5 7.5 %all-to-all-done.3 = f32[32,2,1536]{2,1,0:T(2,128)S(1)} async-done(((f32[32,2,1536]{2,1,0:T(2,128)}), f32[32,2,1536]{2,1,0:T(2,128)S(1)}, u32[]{:S(2)}, u32[]{:S(2)}) %all-to-all-start.3) | async-done | bytes 393248 | tf_op jit(solution)/shard_map/all_to_all | solution.py:353
  113.1 0.1 reduce_sum.9
  113.2 5.0 %collective-permute-start.11 = (f32[2,1536]{1,0:T(2,128)S(1)}, f32[2,1536]{1,0:T(2,128)S(1)}, u32[]{:S(2)}, u32[]{:S(2)}) collective-permute-start(f32[2,1536]{1,0:T(2,128)S(1)} %reduce_sum.9), channel_id=1, source_target_pairs={{0,2},{2,0},{4,6},{6,4},{8,10},{10,8},{12,14},{14,12},{16,18},{18,... | collective-permute-start | bytes 36872 | tf_op jit(solution)/shard_map/ppermute | solution.py:343
  118.2 0.0 collective-permute-done.8
  118.2 0.7 copy.33
  118.9 0.1 collective-permute-done.11
  119.0 0.6 maximum_select_fusion
  (13 shorter events, 0.1 us)
Async XLA Ops:
  0.6 28.0 %copy-start = (bf16[1,64,3072]{2,1,0:T(8,128)(2,1)S(1)}, bf16[1,64,3072]{2,1,0:T(8,128)(2,1)}, u32[]{:S(2)}) copy-start(bf16[1,64,3072]{2,1,0:T(8,128)(2,1)} %param.16) | copy-start | bytes 1179652
  2.1 4.1 %collective-permute-start = (f32[2]{0:T(128)S(1)}, f32[2]{0:T(128)S(1)}, u32[]{:S(2)}, u32[]{:S(2)}) collective-permute-start(f32[2]{0:T(128)S(1)} %pad_maximum_fusion.1.levels), channel_id=1, source_target_pairs={{0,2},{2,0},{4,6},{6,4},{8,10},{10,8},{12,14},{14,12},{16,18},{18,... | collective-permute-start | bytes 32 | tf_op jit(solution)/shard_map/ppermute | solution.py:343
  5.3 1.7 %collective-permute-start.1 = (bf16[48,2304]{1,0:T(8,128)(2,1)}, bf16[48,2304]{1,0:T(8,128)(2,1)S(1)}, u32[]{:S(2)}, u32[]{:S(2)}) collective-permute-start(bf16[48,2304]{1,0:T(8,128)(2,1)} %bitcast.29), channel_id=1, source_target_pairs={{0,2},{2,0},{4,6},{6,4},{8,10},{10,8},{12,14},{14,12},{16,18},{18,... | collective-permute-start | bytes 663560 | tf_op jit(solution)/shard_map/ppermute | solution.py:343
  7.0 0.9 copy-start.1
  8.0 20.7 %copy-start.2 = (f32[1,2,2,3072]{3,2,1,0:T(2,128)S(1)}, f32[1,2,2,3072]{3,2,1,0:T(2,128)}, u32[]{:S(2)}) copy-start(f32[1,2,2,3072]{3,2,1,0:T(2,128)} %param.19) | copy-start | bytes 147460
  28.6 9.6 %copy-start.4 = (bf16[1,1,128,64]{2,3,1,0:T(8,128)(2,1)S(1)}, bf16[1,1,128,64]{2,3,1,0:T(8,128)(2,1)}, u32[]{:S(2)}) copy-start(bf16[1,1,128,64]{2,3,1,0:T(8,128)(2,1)} %param.10) | copy-start | bytes 49156
  28.6 9.8 %copy-start.5 = (bf16[1,1,128,64]{2,3,1,0:T(8,128)(2,1)S(1)}, bf16[1,1,128,64]{2,3,1,0:T(8,128)(2,1)}, u32[]{:S(2)}) copy-start(bf16[1,1,128,64]{2,3,1,0:T(8,128)(2,1)} %param.11) | copy-start | bytes 49156
  28.6 9.9 %copy-start.6 = (bf16[1,1,128,64]{2,3,1,0:T(8,128)(2,1)S(1)}, bf16[1,1,128,64]{2,3,1,0:T(8,128)(2,1)}, u32[]{:S(2)}) copy-start(bf16[1,1,128,64]{2,3,1,0:T(8,128)(2,1)} %param.13) | copy-start | bytes 49156
  28.6 10.0 %copy-start.7 = (bf16[1,1,128,64]{2,3,1,0:T(8,128)(2,1)S(1)}, bf16[1,1,128,64]{2,3,1,0:T(8,128)(2,1)}, u32[]{:S(2)}) copy-start(bf16[1,1,128,64]{2,3,1,0:T(8,128)(2,1)} %param.15) | copy-start | bytes 49156
  30.9 10.4 %copy-start.3 = (bf16[1,768,64]{1,2,0:T(8,128)(2,1)S(1)}, bf16[1,768,64]{1,2,0:T(8,128)(2,1)}, u32[]{:S(2)}) copy-start(bf16[1,768,64]{1,2,0:T(8,128)(2,1)} %param.18) | copy-start | bytes 294916
  30.9 23.9 %all-to-all-start.1 = ((bf16[32,40,256]{2,1,0:T(8,128)(2,1)}), bf16[32,40,256]{2,1,0:T(8,128)(2,1)S(1)}, u32[]{:S(2)}, u32[]{:S(2)}) async-start(bf16[32,40,256]{2,1,0:T(8,128)(2,1)} %get-tuple-element.15), calls=%async_computation.1 | async-start | bytes 1310720 | tf_op jit(solution)/shard_map/all_to_all | solution.py:353
  40.0 2.2 %collective-permute-start.2 = (bf16[128,384]{1,0:T(8,128)(2,1)S(1)}, bf16[128,384]{1,0:T(8,128)(2,1)S(1)}, u32[]{:S(2)}, u32[]{:S(2)}) collective-permute-start(bf16[128,384]{1,0:T(8,128)(2,1)S(1)} %shard_map.115), channel_id=1, source_target_pairs={{0,2},{2,0},{4,6},{6,4},{8,10},{10,8},{12,14},{14,12},{16,18},{18,... | collective-permute-start | bytes 294920 | tf_op jit(solution)/shard_map/ppermute | solution.py:343
  42.2 6.2 %collective-permute-start.3 = (bf16[2,128,384]{2,1,0:T(8,128)(2,1)S(1)}, bf16[2,128,384]{2,1,0:T(8,128)(2,1)S(1)}, u32[]{:S(2)}, u32[]{:S(2)}) collective-permute-start(bf16[2,128,384]{2,1,0:T(8,128)(2,1)S(1)} %pad_maximum_fusion.here), channel_id=1, source_target_pairs={{0,1},{1,0},{2,3},{3,2},{4,5},{5,4},{6,7},{7,6},{8,9},{9,8},{10,11... | collective-permute-start | bytes 589832 | tf_op jit(solution)/shard_map/ppermute | solution.py:347
  58.9 6.0 %collective-permute-start.4 = (f32[256,128]{1,0:T(8,128)S(1)}, f32[256,128]{1,0:T(8,128)S(1)}, u32[]{:S(2)}, u32[]{:S(2)}) collective-permute-start(f32[256,128]{1,0:T(8,128)S(1)} %get-tuple-element.18), channel_id=1, source_target_pairs={{0,2},{2,0},{4,6},{6,4},{8,10},{10,8},{12,14},{14,12},{16,18},{18,... | collective-permute-start | bytes 393224 | tf_op jit(solution)/shard_map/ppermute | solution.py:343
  64.9 5.3 %collective-permute-start.5 = (f32[256,128]{1,0:T(8,128)S(1)}, f32[256,128]{1,0:T(8,128)S(1)}, u32[]{:S(2)}, u32[]{:S(2)}) collective-permute-start(f32[256,128]{1,0:T(8,128)S(1)} %add.18.vel_here), channel_id=1, source_target_pairs={{0,1},{1,0},{2,3},{3,2},{4,5},{5,4},{6,7},{7,6},{8,9},{9,8},{10,11... | collective-permute-start | bytes 393224 | tf_op jit(solution)/shard_map/ppermute | solution.py:347
  70.3 10.5 %collective-permute-start.6 = (f32[256,64]{1,0:T(8,128)S(1)}, f32[256,64]{1,0:T(8,128)S(1)}, u32[]{:S(2)}, u32[]{:S(2)}) collective-permute-start(f32[256,64]{1,0:T(8,128)S(1)} %slice.32), channel_id=1, source_target_pairs={{0,2},{2,0},{4,6},{6,4},{8,10},{10,8},{12,14},{14,12},{16,18},{18,... | collective-permute-start | bytes 196616 | tf_op jit(solution)/shard_map/ppermute | solution.py:343
  76.4 14.2 %all-to-all-start.2 = ((bf16[32,24,128]{2,1,0:T(8,128)(2,1)}), bf16[32,24,128]{2,1,0:T(8,128)(2,1)S(1)}, u32[]{:S(2)}, u32[]{:S(2)}) async-start(bf16[32,24,128]{2,1,0:T(8,128)(2,1)} %shard_map.118), calls=%async_computation.2 | async-start | bytes 393216 | tf_op jit(solution)/shard_map/all_to_all | solution.py:353
  80.9 3.3 %collective-permute-start.7 = (f32[128,64]{1,0:T(8,128)S(1)}, f32[128,64]{1,0:T(8,128)S(1)}, u32[]{:S(2)}, u32[]{:S(2)}) collective-permute-start(f32[128,64]{1,0:T(8,128)S(1)} %slice.38), channel_id=1, source_target_pairs={{0,1},{1,0},{2,3},{3,2},{4,5},{5,4},{6,7},{7,6},{8,9},{9,8},{10,11... | collective-permute-start | bytes 98312 | tf_op jit(solution)/shard_map/ppermute | solution.py:347
  91.7 3.5 %collective-permute-start.9 = (f32[2,1536]{1,0:T(2,128)S(1)}, f32[2,1536]{1,0:T(2,128)S(1)}, u32[]{:S(2)}, u32[]{:S(2)}) collective-permute-start(f32[2,1536]{1,0:T(2,128)S(1)} %get-tuple-element.27), channel_id=1, source_target_pairs={{0,2},{2,0},{4,6},{6,4},{8,10},{10,8},{12,14},{14,12},{16,18},{18,... | collective-permute-start | bytes 36872 | tf_op jit(solution)/shard_map/ppermute | solution.py:343
  95.2 2.6 %collective-permute-start.10 = (f32[2,1536]{1,0:T(2,128)S(1)}, f32[2,1536]{1,0:T(2,128)S(1)}, u32[]{:S(2)}, u32[]{:S(2)}) collective-permute-start(f32[2,1536]{1,0:T(2,128)S(1)} %add.22), channel_id=1, source_target_pairs={{0,1},{1,0},{2,3},{3,2},{4,5},{5,4},{6,7},{7,6},{8,9},{9,8},{10,11... | collective-permute-start | bytes 36872 | tf_op jit(solution)/shard_map/ppermute | solution.py:347
  98.7 14.4 %all-to-all-start.3 = ((f32[32,2,1536]{2,1,0:T(2,128)}), f32[32,2,1536]{2,1,0:T(2,128)S(1)}, u32[]{:S(2)}, u32[]{:S(2)}) async-start(f32[32,2,1536]{2,1,0:T(2,128)} %broadcast_in_dim.5), calls=%async_computation.3 | async-start | bytes 786432 | tf_op jit(solution)/shard_map/all_to_all | solution.py:353
  102.5 15.7 %collective-permute-start.8 = (bf16[128,64]{1,0:T(8,128)(2,1)S(1)}, bf16[128,64]{1,0:T(8,128)(2,1)S(1)}, u32[]{:S(2)}, u32[]{:S(2)}) collective-permute-start(bf16[128,64]{1,0:T(8,128)(2,1)S(1)} %fusion.2), channel_id=1, source_target_pairs={{0,128},{128,0},{1,129},{129,1},{2,130},{130,2},{3,131},{131,3},{4... | collective-permute-start | bytes 49160 | tf_op jit(solution)/shard_map/ppermute | solution.py:453
  113.2 5.9 %collective-permute-start.11 = (f32[2,1536]{1,0:T(2,128)S(1)}, f32[2,1536]{1,0:T(2,128)S(1)}, u32[]{:S(2)}, u32[]{:S(2)}) collective-permute-start(f32[2,1536]{1,0:T(2,128)S(1)} %reduce_sum.9), channel_id=1, source_target_pairs={{0,2},{2,0},{4,6},{6,4},{8,10},{10,8},{12,14},{14,12},{16,18},{18,... | collective-permute-start | bytes 36872 | tf_op jit(solution)/shard_map/ppermute | solution.py:343

commit v3 on v2

v3 whole, which is shorter than its diff:
```python
import functools

import jax
import jax.numpy as jnp
from jax import lax
from jax.experimental import pallas as pl
from jax.experimental.pallas import tpu as pltpu
from jax.sharding import PartitionSpec as P

HEAD_DIM = 128
CHANNELS = 64
EPSILON = 1e-06
F32 = jnp.float32
BF16 = jnp.bfloat16
NT = (((1,), (1,)), ((), ()))
NN = (((1,), (0,)), ((), ()))
TN = (((0,), (0,)), ((), ()))


def dot(a, b, dims=NN):
    return lax.dot_general(a, b, dims, preferred_element_type=F32)


def round_up(value, step):
    return (value + step - 1) // step * step


def rounded(value):
    return value.astype(BF16).astype(F32)


def three_parts(value):
    high = rounded(value)
    middle = rounded(value - high)
    return high, middle, rounded(value - high - middle)


def lane_index(shape):
    return lax.broadcasted_iota(jnp.int32, shape, len(shape) - 1)


def row_index(shape):
    return lax.broadcasted_iota(jnp.int32, shape, len(shape) - 2)


def on_second_core():
    return lax.rem(lax.axis_index("fsdp"), 2) == 1


def on_critic():
    return lax.axis_index("role") == 1


def pack_kernel(noise_levels, replay_levels, base, noise, replay, cotangent, embed, pack):
    critic = on_critic()
    level = noise_levels[0, 0]
    level_two = jnp.where(critic, level, replay_levels[0, 0])
    base_f = base[...].astype(F32)
    noise_f = noise[...].astype(F32)
    input_a = rounded((1.0 - level) * base_f + level * noise_f)
    input_b = jnp.where(critic, input_a, replay[...].astype(F32))
    known = jnp.where(critic, noise_f - base_f, cotangent[...].astype(F32))
    known_high = rounded(known)
    tokens = input_a.shape[0]
    rows = jnp.concatenate([input_a, input_b], axis=0).astype(BF16)
    total = jnp.zeros((2 * tokens, 1), F32)
    width = embed.shape[1]
    for start in range(0, width, 512):
        embedded = dot(rows, embed[:, start : start + 512])
        total = total + jnp.sum(embedded * embedded, axis=-1, keepdims=True)
    scale = lax.rsqrt(total / width + EPSILON)
    lane = lane_index((tokens, 128))
    tail = jnp.zeros((tokens, 128), F32)
    ones = jnp.ones((tokens, 1), F32)
    for which, column in enumerate((scale[:tokens], scale[tokens:], ones * level, ones * level_two)):
        for part, value in enumerate(three_parts(column)):
            tail = jnp.where(lane == which * 3 + part, value, tail)
    pack[:, 0:64] = input_a.astype(BF16)
    pack[:, 64:128] = input_b.astype(BF16)
    pack[:, 128:192] = known_high.astype(BF16)
    pack[:, 192:256] = (known - known_high).astype(BF16)
    pack[:, 256:384] = tail.astype(BF16)


def cut_kernel(weight, keep, send):
    second = on_second_core()
    columns = keep.shape[1]
    left = weight[:, 0:columns].astype(F32)
    right = weight[:, columns:].astype(F32)
    keep[...] = jnp.where(second, right, left).astype(BF16)
    send[...] = jnp.where(second, left, right).astype(BF16)


def weight_kernel(chips, keep, received, out, turned):
    second = on_second_core()
    rows, columns = received.shape
    own = keep[...].astype(F32)
    other = received[...].astype(F32)
    both = [jnp.where(second, other, own), jnp.where(second, own, other)]
    padded = out.shape[2]
    if padded > 2 * rows:
        both.append(jnp.zeros((padded - 2 * rows, columns), F32))
    turned[0:columns, :] = jnp.concatenate(both, axis=0).T
    turned[columns:, :] = jnp.zeros((turned.shape[0] - columns, padded), F32)
    block = columns // chips
    height = out.shape[1]
    row = row_index((height, padded))
    for chip in range(chips):
        piece = turned[chip * block : chip * block + height, :]
        out[chip] = jnp.where(row < block, piece, 0.0).astype(BF16)


def product_kernel(block, taken, embed, modulation, out, halves_out, columns_out):
    critic = on_critic()
    chips, height, padded = taken.shape
    half = block // 2
    stride = halves_out.shape[0] // 2
    width = embed.shape[1]
    depth = width // chips
    row_half = row_index((stride, 1))
    group = 1 if depth % 128 == 0 else 128 // (depth & -depth)
    for start in range(0, chips, group):
        pieces = [taken[chip].astype(F32)[:, 0:depth] for chip in range(start, start + group)]
        joined = jnp.concatenate(pieces, axis=1) if group > 1 else pieces[0]
        span = slice(start * depth, (start + group) * depth)
        columns_out[:, span] = joined.astype(BF16)
        longer = jnp.concatenate([joined, jnp.zeros((stride, joined.shape[1]), F32)], axis=0)
        low = jnp.where(row_half < half, longer[0:stride], 0.0)
        high = jnp.where(row_half < half, longer[half : half + stride], 0.0)
        halves_out[:, span] = jnp.concatenate([low, high], axis=0).astype(BF16)
    weight = columns_out[...]
    embed_b = embed[...]
    embed_f = embed_b.astype(F32)
    modulation_a = modulation[0]
    modulation_b = jnp.where(critic, modulation[1], modulation_a)
    scaled_a = (embed_f * modulation_a[0:1, :]).astype(BF16)
    scaled_b = (embed_f * modulation_b[0:1, :]).astype(BF16)
    first = dot(weight, jnp.concatenate([embed_b, scaled_a], axis=0), NT)
    second = dot(weight, jnp.concatenate([scaled_b, scaled_b], axis=0), NT)
    shifts = []
    for pair in (modulation_a, modulation_b):
        shift = pair[1:2, :]
        high = rounded(shift)
        shifts += [high, shift - high]
    shifts.append(jnp.zeros((4, width), F32))
    offsets = dot(jnp.concatenate(shifts, axis=0).astype(BF16), weight, NT)
    lines = []
    gap = jnp.zeros((1, CHANNELS - block), F32)
    for offset in (offsets[0:1, 0:block] + offsets[1:2, 0:block], offsets[2:3, 0:block] + offsets[3:4, 0:block]):
        high = rounded(offset)
        lines.append(jnp.concatenate([high, gap, offset - high, gap], axis=1))
    low_lanes = lane_index((half, 128)) < CHANNELS
    folded = jnp.where(low_lanes, second[0:half], second[half:block])
    spare = out.shape[1] - block - half - 2
    parts = [first[0:block], folded] + lines
    if spare:
        parts.append(jnp.zeros((spare, 128), F32))
    whole = jnp.concatenate(parts, axis=0).astype(BF16)
    for chip in range(chips):
        out[chip] = whole


def token_rows(packs, sample, start, stop):
    return jnp.concatenate([pack[sample, :, start:stop] for pack in packs], axis=0)


def tail_column(packs, sample, which):
    tail = token_rows(packs, sample, 256, 384).astype(F32)
    at = 3 * which
    return tail[:, at : at + 1] + tail[:, at + 1 : at + 2] + tail[:, at + 2 : at + 3]


def forward(which, packs, matrices, offsets, output_weight, keep, velocity):
    heads = output_weight.shape[0] // HEAD_DIM
    low_lanes = lane_index((1, 128)) < CHANNELS
    rows, scales, levels = [], [], []
    for sample in range(2):
        inputs = token_rows(packs, sample, 0, 128).astype(F32)
        turned = pltpu.roll(inputs, CHANNELS, 1)
        level = tail_column(packs, sample, 2 + which)
        plain, scaled = (turned, inputs) if which else (inputs, turned)
        rows.append(jnp.where(low_lanes, plain, scaled * level).astype(BF16))
        scales.append(tail_column(packs, sample, which))
        levels.append(level[0:1])
    tokens = rows[0].shape[0]
    inputs = jnp.concatenate(rows, axis=0)
    totals = [jnp.zeros((tokens, CHANNELS), F32), jnp.zeros((tokens, CHANNELS), F32)]
    for head in range(heads):
        at = head * 3 * HEAD_DIM
        product = dot(inputs, matrices[at : at + 3 * HEAD_DIM, :], NT)
        offset = offsets[which : which + 1, at : at + 3 * HEAD_DIM]
        for sample in range(2):
            qkv = product[sample * tokens : (sample + 1) * tokens] * scales[sample] + offset * levels[sample]
            qkv = qkv.astype(BF16)
            if keep is not None:
                keep[sample, :, at : at + 3 * HEAD_DIM] = qkv
            query = qkv[:, 0:HEAD_DIM]
            key = qkv[:, HEAD_DIM : 2 * HEAD_DIM]
            value = qkv[:, 2 * HEAD_DIM :]
            scores = dot(query, key, NT) * (HEAD_DIM**-0.5)
            top = jnp.max(scores, axis=-1, keepdims=True)
            powers = jnp.exp(scores - top)
            probs = powers / jnp.sum(powers, axis=-1, keepdims=True)
            mixed = dot(probs.astype(BF16), value).astype(BF16)
            totals[sample] = totals[sample] + dot(mixed, output_weight[head * HEAD_DIM : (head + 1) * HEAD_DIM, :])
    velocity[...] = jnp.concatenate(totals, axis=1)


def second_pass_kernel(
    block, taken, here, there, output_weight, matrices, offsets, keep, velocity, crossing, stacked, stacked_two
):
    chips = taken.shape[0]
    half = block // 2
    low_lanes = lane_index((half, 128)) < CHANNELS
    lines = [[], []]
    for chip in range(chips):
        piece = taken[chip].astype(F32)
        at = chip * block
        stacked[at : at + block, :] = piece[0:block]
        folded = piece[block : block + half]
        turned = pltpu.roll(folded, CHANNELS, 1)
        stacked_two[at : at + half, :] = jnp.where(low_lanes, piece[0:half], turned)
        stacked_two[at + half : at + block, :] = jnp.where(low_lanes, piece[half:block], folded)
        for which in range(2):
            line = piece[block + half + which : block + half + which + 1]
            lines[which].append((line + pltpu.roll(line, CHANNELS, 1))[:, 0:block])
    matrices[...] = stacked[...].astype(BF16)
    joined = [jnp.concatenate(line, axis=1) for line in lines]
    offsets[...] = jnp.concatenate(joined + [jnp.zeros((6, offsets.shape[1]), F32)], axis=0)
    forward(1, (here, there), stacked_two[...].astype(BF16), offsets, output_weight, keep, velocity)
    crossing[...] = pltpu.roll(velocity[...], CHANNELS, 1)


def first_pass_kernel(matrices, offsets, here, there, output_weight, velocity):
    forward(0, (here, there), matrices, offsets, output_weight, None, velocity)


def probs_kernel(kept, out):
    heads = out.shape[0] // 2
    for unit in range(2 * heads):
        at = unit // 2 * 3 * HEAD_DIM
        qkv = kept[unit % 2, :, at : at + 2 * HEAD_DIM]
        scores = dot(qkv[:, HEAD_DIM:], qkv[:, 0:HEAD_DIM], NT) * (HEAD_DIM**-0.5)
        top = jnp.max(scores, axis=0, keepdims=True)
        powers = jnp.exp(scores - top)
        out[unit] = powers / jnp.sum(powers, axis=0, keepdims=True)


def swap_tokens(value):
    half = value.shape[0] // 2
    return jnp.concatenate([value[half:], value[:half]], axis=0)


def backward_kernel(block, kept, probs_turned, here, there, vel_here, vel_there, output_weight, out, gathered, summed):
    critic = on_critic()
    packs = (here, there)
    heads = output_weight.shape[0] // HEAD_DIM
    velocity = vel_here[...] + swap_tokens(vel_there[...])
    lane = lane_index((1, 128))
    grads, rows, levels = [], [], []
    for sample in range(2):
        known = token_rows(packs, sample, 128, 256).astype(F32)
        known = known[:, 0:CHANNELS] + known[:, CHANNELS:]
        total = velocity[:, sample * CHANNELS : (sample + 1) * CHANNELS]
        grads.append(jnp.where(critic, total - known, known).astype(BF16))
        inputs = token_rows(packs, sample, 0, 128).astype(F32)
        inputs = jnp.where(lane < CHANNELS, pltpu.roll(inputs, CHANNELS, 1), inputs)
        level = tail_column(packs, sample, 3)
        levels.append(level[0:1])
        scaled = inputs * (tail_column(packs, sample, 1) * level)
        rows.append(scaled.T.astype(BF16))
    for head in range(heads):
        at = head * 3 * HEAD_DIM
        total, ends = None, None
        for sample in range(2):
            qkv = kept[sample, :, at : at + 3 * HEAD_DIM]
            query = qkv[:, 0:HEAD_DIM]
            key = qkv[:, HEAD_DIM : 2 * HEAD_DIM]
            value = qkv[:, 2 * HEAD_DIM :]
            grad_mixed = dot(grads[sample], output_weight[head * HEAD_DIM : (head + 1) * HEAD_DIM, :], NT).astype(BF16)
            probs = probs_turned[2 * head + sample]
            grad_value = dot(probs.astype(BF16), grad_mixed)
            grad_probs = dot(value, grad_mixed, NT)
            inner = jnp.sum(grad_probs * probs, axis=0, keepdims=True)
            grad_scores = (probs * (grad_probs - inner) * (HEAD_DIM**-0.5)).astype(BF16)
            grad_key = dot(grad_scores, query)
            grad_query = dot(grad_scores, key, TN)
            grad = jnp.concatenate([grad_query, grad_key, grad_value], axis=1).astype(BF16)
            term = dot(rows[sample], grad)
            end = jnp.sum(grad.astype(F32), axis=0, keepdims=True) * levels[sample]
            total = term if total is None else total + term
            ends = end if ends is None else ends + end
        gathered[at : at + 3 * HEAD_DIM, :] = total.T
        summed[:, at : at + 3 * HEAD_DIM] = ends
    columns = heads * 3 * HEAD_DIM
    gathered[columns:, :] = jnp.zeros((gathered.shape[0] - columns, 128), F32)
    chips, height = out.shape[0], out.shape[1]
    half = block // 2
    row = row_index((height, 128))
    low_lanes = lane_index((height, 128)) < CHANNELS
    pad = jnp.zeros((1, 128 - block), F32) if block < 128 else None
    for chip in range(chips):
        at = chip * block
        piece = jnp.where(low_lanes, gathered[at : at + height, :], gathered[at + half : at + half + height, :])
        line = summed[:, at : at + block]
        high = rounded(line)
        pair = [high, line - high]
        if pad is not None:
            pair = [jnp.concatenate([part, pad], axis=1) for part in pair]
        piece = jnp.where(row < half, piece, jnp.where(row == half, pair[0], jnp.where(row == half + 1, pair[1], 0.0)))
        out[chip] = piece.astype(BF16)


def closing_kernel(block, factor, taken, weight, embed, kept, sent):
    second = on_second_core()
    total = taken[0].astype(F32)
    for chip in range(1, taken.shape[0]):
        total = total + taken[chip].astype(F32)
    half = block // 2
    height = total.shape[0]
    row = row_index((height, 128))
    ends = total[half : half + 1] + total[half + 1 : half + 2]
    turned = jnp.where(row < half, total, 0.0).T
    lane = lane_index((1, 128))
    ends_low = jnp.where(lane < half, ends, 0.0)[:, 0:height]
    ends_high = jnp.where(lane < half, pltpu.roll(ends, 128 - half, 1), 0.0)[:, 0:height]
    lower = jnp.concatenate([turned[0:CHANNELS], ends_low, jnp.zeros((7, height), F32)], axis=0)
    upper = jnp.concatenate([turned[CHANNELS:], ends_high, jnp.zeros((7, height), F32)], axis=0)
    joined = jnp.concatenate([lower, upper], axis=1)
    high = joined.astype(BF16)
    low = (joined - high.astype(F32)).astype(BF16)
    middle = embed.shape[1] // 2
    step = middle // 3
    parts = []
    for start in range(0, 2 * middle, step):
        columns = weight[:, start : start + step]
        product = dot(high, columns) + dot(low, columns)
        scale = jnp.sum(product[:CHANNELS] * embed[:, start : start + step].astype(F32), axis=0, keepdims=True)
        parts.append(jnp.concatenate([scale, product[CHANNELS : CHANNELS + 1]], axis=0) * factor)
    left = jnp.concatenate(parts[:3], axis=1)
    right = jnp.concatenate(parts[3:], axis=1)
    kept[...] = jnp.where(second, right, left)
    sent[...] = jnp.where(second, left, right)


def call(kernel, out_shapes, inputs, scalars=0, scratch=(), flops=0, moved=0):
    specs = [pl.BlockSpec(memory_space=pltpu.SMEM)] * scalars
    specs += [pl.BlockSpec(memory_space=pltpu.VMEM)] * (len(inputs) - scalars)
    return pl.pallas_call(
        kernel,
        out_shape=out_shapes,
        in_specs=specs,
        out_specs=jax.tree.map(lambda _: pl.BlockSpec(memory_space=pltpu.VMEM), out_shapes),
        scratch_shapes=list(scratch),
        compiler_params=pltpu.CompilerParams(vmem_limit_bytes=28 * 2**20),
        cost_estimate=pl.CostEstimate(flops=flops, bytes_accessed=moved, transcendentals=0),
    )(*inputs)


def struct(shape, dtype):
    return jax.ShapeDtypeStruct(shape, dtype)


def other_core(value):
    return lax.ppermute(value, "fsdp", [(i, i ^ 1) for i in range(lax.axis_size("fsdp"))])


def other_half(value):
    return lax.ppermute(value, "seq", [(0, 1), (1, 0)])


def between_chips(value):
    count = lax.axis_size("fsdp")
    groups = [list(range(core, count, 2)) for core in range(2)]
    return lax.all_to_all(value, "fsdp", 0, 0, tiled=True, axis_index_groups=groups)


def per_device(
    base_latents,
    noise_latents,
    noise_levels,
    replay_latents,
    replay_levels,
    cotangent,
    embed_weight,
    qkv_weight,
    output_weight,
    modulation,
):
    is_critic = on_critic()
    second_core = on_second_core()
    devices = lax.axis_size("fsdp")
    chips = devices // 2
    embed = embed_weight[0]
    weight = qkv_weight[0]
    width = embed.shape[1]
    columns = weight.shape[1] // 2
    block = columns // chips
    height = round_up(block, 8)
    packed = round_up(block + block // 2 + 2, 8)
    folded = round_up(block // 2 + 2, 8)
    padded = round_up(2 * weight.shape[0], 128)
    tokens = base_latents.shape[2]
    heads = columns // (3 * HEAD_DIM)
    out_rows = output_weight.shape[1] // 2
    out_half = jnp.where(second_core, output_weight[0, out_rows:], output_weight[0, :out_rows])

    keep, send = call(
        cut_kernel,
        (struct((weight.shape[0], columns), BF16), struct((weight.shape[0], columns), BF16)),
        (weight,),
    )
    turned = call(
        functools.partial(weight_kernel, chips),
        struct((chips, height, padded), BF16),
        (keep, other_core(send)),
        scratch=[pltpu.VMEM((columns + height - block, padded), F32)],
    )

    own = call(
        pack_kernel,
        struct((tokens, 384), BF16),
        (
            noise_levels,
            replay_levels,
            base_latents[0, 0],
            noise_latents[0, 0],
            replay_latents[0, 0],
            cotangent[0, 0],
            embed,
        ),
        scalars=2,
    )
    here = jnp.stack([own, other_core(own)])
    there = other_half(here)

    matrices, own_columns = call(
        functools.partial(product_kernel, block),
        (struct((chips, packed, 128), BF16), struct((2 * folded, width), BF16)),
        (between_chips(turned), embed, modulation[0]),
        scratch=[pltpu.VMEM((height, width), BF16)],
    )
    whole, offsets, kept, vel_b, vel_crossing = call(
        functools.partial(second_pass_kernel, block),
        (
            struct((columns, 2 * CHANNELS), BF16),
            struct((8, columns), F32),
            struct((2, 2 * tokens, columns), BF16),
            struct((2 * tokens, 2 * CHANNELS), F32),
            struct((2 * tokens, 2 * CHANNELS), F32),
        ),
        (between_chips(matrices), here, there, out_half),
        scratch=[pltpu.VMEM((columns, 2 * CHANNELS), F32), pltpu.VMEM((columns, 2 * CHANNELS), F32)],
    )
    vel_here = vel_b + other_core(vel_crossing)
    vel_there = other_half(vel_here)
    probs = call(probs_kernel, struct((2 * heads, 2 * tokens, 2 * tokens), F32), (kept,), flops=2 * 10**9)
    vel_there, probs = lax.optimization_barrier((vel_there, probs))
    products = call(
        functools.partial(backward_kernel, block),
        struct((chips, folded, 128), BF16),
        (kept, probs, here, there, vel_here, vel_there, out_half),
        scratch=[pltpu.VMEM((columns + 2 * folded, 128), F32), pltpu.VMEM((1, columns), F32)],
    )
    gathered = between_chips(products)

    vel_a = call(
        first_pass_kernel,
        struct((2 * tokens, 2 * CHANNELS), F32),
        (whole, offsets, here, there, out_half),
        flops=4 * 10**9,
    )
    own_a = vel_a[:, :CHANNELS] + other_core(vel_a[:, CHANNELS:])
    gathered, own_a = lax.optimization_barrier((gathered, own_a))
    own_a = own_a[:tokens] + other_half(own_a[tokens:])
    own_b = vel_here[:tokens, :CHANNELS] + vel_there[tokens:, :CHANNELS]
    sample = own[:, :CHANNELS].astype(F32) - noise_levels[0, 0] * own_a
    payload = jnp.where(is_critic, own_b - own_a, sample).T
    crossed = lax.ppermute(payload.astype(BF16), "role", [(0, 1), (1, 0)]).T

    samples = devices * base_latents.shape[1]
    kept_half, sent_half = call(
        functools.partial(closing_kernel, block, 1.0 / (samples * 2 * tokens)),
        (struct((2, width // 2), F32), struct((2, width // 2), F32)),
        (gathered, own_columns, embed),
    )
    total = kept_half + other_core(sent_half)
    total = (total + other_half(total)).astype(BF16)
    spread = between_chips(jnp.broadcast_to(total[None], (chips,) + total.shape))
    total = jnp.sum(spread.astype(F32), axis=0)
    near_total = other_core(total)
    mod_grads = jnp.where(
        second_core,
        jnp.concatenate([near_total, total], axis=1),
        jnp.concatenate([total, near_total], axis=1),
    )
    return (crossed[None, None], mod_grads[None])


def solution(mesh):
    return jax.shard_map(
        per_device,
        mesh=mesh,
        in_specs=(
            P("role", "fsdp", "seq", None),
            P("role", "fsdp", "seq", None),
            P("role", "fsdp"),
            P("role", "fsdp", "seq", None),
            P("role", "fsdp"),
            P("role", "fsdp", "seq", None),
            P("role", None, None),
            P("role", "fsdp", "seq"),
            P("role", "seq", None),
            P("role", None, None, None),
        ),
        out_specs=(P("role", "fsdp", "seq", None), P("role", None, None)),
        check_vma=False,
    )
```

time: 120 us -> 107 us (0.89)
  waiting for transfers between devices: 32.3 us -> 23.6 us
  Pallas kernels: 18.4 us -> 14.1 us
    all_to_all x3, waiting for transfers between devices: 20.2 us -> 8.43 us  [between_chips(): lax.all_to_all(value, 'fsdp', 0, 0, tiled=True, axis_index_groups=groups)]
    pallas_call x7 -> x9, Pallas kernels: 18.4 us -> 14.1 us  [call(): pl.pallas_call(kernel, out_shape=out_shapes, in_specs=specs, out_specs=ja...]
    ppermute x4, waiting for transfers between devices: 8.03 us -> 10.6 us  [other_half(): return lax.ppermute(value, 'seq', [(0, 1), (1, 0)])]
    ppermute x7 -> x6, starting transfers between devices: 18.3 us -> 16.7 us  [other_core(): lax.ppermute(value, 'fsdp', [(i, i ^ 1) for i in range(lax.axis_size('fsd...]
    ppermute x7 -> x6, waiting for transfers between devices: 4.06 us -> 4.57 us  [other_core(): lax.ppermute(value, 'fsdp', [(i, i ^ 1) for i in range(lax.axis_size('fsd...]
  transfers between devices with their start and end apart: 15 -> 14, of which waited for: 12 -> 13; matrix products, arithmetic and copies ran while one was open for 1% -> 2% of each run, Pallas kernels for 9% -> 4%
where the time goes in v3:
time: 107 us; the launch traced here: 106 us
  starting transfers between devices  41.9 us (39%)
  waiting for transfers between devices  23.6 us (22%)
  blocking collectives  19.7 us (18%)
  Pallas kernels  14.1 us (13%)
  local copies, waits for them, and re-layouts  4.09 us (4%)
  between operations  2.13 us (2%)
    all_to_all x1, blocking collectives, between_chips(): lax.all_to_all(value, 'fsdp', 0, 0, tiled=True, axis_index_groups=groups)  19.7 us
    ppermute x6, starting transfers between devices, other_core(): lax.ppermute(value, 'fsdp', [(i, i ^ 1) for i in range(lax.axis_size('fsd...  16.7 us
    all_to_all x3, starting transfers between devices, between_chips(): lax.all_to_all(value, 'fsdp', 0, 0, tiled=True, axis_index_groups=groups)  16.7 us
    pallas_call x9, Pallas kernels, call(): pl.pallas_call(kernel, out_shape=out_shapes, in_specs=specs, out_specs=ja...  14.1 us
    ppermute x4, waiting for transfers between devices, other_half(): return lax.ppermute(value, 'seq', [(0, 1), (1, 0)])  10.6 us
    all_to_all x3, waiting for transfers between devices, between_chips(): lax.all_to_all(value, 'fsdp', 0, 0, tiled=True, axis_index_groups=groups)  8.43 us
    ppermute x4, starting transfers between devices, other_half(): return lax.ppermute(value, 'seq', [(0, 1), (1, 0)])  5.53 us
    ppermute x6, waiting for transfers between devices, other_core(): lax.ppermute(value, 'fsdp', [(i, i ^ 1) for i in range(lax.axis_size('fsd...  4.57 us
  transfers between devices with their start and end apart: 14, of which 13 were waited for; matrix products, arithmetic and copies ran while one was open for 2% of the time, Pallas kernels for 4%

profile of v3, /device:TPU:1, one launch (start us, length us, event | category | flops | bytes accessed | tf_op | source)
XLA Modules:
  0.0 106.2 jit_solution(10552510686290784858)
XLA Ops:
  0.6 0.0 copy-start
  0.6 0.0 copy-start.1
  0.7 1.0 copy-done.1
  1.6 0.0 copy-start.4
  1.6 0.0 copy-start.5
  1.6 0.0 copy-start.6
  1.6 0.1 shard_map.113
  1.7 0.0 copy-start.7
  1.7 3.3 %collective-permute-start = (bf16[48,1152]{1,0:T(8,128)(2,1)S(1)}, bf16[48,1152]{1,0:T(8,128)(2,1)S(1)}, u32[]{:S(2)}, u32[]{:S(2)}) collective-permute-start(bf16[48,1152]{1,0:T(8,128)(2,1)S(1)} %get-tuple-element.18), channel_id=1, source_target_pairs={{0,2},{2,0},{4,6},{6,4},{8,10},{10,8},{12,14},{14,12},{16,18},{18,... | collective-permute-start | bytes 331784 | tf_op jit(solution)/shard_map/ppermute | solution.py:365
  5.0 1.0 collective-permute-done.received
  6.0 0.2 shard_map.114
  6.2 0.0 copy-start.3
  6.2 19.7 %all_to_all.20.taken = bf16[32,40,128]{2,1,0:T(8,128)(2,1)S(1)} all-to-all(bf16[32,40,128]{2,1,0:T(8,128)(2,1)S(1)} %shard_map.114), channel_id=1, replica_groups={{0,4,8,12,16,20,24,28,32,36,40,44,48,52,56,60,64,68,72,76,80,84,88,92,9..., dimensions={0} | all-to-all | bytes 655360 | tf_op jit(solution)/shard_map/all_to_all | solution.py:375
  26.0 0.0 copy-done
  26.0 0.0 copy-start.2
  26.0 0.8 copy-done.2
  26.8 1.6 %shard_map.115 = (bf16[32,56,128]{2,1,0:T(8,128)(2,1)}, bf16[48,3072]{1,0:T(8,128)(2,1)S(1)}) custom-call(bf16[32,40,128]{2,1,0:T(8,128)(2,1)S(1)} %all_to_all.20.taken, bf16[64,3072]{1,0:T(8,128)(2,1)S(1)} %bitcast.20, f32[2,2,3072]{2,1,0:T(2,128)S(1)} %bitcast.29), custom_call_target="tpu_custom_call" | custom-call | tf_op jit(solution)/shard_map/pallas_call | solution.py:349
  28.4 7.5 %all-to-all-start.1 = ((bf16[32,56,128]{2,1,0:T(8,128)(2,1)}), bf16[32,56,128]{2,1,0:T(8,128)(2,1)S(1)}, u32[]{:S(2)}, u32[]{:S(2)}) async-start(bf16[32,56,128]{2,1,0:T(8,128)(2,1)} %get-tuple-element.19), calls=%async_computation.1 | async-start | bytes 917504 | tf_op jit(solution)/shard_map/all_to_all | solution.py:375
  37.2 0.0 copy-done.4
  37.2 0.1 copy.34
  37.3 0.0 copy-done.5
  37.3 0.1 copy.35
  37.5 0.0 copy-done.6
  37.5 0.1 copy.36
  37.6 0.0 copy-done.7
  37.6 0.1 copy.37
  37.7 0.7 shard_map.116
  38.4 1.3 %collective-permute-start.1 = (bf16[128,384]{1,0:T(8,128)(2,1)S(1)}, bf16[128,384]{1,0:T(8,128)(2,1)S(1)}, u32[]{:S(2)}, u32[]{:S(2)}) collective-permute-start(bf16[128,384]{1,0:T(8,128)(2,1)S(1)} %shard_map.116), channel_id=1, source_target_pairs={{0,2},{2,0},{4,6},{6,4},{8,10},{10,8},{12,14},{14,12},{16,18},{18,... | collective-permute-start | bytes 294920 | tf_op jit(solution)/shard_map/ppermute | solution.py:365
  39.7 0.0 copy-done.3
  39.7 0.1 copy.43
  39.8 0.1 copy.42
  40.0 0.7 collective-permute-done.1
  40.7 1.4 %collective-permute-start.2 = (bf16[2,128,384]{2,1,0:T(8,128)(2,1)S(1)}, bf16[2,128,384]{2,1,0:T(8,128)(2,1)S(1)}, u32[]{:S(2)}, u32[]{:S(2)}) collective-permute-start(bf16[2,128,384]{2,1,0:T(8,128)(2,1)S(1)} %pad_maximum_fusion.here), channel_id=1, source_target_pairs={{0,1},{1,0},{2,3},{3,2},{4,5},{5,4},{6,7},{7,6},{8,9},{9,8},{10,11... | collective-permute-start | bytes 589832 | tf_op jit(solution)/shard_map/ppermute | solution.py:369
  42.1 4.8 %collective-permute-done.2.there = bf16[2,128,384]{2,1,0:T(8,128)(2,1)S(1)} collective-permute-done((bf16[2,128,384]{2,1,0:T(8,128)(2,1)S(1)}, bf16[2,128,384]{2,1,0:T(8,128)(2,1)S(1)}, u32[]{:S(2)}, u32[]{:S(2)}) %collective-permute-start.2) | collective-permute-done | bytes 196640 | tf_op jit(solution)/shard_map/ppermute | solution.py:369
  46.9 1.4 %all-to-all-done.1.taken = bf16[32,56,128]{2,1,0:T(8,128)(2,1)S(1)} async-done(((bf16[32,56,128]{2,1,0:T(8,128)(2,1)}), bf16[32,56,128]{2,1,0:T(8,128)(2,1)S(1)}, u32[]{:S(2)}, u32[]{:S(2)}) %all-to-all-start.1) | async-done | bytes 458784 | tf_op jit(solution)/shard_map/all_to_all | solution.py:375
  48.3 2.9 %shard_map.117 = (bf16[1152,128]{1,0:T(8,128)(2,1)S(1)}, f32[8,1152]{1,0:T(8,128)S(1)}, bf16[2,256,1152]{2,1,0:T(8,128)(2,1)S(1)}, f32[256,128]{1,0:T(8,128)S(1)}, f32[256,128]{1,0:T(8,128)S(1)}) custom-call(bf16[32,56,128]{2,1,0:T(8,128)(2,1)S(1)} %all-to-all-done.1.taken, bf16[2,128,384]{2,1,0:T(8,128)(2,1)S(1)} %pad_maximum_fusion.here, ...), custom_call_target="tpu_custom_call" | custom-call | tf_op jit(solution)/shard_map/pallas_call | solution.py:349
  51.2 4.3 %collective-permute-start.3 = (f32[256,128]{1,0:T(8,128)S(1)}, f32[256,128]{1,0:T(8,128)S(1)}, u32[]{:S(2)}, u32[]{:S(2)}) collective-permute-start(f32[256,128]{1,0:T(8,128)S(1)} %get-tuple-element.21), channel_id=1, source_target_pairs={{0,2},{2,0},{4,6},{6,4},{8,10},{10,8},{12,14},{14,12},{16,18},{18,... | collective-permute-start | bytes 393224 | tf_op jit(solution)/shard_map/ppermute | solution.py:365
  55.5 1.0 collective-permute-done.3
  56.5 1.4 %collective-permute-start.4 = (f32[256,128]{1,0:T(8,128)S(1)}, f32[256,128]{1,0:T(8,128)S(1)}, u32[]{:S(2)}, u32[]{:S(2)}) collective-permute-start(f32[256,128]{1,0:T(8,128)S(1)} %add.18.vel_here), channel_id=1, source_target_pairs={{0,1},{1,0},{2,3},{3,2},{4,5},{5,4},{6,7},{7,6},{8,9},{9,8},{10,11... | collective-permute-start | bytes 393224 | tf_op jit(solution)/shard_map/ppermute | solution.py:369
  57.9 0.7 shard_map.118.probs_turned
  58.7 2.7 %collective-permute-done.4.vel_there = f32[256,128]{1,0:T(8,128)S(1)} collective-permute-done((f32[256,128]{1,0:T(8,128)S(1)}, f32[256,128]{1,0:T(8,128)S(1)}, u32[]{:S(2)}, u32[]{:S(2)}) %collective-permute-start.4) | collective-permute-done | bytes 131104 | tf_op jit(solution)/shard_map/ppermute | solution.py:369
  61.3 4.6 %shard_map.119 = bf16[32,24,128]{2,1,0:T(8,128)(2,1)} custom-call(bf16[2,256,1152]{2,1,0:T(8,128)(2,1)S(1)} %get-tuple-element.22.kept, f32[6,256,256]{2,1,0:T(8,128)S(1)} %shard_map.118.probs_turned, bf16[2,128,384]{2,1,0:T(8,128)(2,1)S(1)} %pad_maximum_fusion.here, bf16[2,128,384]{2,1,0:T(8,128)(2,1)S(1)} %collective-permute-done.2.there, ...), custom_call_target="tpu_custom_call" | custom-call | tf_op jit(solution)/shard_map/pallas_call | solution.py:349
  65.9 5.3 %all-to-all-start.2 = ((bf16[32,24,128]{2,1,0:T(8,128)(2,1)}), bf16[32,24,128]{2,1,0:T(8,128)(2,1)S(1)}, u32[]{:S(2)}, u32[]{:S(2)}) async-start(bf16[32,24,128]{2,1,0:T(8,128)(2,1)} %shard_map.119), calls=%async_computation.2 | async-start | bytes 393216 | tf_op jit(solution)/shard_map/all_to_all | solution.py:375
  71.2 2.7 %shard_map.120 = f32[256,128]{1,0:T(8,128)S(1)} custom-call(bf16[1152,128]{1,0:T(8,128)(2,1)S(1)} %get-tuple-element.25.matrices, f32[8,1152]{1,0:T(8,128)S(1)} %get-tuple-element.26.offsets, bf16[2,128,384]{2,1,0:T(8,128)(2,1)S(1)} %pad_maximum_fusion.here, bf16[2,128,384]{2,1,0:T(8,128)(2,1)S(1)} %collective-permute-done.2.there, ...), custom_call_target="tpu_custom_call" | custom-call | flops 4000000000 | tf_op jit(solution)/shard_map/pallas_call | solution.py:349
  73.9 0.1 slice.38
  74.0 1.6 %collective-permute-start.5 = (f32[256,64]{1,0:T(8,128)S(1)}, f32[256,64]{1,0:T(8,128)S(1)}, u32[]{:S(2)}, u32[]{:S(2)}) collective-permute-start(f32[256,64]{1,0:T(8,128)S(1)} %slice.38), channel_id=1, source_target_pairs={{0,2},{2,0},{4,6},{6,4},{8,10},{10,8},{12,14},{14,12},{16,18},{18,... | collective-permute-start | bytes 196616 | tf_op jit(solution)/shard_map/ppermute | solution.py:365
  75.6 1.0 collective-permute-done.5
  76.6 3.9 %all-to-all-done.2.taken = bf16[32,24,128]{2,1,0:T(8,128)(2,1)S(1)} async-done(((bf16[32,24,128]{2,1,0:T(8,128)(2,1)}), bf16[32,24,128]{2,1,0:T(8,128)(2,1)S(1)}, u32[]{:S(2)}, u32[]{:S(2)}) %all-to-all-start.2) | async-done | bytes 196640 | tf_op jit(solution)/shard_map/all_to_all | solution.py:375
  80.4 0.6 shard_map.121
  81.0 3.0 %collective-permute-start.8 = (f32[2,1536]{1,0:T(2,128)S(1)}, f32[2,1536]{1,0:T(2,128)S(1)}, u32[]{:S(2)}, u32[]{:S(2)}) collective-permute-start(f32[2,1536]{1,0:T(2,128)S(1)} %get-tuple-element.31), channel_id=1, source_target_pairs={{0,2},{2,0},{4,6},{6,4},{8,10},{10,8},{12,14},{14,12},{16,18},{18,... | collective-permute-start | bytes 36872 | tf_op jit(solution)/shard_map/ppermute | solution.py:365
  84.0 0.8 collective-permute-done.8
  84.9 1.4 %collective-permute-start.9 = (f32[2,1536]{1,0:T(2,128)S(1)}, f32[2,1536]{1,0:T(2,128)S(1)}, u32[]{:S(2)}, u32[]{:S(2)}) collective-permute-start(f32[2,1536]{1,0:T(2,128)S(1)} %add.22), channel_id=1, source_target_pairs={{0,1},{1,0},{2,3},{3,2},{4,5},{5,4},{6,7},{7,6},{8,9},{9,8},{10,11... | collective-permute-start | bytes 36872 | tf_op jit(solution)/shard_map/ppermute | solution.py:369
  86.3 1.2 %collective-permute-done.9 = f32[2,1536]{1,0:T(2,128)S(1)} collective-permute-done((f32[2,1536]{1,0:T(2,128)S(1)}, f32[2,1536]{1,0:T(2,128)S(1)}, u32[]{:S(2)}, u32[]{:S(2)}) %collective-permute-start.9) | collective-permute-done | bytes 12320 | tf_op jit(solution)/shard_map/ppermute | solution.py:369
  87.5 0.8 broadcast_in_dim.5
  88.3 3.9 %all-to-all-start.3 = ((bf16[32,2,1536]{2,1,0:T(2,128)(2,1)}), bf16[32,2,1536]{2,1,0:T(2,128)(2,1)S(1)}, u32[]{:S(2)}, u32[]{:S(2)}) async-start(bf16[32,2,1536]{2,1,0:T(2,128)(2,1)} %broadcast_in_dim.5), calls=%async_computation.3 | async-start | bytes 393216 | tf_op jit(solution)/shard_map/all_to_all | solution.py:375
  92.2 1.4 %collective-permute-start.6 = (f32[128,64]{1,0:T(8,128)S(1)}, f32[128,64]{1,0:T(8,128)S(1)}, u32[]{:S(2)}, u32[]{:S(2)}) collective-permute-start(f32[128,64]{1,0:T(8,128)S(1)} %slice.34), channel_id=1, source_target_pairs={{0,1},{1,0},{2,3},{3,2},{4,5},{5,4},{6,7},{7,6},{8,9},{9,8},{10,11... | collective-permute-start | bytes 98312 | tf_op jit(solution)/shard_map/ppermute | solution.py:369
  93.6 1.8 %collective-permute-done.6 = f32[128,64]{1,0:T(8,128)S(1)} collective-permute-done((f32[128,64]{1,0:T(8,128)S(1)}, f32[128,64]{1,0:T(8,128)S(1)}, u32[]{:S(2)}, u32[]{:S(2)}) %collective-permute-start.6) | collective-permute-done | bytes 32800 | tf_op jit(solution)/shard_map/ppermute | solution.py:369
  95.4 3.0 %collective-permute-start.7 = (bf16[64,128]{0,1:T(8,128)(2,1)S(1)}, bf16[64,128]{0,1:T(8,128)(2,1)S(1)}, u32[]{:S(2)}, u32[]{:S(2)}) collective-permute-start(bf16[64,128]{0,1:T(8,128)(2,1)S(1)} %fusion.3), channel_id=1, source_target_pairs={{0,128},{128,0},{1,129},{129,1},{2,130},{130,2},{3,131},{131,3},{4... | collective-permute-start | bytes 49160 | tf_op jit(solution)/shard_map/ppermute | solution.py:479
  98.4 3.1 %all-to-all-done.3 = bf16[32,2,1536]{2,1,0:T(2,128)(2,1)S(1)} async-done(((bf16[32,2,1536]{2,1,0:T(2,128)(2,1)}), bf16[32,2,1536]{2,1,0:T(2,128)(2,1)S(1)}, u32[]{:S(2)}, u32[]{:S(2)}) %all-to-all-start.3) | async-done | bytes 196640 | tf_op jit(solution)/shard_map/all_to_all | solution.py:375
  101.6 3.2 %collective-permute-start.10 = (f32[2,1536]{1,0:T(2,128)S(1)}, f32[2,1536]{1,0:T(2,128)S(1)}, u32[]{:S(2)}, u32[]{:S(2)}) collective-permute-start(f32[2,1536]{1,0:T(2,128)S(1)} %convert_reduce_fusion), channel_id=1, source_target_pairs={{0,2},{2,0},{4,6},{6,4},{8,10},{10,8},{12,14},{14,12},{16,18},{18,... | collective-permute-start | bytes 36872 | tf_op jit(solution)/shard_map/ppermute | solution.py:365
  104.8 0.0 collective-permute-done.7
  104.8 0.7 copy.41
  105.5 0.1 collective-permute-done.10
  105.6 0.6 maximum_select_fusion
  (10 shorter events, 0.2 us)
Async XLA Ops:
  0.6 25.3 %copy-start = (bf16[1,64,3072]{2,1,0:T(8,128)(2,1)S(1)}, bf16[1,64,3072]{2,1,0:T(8,128)(2,1)}, u32[]{:S(2)}) copy-start(bf16[1,64,3072]{2,1,0:T(8,128)(2,1)} %param.16) | copy-start | bytes 1179652
  0.6 1.0 copy-start.1
  1.6 35.6 %copy-start.4 = (bf16[1,1,128,64]{2,3,1,0:T(8,128)(2,1)S(1)}, bf16[1,1,128,64]{2,3,1,0:T(8,128)(2,1)}, u32[]{:S(2)}) copy-start(bf16[1,1,128,64]{2,3,1,0:T(8,128)(2,1)} %param.10) | copy-start | bytes 49156
  1.6 35.7 %copy-start.5 = (bf16[1,1,128,64]{2,3,1,0:T(8,128)(2,1)S(1)}, bf16[1,1,128,64]{2,3,1,0:T(8,128)(2,1)}, u32[]{:S(2)}) copy-start(bf16[1,1,128,64]{2,3,1,0:T(8,128)(2,1)} %param.11) | copy-start | bytes 49156
  1.6 35.8 %copy-start.6 = (bf16[1,1,128,64]{2,3,1,0:T(8,128)(2,1)S(1)}, bf16[1,1,128,64]{2,3,1,0:T(8,128)(2,1)}, u32[]{:S(2)}) copy-start(bf16[1,1,128,64]{2,3,1,0:T(8,128)(2,1)} %param.13) | copy-start | bytes 49156
  1.7 35.9 %copy-start.7 = (bf16[1,1,128,64]{2,3,1,0:T(8,128)(2,1)S(1)}, bf16[1,1,128,64]{2,3,1,0:T(8,128)(2,1)}, u32[]{:S(2)}) copy-start(bf16[1,1,128,64]{2,3,1,0:T(8,128)(2,1)} %param.15) | copy-start | bytes 49156
  1.7 4.3 %collective-permute-start = (bf16[48,1152]{1,0:T(8,128)(2,1)S(1)}, bf16[48,1152]{1,0:T(8,128)(2,1)S(1)}, u32[]{:S(2)}, u32[]{:S(2)}) collective-permute-start(bf16[48,1152]{1,0:T(8,128)(2,1)S(1)} %get-tuple-element.18), channel_id=1, source_target_pairs={{0,2},{2,0},{4,6},{6,4},{8,10},{10,8},{12,14},{14,12},{16,18},{18,... | collective-permute-start | bytes 331784 | tf_op jit(solution)/shard_map/ppermute | solution.py:365
  6.2 33.5 %copy-start.3 = (bf16[1,768,64]{1,2,0:T(8,128)(2,1)S(1)}, bf16[1,768,64]{1,2,0:T(8,128)(2,1)}, u32[]{:S(2)}) copy-start(bf16[1,768,64]{1,2,0:T(8,128)(2,1)} %param.18) | copy-start | bytes 294916
  26.0 0.8 copy-start.2
  28.4 19.9 %all-to-all-start.1 = ((bf16[32,56,128]{2,1,0:T(8,128)(2,1)}), bf16[32,56,128]{2,1,0:T(8,128)(2,1)S(1)}, u32[]{:S(2)}, u32[]{:S(2)}) async-start(bf16[32,56,128]{2,1,0:T(8,128)(2,1)} %get-tuple-element.19), calls=%async_computation.1 | async-start | bytes 917504 | tf_op jit(solution)/shard_map/all_to_all | solution.py:375
  38.4 2.2 %collective-permute-start.1 = (bf16[128,384]{1,0:T(8,128)(2,1)S(1)}, bf16[128,384]{1,0:T(8,128)(2,1)S(1)}, u32[]{:S(2)}, u32[]{:S(2)}) collective-permute-start(bf16[128,384]{1,0:T(8,128)(2,1)S(1)} %shard_map.116), channel_id=1, source_target_pairs={{0,2},{2,0},{4,6},{6,4},{8,10},{10,8},{12,14},{14,12},{16,18},{18,... | collective-permute-start | bytes 294920 | tf_op jit(solution)/shard_map/ppermute | solution.py:365
  40.7 6.2 %collective-permute-start.2 = (bf16[2,128,384]{2,1,0:T(8,128)(2,1)S(1)}, bf16[2,128,384]{2,1,0:T(8,128)(2,1)S(1)}, u32[]{:S(2)}, u32[]{:S(2)}) collective-permute-start(bf16[2,128,384]{2,1,0:T(8,128)(2,1)S(1)} %pad_maximum_fusion.here), channel_id=1, source_target_pairs={{0,1},{1,0},{2,3},{3,2},{4,5},{5,4},{6,7},{7,6},{8,9},{9,8},{10,11... | collective-permute-start | bytes 589832 | tf_op jit(solution)/shard_map/ppermute | solution.py:369
  51.2 5.3 %collective-permute-start.3 = (f32[256,128]{1,0:T(8,128)S(1)}, f32[256,128]{1,0:T(8,128)S(1)}, u32[]{:S(2)}, u32[]{:S(2)}) collective-permute-start(f32[256,128]{1,0:T(8,128)S(1)} %get-tuple-element.21), channel_id=1, source_target_pairs={{0,2},{2,0},{4,6},{6,4},{8,10},{10,8},{12,14},{14,12},{16,18},{18,... | collective-permute-start | bytes 393224 | tf_op jit(solution)/shard_map/ppermute | solution.py:365
  56.5 4.8 %collective-permute-start.4 = (f32[256,128]{1,0:T(8,128)S(1)}, f32[256,128]{1,0:T(8,128)S(1)}, u32[]{:S(2)}, u32[]{:S(2)}) collective-permute-start(f32[256,128]{1,0:T(8,128)S(1)} %add.18.vel_here), channel_id=1, source_target_pairs={{0,1},{1,0},{2,3},{3,2},{4,5},{5,4},{6,7},{7,6},{8,9},{9,8},{10,11... | collective-permute-start | bytes 393224 | tf_op jit(solution)/shard_map/ppermute | solution.py:369
  65.9 14.5 %all-to-all-start.2 = ((bf16[32,24,128]{2,1,0:T(8,128)(2,1)}), bf16[32,24,128]{2,1,0:T(8,128)(2,1)S(1)}, u32[]{:S(2)}, u32[]{:S(2)}) async-start(bf16[32,24,128]{2,1,0:T(8,128)(2,1)} %shard_map.119), calls=%async_computation.2 | async-start | bytes 393216 | tf_op jit(solution)/shard_map/all_to_all | solution.py:375
  74.0 2.5 %collective-permute-start.5 = (f32[256,64]{1,0:T(8,128)S(1)}, f32[256,64]{1,0:T(8,128)S(1)}, u32[]{:S(2)}, u32[]{:S(2)}) collective-permute-start(f32[256,64]{1,0:T(8,128)S(1)} %slice.38), channel_id=1, source_target_pairs={{0,2},{2,0},{4,6},{6,4},{8,10},{10,8},{12,14},{14,12},{16,18},{18,... | collective-permute-start | bytes 196616 | tf_op jit(solution)/shard_map/ppermute | solution.py:365
  81.0 3.9 %collective-permute-start.8 = (f32[2,1536]{1,0:T(2,128)S(1)}, f32[2,1536]{1,0:T(2,128)S(1)}, u32[]{:S(2)}, u32[]{:S(2)}) collective-permute-start(f32[2,1536]{1,0:T(2,128)S(1)} %get-tuple-element.31), channel_id=1, source_target_pairs={{0,2},{2,0},{4,6},{6,4},{8,10},{10,8},{12,14},{14,12},{16,18},{18,... | collective-permute-start | bytes 36872 | tf_op jit(solution)/shard_map/ppermute | solution.py:365
  84.9 2.6 %collective-permute-start.9 = (f32[2,1536]{1,0:T(2,128)S(1)}, f32[2,1536]{1,0:T(2,128)S(1)}, u32[]{:S(2)}, u32[]{:S(2)}) collective-permute-start(f32[2,1536]{1,0:T(2,128)S(1)} %add.22), channel_id=1, source_target_pairs={{0,1},{1,0},{2,3},{3,2},{4,5},{5,4},{6,7},{7,6},{8,9},{9,8},{10,11... | collective-permute-start | bytes 36872 | tf_op jit(solution)/shard_map/ppermute | solution.py:369
  88.3 13.3 %all-to-all-start.3 = ((bf16[32,2,1536]{2,1,0:T(2,128)(2,1)}), bf16[32,2,1536]{2,1,0:T(2,128)(2,1)S(1)}, u32[]{:S(2)}, u32[]{:S(2)}) async-start(bf16[32,2,1536]{2,1,0:T(2,128)(2,1)} %broadcast_in_dim.5), calls=%async_computation.3 | async-start | bytes 393216 | tf_op jit(solution)/shard_map/all_to_all | solution.py:375
  92.2 3.2 %collective-permute-start.6 = (f32[128,64]{1,0:T(8,128)S(1)}, f32[128,64]{1,0:T(8,128)S(1)}, u32[]{:S(2)}, u32[]{:S(2)}) collective-permute-start(f32[128,64]{1,0:T(8,128)S(1)} %slice.34), channel_id=1, source_target_pairs={{0,1},{1,0},{2,3},{3,2},{4,5},{5,4},{6,7},{7,6},{8,9},{9,8},{10,11... | collective-permute-start | bytes 98312 | tf_op jit(solution)/shard_map/ppermute | solution.py:369
  95.4 9.4 %collective-permute-start.7 = (bf16[64,128]{0,1:T(8,128)(2,1)S(1)}, bf16[64,128]{0,1:T(8,128)(2,1)S(1)}, u32[]{:S(2)}, u32[]{:S(2)}) collective-permute-start(bf16[64,128]{0,1:T(8,128)(2,1)S(1)} %fusion.3), channel_id=1, source_target_pairs={{0,128},{128,0},{1,129},{129,1},{2,130},{130,2},{3,131},{131,3},{4... | collective-permute-start | bytes 49160 | tf_op jit(solution)/shard_map/ppermute | solution.py:479
  101.6 4.0 %collective-permute-start.10 = (f32[2,1536]{1,0:T(2,128)S(1)}, f32[2,1536]{1,0:T(2,128)S(1)}, u32[]{:S(2)}, u32[]{:S(2)}) collective-permute-start(f32[2,1536]{1,0:T(2,128)S(1)} %convert_reduce_fusion), channel_id=1, source_target_pairs={{0,2},{2,0},{4,6},{6,4},{8,10},{10,8},{12,14},{14,12},{16,18},{18,... | collective-permute-start | bytes 36872 | tf_op jit(solution)/shard_map/ppermute | solution.py:365

commit v4 on v3

--- a/solution.py
+++ b/solution.py
@@ -51,8 +51,23 @@
     return lax.axis_index("role") == 1
 
 
-def pack_kernel(noise_levels, replay_levels, base, noise, replay, cotangent, embed, pack):
+def pack_kernel(noise_levels, replay_levels, base, noise, replay, cotangent, embed, modulation, pack, stack):
     critic = on_critic()
+    modulation_a = modulation[0]
+    modulation_b = jnp.where(critic, modulation[1], modulation_a)
+    embed_f = embed[...].astype(F32)
+    scaled_b = (embed_f * modulation_b[0:1, :]).astype(BF16)
+    stack[0:64, :] = embed[...]
+    stack[64:128, :] = (embed_f * modulation_a[0:1, :]).astype(BF16)
+    stack[128:192, :] = scaled_b
+    stack[192:256, :] = scaled_b
+    shifts = []
+    for pair in (modulation_a, modulation_b):
+        shift = pair[1:2, :]
+        high = rounded(shift)
+        shifts += [high, shift - high]
+    shifts.append(jnp.zeros((12, embed.shape[1]), F32))
+    stack[256:272, :] = jnp.concatenate(shifts, axis=0).astype(BF16)
     level = noise_levels[0, 0]
     level_two = jnp.where(critic, level, replay_levels[0, 0])
     base_f = base[...].astype(F32)
@@ -82,20 +97,16 @@
     pack[:, 256:384] = tail.astype(BF16)
 
 
-def cut_kernel(weight, keep, send):
-    second = on_second_core()
+def cut_kernel(weight, keep):
     columns = keep.shape[1]
-    left = weight[:, 0:columns].astype(F32)
-    right = weight[:, columns:].astype(F32)
-    keep[...] = jnp.where(second, right, left).astype(BF16)
-    send[...] = jnp.where(second, left, right).astype(BF16)
+    keep[...] = jnp.where(on_second_core(), weight[:, columns:].astype(F32), weight[:, 0:columns].astype(F32)).astype(BF16)
 
 
 def weight_kernel(chips, keep, received, out, turned):
     second = on_second_core()
-    rows, columns = received.shape
+    rows, columns = keep.shape
     own = keep[...].astype(F32)
-    other = received[...].astype(F32)
+    other = jnp.where(second, received[:, columns:].astype(F32), received[:, 0:columns].astype(F32))
     both = [jnp.where(second, other, own), jnp.where(second, own, other)]
     padded = out.shape[2]
     if padded > 2 * rows:
@@ -110,12 +121,11 @@
         out[chip] = jnp.where(row < block, piece, 0.0).astype(BF16)
 
 
-def product_kernel(block, taken, embed, modulation, out, halves_out, columns_out):
-    critic = on_critic()
+def product_kernel(block, taken, stack, out, halves_out, columns_out):
     chips, height, padded = taken.shape
     half = block // 2
     stride = halves_out.shape[0] // 2
-    width = embed.shape[1]
+    width = stack.shape[1]
     depth = width // chips
     row_half = row_index((stride, 1))
     group = 1 if depth % 128 == 0 else 128 // (depth & -depth)
@@ -129,21 +139,9 @@
         high = jnp.where(row_half < half, longer[half : half + stride], 0.0)
         halves_out[:, span] = jnp.concatenate([low, high], axis=0).astype(BF16)
     weight = columns_out[...]
-    embed_b = embed[...]
-    embed_f = embed_b.astype(F32)
-    modulation_a = modulation[0]
-    modulation_b = jnp.where(critic, modulation[1], modulation_a)
-    scaled_a = (embed_f * modulation_a[0:1, :]).astype(BF16)
-    scaled_b = (embed_f * modulation_b[0:1, :]).astype(BF16)
-    first = dot(weight, jnp.concatenate([embed_b, scaled_a], axis=0), NT)
-    second = dot(weight, jnp.concatenate([scaled_b, scaled_b], axis=0), NT)
-    shifts = []
-    for pair in (modulation_a, modulation_b):
-        shift = pair[1:2, :]
-        high = rounded(shift)
-        shifts += [high, shift - high]
-    shifts.append(jnp.zeros((4, width), F32))
-    offsets = dot(jnp.concatenate(shifts, axis=0).astype(BF16), weight, NT)
+    products = dot(weight, stack[0:256, :], NT)
+    first, second = products[:, 0:128], products[:, 128:256]
+    offsets = dot(stack[256:272, :], weight, NT)
     lines = []
     gap = jnp.zeros((1, CHANNELS - block), F32)
     for offset in (offsets[0:1, 0:block] + offsets[1:2, 0:block], offsets[2:3, 0:block] + offsets[3:4, 0:block]):
@@ -170,44 +168,79 @@
     return tail[:, at : at + 1] + tail[:, at + 1 : at + 2] + tail[:, at + 2 : at + 3]
 
 
-def forward(which, packs, matrices, offsets, output_weight, keep, velocity):
-    heads = output_weight.shape[0] // HEAD_DIM
+def forward(which, packs, matrices, offsets, output_turned, keep, keep_turned, probs_out, velocity):
+    heads = output_turned.shape[1] // HEAD_DIM
     low_lanes = lane_index((1, 128)) < CHANNELS
-    rows, scales, levels = [], [], []
+    rows, scales, levels, turned_scales = [], [], [], []
     for sample in range(2):
         inputs = token_rows(packs, sample, 0, 128).astype(F32)
         turned = pltpu.roll(inputs, CHANNELS, 1)
         level = tail_column(packs, sample, 2 + which)
         plain, scaled = (turned, inputs) if which else (inputs, turned)
-        rows.append(jnp.where(low_lanes, plain, scaled * level).astype(BF16))
-        scales.append(tail_column(packs, sample, which))
+        rows.append(jnp.where(low_lanes, plain, scaled * level))
+        scale = tail_column(packs, sample, which)
+        scales.append(scale)
         levels.append(level[0:1])
+        turned_scales.append(jnp.broadcast_to(scale, (scale.shape[0], 128)).T[0:1])
     tokens = rows[0].shape[0]
     inputs = jnp.concatenate(rows, axis=0)
-    totals = [jnp.zeros((tokens, CHANNELS), F32), jnp.zeros((tokens, CHANNELS), F32)]
+    turned = inputs.T.astype(BF16)
+    inputs = inputs.astype(BF16)
+    offset = offsets[which : which + 1, :]
+    columns = offset.shape[1]
+    offset_turned = jnp.broadcast_to(offset, (128, columns)).T[:, 0:1]
+    units = []
     for head in range(heads):
         at = head * 3 * HEAD_DIM
-        product = dot(inputs, matrices[at : at + 3 * HEAD_DIM, :], NT)
-        offset = offsets[which : which + 1, at : at + 3 * HEAD_DIM]
+        span = slice(at, at + 3 * HEAD_DIM)
+        matrix = matrices[span, :]
+        if keep is None:
+            product = dot(inputs, matrix[HEAD_DIM : 2 * HEAD_DIM], NT)
+        else:
+            product = dot(inputs, matrix, NT)
+        product_turned = dot(matrix, turned)
         for sample in range(2):
-            qkv = product[sample * tokens : (sample + 1) * tokens] * scales[sample] + offset * levels[sample]
-            qkv = qkv.astype(BF16)
+            own = slice(sample * tokens, (sample + 1) * tokens)
+            line = offset[:, span] if keep is not None else offset[:, at + HEAD_DIM : at + 2 * HEAD_DIM]
+            qkv = (product[own] * scales[sample] + line * levels[sample]).astype(BF16)
+            flipped = product_turned[:, own] * turned_scales[sample] + offset_turned[span] * levels[sample]
+            flipped = flipped.astype(BF16)
+            key = qkv
             if keep is not None:
-                keep[sample, :, at : at + 3 * HEAD_DIM] = qkv
-            query = qkv[:, 0:HEAD_DIM]
-            key = qkv[:, HEAD_DIM : 2 * HEAD_DIM]
-            value = qkv[:, 2 * HEAD_DIM :]
-            scores = dot(query, key, NT) * (HEAD_DIM**-0.5)
-            top = jnp.max(scores, axis=-1, keepdims=True)
-            powers = jnp.exp(scores - top)
-            probs = powers / jnp.sum(powers, axis=-1, keepdims=True)
-            mixed = dot(probs.astype(BF16), value).astype(BF16)
-            totals[sample] = totals[sample] + dot(mixed, output_weight[head * HEAD_DIM : (head + 1) * HEAD_DIM, :])
-    velocity[...] = jnp.concatenate(totals, axis=1)
+                keep[sample, :, span] = qkv
+                keep_turned[2 * head + sample] = flipped[HEAD_DIM : 2 * HEAD_DIM]
+                key = qkv[:, HEAD_DIM : 2 * HEAD_DIM]
+            units.append((key, flipped[0:HEAD_DIM], flipped[2 * HEAD_DIM :]))
+    totals = [None, None]
+    scores = [dot(key, query) * (HEAD_DIM**-0.5) for key, query, _ in units]
+    for unit, score in enumerate(scores):
+        powers = jnp.exp(score - jnp.max(score, axis=0, keepdims=True))
+        probs = powers * (1.0 / jnp.sum(powers, axis=0, keepdims=True))
+        if probs_out is not None:
+            probs_out[unit] = probs
+        mixed = dot(units[unit][2], probs.astype(BF16)).astype(BF16)
+        head = unit // 2
+        term = dot(output_turned[:, head * HEAD_DIM : (head + 1) * HEAD_DIM], mixed)
+        before = totals[unit % 2]
+        totals[unit % 2] = term if before is None else before + term
+    velocity[...] = jnp.concatenate(totals, axis=0).T
 
 
 def second_pass_kernel(
-    block, taken, here, there, output_weight, matrices, offsets, keep, velocity, crossing, stacked, stacked_two
+    block,
+    taken,
+    here,
+    there,
+    output_turned,
+    matrices,
+    offsets,
+    keep,
+    keep_turned,
+    probs,
+    velocity,
+    crossing,
+    stacked,
+    stacked_two,
 ):
     chips = taken.shape[0]
     half = block // 2
@@ -227,23 +260,13 @@
     matrices[...] = stacked[...].astype(BF16)
     joined = [jnp.concatenate(line, axis=1) for line in lines]
     offsets[...] = jnp.concatenate(joined + [jnp.zeros((6, offsets.shape[1]), F32)], axis=0)
-    forward(1, (here, there), stacked_two[...].astype(BF16), offsets, output_weight, keep, velocity)
+    both = stacked_two[...].astype(BF16)
+    forward(1, (here, there), both, offsets, output_turned, keep, keep_turned, probs, velocity)
     crossing[...] = pltpu.roll(velocity[...], CHANNELS, 1)
 
 
-def first_pass_kernel(matrices, offsets, here, there, output_weight, velocity):
-    forward(0, (here, there), matrices, offsets, output_weight, None, velocity)
-
-
-def probs_kernel(kept, out):
-    heads = out.shape[0] // 2
-    for unit in range(2 * heads):
-        at = unit // 2 * 3 * HEAD_DIM
-        qkv = kept[unit % 2, :, at : at + 2 * HEAD_DIM]
-        scores = dot(qkv[:, HEAD_DIM:], qkv[:, 0:HEAD_DIM], NT) * (HEAD_DIM**-0.5)
-        top = jnp.max(scores, axis=0, keepdims=True)
-        powers = jnp.exp(scores - top)
-        out[unit] = powers / jnp.sum(powers, axis=0, keepdims=True)
+def first_pass_kernel(matrices, offsets, here, there, output_turned, velocity):
+    forward(0, (here, there), matrices, offsets, output_turned, None, None, None, velocity)
 
 
 def swap_tokens(value):
@@ -251,47 +274,65 @@
     return jnp.concatenate([value[half:], value[:half]], axis=0)
 
 
-def backward_kernel(block, kept, probs_turned, here, there, vel_here, vel_there, output_weight, out, gathered, summed):
+def backward_kernel(
+    block, kept, keys_turned, probs_turned, here, there, vel_here, vel_there, output_turned, out, gathered, summed
+):
     critic = on_critic()
     packs = (here, there)
-    heads = output_weight.shape[0] // HEAD_DIM
+    heads = output_turned.shape[1] // HEAD_DIM
     velocity = vel_here[...] + swap_tokens(vel_there[...])
     lane = lane_index((1, 128))
-    grads, rows, levels = [], [], []
+    known = []
     for sample in range(2):
-        known = token_rows(packs, sample, 128, 256).astype(F32)
-        known = known[:, 0:CHANNELS] + known[:, CHANNELS:]
-        total = velocity[:, sample * CHANNELS : (sample + 1) * CHANNELS]
-        grads.append(jnp.where(critic, total - known, known).astype(BF16))
-        inputs = token_rows(packs, sample, 0, 128).astype(F32)
-        inputs = jnp.where(lane < CHANNELS, pltpu.roll(inputs, CHANNELS, 1), inputs)
+        part = token_rows(packs, sample, 128, 256).astype(F32)
+        known.append(part[:, 0:CHANNELS] + part[:, CHANNELS:])
+    known = jnp.concatenate(known, axis=1)
+    grad_velocity = jnp.where(critic, velocity - known, known)
+    grads_turned = grad_velocity.T.astype(BF16)
+    grads = grad_velocity.astype(BF16)
+    inputs, rows, levels = [], [], []
+    for sample in range(2):
+        packed = token_rows(packs, sample, 0, 128).astype(F32)
+        packed = jnp.where(lane < CHANNELS, pltpu.roll(packed, CHANNELS, 1), packed)
         level = tail_column(packs, sample, 3)
         levels.append(level[0:1])
-        scaled = inputs * (tail_column(packs, sample, 1) * level)
+        scaled = packed * (tail_column(packs, sample, 1) * level)
+        inputs.append(scaled.astype(BF16))
         rows.append(scaled.T.astype(BF16))
+    grad_mixed, grad_probs = [], []
+    for unit in range(2 * heads):
+        head, sample = unit // 2, unit % 2
+        weight = output_turned[:, head * HEAD_DIM : (head + 1) * HEAD_DIM]
+        lanes = slice(sample * CHANNELS, (sample + 1) * CHANNELS)
+        grad_mixed.append(dot(grads[:, lanes], weight).astype(BF16))
+        turned = dot(weight, grads_turned[lanes], TN).astype(BF16)
+        value = kept[sample, :, head * 3 * HEAD_DIM + 2 * HEAD_DIM : (head + 1) * 3 * HEAD_DIM]
+        grad_probs.append(dot(value, turned))
     for head in range(heads):
         at = head * 3 * HEAD_DIM
-        total, ends = None, None
+        query_total, rest_total = None, None
+        ends = []
         for sample in range(2):
-            qkv = kept[sample, :, at : at + 3 * HEAD_DIM]
-            query = qkv[:, 0:HEAD_DIM]
-            key = qkv[:, HEAD_DIM : 2 * HEAD_DIM]
-            value = qkv[:, 2 * HEAD_DIM :]
-            grad_mixed = dot(grads[sample], output_weight[head * HEAD_DIM : (head + 1) * HEAD_DIM, :], NT).astype(BF16)
-            probs = probs_turned[2 * head + sample]
-            grad_value = dot(probs.astype(BF16), grad_mixed)
-            grad_probs = dot(value, grad_mixed, NT)
-            inner = jnp.sum(grad_probs * probs, axis=0, keepdims=True)
-            grad_scores = (probs * (grad_probs - inner) * (HEAD_DIM**-0.5)).astype(BF16)
-            grad_key = dot(grad_scores, query)
-            grad_query = dot(grad_scores, key, TN)
-            grad = jnp.concatenate([grad_query, grad_key, grad_value], axis=1).astype(BF16)
-            term = dot(rows[sample], grad)
-            end = jnp.sum(grad.astype(F32), axis=0, keepdims=True) * levels[sample]
-            total = term if total is None else total + term
-            ends = end if ends is None else ends + end
-        gathered[at : at + 3 * HEAD_DIM, :] = total.T
-        summed[:, at : at + 3 * HEAD_DIM] = ends
+            unit = 2 * head + sample
+            probs = probs_turned[unit]
+            grad = grad_probs[unit]
+            inner = jnp.sum(grad * probs, axis=0, keepdims=True)
+            grad_scores = (probs * (grad - inner) * (HEAD_DIM**-0.5)).astype(BF16)
+            grad_value = dot(probs.astype(BF16), grad_mixed[unit])
+            grad_key = dot(grad_scores, kept[sample, :, at : at + HEAD_DIM])
+            grad_query = dot(keys_turned[unit], grad_scores).astype(BF16)
+            rest = jnp.concatenate([grad_key, grad_value], axis=1).astype(BF16)
+            query_term = dot(grad_query, inputs[sample])
+            rest_term = dot(rows[sample], rest)
+            query_total = query_term if query_total is None else query_total + query_term
+            rest_total = rest_term if rest_total is None else rest_total + rest_term
+            turned_sum = jnp.sum(grad_query.astype(F32), axis=1, keepdims=True)
+            turned_sum = jnp.broadcast_to(turned_sum, (HEAD_DIM, 128)).T[0:1]
+            rest_sum = jnp.sum(rest.astype(F32), axis=0, keepdims=True)
+            ends.append(jnp.concatenate([turned_sum, rest_sum], axis=1) * levels[sample])
+        gathered[at : at + HEAD_DIM, :] = query_total
+        gathered[at + HEAD_DIM : at + 3 * HEAD_DIM, :] = rest_total.T
+        summed[:, at : at + 3 * HEAD_DIM] = ends[0] + ends[1]
     columns = heads * 3 * HEAD_DIM
     gathered[columns:, :] = jnp.zeros((gathered.shape[0] - columns, 128), F32)
     chips, height = out.shape[0], out.shape[1]
@@ -402,81 +443,84 @@
     padded = round_up(2 * weight.shape[0], 128)
     tokens = base_latents.shape[2]
     heads = columns // (3 * HEAD_DIM)
-    out_rows = output_weight.shape[1] // 2
-    out_half = jnp.where(second_core, output_weight[0, out_rows:], output_weight[0, :out_rows])
-
-    keep, send = call(
-        cut_kernel,
-        (struct((weight.shape[0], columns), BF16), struct((weight.shape[0], columns), BF16)),
-        (weight,),
-    )
+    out_columns = output_weight.shape[1] // 2
+    output_turned = output_weight[0].T
+    output_turned = jnp.where(second_core, output_turned[:, out_columns:], output_turned[:, :out_columns])
+
+    received = other_core(weight)
+    keep = call(cut_kernel, struct((weight.shape[0], columns), BF16), (weight,))
     turned = call(
         functools.partial(weight_kernel, chips),
         struct((chips, height, padded), BF16),
-        (keep, other_core(send)),
+        (keep, received),
         scratch=[pltpu.VMEM((columns + height - block, padded), F32)],
     )
-
-    own = call(
+    turned, first_levels = lax.optimization_barrier((turned, noise_levels))
+    taken = between_chips(turned)
+
+    own, stack = call(
         pack_kernel,
-        struct((tokens, 384), BF16),
+        (struct((tokens, 384), BF16), struct((272, width), BF16)),
         (
-            noise_levels,
+            first_levels,
             replay_levels,
             base_latents[0, 0],
             noise_latents[0, 0],
             replay_latents[0, 0],
             cotangent[0, 0],
             embed,
+            modulation[0],
         ),
         scalars=2,
     )
     here = jnp.stack([own, other_core(own)])
+    taken, here = lax.optimization_barrier((taken, here))
     there = other_half(here)
 
     matrices, own_columns = call(
         functools.partial(product_kernel, block),
         (struct((chips, packed, 128), BF16), struct((2 * folded, width), BF16)),
-        (between_chips(turned), embed, modulation[0]),
+        (taken, stack),
         scratch=[pltpu.VMEM((height, width), BF16)],
     )
-    whole, offsets, kept, vel_b, vel_crossing = call(
+    whole, offsets, kept, keys_turned, probs, vel_b, vel_crossing = call(
         functools.partial(second_pass_kernel, block),
         (
             struct((columns, 2 * CHANNELS), BF16),
             struct((8, columns), F32),
             struct((2, 2 * tokens, columns), BF16),
+            struct((2 * heads, HEAD_DIM, 2 * tokens), BF16),
+            struct((2 * heads, 2 * tokens, 2 * tokens), F32),
             struct((2 * tokens, 2 * CHANNELS), F32),
             struct((2 * tokens, 2 * CHANNELS), F32),
         ),
-        (between_chips(matrices), here, there, out_half),
+        (between_chips(matrices), here, there, output_turned),
         scratch=[pltpu.VMEM((columns, 2 * CHANNELS), F32), pltpu.VMEM((columns, 2 * CHANNELS), F32)],
     )
     vel_here = vel_b + other_core(vel_crossing)
     vel_there = other_half(vel_here)
-    probs = call(probs_kernel, struct((2 * heads, 2 * tokens, 2 * tokens), F32), (kept,), flops=2 * 10**9)
-    vel_there, probs = lax.optimization_barrier((vel_there, probs))
+    vel_a = call(
+        first_pass_kernel,
+        struct((2 * tokens, 2 * CHANNELS), F32),
+        (whole, offsets, here, there, output_turned),
+        flops=4 * 10**9,
+    )
+    vel_there, vel_a = lax.optimization_barrier((vel_there, vel_a))
     products = call(
         functools.partial(backward_kernel, block),
         struct((chips, folded, 128), BF16),
-        (kept, probs, here, there, vel_here, vel_there, out_half),
+        (kept, keys_turned, probs, here, there, vel_here, vel_there, output_turned),
         scratch=[pltpu.VMEM((columns + 2 * folded, 128), F32), pltpu.VMEM((1, columns), F32)],
     )
     gathered = between_chips(products)
 
-    vel_a = call(
-        first_pass_kernel,
-        struct((2 * tokens, 2 * CHANNELS), F32),
-        (whole, offsets, here, there, out_half),
-        flops=4 * 10**9,
-    )
     own_a = vel_a[:, :CHANNELS] + other_core(vel_a[:, CHANNELS:])
-    gathered, own_a = lax.optimization_barrier((gathered, own_a))
     own_a = own_a[:tokens] + other_half(own_a[tokens:])
     own_b = vel_here[:tokens, :CHANNELS] + vel_there[tokens:, :CHANNELS]
     sample = own[:, :CHANNELS].astype(F32) - noise_levels[0, 0] * own_a
-    payload = jnp.where(is_critic, own_b - own_a, sample).T
-    crossed = lax.ppermute(payload.astype(BF16), "role", [(0, 1), (1, 0)]).T
+    payload = jnp.where(is_critic, own_b - own_a, sample).T.astype(BF16)
+    gathered, payload = lax.optimization_barrier((gathered, payload))
+    crossed = lax.ppermute(payload, "role", [(0, 1), (1, 0)]).T
 
     samples = devices * base_latents.shape[1]
     kept_half, sent_half = call(

time: 107 us -> 106 us (level)
  blocking collectives: 19.7 us -> 0 us
  waiting for transfers between devices: 23.6 us -> 36.8 us
  starting transfers between devices: 41.9 us -> 49.7 us
  Pallas kernels: 14.1 us -> 11.3 us
    all_to_all x1 -> x0, blocking collectives: 19.7 us -> none  [between_chips(): lax.all_to_all(value, 'fsdp', 0, 0, tiled=True, axis_index_groups=groups)]
    all_to_all x3 -> x4, waiting for transfers between devices: 8.43 us -> 24.8 us  [between_chips(): lax.all_to_all(value, 'fsdp', 0, 0, tiled=True, axis_index_groups=groups)]
    all_to_all x3 -> x4, starting transfers between devices: 16.7 us -> 25.8 us  [between_chips(): lax.all_to_all(value, 'fsdp', 0, 0, tiled=True, axis_index_groups=groups)]
    pallas_call x9 -> x8, Pallas kernels: 14.1 us -> 11.3 us  [call(): pl.pallas_call(kernel, out_shape=out_shapes, in_specs=specs, out_specs=ja...]
    ppermute x4, waiting for transfers between devices: 10.6 us -> 8.83 us  [other_half(): return lax.ppermute(value, 'seq', [(0, 1), (1, 0)])]
    ppermute x6, starting transfers between devices: 16.7 us -> 15.3 us  [other_core(): lax.ppermute(value, 'fsdp', [(i, i ^ 1) for i in range(lax.axis_size('fsd...]
    ppermute x6, waiting for transfers between devices: 4.57 us -> 3.21 us  [other_core(): lax.ppermute(value, 'fsdp', [(i, i ^ 1) for i in range(lax.axis_size('fsd...]
    unnamed x23 -> x21, local copies, waits for them, and re-layouts: 3.2 us -> 2.11 us
  transfers between devices with their start and end apart: 14 -> 15, of which waited for: 13 -> 13; matrix products, arithmetic and copies ran while one was open for 2% -> 2% of each run, Pallas kernels for 4% -> 5%
where the time goes in v4:
time: 106 us; the launch traced here: 105 us
  starting transfers between devices  49.7 us (47%)
  waiting for transfers between devices  36.8 us (35%)
  Pallas kernels  11.3 us (11%)
  local copies, waits for them, and re-layouts  3.67 us (3%)
  between operations  2.13 us (2%)
  other arithmetic  1.68 us (2%)
    all_to_all x4, starting transfers between devices, between_chips(): lax.all_to_all(value, 'fsdp', 0, 0, tiled=True, axis_index_groups=groups)  25.8 us
    all_to_all x4, waiting for transfers between devices, between_chips(): lax.all_to_all(value, 'fsdp', 0, 0, tiled=True, axis_index_groups=groups)  24.8 us
    ppermute x6, starting transfers between devices, other_core(): lax.ppermute(value, 'fsdp', [(i, i ^ 1) for i in range(lax.axis_size('fsd...  15.3 us
    pallas_call x8, Pallas kernels, call(): pl.pallas_call(kernel, out_shape=out_shapes, in_specs=specs, out_specs=ja...  11.3 us
    ppermute x4, waiting for transfers between devices, other_half(): return lax.ppermute(value, 'seq', [(0, 1), (1, 0)])  8.83 us
    ppermute x4, starting transfers between devices, other_half(): return lax.ppermute(value, 'seq', [(0, 1), (1, 0)])  5.53 us
    ppermute x6, waiting for transfers between devices, other_core(): lax.ppermute(value, 'fsdp', [(i, i ^ 1) for i in range(lax.axis_size('fsd...  3.21 us
    ppermute x1, starting transfers between devices, per_device(): crossed = lax.ppermute(payload, 'role', [(0, 1), (1, 0)]).T  3 us
  transfers between devices with their start and end apart: 15, of which 13 were waited for; matrix products, arithmetic and copies ran while one was open for 2% of the time, Pallas kernels for 5%

profile of v4, /device:TPU:1, one launch (start us, length us, event | category | flops | bytes accessed | tf_op | source)
XLA Modules:
  0.0 105.2 jit_solution(10415135518435456974)
XLA Ops:
  0.6 0.0 copy-start
  0.6 3.3 %collective-permute-start = (bf16[48,2304]{1,0:T(8,128)(2,1)}, bf16[48,2304]{1,0:T(8,128)(2,1)S(1)}, u32[]{:S(2)}, u32[]{:S(2)}) collective-permute-start(bf16[48,2304]{1,0:T(8,128)(2,1)} %bitcast.23), channel_id=1, source_target_pairs={{0,2},{2,0},{4,6},{6,4},{8,10},{10,8},{12,14},{14,12},{16,18},{18,... | collective-permute-start | bytes 663560 | tf_op jit(solution)/shard_map/ppermute | solution.py:406
  4.0 0.0 copy-start.1
  4.0 0.9 copy-done.1
  4.9 0.0 copy-start.4
  4.9 0.0 copy-start.5
  4.9 0.0 copy-start.6
  4.9 0.0 copy-start.7
  4.9 0.0 copy-start.2
  5.0 0.3 collective-permute-done.received
  5.3 1.0 shard_map.114
  6.2 9.3 %all-to-all-start = ((bf16[32,40,128]{2,1,0:T(8,128)(2,1)}), bf16[32,40,128]{2,1,0:T(8,128)(2,1)S(1)}, u32[]{:S(2)}, u32[]{:S(2)}) async-start(bf16[32,40,128]{2,1,0:T(8,128)(2,1)} %shard_map.114), calls=%async_computation | async-start | bytes 655360 | tf_op jit(solution)/shard_map/all_to_all | solution.py:416
  16.8 0.0 copy-done.4
  16.8 0.1 copy.28
  17.0 0.0 copy-done.5
  17.0 0.1 copy.29
  17.1 0.0 copy-done.6
  17.1 0.1 copy.30
  17.2 0.0 copy-done.7
  17.2 0.1 copy.31
  17.3 0.0 copy-done
  17.4 0.0 copy-done.2
  17.4 1.0 shard_map.115
  18.4 0.7 collective-permute-start.1
  19.1 0.9 collective-permute-done.1
  20.0 0.0 copy-start.3
  20.1 5.9 %all-to-all-done.taken = bf16[32,40,128]{2,1,0:T(8,128)(2,1)S(1)} async-done(((bf16[32,40,128]{2,1,0:T(8,128)(2,1)}), bf16[32,40,128]{2,1,0:T(8,128)(2,1)S(1)}, u32[]{:S(2)}, u32[]{:S(2)}) %all-to-all-start) | async-done | bytes 327712 | tf_op jit(solution)/shard_map/all_to_all | solution.py:416
  26.0 1.6 %shard_map.116 = (bf16[32,56,128]{2,1,0:T(8,128)(2,1)}, bf16[48,3072]{1,0:T(8,128)(2,1)S(1)}) custom-call(bf16[32,40,128]{2,1,0:T(8,128)(2,1)S(1)} %all-to-all-done.taken, bf16[272,3072]{1,0:T(8,128)(2,1)S(1)} %get-tuple-element.27.stack), custom_call_target="tpu_custom_call" | custom-call | tf_op jit(solution)/shard_map/pallas_call | solution.py:390
  27.6 7.5 %all-to-all-start.1 = ((bf16[32,56,128]{2,1,0:T(8,128)(2,1)}), bf16[32,56,128]{2,1,0:T(8,128)(2,1)S(1)}, u32[]{:S(2)}, u32[]{:S(2)}) async-start(bf16[32,56,128]{2,1,0:T(8,128)(2,1)} %get-tuple-element.28), calls=%async_computation.1 | async-start | bytes 917504 | tf_op jit(solution)/shard_map/all_to_all | solution.py:416
  35.1 1.4 %collective-permute-start.2 = (bf16[2,128,384]{2,1,0:T(8,128)(2,1)S(1)}, bf16[2,128,384]{2,1,0:T(8,128)(2,1)S(1)}, u32[]{:S(2)}, u32[]{:S(2)}) collective-permute-start(bf16[2,128,384]{2,1,0:T(8,128)(2,1)S(1)} %pad_maximum_fusion.here), channel_id=1, source_target_pairs={{0,1},{1,0},{2,3},{3,2},{4,5},{5,4},{6,7},{7,6},{8,9},{9,8},{10,11... | collective-permute-start | bytes 589832 | tf_op jit(solution)/shard_map/ppermute | solution.py:410
  36.5 0.0 copy-done.3
  36.5 3.9 %collective-permute-done.2.there = bf16[2,128,384]{2,1,0:T(8,128)(2,1)S(1)} collective-permute-done((bf16[2,128,384]{2,1,0:T(8,128)(2,1)S(1)}, bf16[2,128,384]{2,1,0:T(8,128)(2,1)S(1)}, u32[]{:S(2)}, u32[]{:S(2)}) %collective-permute-start.2) | collective-permute-done | bytes 196640 | tf_op jit(solution)/shard_map/ppermute | solution.py:410
  40.3 7.1 %all-to-all-done.1.taken = bf16[32,56,128]{2,1,0:T(8,128)(2,1)S(1)} async-done(((bf16[32,56,128]{2,1,0:T(8,128)(2,1)}), bf16[32,56,128]{2,1,0:T(8,128)(2,1)S(1)}, u32[]{:S(2)}, u32[]{:S(2)}) %all-to-all-start.1) | async-done | bytes 458784 | tf_op jit(solution)/shard_map/all_to_all | solution.py:416
  47.5 2.4 %shard_map.117 = (bf16[1152,128]{1,0:T(8,128)(2,1)S(1)}, f32[8,1152]{1,0:T(8,128)S(1)}, bf16[2,256,1152]{2,1,0:T(8,128)(2,1)S(1)}, bf16[6,128,256]{2,1,0:T(8,128...) custom-call(bf16[32,56,128]{2,1,0:T(8,128)(2,1)S(1)} %all-to-all-done.1.taken, ...), custom_call_target="tpu_custom_call" | custom-call | tf_op jit(solution)/shard_map/pallas_call | solution.py:390
  49.9 4.3 %collective-permute-start.3 = (f32[256,128]{1,0:T(8,128)S(1)}, f32[256,128]{1,0:T(8,128)S(1)}, u32[]{:S(2)}, u32[]{:S(2)}) collective-permute-start(f32[256,128]{1,0:T(8,128)S(1)} %get-tuple-element.34), channel_id=1, source_target_pairs={{0,2},{2,0},{4,6},{6,4},{8,10},{10,8},{12,14},{14,12},{16,18},{18,... | collective-permute-start | bytes 393224 | tf_op jit(solution)/shard_map/ppermute | solution.py:406
  54.2 1.0 collective-permute-done.3
  55.2 1.4 %collective-permute-start.4 = (f32[256,128]{1,0:T(8,128)S(1)}, f32[256,128]{1,0:T(8,128)S(1)}, u32[]{:S(2)}, u32[]{:S(2)}) collective-permute-start(f32[256,128]{1,0:T(8,128)S(1)} %add.18.vel_here), channel_id=1, source_target_pairs={{0,1},{1,0},{2,3},{3,2},{4,5},{5,4},{6,7},{7,6},{8,9},{9,8},{10,11... | collective-permute-start | bytes 393224 | tf_op jit(solution)/shard_map/ppermute | solution.py:410
  56.6 1.8 %shard_map.118 = f32[256,128]{1,0:T(8,128)S(1)} custom-call(bf16[1152,128]{1,0:T(8,128)(2,1)S(1)} %get-tuple-element.35.matrices, f32[8,1152]{1,0:T(8,128)S(1)} %get-tuple-element.36.offsets, bf16[2,128,384]{2,1,0:T(8,128)(2,1)S(1)} %pad_maximum_fusion.here, bf16[2,128,384]{2,1,0:T(8,128)(2,1)S(1)} %collective-permute-done.2.there, ...), custom_call_target="tpu_custom_call" | custom-call | flops 4000000000 | tf_op jit(solution)/shard_map/pallas_call | solution.py:390
  58.4 1.6 %collective-permute-done.4.vel_there = f32[256,128]{1,0:T(8,128)S(1)} collective-permute-done((f32[256,128]{1,0:T(8,128)S(1)}, f32[256,128]{1,0:T(8,128)S(1)}, u32[]{:S(2)}, u32[]{:S(2)}) %collective-permute-start.4) | collective-permute-done | bytes 131104 | tf_op jit(solution)/shard_map/ppermute | solution.py:410
  60.0 0.8 slice.32
  60.8 1.2 %collective-permute-start.5 = (f32[256,64]{1,0:T(8,128)}, f32[256,64]{1,0:T(8,128)}, u32[]{:S(2)}, u32[]{:S(2)}) collective-permute-start(f32[256,64]{1,0:T(8,128)} %slice.32), channel_id=1, source_target_pairs={{0,2},{2,0},{4,6},{6,4},{8,10},{10,8},{12,14},{14,12},{16,18},{18,... | collective-permute-start | bytes 196616 | tf_op jit(solution)/shard_map/ppermute | solution.py:406
  62.0 2.9 %shard_map.119 = bf16[32,24,128]{2,1,0:T(8,128)(2,1)} custom-call(bf16[2,256,1152]{2,1,0:T(8,128)(2,1)S(1)} %get-tuple-element.30.kept, bf16[6,128,256]{2,1,0:T(8,128)(2,1)S(1)} %get-tuple-element.31.keys_turned, f32[6,256,256]{2,1,0:T(8,128)S(1)} %get-tuple-element.32.probs_turned, bf16[2,128,384]{2,1,0:T(8,128)(2,1)S(1)} %pad_maximum_fusion.here, ...), custom_call_target="tpu_custom_call" | custom-call | tf_op jit(solution)/shard_map/pallas_call | solution.py:390
  64.9 5.1 %all-to-all-start.2 = ((bf16[32,24,128]{2,1,0:T(8,128)(2,1)}), bf16[32,24,128]{2,1,0:T(8,128)(2,1)S(1)}, u32[]{:S(2)}, u32[]{:S(2)}) async-start(bf16[32,24,128]{2,1,0:T(8,128)(2,1)} %shard_map.119), calls=%async_computation.2 | async-start | bytes 393216 | tf_op jit(solution)/shard_map/all_to_all | solution.py:416
  70.0 0.0 collective-permute-done.5
  70.1 0.9 slice_add_fusion
  71.0 1.4 %collective-permute-start.6 = (f32[128,64]{1,0:T(8,128)S(1)}, f32[128,64]{1,0:T(8,128)S(1)}, u32[]{:S(2)}, u32[]{:S(2)}) collective-permute-start(f32[128,64]{1,0:T(8,128)S(1)} %slice.40), channel_id=1, source_target_pairs={{0,1},{1,0},{2,3},{3,2},{4,5},{5,4},{6,7},{7,6},{8,9},{9,8},{10,11... | collective-permute-start | bytes 98312 | tf_op jit(solution)/shard_map/ppermute | solution.py:410
  72.4 2.1 %collective-permute-done.6 = f32[128,64]{1,0:T(8,128)S(1)} collective-permute-done((f32[128,64]{1,0:T(8,128)S(1)}, f32[128,64]{1,0:T(8,128)S(1)}, u32[]{:S(2)}, u32[]{:S(2)}) %collective-permute-start.6) | collective-permute-done | bytes 32800 | tf_op jit(solution)/shard_map/ppermute | solution.py:410
  74.5 5.3 %all-to-all-done.2.taken = bf16[32,24,128]{2,1,0:T(8,128)(2,1)S(1)} async-done(((bf16[32,24,128]{2,1,0:T(8,128)(2,1)}), bf16[32,24,128]{2,1,0:T(8,128)(2,1)S(1)}, u32[]{:S(2)}, u32[]{:S(2)}) %all-to-all-start.2) | async-done | bytes 196640 | tf_op jit(solution)/shard_map/all_to_all | solution.py:416
  79.8 0.6 shard_map.120
  80.4 2.6 %collective-permute-start.8 = (f32[2,1536]{1,0:T(2,128)S(1)}, f32[2,1536]{1,0:T(2,128)S(1)}, u32[]{:S(2)}, u32[]{:S(2)}) collective-permute-start(f32[2,1536]{1,0:T(2,128)S(1)} %get-tuple-element.43), channel_id=1, source_target_pairs={{0,2},{2,0},{4,6},{6,4},{8,10},{10,8},{12,14},{14,12},{16,18},{18,... | collective-permute-start | bytes 36872 | tf_op jit(solution)/shard_map/ppermute | solution.py:406
  83.0 0.8 collective-permute-done.8
  83.8 1.4 %collective-permute-start.9 = (f32[2,1536]{1,0:T(2,128)S(1)}, f32[2,1536]{1,0:T(2,128)S(1)}, u32[]{:S(2)}, u32[]{:S(2)}) collective-permute-start(f32[2,1536]{1,0:T(2,128)S(1)} %add.22), channel_id=1, source_target_pairs={{0,1},{1,0},{2,3},{3,2},{4,5},{5,4},{6,7},{7,6},{8,9},{9,8},{10,11... | collective-permute-start | bytes 36872 | tf_op jit(solution)/shard_map/ppermute | solution.py:410
  85.2 1.2 %collective-permute-done.9 = f32[2,1536]{1,0:T(2,128)S(1)} collective-permute-done((f32[2,1536]{1,0:T(2,128)S(1)}, f32[2,1536]{1,0:T(2,128)S(1)}, u32[]{:S(2)}, u32[]{:S(2)}) %collective-permute-start.9) | collective-permute-done | bytes 12320 | tf_op jit(solution)/shard_map/ppermute | solution.py:410
  86.5 0.8 broadcast_in_dim.5
  87.3 3.9 %all-to-all-start.3 = ((bf16[32,2,1536]{2,1,0:T(2,128)(2,1)}), bf16[32,2,1536]{2,1,0:T(2,128)(2,1)S(1)}, u32[]{:S(2)}, u32[]{:S(2)}) async-start(bf16[32,2,1536]{2,1,0:T(2,128)(2,1)} %broadcast_in_dim.5), calls=%async_computation.3 | async-start | bytes 393216 | tf_op jit(solution)/shard_map/all_to_all | solution.py:416
  91.1 3.0 %collective-permute-start.7 = (bf16[64,128]{0,1:T(8,128)(2,1)S(1)}, bf16[64,128]{0,1:T(8,128)(2,1)S(1)}, u32[]{:S(2)}, u32[]{:S(2)}) collective-permute-start(bf16[64,128]{0,1:T(8,128)(2,1)S(1)} %fusion.3), channel_id=1, source_target_pairs={{0,128},{128,0},{1,129},{129,1},{2,130},{130,2},{3,131},{131,3},{4... | collective-permute-start | bytes 49160 | tf_op jit(solution)/shard_map/ppermute | solution.py:523
  94.1 6.4 %all-to-all-done.3 = bf16[32,2,1536]{2,1,0:T(2,128)(2,1)S(1)} async-done(((bf16[32,2,1536]{2,1,0:T(2,128)(2,1)}), bf16[32,2,1536]{2,1,0:T(2,128)(2,1)S(1)}, u32[]{:S(2)}, u32[]{:S(2)}) %all-to-all-start.3) | async-done | bytes 196640 | tf_op jit(solution)/shard_map/all_to_all | solution.py:416
  100.6 3.2 %collective-permute-start.10 = (f32[2,1536]{1,0:T(2,128)S(1)}, f32[2,1536]{1,0:T(2,128)S(1)}, u32[]{:S(2)}, u32[]{:S(2)}) collective-permute-start(f32[2,1536]{1,0:T(2,128)S(1)} %convert_reduce_fusion), channel_id=1, source_target_pairs={{0,2},{2,0},{4,6},{6,4},{8,10},{10,8},{12,14},{14,12},{16,18},{18,... | collective-permute-start | bytes 36872 | tf_op jit(solution)/shard_map/ppermute | solution.py:406
  103.8 0.0 collective-permute-done.7
  103.8 0.7 copy.33
  104.5 0.1 collective-permute-done.10
  104.6 0.6 maximum_select_fusion
  (9 shorter events, 0.2 us)
Async XLA Ops:
  0.6 16.7 %copy-start = (bf16[1,64,3072]{2,1,0:T(8,128)(2,1)S(1)}, bf16[1,64,3072]{2,1,0:T(8,128)(2,1)}, u32[]{:S(2)}) copy-start(bf16[1,64,3072]{2,1,0:T(8,128)(2,1)} %param.16) | copy-start | bytes 1179652
  0.6 4.6 %collective-permute-start = (bf16[48,2304]{1,0:T(8,128)(2,1)}, bf16[48,2304]{1,0:T(8,128)(2,1)S(1)}, u32[]{:S(2)}, u32[]{:S(2)}) collective-permute-start(bf16[48,2304]{1,0:T(8,128)(2,1)} %bitcast.23), channel_id=1, source_target_pairs={{0,2},{2,0},{4,6},{6,4},{8,10},{10,8},{12,14},{14,12},{16,18},{18,... | collective-permute-start | bytes 663560 | tf_op jit(solution)/shard_map/ppermute | solution.py:406
  4.0 0.9 copy-start.1
  4.9 11.9 %copy-start.4 = (bf16[1,1,128,64]{2,3,1,0:T(8,128)(2,1)S(1)}, bf16[1,1,128,64]{2,3,1,0:T(8,128)(2,1)}, u32[]{:S(2)}) copy-start(bf16[1,1,128,64]{2,3,1,0:T(8,128)(2,1)} %param.10) | copy-start | bytes 49156
  4.9 12.1 %copy-start.5 = (bf16[1,1,128,64]{2,3,1,0:T(8,128)(2,1)S(1)}, bf16[1,1,128,64]{2,3,1,0:T(8,128)(2,1)}, u32[]{:S(2)}) copy-start(bf16[1,1,128,64]{2,3,1,0:T(8,128)(2,1)} %param.11) | copy-start | bytes 49156
  4.9 12.2 %copy-start.6 = (bf16[1,1,128,64]{2,3,1,0:T(8,128)(2,1)S(1)}, bf16[1,1,128,64]{2,3,1,0:T(8,128)(2,1)}, u32[]{:S(2)}) copy-start(bf16[1,1,128,64]{2,3,1,0:T(8,128)(2,1)} %param.13) | copy-start | bytes 49156
  4.9 12.3 %copy-start.7 = (bf16[1,1,128,64]{2,3,1,0:T(8,128)(2,1)S(1)}, bf16[1,1,128,64]{2,3,1,0:T(8,128)(2,1)}, u32[]{:S(2)}) copy-start(bf16[1,1,128,64]{2,3,1,0:T(8,128)(2,1)} %param.15) | copy-start | bytes 49156
  4.9 12.4 %copy-start.2 = (f32[1,2,2,3072]{3,2,1,0:T(2,128)S(1)}, f32[1,2,2,3072]{3,2,1,0:T(2,128)}, u32[]{:S(2)}) copy-start(f32[1,2,2,3072]{3,2,1,0:T(2,128)} %param.19) | copy-start | bytes 147460
  6.2 19.8 %all-to-all-start = ((bf16[32,40,128]{2,1,0:T(8,128)(2,1)}), bf16[32,40,128]{2,1,0:T(8,128)(2,1)S(1)}, u32[]{:S(2)}, u32[]{:S(2)}) async-start(bf16[32,40,128]{2,1,0:T(8,128)(2,1)} %shard_map.114), calls=%async_computation | async-start | bytes 655360 | tf_op jit(solution)/shard_map/all_to_all | solution.py:416
  18.4 1.7 %collective-permute-start.1 = (bf16[128,384]{1,0:T(8,128)(2,1)S(1)}, bf16[128,384]{1,0:T(8,128)(2,1)S(1)}, u32[]{:S(2)}, u32[]{:S(2)}) collective-permute-start(bf16[128,384]{1,0:T(8,128)(2,1)S(1)} %get-tuple-element.25), channel_id=1, source_target_pairs={{0,2},{2,0},{4,6},{6,4},{8,10},{10,8},{12,14},{14,12},{16,18},{18,... | collective-permute-start | bytes 294920 | tf_op jit(solution)/shard_map/ppermute | solution.py:406
  20.0 16.4 %copy-start.3 = (bf16[1,768,64]{1,2,0:T(8,128)(2,1)S(1)}, bf16[1,768,64]{1,2,0:T(8,128)(2,1)}, u32[]{:S(2)}) copy-start(bf16[1,768,64]{1,2,0:T(8,128)(2,1)} %param.18) | copy-start | bytes 294916
  27.6 19.9 %all-to-all-start.1 = ((bf16[32,56,128]{2,1,0:T(8,128)(2,1)}), bf16[32,56,128]{2,1,0:T(8,128)(2,1)S(1)}, u32[]{:S(2)}, u32[]{:S(2)}) async-start(bf16[32,56,128]{2,1,0:T(8,128)(2,1)} %get-tuple-element.28), calls=%async_computation.1 | async-start | bytes 917504 | tf_op jit(solution)/shard_map/all_to_all | solution.py:416
  35.1 5.3 %collective-permute-start.2 = (bf16[2,128,384]{2,1,0:T(8,128)(2,1)S(1)}, bf16[2,128,384]{2,1,0:T(8,128)(2,1)S(1)}, u32[]{:S(2)}, u32[]{:S(2)}) collective-permute-start(bf16[2,128,384]{2,1,0:T(8,128)(2,1)S(1)} %pad_maximum_fusion.here), channel_id=1, source_target_pairs={{0,1},{1,0},{2,3},{3,2},{4,5},{5,4},{6,7},{7,6},{8,9},{9,8},{10,11... | collective-permute-start | bytes 589832 | tf_op jit(solution)/shard_map/ppermute | solution.py:410
  49.9 5.3 %collective-permute-start.3 = (f32[256,128]{1,0:T(8,128)S(1)}, f32[256,128]{1,0:T(8,128)S(1)}, u32[]{:S(2)}, u32[]{:S(2)}) collective-permute-start(f32[256,128]{1,0:T(8,128)S(1)} %get-tuple-element.34), channel_id=1, source_target_pairs={{0,2},{2,0},{4,6},{6,4},{8,10},{10,8},{12,14},{14,12},{16,18},{18,... | collective-permute-start | bytes 393224 | tf_op jit(solution)/shard_map/ppermute | solution.py:406
  55.2 4.8 %collective-permute-start.4 = (f32[256,128]{1,0:T(8,128)S(1)}, f32[256,128]{1,0:T(8,128)S(1)}, u32[]{:S(2)}, u32[]{:S(2)}) collective-permute-start(f32[256,128]{1,0:T(8,128)S(1)} %add.18.vel_here), channel_id=1, source_target_pairs={{0,1},{1,0},{2,3},{3,2},{4,5},{5,4},{6,7},{7,6},{8,9},{9,8},{10,11... | collective-permute-start | bytes 393224 | tf_op jit(solution)/shard_map/ppermute | solution.py:410
  60.8 9.3 %collective-permute-start.5 = (f32[256,64]{1,0:T(8,128)}, f32[256,64]{1,0:T(8,128)}, u32[]{:S(2)}, u32[]{:S(2)}) collective-permute-start(f32[256,64]{1,0:T(8,128)} %slice.32), channel_id=1, source_target_pairs={{0,2},{2,0},{4,6},{6,4},{8,10},{10,8},{12,14},{14,12},{16,18},{18,... | collective-permute-start | bytes 196616 | tf_op jit(solution)/shard_map/ppermute | solution.py:406
  64.9 14.9 %all-to-all-start.2 = ((bf16[32,24,128]{2,1,0:T(8,128)(2,1)}), bf16[32,24,128]{2,1,0:T(8,128)(2,1)S(1)}, u32[]{:S(2)}, u32[]{:S(2)}) async-start(bf16[32,24,128]{2,1,0:T(8,128)(2,1)} %shard_map.119), calls=%async_computation.2 | async-start | bytes 393216 | tf_op jit(solution)/shard_map/all_to_all | solution.py:416
  71.0 3.5 %collective-permute-start.6 = (f32[128,64]{1,0:T(8,128)S(1)}, f32[128,64]{1,0:T(8,128)S(1)}, u32[]{:S(2)}, u32[]{:S(2)}) collective-permute-start(f32[128,64]{1,0:T(8,128)S(1)} %slice.40), channel_id=1, source_target_pairs={{0,1},{1,0},{2,3},{3,2},{4,5},{5,4},{6,7},{7,6},{8,9},{9,8},{10,11... | collective-permute-start | bytes 98312 | tf_op jit(solution)/shard_map/ppermute | solution.py:410
  80.4 3.4 %collective-permute-start.8 = (f32[2,1536]{1,0:T(2,128)S(1)}, f32[2,1536]{1,0:T(2,128)S(1)}, u32[]{:S(2)}, u32[]{:S(2)}) collective-permute-start(f32[2,1536]{1,0:T(2,128)S(1)} %get-tuple-element.43), channel_id=1, source_target_pairs={{0,2},{2,0},{4,6},{6,4},{8,10},{10,8},{12,14},{14,12},{16,18},{18,... | collective-permute-start | bytes 36872 | tf_op jit(solution)/shard_map/ppermute | solution.py:406
  83.8 2.6 %collective-permute-start.9 = (f32[2,1536]{1,0:T(2,128)S(1)}, f32[2,1536]{1,0:T(2,128)S(1)}, u32[]{:S(2)}, u32[]{:S(2)}) collective-permute-start(f32[2,1536]{1,0:T(2,128)S(1)} %add.22), channel_id=1, source_target_pairs={{0,1},{1,0},{2,3},{3,2},{4,5},{5,4},{6,7},{7,6},{8,9},{9,8},{10,11... | collective-permute-start | bytes 36872 | tf_op jit(solution)/shard_map/ppermute | solution.py:410
  87.3 13.3 %all-to-all-start.3 = ((bf16[32,2,1536]{2,1,0:T(2,128)(2,1)}), bf16[32,2,1536]{2,1,0:T(2,128)(2,1)S(1)}, u32[]{:S(2)}, u32[]{:S(2)}) async-start(bf16[32,2,1536]{2,1,0:T(2,128)(2,1)} %broadcast_in_dim.5), calls=%async_computation.3 | async-start | bytes 393216 | tf_op jit(solution)/shard_map/all_to_all | solution.py:416
  91.1 12.7 %collective-permute-start.7 = (bf16[64,128]{0,1:T(8,128)(2,1)S(1)}, bf16[64,128]{0,1:T(8,128)(2,1)S(1)}, u32[]{:S(2)}, u32[]{:S(2)}) collective-permute-start(bf16[64,128]{0,1:T(8,128)(2,1)S(1)} %fusion.3), channel_id=1, source_target_pairs={{0,128},{128,0},{1,129},{129,1},{2,130},{130,2},{3,131},{131,3},{4... | collective-permute-start | bytes 49160 | tf_op jit(solution)/shard_map/ppermute | solution.py:523
  100.6 4.0 %collective-permute-start.10 = (f32[2,1536]{1,0:T(2,128)S(1)}, f32[2,1536]{1,0:T(2,128)S(1)}, u32[]{:S(2)}, u32[]{:S(2)}) collective-permute-start(f32[2,1536]{1,0:T(2,128)S(1)} %convert_reduce_fusion), channel_id=1, source_target_pairs={{0,2},{2,0},{4,6},{6,4},{8,10},{10,8},{12,14},{14,12},{16,18},{18,... | collective-permute-start | bytes 36872 | tf_op jit(solution)/shard_map/ppermute | solution.py:406

commit v5 on v4

--- a/solution.py
+++ b/solution.py
@@ -51,7 +51,7 @@
     return lax.axis_index("role") == 1
 
 
-def pack_kernel(noise_levels, replay_levels, base, noise, replay, cotangent, embed, modulation, pack, stack):
+def pack_kernel(noise_levels, replay_levels, base, noise, replay, cotangent, embed, modulation, after, pack, stack):
     critic = on_critic()
     modulation_a = modulation[0]
     modulation_b = jnp.where(critic, modulation[1], modulation_a)
@@ -97,31 +97,48 @@
     pack[:, 256:384] = tail.astype(BF16)
 
 
-def cut_kernel(weight, keep):
-    columns = keep.shape[1]
-    keep[...] = jnp.where(on_second_core(), weight[:, columns:].astype(F32), weight[:, 0:columns].astype(F32)).astype(BF16)
-
-
-def weight_kernel(chips, keep, received, out, turned):
+def turn_rows(rows, padded, second):
+    count, columns = rows.shape
+    empty = jnp.zeros((count, columns), F32)
+    parts = [jnp.where(second, empty, rows), jnp.where(second, rows, empty)]
+    if padded > 2 * count:
+        parts.append(jnp.zeros((padded - 2 * count, columns), F32))
+    return jnp.concatenate(parts, axis=0).T
+
+
+def half_columns(weight, second):
+    columns = weight.shape[1] // 2
+    start = pl.multiple_of(jnp.where(second, columns, 0), 128)
+    return weight[:, pl.ds(start, columns)].astype(F32)
+
+
+def own_rows_kernel(weight, out):
     second = on_second_core()
-    rows, columns = keep.shape
-    own = keep[...].astype(F32)
-    other = jnp.where(second, received[:, columns:].astype(F32), received[:, 0:columns].astype(F32))
-    both = [jnp.where(second, other, own), jnp.where(second, own, other)]
-    padded = out.shape[2]
-    if padded > 2 * rows:
-        both.append(jnp.zeros((padded - 2 * rows, columns), F32))
-    turned[0:columns, :] = jnp.concatenate(both, axis=0).T
+    out[...] = turn_rows(half_columns(weight, second), out.shape[1], second)
+
+
+def weight_kernel(chips, own, received, out, turned, blocks, copied):
+    second = on_second_core()
+    columns, padded = own.shape
+    turned[0:columns, :] = own[...] + turn_rows(half_columns(received, second), padded, jnp.logical_not(second))
     turned[columns:, :] = jnp.zeros((turned.shape[0] - columns, padded), F32)
     block = columns // chips
     height = out.shape[1]
     row = row_index((height, padded))
+    group = 8
+    copies = []
     for chip in range(chips):
         piece = turned[chip * block : chip * block + height, :]
-        out[chip] = jnp.where(row < block, piece, 0.0).astype(BF16)
-
-
-def product_kernel(block, taken, stack, out, halves_out, columns_out):
+        blocks[chip] = jnp.where(row < block, piece, 0.0).astype(BF16)
+        if chip % group == group - 1:
+            span = pl.ds(chip + 1 - group, group)
+            copies.append(pltpu.make_async_copy(blocks.at[span], out.at[span], copied.at[len(copies)]))
+            copies[-1].start()
+    for copy in copies:
+        copy.wait()
+
+
+def product_kernel(block, taken, stack, after, out, halves_out, columns_out):
     chips, height, padded = taken.shape
     half = block // 2
     stride = halves_out.shape[0] // 2
@@ -265,8 +282,9 @@
     crossing[...] = pltpu.roll(velocity[...], CHANNELS, 1)
 
 
-def first_pass_kernel(matrices, offsets, here, there, output_turned, velocity):
+def first_pass_kernel(matrices, offsets, here, there, output_turned, after, velocity, crossing):
     forward(0, (here, there), matrices, offsets, output_turned, None, None, None, velocity)
+    crossing[...] = pltpu.roll(velocity[...], CHANNELS, 1)
 
 
 def swap_tokens(value):
@@ -275,7 +293,21 @@
 
 
 def backward_kernel(
-    block, kept, keys_turned, probs_turned, here, there, vel_here, vel_there, output_turned, out, gathered, summed
+    block,
+    kept,
+    keys_turned,
+    probs_turned,
+    here,
+    there,
+    vel_here,
+    vel_there,
+    output_turned,
+    after,
+    out,
+    gathered,
+    summed,
+    blocks,
+    copied,
 ):
     critic = on_critic()
     packs = (here, there)
@@ -308,6 +340,14 @@
         turned = dot(weight, grads_turned[lanes], TN).astype(BF16)
         value = kept[sample, :, head * 3 * HEAD_DIM + 2 * HEAD_DIM : (head + 1) * 3 * HEAD_DIM]
         grad_probs.append(dot(value, turned))
+    columns = heads * 3 * HEAD_DIM
+    gathered[columns:, :] = jnp.zeros((gathered.shape[0] - columns, 128), F32)
+    height = out.shape[1]
+    half = block // 2
+    row = row_index((height, 128))
+    low_lanes = lane_index((height, 128)) < CHANNELS
+    pad = jnp.zeros((1, 128 - block), F32) if block < 128 else None
+    copies = []
     for head in range(heads):
         at = head * 3 * HEAD_DIM
         query_total, rest_total = None, None
@@ -333,26 +373,26 @@
         gathered[at : at + HEAD_DIM, :] = query_total
         gathered[at + HEAD_DIM : at + 3 * HEAD_DIM, :] = rest_total.T
         summed[:, at : at + 3 * HEAD_DIM] = ends[0] + ends[1]
-    columns = heads * 3 * HEAD_DIM
-    gathered[columns:, :] = jnp.zeros((gathered.shape[0] - columns, 128), F32)
-    chips, height = out.shape[0], out.shape[1]
-    half = block // 2
-    row = row_index((height, 128))
-    low_lanes = lane_index((height, 128)) < CHANNELS
-    pad = jnp.zeros((1, 128 - block), F32) if block < 128 else None
-    for chip in range(chips):
-        at = chip * block
-        piece = jnp.where(low_lanes, gathered[at : at + height, :], gathered[at + half : at + half + height, :])
-        line = summed[:, at : at + block]
-        high = rounded(line)
-        pair = [high, line - high]
-        if pad is not None:
-            pair = [jnp.concatenate([part, pad], axis=1) for part in pair]
-        piece = jnp.where(row < half, piece, jnp.where(row == half, pair[0], jnp.where(row == half + 1, pair[1], 0.0)))
-        out[chip] = piece.astype(BF16)
-
-
-def closing_kernel(block, factor, taken, weight, embed, kept, sent):
+        start = columns * head // heads // block
+        stop = columns * (head + 1) // heads // block
+        for chip in range(start, stop):
+            base = chip * block
+            piece = jnp.where(low_lanes, gathered[base : base + height, :], gathered[base + half : base + half + height, :])
+            line = summed[:, base : base + block]
+            high = rounded(line)
+            pair = [high, line - high]
+            if pad is not None:
+                pair = [jnp.concatenate([part, pad], axis=1) for part in pair]
+            tail = jnp.where(row == half, pair[0], jnp.where(row == half + 1, pair[1], 0.0))
+            blocks[chip] = jnp.where(row < half, piece, tail).astype(BF16)
+        span = pl.ds(start, stop - start)
+        copies.append(pltpu.make_async_copy(blocks.at[span], out.at[span], copied.at[head]))
+        copies[-1].start()
+    for copy in copies:
+        copy.wait()
+
+
+def closing_kernel(block, factor, taken, weight, embed, after, kept, sent):
     second = on_second_core()
     total = taken[0].astype(F32)
     for chip in range(1, taken.shape[0]):
@@ -378,24 +418,55 @@
         product = dot(high, columns) + dot(low, columns)
         scale = jnp.sum(product[:CHANNELS] * embed[:, start : start + step].astype(F32), axis=0, keepdims=True)
         parts.append(jnp.concatenate([scale, product[CHANNELS : CHANNELS + 1]], axis=0) * factor)
-    left = jnp.concatenate(parts[:3], axis=1)
-    right = jnp.concatenate(parts[3:], axis=1)
-    kept[...] = jnp.where(second, right, left)
-    sent[...] = jnp.where(second, left, right)
-
-
-def call(kernel, out_shapes, inputs, scalars=0, scratch=(), flops=0, moved=0):
+    sides = []
+    for side in (parts[:3], parts[3:]):
+        lines = [part[which : which + 1, i : i + 128] for which in range(2) for part in side for i in range(0, step, 128)]
+        sides.append(jnp.concatenate(lines, axis=0))
+    kept[...] = jnp.where(second, sides[1], sides[0])
+    sent[...] = jnp.where(second, sides[0], sides[1])
+
+
+def payload_kernel(noise_levels, own, a_here, a_there, b_here, b_there, out):
+    tokens = own.shape[0]
+    own_a = a_here[0:tokens, 0:CHANNELS] + a_there[...]
+    own_b = b_here[0:tokens, 0:CHANNELS] + b_there[tokens:, 0:CHANNELS]
+    sample = own[:, 0:CHANNELS].astype(F32) - noise_levels[0, 0] * own_a
+    out[...] = jnp.where(on_critic(), own_b - own_a, sample).T.astype(BF16)
+
+
+def spread_kernel(total, other, crossed, out, crossed_out):
+    line = (total[...] + other[...]).astype(BF16)
+    for chip in range(out.shape[0]):
+        out[chip] = line
+    crossed_out[...] = crossed[...]
+
+
+def join_kernel(total, near, out):
+    second = on_second_core()
+    count = total.shape[0] // 2
+    left = jnp.where(second, near[...], total[...])
+    right = jnp.where(second, total[...], near[...])
+    for which in range(2):
+        for side, half in enumerate((left, right)):
+            for i in range(count):
+                at = (side * count + i) * 128
+                out[which : which + 1, at : at + 128] = half[which * count + i : which * count + i + 1, :]
+
+
+def call(kernel, out_shapes, inputs, scalars=0, scratch=(), flops=0, after=(), far_out=False):
     specs = [pl.BlockSpec(memory_space=pltpu.SMEM)] * scalars
     specs += [pl.BlockSpec(memory_space=pltpu.VMEM)] * (len(inputs) - scalars)
+    specs += [pl.BlockSpec(memory_space=pl.ANY)] * len(after)
+    space = pl.ANY if far_out else pltpu.VMEM
     return pl.pallas_call(
         kernel,
         out_shape=out_shapes,
         in_specs=specs,
-        out_specs=jax.tree.map(lambda _: pl.BlockSpec(memory_space=pltpu.VMEM), out_shapes),
+        out_specs=jax.tree.map(lambda _: pl.BlockSpec(memory_space=space), out_shapes),
         scratch_shapes=list(scratch),
         compiler_params=pltpu.CompilerParams(vmem_limit_bytes=28 * 2**20),
-        cost_estimate=pl.CostEstimate(flops=flops, bytes_accessed=moved, transcendentals=0),
-    )(*inputs)
+        cost_estimate=pl.CostEstimate(flops=flops, bytes_accessed=0, transcendentals=0),
+    )(*inputs, *after)
 
 
 def struct(shape, dtype):
@@ -428,7 +499,6 @@
     output_weight,
     modulation,
 ):
-    is_critic = on_critic()
     second_core = on_second_core()
     devices = lax.axis_size("fsdp")
     chips = devices // 2
@@ -448,21 +518,25 @@
     output_turned = jnp.where(second_core, output_turned[:, out_columns:], output_turned[:, :out_columns])
 
     received = other_core(weight)
-    keep = call(cut_kernel, struct((weight.shape[0], columns), BF16), (weight,))
+    own_turned = call(own_rows_kernel, struct((columns, padded), F32), (weight,))
     turned = call(
         functools.partial(weight_kernel, chips),
         struct((chips, height, padded), BF16),
-        (keep, received),
-        scratch=[pltpu.VMEM((columns + height - block, padded), F32)],
-    )
-    turned, first_levels = lax.optimization_barrier((turned, noise_levels))
+        (own_turned, received),
+        scratch=[
+            pltpu.VMEM((columns + height - block, padded), F32),
+            pltpu.VMEM((chips, height, padded), BF16),
+            pltpu.SemaphoreType.DMA((chips // 8,)),
+        ],
+        far_out=True,
+    )
     taken = between_chips(turned)
 
     own, stack = call(
         pack_kernel,
         (struct((tokens, 384), BF16), struct((272, width), BF16)),
         (
-            first_levels,
+            noise_levels,
             replay_levels,
             base_latents[0, 0],
             noise_latents[0, 0],
@@ -472,9 +546,9 @@
             modulation[0],
         ),
         scalars=2,
+        after=(turned,),
     )
     here = jnp.stack([own, other_core(own)])
-    taken, here = lax.optimization_barrier((taken, here))
     there = other_half(here)
 
     matrices, own_columns = call(
@@ -482,6 +556,7 @@
         (struct((chips, packed, 128), BF16), struct((2 * folded, width), BF16)),
         (taken, stack),
         scratch=[pltpu.VMEM((height, width), BF16)],
+        after=(there,),
     )
     whole, offsets, kept, keys_turned, probs, vel_b, vel_crossing = call(
         functools.partial(second_pass_kernel, block),
@@ -499,46 +574,53 @@
     )
     vel_here = vel_b + other_core(vel_crossing)
     vel_there = other_half(vel_here)
-    vel_a = call(
+    vel_a, vel_a_crossing = call(
         first_pass_kernel,
-        struct((2 * tokens, 2 * CHANNELS), F32),
+        (struct((2 * tokens, 2 * CHANNELS), F32), struct((2 * tokens, 2 * CHANNELS), F32)),
         (whole, offsets, here, there, output_turned),
         flops=4 * 10**9,
-    )
-    vel_there, vel_a = lax.optimization_barrier((vel_there, vel_a))
+        after=(vel_here,),
+    )
+    vel_a_here = vel_a + other_core(vel_a_crossing)
     products = call(
         functools.partial(backward_kernel, block),
         struct((chips, folded, 128), BF16),
         (kept, keys_turned, probs, here, there, vel_here, vel_there, output_turned),
-        scratch=[pltpu.VMEM((columns + 2 * folded, 128), F32), pltpu.VMEM((1, columns), F32)],
-    )
-    gathered = between_chips(products)
-
-    own_a = vel_a[:, :CHANNELS] + other_core(vel_a[:, CHANNELS:])
-    own_a = own_a[:tokens] + other_half(own_a[tokens:])
-    own_b = vel_here[:tokens, :CHANNELS] + vel_there[tokens:, :CHANNELS]
-    sample = own[:, :CHANNELS].astype(F32) - noise_levels[0, 0] * own_a
-    payload = jnp.where(is_critic, own_b - own_a, sample).T.astype(BF16)
-    gathered, payload = lax.optimization_barrier((gathered, payload))
-    crossed = lax.ppermute(payload, "role", [(0, 1), (1, 0)]).T
+        scratch=[
+            pltpu.VMEM((columns + 2 * folded, 128), F32),
+            pltpu.VMEM((1, columns), F32),
+            pltpu.VMEM((chips, folded, 128), BF16),
+            pltpu.SemaphoreType.DMA((heads,)),
+        ],
+        after=(vel_a,),
+        far_out=True,
+    )
+
+    payload = call(
+        payload_kernel,
+        struct((CHANNELS, tokens), BF16),
+        (noise_levels, own, vel_a_here, other_half(vel_a_here[tokens:, :CHANNELS]), vel_here, vel_there),
+        scalars=1,
+    )
+    crossed = lax.ppermute(payload, "role", [(0, 1), (1, 0)])
 
     samples = devices * base_latents.shape[1]
+    lines = width // 128
     kept_half, sent_half = call(
         functools.partial(closing_kernel, block, 1.0 / (samples * 2 * tokens)),
-        (struct((2, width // 2), F32), struct((2, width // 2), F32)),
-        (gathered, own_columns, embed),
+        (struct((lines, 128), F32), struct((lines, 128), F32)),
+        (between_chips(products), own_columns, embed),
+        after=(payload,),
     )
     total = kept_half + other_core(sent_half)
-    total = (total + other_half(total)).astype(BF16)
-    spread = between_chips(jnp.broadcast_to(total[None], (chips,) + total.shape))
-    total = jnp.sum(spread.astype(F32), axis=0)
-    near_total = other_core(total)
-    mod_grads = jnp.where(
-        second_core,
-        jnp.concatenate([near_total, total], axis=1),
-        jnp.concatenate([total, near_total], axis=1),
-    )
-    return (crossed[None, None], mod_grads[None])
+    spread, crossed = call(
+        spread_kernel,
+        (struct((chips, lines, 128), BF16), struct(crossed.shape, BF16)),
+        (total, other_half(total), crossed),
+    )
+    total = jnp.sum(between_chips(spread).astype(F32), axis=0)
+    mod_grads = call(join_kernel, struct((2, width), F32), (total, other_core(total)))
+    return (crossed.T[None, None], mod_grads[None])
 
 
 def solution(mesh):

time: 106 us -> 109 us (1.028)
  blocking collectives: 0 us -> 13.9 us
  waiting for transfers between devices: 36.8 us -> 30 us
  local copies, waits for them, and re-layouts: 3.67 us -> 1.43 us
  starting transfers between devices: 49.7 us -> 47.8 us
  other arithmetic: 1.68 us -> 0.11 us
  Pallas kernels: 11.3 us -> 12.8 us
    all_to_all x0 -> x1, blocking collectives: none -> 13.9 us  [between_chips(): lax.all_to_all(value, 'fsdp', 0, 0, tiled=True, axis_index_groups=groups)]
    all_to_all x4 -> x3, waiting for transfers between devices: 24.8 us -> 15.2 us  [between_chips(): lax.all_to_all(value, 'fsdp', 0, 0, tiled=True, axis_index_groups=groups)]
    all_to_all x4 -> x3, starting transfers between devices: 25.8 us -> 23.9 us  [between_chips(): lax.all_to_all(value, 'fsdp', 0, 0, tiled=True, axis_index_groups=groups)]
    pallas_call x8 -> x11, Pallas kernels: 11.3 us -> 12.8 us  [call(): pl.pallas_call(kernel, out_shape=out_shapes, in_specs=specs, out_specs=ja...]
  transfers between devices with their start and end apart: 15 -> 14, of which waited for: 13 -> 12; matrix products, arithmetic and copies ran while one was open for 2% -> 0% of each run, Pallas kernels for 5% -> 3%
where the time goes in v5:
time: 109 us; the launch traced here: 108 us
  starting transfers between devices  47.8 us (44%)
  waiting for transfers between devices  30 us (28%)
  blocking collectives  13.9 us (13%)
  Pallas kernels  12.8 us (12%)
  between operations  2.14 us (2%)
  local copies, waits for them, and re-layouts  1.43 us (1%)
    all_to_all x3, starting transfers between devices, between_chips(): lax.all_to_all(value, 'fsdp', 0, 0, tiled=True, axis_index_groups=groups)  23.9 us
    ppermute x6, starting transfers between devices, other_core(): lax.ppermute(value, 'fsdp', [(i, i ^ 1) for i in range(lax.axis_size('fsd...  16.4 us
    all_to_all x3, waiting for transfers between devices, between_chips(): lax.all_to_all(value, 'fsdp', 0, 0, tiled=True, axis_index_groups=groups)  15.2 us
    all_to_all x1, blocking collectives, between_chips(): lax.all_to_all(value, 'fsdp', 0, 0, tiled=True, axis_index_groups=groups)  13.9 us
    pallas_call x11, Pallas kernels, call(): pl.pallas_call(kernel, out_shape=out_shapes, in_specs=specs, out_specs=ja...  12.8 us
    ppermute x4, waiting for transfers between devices, other_half(): return lax.ppermute(value, 'seq', [(0, 1), (1, 0)])  9.87 us
    ppermute x4, starting transfers between devices, other_half(): return lax.ppermute(value, 'seq', [(0, 1), (1, 0)])  4.55 us
    ppermute x6, waiting for transfers between devices, other_core(): lax.ppermute(value, 'fsdp', [(i, i ^ 1) for i in range(lax.axis_size('fsd...  4.13 us
  transfers between devices with their start and end apart: 14, of which 12 were waited for; matrix products, arithmetic and copies ran while one was open for 0% of the time, Pallas kernels for 3%

profile of v5, /device:TPU:1, one launch (start us, length us, event | category | flops | bytes accessed | tf_op | source)
XLA Modules:
  0.0 108.2 jit_solution(3657252991389625474)
XLA Ops:
  0.6 0.0 copy-start
  0.6 3.3 %collective-permute-start = (bf16[48,2304]{1,0:T(8,128)(2,1)}, bf16[48,2304]{1,0:T(8,128)(2,1)S(1)}, u32[]{:S(2)}, u32[]{:S(2)}) collective-permute-start(bf16[48,2304]{1,0:T(8,128)(2,1)} %bitcast.19), channel_id=1, source_target_pairs={{0,2},{2,0},{4,6},{6,4},{8,10},{10,8},{12,14},{14,12},{16,18},{18,... | collective-permute-start | bytes 663560 | tf_op jit(solution)/shard_map/ppermute | solution.py:477
  4.0 0.0 copy-start.1
  4.0 0.9 copy-done.1
  4.9 0.0 copy-start.5
  4.9 0.0 copy-start.6
  4.9 0.0 copy-start.7
  4.9 0.0 copy-start.8
  4.9 0.0 copy-start.2
  4.9 0.2 shard_map.113.own
  5.1 0.2 collective-permute-done.received
  5.3 0.9 shard_map.114.after
  6.2 9.3 %all-to-all-start = ((bf16[32,40,128]{2,1,0:T(8,128)(2,1)}), bf16[32,40,128]{2,1,0:T(8,128)(2,1)S(1)}, u32[]{:S(2)}, u32[]{:S(2)}) async-start(bf16[32,40,128]{2,1,0:T(8,128)(2,1)} %shard_map.114.after), calls=%async_computation | async-start | bytes 655360 | tf_op jit(solution)/shard_map/all_to_all | solution.py:487
  16.8 0.0 copy-done.5
  16.8 0.1 copy.12
  16.9 0.0 copy-done.6
  16.9 0.1 copy.13
  17.0 0.0 copy-done.7
  17.1 0.1 copy.14
  17.2 0.0 copy-done.8
  17.2 0.1 copy.15
  17.3 0.0 copy-done
  17.3 0.0 copy-done.2
  17.3 1.0 shard_map.115
  18.3 0.7 collective-permute-start.1
  19.1 0.9 collective-permute-done.1
  20.0 0.0 copy-start.4
  20.0 1.4 %collective-permute-start.2 = (bf16[2,128,384]{2,1,0:T(8,128)(2,1)S(1)}, bf16[2,128,384]{2,1,0:T(8,128)(2,1)S(1)}, u32[]{:S(2)}, u32[]{:S(2)}) collective-permute-start(bf16[2,128,384]{2,1,0:T(8,128)(2,1)S(1)} %pad_maximum_fusion.here), channel_id=1, source_target_pairs={{0,1},{1,0},{2,3},{3,2},{4,5},{5,4},{6,7},{7,6},{8,9},{9,8},{10,11... | collective-permute-start | bytes 589832 | tf_op jit(solution)/shard_map/ppermute | solution.py:481
  21.4 4.8 %collective-permute-done.2.after.there = bf16[2,128,384]{2,1,0:T(8,128)(2,1)S(1)} collective-permute-done((bf16[2,128,384]{2,1,0:T(8,128)(2,1)S(1)}, bf16[2,128,384]{2,1,0:T(8,128)(2,1)S(1)}, u32[]{:S(2)}, u32[]{:S(2)}) %collective-permute-start.2) | collective-permute-done | bytes 196640 | tf_op jit(solution)/shard_map/ppermute | solution.py:481
  26.3 0.0 all-to-all-done.taken
  26.3 1.5 %shard_map.116 = (bf16[32,56,128]{2,1,0:T(8,128)(2,1)}, bf16[48,3072]{1,0:T(8,128)(2,1)S(1)}) custom-call(bf16[32,40,128]{2,1,0:T(8,128)(2,1)S(1)} %all-to-all-done.taken, bf16[272,3072]{1,0:T(8,128)(2,1)S(1)} %get-tuple-element.19.stack, bf16[2,128,384]{2,1,0:T(8,128)(2,1)S(1)} %collective-permute-done.2.after.there), custom_call_target="tpu_custom_call" | custom-call | tf_op jit(solution)/shard_map/pallas_call | solution.py:461
  27.8 9.5 %all-to-all-start.1 = ((bf16[32,56,128]{2,1,0:T(8,128)(2,1)}), bf16[32,56,128]{2,1,0:T(8,128)(2,1)S(1)}, u32[]{:S(2)}, u32[]{:S(2)}) async-start(bf16[32,56,128]{2,1,0:T(8,128)(2,1)} %get-tuple-element.21), calls=%async_computation.1 | async-start | bytes 917504 | tf_op jit(solution)/shard_map/all_to_all | solution.py:487
  37.3 0.0 copy-done.4
  37.3 12.2 %all-to-all-done.1.taken = bf16[32,56,128]{2,1,0:T(8,128)(2,1)S(1)} async-done(((bf16[32,56,128]{2,1,0:T(8,128)(2,1)}), bf16[32,56,128]{2,1,0:T(8,128)(2,1)S(1)}, u32[]{:S(2)}, u32[]{:S(2)}) %all-to-all-start.1) | async-done | bytes 458784 | tf_op jit(solution)/shard_map/all_to_all | solution.py:487
  49.5 2.4 %shard_map.117 = (bf16[1152,128]{1,0:T(8,128)(2,1)S(1)}, f32[8,1152]{1,0:T(8,128)S(1)}, bf16[2,256,1152]{2,1,0:T(8,128)(2,1)S(1)}, bf16[6,128,256]{2,1,0:T(8,128...) custom-call(bf16[32,56,128]{2,1,0:T(8,128)(2,1)S(1)} %all-to-all-done.1.taken, ...), custom_call_target="tpu_custom_call" | custom-call | tf_op jit(solution)/shard_map/pallas_call | solution.py:461
  51.9 4.5 %collective-permute-start.3 = (f32[256,128]{1,0:T(8,128)S(1)}, f32[256,128]{1,0:T(8,128)S(1)}, u32[]{:S(2)}, u32[]{:S(2)}) collective-permute-start(f32[256,128]{1,0:T(8,128)S(1)} %get-tuple-element.26), channel_id=1, source_target_pairs={{0,2},{2,0},{4,6},{6,4},{8,10},{10,8},{12,14},{14,12},{16,18},{18,... | collective-permute-start | bytes 393224 | tf_op jit(solution)/shard_map/ppermute | solution.py:477
  56.4 1.0 collective-permute-done.3
  57.4 1.4 %collective-permute-start.4 = (f32[256,128]{1,0:T(8,128)S(1)}, f32[256,128]{1,0:T(8,128)S(1)}, u32[]{:S(2)}, u32[]{:S(2)}) collective-permute-start(f32[256,128]{1,0:T(8,128)S(1)} %add.9.after.vel_here.b_here), channel_id=1, source_target_pairs={{0,1},{1,0},{2,3},{3,2},{4,5},{5,4},{6,7},{7,6},{8,9},{9,8},{10,11... | collective-permute-start | bytes 393224 | tf_op jit(solution)/shard_map/ppermute | solution.py:481
  58.8 1.9 %shard_map.118 = (f32[256,128]{1,0:T(8,128)S(1)}, f32[256,128]{1,0:T(8,128)S(1)}) custom-call(bf16[1152,128]{1,0:T(8,128)(2,1)S(1)} %get-tuple-element.27.matrices, f32[8,1152]{1,0:T(8,128)S(1)} %get-tuple-element.28.offsets, bf16[2,128,384]{2,1,0:T(8,128)(2,1)S(1)} %pad_maximum_fusion.here, bf16[2,128,384]{2,1,0:T(8,128)(2,1)S(1)} %collective-permute-done.2.after.there, ...), custom_call_target="tpu_custom_call" | custom-call | flops 4000000000 | tf_op jit(solution)/shard_map/pallas_call | solution.py:461
  60.7 0.0 copy-start.3
  60.7 1.5 %collective-permute-done.4.vel_there.b_there = f32[256,128]{1,0:T(8,128)S(1)} collective-permute-done((f32[256,128]{1,0:T(8,128)S(1)}, f32[256,128]{1,0:T(8,128)S(1)}, u32[]{:S(2)}, u32[]{:S(2)}) %collective-permute-start.4) | collective-permute-done | bytes 131104 | tf_op jit(solution)/shard_map/ppermute | solution.py:481
  62.3 3.0 %shard_map.119 = bf16[32,24,128]{2,1,0:T(8,128)(2,1)} custom-call(bf16[2,256,1152]{2,1,0:T(8,128)(2,1)S(1)} %get-tuple-element.22.kept, bf16[6,128,256]{2,1,0:T(8,128)(2,1)S(1)} %get-tuple-element.23.keys_turned, f32[6,256,256]{2,1,0:T(8,128)S(1)} %get-tuple-element.24.probs_turned, bf16[2,128,384]{2,1,0:T(8,128)(2,1)S(1)} %pad_maximum_fusion.here, ...), custom_call_target="tpu_custom_call" | custom-call | tf_op jit(solution)/shard_map/pallas_call | solution.py:461
  65.2 0.0 copy-done.3
  65.2 5.1 %all-to-all-start.2 = ((bf16[32,24,128]{2,1,0:T(8,128)(2,1)}), bf16[32,24,128]{2,1,0:T(8,128)(2,1)S(1)}, u32[]{:S(2)}, u32[]{:S(2)}) async-start(bf16[32,24,128]{2,1,0:T(8,128)(2,1)} %shard_map.119), calls=%async_computation.2 | async-start | bytes 393216 | tf_op jit(solution)/shard_map/all_to_all | solution.py:487
  70.4 1.6 %collective-permute-start.5 = (f32[256,128]{1,0:T(8,128)}, f32[256,128]{1,0:T(8,128)S(1)}, u32[]{:S(2)}, u32[]{:S(2)}) collective-permute-start(f32[256,128]{1,0:T(8,128)} %copy-done.3), channel_id=1, source_target_pairs={{0,2},{2,0},{4,6},{6,4},{8,10},{10,8},{12,14},{14,12},{16,18},{18,... | collective-permute-start | bytes 393224 | tf_op jit(solution)/shard_map/ppermute | solution.py:477
  71.9 1.2 %collective-permute-done.5 = f32[256,128]{1,0:T(8,128)S(1)} collective-permute-done((f32[256,128]{1,0:T(8,128)}, f32[256,128]{1,0:T(8,128)S(1)}, u32[]{:S(2)}, u32[]{:S(2)}) %collective-permute-start.5) | collective-permute-done | bytes 131104 | tf_op jit(solution)/shard_map/ppermute | solution.py:477
  73.2 1.4 %collective-permute-start.6 = (f32[128,64]{1,0:T(8,128)S(1)}, f32[128,64]{1,0:T(8,128)S(1)}, u32[]{:S(2)}, u32[]{:S(2)}) collective-permute-start(f32[128,64]{1,0:T(8,128)S(1)} %slice.14), channel_id=1, source_target_pairs={{0,1},{1,0},{2,3},{3,2},{4,5},{5,4},{6,7},{7,6},{8,9},{9,8},{10,11... | collective-permute-start | bytes 98312 | tf_op jit(solution)/shard_map/ppermute | solution.py:481
  74.6 2.1 %collective-permute-done.6.a_there = f32[128,64]{1,0:T(8,128)S(1)} collective-permute-done((f32[128,64]{1,0:T(8,128)S(1)}, f32[128,64]{1,0:T(8,128)S(1)}, u32[]{:S(2)}, u32[]{:S(2)}) %collective-permute-start.6) | collective-permute-done | bytes 32800 | tf_op jit(solution)/shard_map/ppermute | solution.py:481
  76.7 0.1 shard_map.120.after
  76.7 3.0 %all-to-all-done.2.taken = bf16[32,24,128]{2,1,0:T(8,128)(2,1)S(1)} async-done(((bf16[32,24,128]{2,1,0:T(8,128)(2,1)}), bf16[32,24,128]{2,1,0:T(8,128)(2,1)S(1)}, u32[]{:S(2)}, u32[]{:S(2)}) %all-to-all-start.2) | async-done | bytes 196640 | tf_op jit(solution)/shard_map/all_to_all | solution.py:487
  79.8 0.6 shard_map.121
  80.4 3.0 %collective-permute-start.7 = (f32[24,128]{1,0:T(8,128)S(1)}, f32[24,128]{1,0:T(8,128)S(1)}, u32[]{:S(2)}, u32[]{:S(2)}) collective-permute-start(f32[24,128]{1,0:T(8,128)S(1)} %get-tuple-element.33), channel_id=1, source_target_pairs={{0,2},{2,0},{4,6},{6,4},{8,10},{10,8},{12,14},{14,12},{16,18},{18,... | collective-permute-start | bytes 36872 | tf_op jit(solution)/shard_map/ppermute | solution.py:477
  83.4 2.9 %collective-permute-start.9 = (bf16[64,128]{1,0:T(8,128)(2,1)S(1)}, bf16[64,128]{1,0:T(8,128)(2,1)S(1)}, u32[]{:S(2)}, u32[]{:S(2)}) collective-permute-start(bf16[64,128]{1,0:T(8,128)(2,1)S(1)} %shard_map.120.after), channel_id=1, source_target_pairs={{0,128},{128,0},{1,129},{129,1},{2,130},{130,2},{3,131},{131,3},{4... | collective-permute-start | bytes 49160 | tf_op jit(solution)/shard_map/ppermute | solution.py:605
  86.3 0.0 collective-permute-done.7
  86.3 0.4 collective-permute-start.8
  86.7 0.8 collective-permute-done.9.crossed
  87.5 1.4 %collective-permute-done.8.other = f32[24,128]{1,0:T(8,128)S(1)} collective-permute-done((f32[24,128]{1,0:T(8,128)S(1)}, f32[24,128]{1,0:T(8,128)S(1)}, u32[]{:S(2)}, u32[]{:S(2)}) %collective-permute-start.8) | collective-permute-done | bytes 12320 | tf_op jit(solution)/shard_map/ppermute | solution.py:481
  88.9 0.6 shard_map.122
  89.5 13.9 %all_to_all.20 = bf16[32,24,128]{2,1,0:T(8,128)(2,1)S(1)} all-to-all(bf16[32,24,128]{2,1,0:T(8,128)(2,1)S(1)} %get-tuple-element.35), channel_id=1, replica_groups={{0,4,8,12,16,20,24,28,32,36,40,44,48,52,56,60,64,68,72,76,80,84,88,92,9..., dimensions={0} | all-to-all | bytes 393216 | tf_op jit(solution)/shard_map/all_to_all | solution.py:487
  103.5 3.2 %collective-permute-start.10 = (f32[24,128]{1,0:T(8,128)S(1)}, f32[24,128]{1,0:T(8,128)S(1)}, u32[]{:S(2)}, u32[]{:S(2)}) collective-permute-start(f32[24,128]{1,0:T(8,128)S(1)} %convert_reduce_fusion.total), channel_id=1, source_target_pairs={{0,2},{2,0},{4,6},{6,4},{8,10},{10,8},{12,14},{14,12},{16,18},{18,... | collective-permute-start | bytes 36872 | tf_op jit(solution)/shard_map/ppermute | solution.py:477
  106.7 0.8 collective-permute-done.10.near
  107.5 0.6 shard_map.123
  (7 shorter events, 0.1 us)
Async XLA Ops:
  0.6 16.7 %copy-start = (bf16[1,64,3072]{2,1,0:T(8,128)(2,1)S(1)}, bf16[1,64,3072]{2,1,0:T(8,128)(2,1)}, u32[]{:S(2)}) copy-start(bf16[1,64,3072]{2,1,0:T(8,128)(2,1)} %param.16) | copy-start | bytes 1179652
  0.6 4.6 %collective-permute-start = (bf16[48,2304]{1,0:T(8,128)(2,1)}, bf16[48,2304]{1,0:T(8,128)(2,1)S(1)}, u32[]{:S(2)}, u32[]{:S(2)}) collective-permute-start(bf16[48,2304]{1,0:T(8,128)(2,1)} %bitcast.19), channel_id=1, source_target_pairs={{0,2},{2,0},{4,6},{6,4},{8,10},{10,8},{12,14},{14,12},{16,18},{18,... | collective-permute-start | bytes 663560 | tf_op jit(solution)/shard_map/ppermute | solution.py:477
  4.0 0.9 copy-start.1
  4.9 11.9 %copy-start.5 = (bf16[1,1,128,64]{2,3,1,0:T(8,128)(2,1)S(1)}, bf16[1,1,128,64]{2,3,1,0:T(8,128)(2,1)}, u32[]{:S(2)}) copy-start(bf16[1,1,128,64]{2,3,1,0:T(8,128)(2,1)} %param.10) | copy-start | bytes 49156
  4.9 12.0 %copy-start.6 = (bf16[1,1,128,64]{2,3,1,0:T(8,128)(2,1)S(1)}, bf16[1,1,128,64]{2,3,1,0:T(8,128)(2,1)}, u32[]{:S(2)}) copy-start(bf16[1,1,128,64]{2,3,1,0:T(8,128)(2,1)} %param.11) | copy-start | bytes 49156
  4.9 12.1 %copy-start.7 = (bf16[1,1,128,64]{2,3,1,0:T(8,128)(2,1)S(1)}, bf16[1,1,128,64]{2,3,1,0:T(8,128)(2,1)}, u32[]{:S(2)}) copy-start(bf16[1,1,128,64]{2,3,1,0:T(8,128)(2,1)} %param.13) | copy-start | bytes 49156
  4.9 12.3 %copy-start.8 = (bf16[1,1,128,64]{2,3,1,0:T(8,128)(2,1)S(1)}, bf16[1,1,128,64]{2,3,1,0:T(8,128)(2,1)}, u32[]{:S(2)}) copy-start(bf16[1,1,128,64]{2,3,1,0:T(8,128)(2,1)} %param.15) | copy-start | bytes 49156
  4.9 12.4 %copy-start.2 = (f32[1,2,2,3072]{3,2,1,0:T(2,128)S(1)}, f32[1,2,2,3072]{3,2,1,0:T(2,128)}, u32[]{:S(2)}) copy-start(f32[1,2,2,3072]{3,2,1,0:T(2,128)} %param.19) | copy-start | bytes 147460
  6.2 20.1 %all-to-all-start = ((bf16[32,40,128]{2,1,0:T(8,128)(2,1)}), bf16[32,40,128]{2,1,0:T(8,128)(2,1)S(1)}, u32[]{:S(2)}, u32[]{:S(2)}) async-start(bf16[32,40,128]{2,1,0:T(8,128)(2,1)} %shard_map.114.after), calls=%async_computation | async-start | bytes 655360 | tf_op jit(solution)/shard_map/all_to_all | solution.py:487
  18.3 1.7 %collective-permute-start.1 = (bf16[128,384]{1,0:T(8,128)(2,1)S(1)}, bf16[128,384]{1,0:T(8,128)(2,1)S(1)}, u32[]{:S(2)}, u32[]{:S(2)}) collective-permute-start(bf16[128,384]{1,0:T(8,128)(2,1)S(1)} %get-tuple-element.20.own), channel_id=1, source_target_pairs={{0,2},{2,0},{4,6},{6,4},{8,10},{10,8},{12,14},{14,12},{16,18},{18,... | collective-permute-start | bytes 294920 | tf_op jit(solution)/shard_map/ppermute | solution.py:477
  20.0 17.3 %copy-start.4 = (bf16[1,768,64]{1,2,0:T(8,128)(2,1)S(1)}, bf16[1,768,64]{1,2,0:T(8,128)(2,1)}, u32[]{:S(2)}) copy-start(bf16[1,768,64]{1,2,0:T(8,128)(2,1)} %param.18) | copy-start | bytes 294916
  20.0 6.2 %collective-permute-start.2 = (bf16[2,128,384]{2,1,0:T(8,128)(2,1)S(1)}, bf16[2,128,384]{2,1,0:T(8,128)(2,1)S(1)}, u32[]{:S(2)}, u32[]{:S(2)}) collective-permute-start(bf16[2,128,384]{2,1,0:T(8,128)(2,1)S(1)} %pad_maximum_fusion.here), channel_id=1, source_target_pairs={{0,1},{1,0},{2,3},{3,2},{4,5},{5,4},{6,7},{7,6},{8,9},{9,8},{10,11... | collective-permute-start | bytes 589832 | tf_op jit(solution)/shard_map/ppermute | solution.py:481
  27.8 21.7 %all-to-all-start.1 = ((bf16[32,56,128]{2,1,0:T(8,128)(2,1)}), bf16[32,56,128]{2,1,0:T(8,128)(2,1)S(1)}, u32[]{:S(2)}, u32[]{:S(2)}) async-start(bf16[32,56,128]{2,1,0:T(8,128)(2,1)} %get-tuple-element.21), calls=%async_computation.1 | async-start | bytes 917504 | tf_op jit(solution)/shard_map/all_to_all | solution.py:487
  51.9 5.5 %collective-permute-start.3 = (f32[256,128]{1,0:T(8,128)S(1)}, f32[256,128]{1,0:T(8,128)S(1)}, u32[]{:S(2)}, u32[]{:S(2)}) collective-permute-start(f32[256,128]{1,0:T(8,128)S(1)} %get-tuple-element.26), channel_id=1, source_target_pairs={{0,2},{2,0},{4,6},{6,4},{8,10},{10,8},{12,14},{14,12},{16,18},{18,... | collective-permute-start | bytes 393224 | tf_op jit(solution)/shard_map/ppermute | solution.py:477
  57.4 4.8 %collective-permute-start.4 = (f32[256,128]{1,0:T(8,128)S(1)}, f32[256,128]{1,0:T(8,128)S(1)}, u32[]{:S(2)}, u32[]{:S(2)}) collective-permute-start(f32[256,128]{1,0:T(8,128)S(1)} %add.9.after.vel_here.b_here), channel_id=1, source_target_pairs={{0,1},{1,0},{2,3},{3,2},{4,5},{5,4},{6,7},{7,6},{8,9},{9,8},{10,11... | collective-permute-start | bytes 393224 | tf_op jit(solution)/shard_map/ppermute | solution.py:481
  60.7 4.5 %copy-start.3 = (f32[256,128]{1,0:T(8,128)}, f32[256,128]{1,0:T(8,128)S(1)}, u32[]{:S(2)}) copy-start(f32[256,128]{1,0:T(8,128)S(1)} %get-tuple-element.31) | copy-start | bytes 393220
  65.2 14.5 %all-to-all-start.2 = ((bf16[32,24,128]{2,1,0:T(8,128)(2,1)}), bf16[32,24,128]{2,1,0:T(8,128)(2,1)S(1)}, u32[]{:S(2)}, u32[]{:S(2)}) async-start(bf16[32,24,128]{2,1,0:T(8,128)(2,1)} %shard_map.119), calls=%async_computation.2 | async-start | bytes 393216 | tf_op jit(solution)/shard_map/all_to_all | solution.py:487
  70.4 2.8 %collective-permute-start.5 = (f32[256,128]{1,0:T(8,128)}, f32[256,128]{1,0:T(8,128)S(1)}, u32[]{:S(2)}, u32[]{:S(2)}) collective-permute-start(f32[256,128]{1,0:T(8,128)} %copy-done.3), channel_id=1, source_target_pairs={{0,2},{2,0},{4,6},{6,4},{8,10},{10,8},{12,14},{14,12},{16,18},{18,... | collective-permute-start | bytes 393224 | tf_op jit(solution)/shard_map/ppermute | solution.py:477
  73.2 3.5 %collective-permute-start.6 = (f32[128,64]{1,0:T(8,128)S(1)}, f32[128,64]{1,0:T(8,128)S(1)}, u32[]{:S(2)}, u32[]{:S(2)}) collective-permute-start(f32[128,64]{1,0:T(8,128)S(1)} %slice.14), channel_id=1, source_target_pairs={{0,1},{1,0},{2,3},{3,2},{4,5},{5,4},{6,7},{7,6},{8,9},{9,8},{10,11... | collective-permute-start | bytes 98312 | tf_op jit(solution)/shard_map/ppermute | solution.py:481
  80.4 6.0 %collective-permute-start.7 = (f32[24,128]{1,0:T(8,128)S(1)}, f32[24,128]{1,0:T(8,128)S(1)}, u32[]{:S(2)}, u32[]{:S(2)}) collective-permute-start(f32[24,128]{1,0:T(8,128)S(1)} %get-tuple-element.33), channel_id=1, source_target_pairs={{0,2},{2,0},{4,6},{6,4},{8,10},{10,8},{12,14},{14,12},{16,18},{18,... | collective-permute-start | bytes 36872 | tf_op jit(solution)/shard_map/ppermute | solution.py:477
  83.4 4.1 %collective-permute-start.9 = (bf16[64,128]{1,0:T(8,128)(2,1)S(1)}, bf16[64,128]{1,0:T(8,128)(2,1)S(1)}, u32[]{:S(2)}, u32[]{:S(2)}) collective-permute-start(bf16[64,128]{1,0:T(8,128)(2,1)S(1)} %shard_map.120.after), channel_id=1, source_target_pairs={{0,128},{128,0},{1,129},{129,1},{2,130},{130,2},{3,131},{131,3},{4... | collective-permute-start | bytes 49160 | tf_op jit(solution)/shard_map/ppermute | solution.py:605
  86.3 2.5 %collective-permute-start.8 = (f32[24,128]{1,0:T(8,128)S(1)}, f32[24,128]{1,0:T(8,128)S(1)}, u32[]{:S(2)}, u32[]{:S(2)}) collective-permute-start(f32[24,128]{1,0:T(8,128)S(1)} %add.11.total), channel_id=1, source_target_pairs={{0,1},{1,0},{2,3},{3,2},{4,5},{5,4},{6,7},{7,6},{8,9},{9,8},{10,11... | collective-permute-start | bytes 36872 | tf_op jit(solution)/shard_map/ppermute | solution.py:481
  103.5 4.0 %collective-permute-start.10 = (f32[24,128]{1,0:T(8,128)S(1)}, f32[24,128]{1,0:T(8,128)S(1)}, u32[]{:S(2)}, u32[]{:S(2)}) collective-permute-start(f32[24,128]{1,0:T(8,128)S(1)} %convert_reduce_fusion.total), channel_id=1, source_target_pairs={{0,2},{2,0},{4,6},{6,4},{8,10},{10,8},{12,14},{14,12},{16,18},{18,... | collective-permute-start | bytes 36872 | tf_op jit(solution)/shard_map/ppermute | solution.py:477

commit v6 on v5

--- a/solution.py
+++ b/solution.py
@@ -121,15 +121,19 @@
     second = on_second_core()
     columns, padded = own.shape
     turned[0:columns, :] = own[...] + turn_rows(half_columns(received, second), padded, jnp.logical_not(second))
-    turned[columns:, :] = jnp.zeros((turned.shape[0] - columns, padded), F32)
     block = columns // chips
     height = out.shape[1]
-    row = row_index((height, padded))
+    spare = padded // 4
+    upper_lanes = lane_index((16, padded)) >= padded - spare
     group = 8
     copies = []
     for chip in range(chips):
         piece = turned[chip * block : chip * block + height, :]
-        blocks[chip] = jnp.where(row < block, piece, 0.0).astype(BF16)
+        last = turned[chip * block + height : (chip + 1) * block, :]
+        lines = [pltpu.roll(last, padded - spare * (part + 1), 1) for part in range(3)]
+        lines.append(jnp.zeros_like(last))
+        top = jnp.where(upper_lanes, jnp.concatenate(lines, axis=0), piece[0:16])
+        blocks[chip] = jnp.concatenate([top, piece[16:]], axis=0).astype(BF16)
         if chip % group == group - 1:
             span = pl.ds(chip + 1 - group, group)
             copies.append(pltpu.make_async_copy(blocks.at[span], out.at[span], copied.at[len(copies)]))
@@ -138,23 +142,28 @@
         copy.wait()
 
 
-def product_kernel(block, taken, stack, after, out, halves_out, columns_out):
+def product_kernel(block, taken, stack, out, columns_out):
     chips, height, padded = taken.shape
     half = block // 2
-    stride = halves_out.shape[0] // 2
     width = stack.shape[1]
     depth = width // chips
-    row_half = row_index((stride, 1))
-    group = 1 if depth % 128 == 0 else 128 // (depth & -depth)
+    group = 128 // (depth & -depth)
+    spare = padded - depth
+    lane = lane_index((4, padded))
     for start in range(0, chips, group):
-        pieces = [taken[chip].astype(F32)[:, 0:depth] for chip in range(start, start + group)]
-        joined = jnp.concatenate(pieces, axis=1) if group > 1 else pieces[0]
+        mains, lasts = [], []
+        for chip in range(start, start + group):
+            piece = taken[chip].astype(F32)
+            mains.append(piece[:, 0:depth])
+            top, next_top = piece[0:8], piece[8:16]
+            low = pltpu.roll(top, spare, 1)[0:4]
+            middle = pltpu.roll(top, 2 * spare, 1)[4:8]
+            high = pltpu.roll(next_top, 3 * spare, 1)[0:4]
+            lasts.append(jnp.where(lane < spare, low, jnp.where(lane < 2 * spare, middle, high))[:, 0:depth])
+        last = jnp.concatenate(lasts, axis=1)
+        joined = jnp.concatenate([jnp.concatenate(mains, axis=1), last, jnp.zeros_like(last)], axis=0)
         span = slice(start * depth, (start + group) * depth)
         columns_out[:, span] = joined.astype(BF16)
-        longer = jnp.concatenate([joined, jnp.zeros((stride, joined.shape[1]), F32)], axis=0)
-        low = jnp.where(row_half < half, longer[0:stride], 0.0)
-        high = jnp.where(row_half < half, longer[half : half + stride], 0.0)
-        halves_out[:, span] = jnp.concatenate([low, high], axis=0).astype(BF16)
     weight = columns_out[...]
     products = dot(weight, stack[0:256, :], NT)
     first, second = products[:, 0:128], products[:, 128:256]
@@ -401,13 +410,10 @@
     height = total.shape[0]
     row = row_index((height, 128))
     ends = total[half : half + 1] + total[half + 1 : half + 2]
-    turned = jnp.where(row < half, total, 0.0).T
-    lane = lane_index((1, 128))
-    ends_low = jnp.where(lane < half, ends, 0.0)[:, 0:height]
-    ends_high = jnp.where(lane < half, pltpu.roll(ends, 128 - half, 1), 0.0)[:, 0:height]
-    lower = jnp.concatenate([turned[0:CHANNELS], ends_low, jnp.zeros((7, height), F32)], axis=0)
-    upper = jnp.concatenate([turned[CHANNELS:], ends_high, jnp.zeros((7, height), F32)], axis=0)
-    joined = jnp.concatenate([lower, upper], axis=1)
+    lines = [jnp.where(row < half, total, 0.0), jnp.zeros((128 - height, 128), F32)]
+    turned = jnp.concatenate(lines, axis=0).T
+    products = turned[0:CHANNELS] + pltpu.roll(turned[CHANNELS:], half, 1)
+    joined = jnp.concatenate([products, ends, jnp.zeros((7, 128), F32)], axis=0)[:, 0 : weight.shape[0]]
     high = joined.astype(BF16)
     low = (joined - high.astype(F32)).astype(BF16)
     middle = embed.shape[1] // 2
@@ -434,14 +440,14 @@
     out[...] = jnp.where(on_critic(), own_b - own_a, sample).T.astype(BF16)
 
 
-def spread_kernel(total, other, crossed, out, crossed_out):
+def spread_kernel(total, other, out):
     line = (total[...] + other[...]).astype(BF16)
     for chip in range(out.shape[0]):
         out[chip] = line
+
+
+def join_kernel(total, near, crossed, out, crossed_out):
     crossed_out[...] = crossed[...]
-
-
-def join_kernel(total, near, out):
     second = on_second_core()
     count = total.shape[0] // 2
     left = jnp.where(second, near[...], total[...])
@@ -507,7 +513,7 @@
     width = embed.shape[1]
     columns = weight.shape[1] // 2
     block = columns // chips
-    height = round_up(block, 8)
+    height = block - 4
     packed = round_up(block + block // 2 + 2, 8)
     folded = round_up(block // 2 + 2, 8)
     padded = round_up(2 * weight.shape[0], 128)
@@ -524,7 +530,7 @@
         struct((chips, height, padded), BF16),
         (own_turned, received),
         scratch=[
-            pltpu.VMEM((columns + height - block, padded), F32),
+            pltpu.VMEM((columns, padded), F32),
             pltpu.VMEM((chips, height, padded), BF16),
             pltpu.SemaphoreType.DMA((chips // 8,)),
         ],
@@ -553,10 +559,8 @@
 
     matrices, own_columns = call(
         functools.partial(product_kernel, block),
-        (struct((chips, packed, 128), BF16), struct((2 * folded, width), BF16)),
+        (struct((chips, packed, 128), BF16), struct((height + 8, width), BF16)),
         (taken, stack),
-        scratch=[pltpu.VMEM((height, width), BF16)],
-        after=(there,),
     )
     whole, offsets, kept, keys_turned, probs, vel_b, vel_crossing = call(
         functools.partial(second_pass_kernel, block),
@@ -613,13 +617,13 @@
         after=(payload,),
     )
     total = kept_half + other_core(sent_half)
-    spread, crossed = call(
-        spread_kernel,
-        (struct((chips, lines, 128), BF16), struct(crossed.shape, BF16)),
-        (total, other_half(total), crossed),
-    )
+    spread = call(spread_kernel, struct((chips, lines, 128), BF16), (total, other_half(total)))
     total = jnp.sum(between_chips(spread).astype(F32), axis=0)
-    mod_grads = call(join_kernel, struct((2, width), F32), (total, other_core(total)))
+    mod_grads, crossed = call(
+        join_kernel,
+        (struct((2, width), F32), struct(crossed.shape, BF16)),
+        (total, other_core(total), crossed),
+    )
     return (crossed.T[None, None], mod_grads[None])
 
 

time: 109 us -> 103 us (0.945)
  blocking collectives: 13.9 us -> 0 us
  waiting for transfers between devices: 30 us -> 34.5 us
  starting transfers between devices: 47.8 us -> 51.3 us
    all_to_all x1 -> x0, blocking collectives: 13.9 us -> none  [between_chips(): lax.all_to_all(value, 'fsdp', 0, 0, tiled=True, axis_index_groups=groups)]
    all_to_all x3 -> x4, waiting for transfers between devices: 15.2 us -> 20 us  [between_chips(): lax.all_to_all(value, 'fsdp', 0, 0, tiled=True, axis_index_groups=groups)]
    all_to_all x3 -> x4, starting transfers between devices: 23.9 us -> 25.7 us  [between_chips(): lax.all_to_all(value, 'fsdp', 0, 0, tiled=True, axis_index_groups=groups)]
  transfers between devices with their start and end apart: 14 -> 15, of which waited for: 12 -> 14; matrix products, arithmetic and copies ran while one was open for 0% -> 1% of each run, Pallas kernels for 3% -> 3%
where the time goes in v6:
time: 103 us
  starting transfers between devices  51.3 us (50%)
  waiting for transfers between devices  34.5 us (33%)
  Pallas kernels  13.1 us (13%)
  between operations  2.11 us (2%)
  local copies, waits for them, and re-layouts  1.42 us (1%)
    all_to_all x4, starting transfers between devices, between_chips(): lax.all_to_all(value, 'fsdp', 0, 0, tiled=True, axis_index_groups=groups)  25.7 us
    all_to_all x4, waiting for transfers between devices, between_chips(): lax.all_to_all(value, 'fsdp', 0, 0, tiled=True, axis_index_groups=groups)  20 us
    ppermute x6, starting transfers between devices, other_core(): lax.ppermute(value, 'fsdp', [(i, i ^ 1) for i in range(lax.axis_size('fsd...  17.1 us
    pallas_call x11, Pallas kernels, call(): pl.pallas_call(kernel, out_shape=out_shapes, in_specs=specs, out_specs=ja...  13.1 us
    ppermute x4, waiting for transfers between devices, other_half(): return lax.ppermute(value, 'seq', [(0, 1), (1, 0)])  9.74 us
    ppermute x4, starting transfers between devices, other_half(): return lax.ppermute(value, 'seq', [(0, 1), (1, 0)])  5.45 us
    ppermute x6, waiting for transfers between devices, other_core(): lax.ppermute(value, 'fsdp', [(i, i ^ 1) for i in range(lax.axis_size('fsd...  4.75 us
    ppermute x1, starting transfers between devices, per_device(): crossed = lax.ppermute(payload, 'role', [(0, 1), (1, 0)])  3 us
  transfers between devices with their start and end apart: 15, of which 14 were waited for; matrix products, arithmetic and copies ran while one was open for 1% of the time, Pallas kernels for 3%

profile of v6, /device:TPU:1, one launch (start us, length us, event | category | flops | bytes accessed | tf_op | source)
XLA Modules:
  0.0 102.5 jit_solution(6868424745195056104)
XLA Ops:
  0.6 0.0 copy-start
  0.6 3.3 %collective-permute-start = (bf16[48,2304]{1,0:T(8,128)(2,1)}, bf16[48,2304]{1,0:T(8,128)(2,1)S(1)}, u32[]{:S(2)}, u32[]{:S(2)}) collective-permute-start(bf16[48,2304]{1,0:T(8,128)(2,1)} %bitcast.19), channel_id=1, source_target_pairs={{0,2},{2,0},{4,6},{6,4},{8,10},{10,8},{12,14},{14,12},{16,18},{18,... | collective-permute-start | bytes 663560 | tf_op jit(solution)/shard_map/ppermute | solution.py:483
  4.0 0.0 copy-start.1
  4.0 0.9 copy-done.1
  4.9 0.0 copy-start.4
  4.9 0.0 copy-start.5
  4.9 0.0 copy-start.6
  4.9 0.0 copy-start.7
  4.9 0.0 copy-start.2
  4.9 0.2 shard_map.113.own
  5.1 0.2 collective-permute-done.received
  5.3 1.0 shard_map.114.after
  6.3 9.3 %all-to-all-start = ((bf16[32,32,128]{2,1,0:T(8,128)(2,1)}), bf16[32,32,128]{2,1,0:T(8,128)(2,1)S(1)}, u32[]{:S(2)}, u32[]{:S(2)}) async-start(bf16[32,32,128]{2,1,0:T(8,128)(2,1)} %shard_map.114.after), calls=%async_computation | async-start | bytes 524288 | tf_op jit(solution)/shard_map/all_to_all | solution.py:493
  16.9 0.0 copy-done.4
  16.9 0.1 copy.12
  17.0 0.0 copy-done.5
  17.0 0.1 copy.13
  17.1 0.0 copy-done.6
  17.1 0.1 copy.14
  17.3 0.0 copy-done.7
  17.3 0.1 copy.15
  17.4 0.0 copy-done
  17.4 0.0 copy-done.2
  17.4 1.0 shard_map.115
  18.4 6.8 %all-to-all-done.taken = bf16[32,32,128]{2,1,0:T(8,128)(2,1)S(1)} async-done(((bf16[32,32,128]{2,1,0:T(8,128)(2,1)}), bf16[32,32,128]{2,1,0:T(8,128)(2,1)S(1)}, u32[]{:S(2)}, u32[]{:S(2)}) %all-to-all-start) | async-done | bytes 262176 | tf_op jit(solution)/shard_map/all_to_all | solution.py:493
  25.3 0.0 copy-start.3
  25.3 1.6 %shard_map.116 = (bf16[32,56,128]{2,1,0:T(8,128)(2,1)}, bf16[40,3072]{1,0:T(8,128)(2,1)S(1)}) custom-call(bf16[32,32,128]{2,1,0:T(8,128)(2,1)S(1)} %all-to-all-done.taken, bf16[272,3072]{1,0:T(8,128)(2,1)S(1)} %get-tuple-element.19.stack), custom_call_target="tpu_custom_call" | custom-call | tf_op jit(solution)/shard_map/pallas_call | solution.py:467
  26.9 6.7 %all-to-all-start.1 = ((bf16[32,56,128]{2,1,0:T(8,128)(2,1)}), bf16[32,56,128]{2,1,0:T(8,128)(2,1)S(1)}, u32[]{:S(2)}, u32[]{:S(2)}) async-start(bf16[32,56,128]{2,1,0:T(8,128)(2,1)} %get-tuple-element.20), calls=%async_computation.1 | async-start | bytes 917504 | tf_op jit(solution)/shard_map/all_to_all | solution.py:493
  33.6 1.5 %collective-permute-start.1 = (bf16[128,384]{1,0:T(8,128)(2,1)S(1)}, bf16[128,384]{1,0:T(8,128)(2,1)S(1)}, u32[]{:S(2)}, u32[]{:S(2)}) collective-permute-start(bf16[128,384]{1,0:T(8,128)(2,1)S(1)} %get-tuple-element.21.own), channel_id=1, source_target_pairs={{0,2},{2,0},{4,6},{6,4},{8,10},{10,8},{12,14},{14,12},{16,18},{18,... | collective-permute-start | bytes 294920 | tf_op jit(solution)/shard_map/ppermute | solution.py:483
  35.1 0.9 collective-permute-done.1
  36.1 1.4 %collective-permute-start.2 = (bf16[2,128,384]{2,1,0:T(8,128)(2,1)S(1)}, bf16[2,128,384]{2,1,0:T(8,128)(2,1)S(1)}, u32[]{:S(2)}, u32[]{:S(2)}) collective-permute-start(bf16[2,128,384]{2,1,0:T(8,128)(2,1)S(1)} %pad_maximum_fusion.here), channel_id=1, source_target_pairs={{0,1},{1,0},{2,3},{3,2},{4,5},{5,4},{6,7},{7,6},{8,9},{9,8},{10,11... | collective-permute-start | bytes 589832 | tf_op jit(solution)/shard_map/ppermute | solution.py:487
  37.5 0.0 copy-done.3
  37.5 4.8 %collective-permute-done.2.there = bf16[2,128,384]{2,1,0:T(8,128)(2,1)S(1)} collective-permute-done((bf16[2,128,384]{2,1,0:T(8,128)(2,1)S(1)}, bf16[2,128,384]{2,1,0:T(8,128)(2,1)S(1)}, u32[]{:S(2)}, u32[]{:S(2)}) %collective-permute-start.2) | collective-permute-done | bytes 196640 | tf_op jit(solution)/shard_map/ppermute | solution.py:487
  42.3 3.5 %all-to-all-done.1.taken = bf16[32,56,128]{2,1,0:T(8,128)(2,1)S(1)} async-done(((bf16[32,56,128]{2,1,0:T(8,128)(2,1)}), bf16[32,56,128]{2,1,0:T(8,128)(2,1)S(1)}, u32[]{:S(2)}, u32[]{:S(2)}) %all-to-all-start.1) | async-done | bytes 458784 | tf_op jit(solution)/shard_map/all_to_all | solution.py:493
  45.8 2.4 %shard_map.117 = (bf16[1152,128]{1,0:T(8,128)(2,1)S(1)}, f32[8,1152]{1,0:T(8,128)S(1)}, bf16[2,256,1152]{2,1,0:T(8,128)(2,1)S(1)}, bf16[6,128,256]{2,1,0:T(8,128...) custom-call(bf16[32,56,128]{2,1,0:T(8,128)(2,1)S(1)} %all-to-all-done.1.taken, ...), custom_call_target="tpu_custom_call" | custom-call | tf_op jit(solution)/shard_map/pallas_call | solution.py:467
  48.3 4.5 %collective-permute-start.3 = (f32[256,128]{1,0:T(8,128)S(1)}, f32[256,128]{1,0:T(8,128)S(1)}, u32[]{:S(2)}, u32[]{:S(2)}) collective-permute-start(f32[256,128]{1,0:T(8,128)S(1)} %get-tuple-element.26), channel_id=1, source_target_pairs={{0,2},{2,0},{4,6},{6,4},{8,10},{10,8},{12,14},{14,12},{16,18},{18,... | collective-permute-start | bytes 393224 | tf_op jit(solution)/shard_map/ppermute | solution.py:483
  52.7 1.0 collective-permute-done.3
  53.7 1.4 %collective-permute-start.4 = (f32[256,128]{1,0:T(8,128)S(1)}, f32[256,128]{1,0:T(8,128)S(1)}, u32[]{:S(2)}, u32[]{:S(2)}) collective-permute-start(f32[256,128]{1,0:T(8,128)S(1)} %add.9.after.vel_here.b_here), channel_id=1, source_target_pairs={{0,1},{1,0},{2,3},{3,2},{4,5},{5,4},{6,7},{7,6},{8,9},{9,8},{10,11... | collective-permute-start | bytes 393224 | tf_op jit(solution)/shard_map/ppermute | solution.py:487
  55.1 1.9 %shard_map.118 = (f32[256,128]{1,0:T(8,128)S(1)}, f32[256,128]{1,0:T(8,128)S(1)}) custom-call(bf16[1152,128]{1,0:T(8,128)(2,1)S(1)} %get-tuple-element.27.matrices, f32[8,1152]{1,0:T(8,128)S(1)} %get-tuple-element.28.offsets, bf16[2,128,384]{2,1,0:T(8,128)(2,1)S(1)} %pad_maximum_fusion.here, bf16[2,128,384]{2,1,0:T(8,128)(2,1)S(1)} %collective-permute-done.2.there, ...), custom_call_target="tpu_custom_call" | custom-call | flops 4000000000 | tf_op jit(solution)/shard_map/pallas_call | solution.py:467
  57.0 1.6 %collective-permute-done.4.vel_there.b_there = f32[256,128]{1,0:T(8,128)S(1)} collective-permute-done((f32[256,128]{1,0:T(8,128)S(1)}, f32[256,128]{1,0:T(8,128)S(1)}, u32[]{:S(2)}, u32[]{:S(2)}) %collective-permute-start.4) | collective-permute-done | bytes 131104 | tf_op jit(solution)/shard_map/ppermute | solution.py:487
  58.6 3.1 %shard_map.119 = bf16[32,24,128]{2,1,0:T(8,128)(2,1)} custom-call(bf16[2,256,1152]{2,1,0:T(8,128)(2,1)S(1)} %get-tuple-element.22.kept, bf16[6,128,256]{2,1,0:T(8,128)(2,1)S(1)} %get-tuple-element.23.keys_turned, f32[6,256,256]{2,1,0:T(8,128)S(1)} %get-tuple-element.24.probs_turned, bf16[2,128,384]{2,1,0:T(8,128)(2,1)S(1)} %pad_maximum_fusion.here, ...), custom_call_target="tpu_custom_call" | custom-call | tf_op jit(solution)/shard_map/pallas_call | solution.py:467
  61.6 5.1 %all-to-all-start.2 = ((bf16[32,24,128]{2,1,0:T(8,128)(2,1)}), bf16[32,24,128]{2,1,0:T(8,128)(2,1)S(1)}, u32[]{:S(2)}, u32[]{:S(2)}) async-start(bf16[32,24,128]{2,1,0:T(8,128)(2,1)} %shard_map.119), calls=%async_computation.2 | async-start | bytes 393216 | tf_op jit(solution)/shard_map/all_to_all | solution.py:493
  66.8 1.6 %collective-permute-start.5 = (f32[256,128]{1,0:T(8,128)S(1)}, f32[256,128]{1,0:T(8,128)S(1)}, u32[]{:S(2)}, u32[]{:S(2)}) collective-permute-start(f32[256,128]{1,0:T(8,128)S(1)} %get-tuple-element.31), channel_id=1, source_target_pairs={{0,2},{2,0},{4,6},{6,4},{8,10},{10,8},{12,14},{14,12},{16,18},{18,... | collective-permute-start | bytes 393224 | tf_op jit(solution)/shard_map/ppermute | solution.py:483
  68.3 1.0 collective-permute-done.5
  69.3 1.4 %collective-permute-start.6 = (f32[128,64]{1,0:T(8,128)S(1)}, f32[128,64]{1,0:T(8,128)S(1)}, u32[]{:S(2)}, u32[]{:S(2)}) collective-permute-start(f32[128,64]{1,0:T(8,128)S(1)} %slice.14), channel_id=1, source_target_pairs={{0,1},{1,0},{2,3},{3,2},{4,5},{5,4},{6,7},{7,6},{8,9},{9,8},{10,11... | collective-permute-start | bytes 98312 | tf_op jit(solution)/shard_map/ppermute | solution.py:487
  70.7 2.1 %collective-permute-done.6.a_there = f32[128,64]{1,0:T(8,128)S(1)} collective-permute-done((f32[128,64]{1,0:T(8,128)S(1)}, f32[128,64]{1,0:T(8,128)S(1)}, u32[]{:S(2)}, u32[]{:S(2)}) %collective-permute-start.6) | collective-permute-done | bytes 32800 | tf_op jit(solution)/shard_map/ppermute | solution.py:487
  72.8 0.1 shard_map.120.after
  72.9 3.2 %all-to-all-done.2.taken = bf16[32,24,128]{2,1,0:T(8,128)(2,1)S(1)} async-done(((bf16[32,24,128]{2,1,0:T(8,128)(2,1)}), bf16[32,24,128]{2,1,0:T(8,128)(2,1)S(1)}, u32[]{:S(2)}, u32[]{:S(2)}) %all-to-all-start.2) | async-done | bytes 196640 | tf_op jit(solution)/shard_map/all_to_all | solution.py:493
  76.2 0.6 shard_map.121
  76.7 3.0 %collective-permute-start.7 = (f32[24,128]{1,0:T(8,128)S(1)}, f32[24,128]{1,0:T(8,128)S(1)}, u32[]{:S(2)}, u32[]{:S(2)}) collective-permute-start(f32[24,128]{1,0:T(8,128)S(1)} %get-tuple-element.33), channel_id=1, source_target_pairs={{0,2},{2,0},{4,6},{6,4},{8,10},{10,8},{12,14},{14,12},{16,18},{18,... | collective-permute-start | bytes 36872 | tf_op jit(solution)/shard_map/ppermute | solution.py:483
  79.8 0.8 collective-permute-done.7
  80.6 1.3 %collective-permute-start.8 = (f32[24,128]{1,0:T(8,128)S(1)}, f32[24,128]{1,0:T(8,128)S(1)}, u32[]{:S(2)}, u32[]{:S(2)}) collective-permute-start(f32[24,128]{1,0:T(8,128)S(1)} %add.11.total), channel_id=1, source_target_pairs={{0,1},{1,0},{2,3},{3,2},{4,5},{5,4},{6,7},{7,6},{8,9},{9,8},{10,11... | collective-permute-start | bytes 36872 | tf_op jit(solution)/shard_map/ppermute | solution.py:487
  81.9 1.2 %collective-permute-done.8.other = f32[24,128]{1,0:T(8,128)S(1)} collective-permute-done((f32[24,128]{1,0:T(8,128)S(1)}, f32[24,128]{1,0:T(8,128)S(1)}, u32[]{:S(2)}, u32[]{:S(2)}) %collective-permute-start.8) | collective-permute-done | bytes 12320 | tf_op jit(solution)/shard_map/ppermute | solution.py:487
  83.2 0.7 shard_map.122
  83.9 4.6 %all-to-all-start.3 = ((bf16[32,24,128]{2,1,0:T(8,128)(2,1)}), bf16[32,24,128]{2,1,0:T(8,128)(2,1)S(1)}, u32[]{:S(2)}, u32[]{:S(2)}) async-start(bf16[32,24,128]{2,1,0:T(8,128)(2,1)} %shard_map.122), calls=%async_computation.3 | async-start | bytes 393216 | tf_op jit(solution)/shard_map/all_to_all | solution.py:493
  88.4 3.0 %collective-permute-start.10 = (bf16[64,128]{1,0:T(8,128)(2,1)S(1)}, bf16[64,128]{1,0:T(8,128)(2,1)S(1)}, u32[]{:S(2)}, u32[]{:S(2)}) collective-permute-start(bf16[64,128]{1,0:T(8,128)(2,1)S(1)} %shard_map.120.after), channel_id=1, source_target_pairs={{0,128},{128,0},{1,129},{129,1},{2,130},{130,2},{3,131},{131,3},{4... | collective-permute-start | bytes 49160 | tf_op jit(solution)/shard_map/ppermute | solution.py:609
  91.4 6.4 %all-to-all-done.3 = bf16[32,24,128]{2,1,0:T(8,128)(2,1)S(1)} async-done(((bf16[32,24,128]{2,1,0:T(8,128)(2,1)}), bf16[32,24,128]{2,1,0:T(8,128)(2,1)S(1)}, u32[]{:S(2)}, u32[]{:S(2)}) %all-to-all-start.3) | async-done | bytes 196640 | tf_op jit(solution)/shard_map/all_to_all | solution.py:493
  97.9 3.2 %collective-permute-start.9 = (f32[24,128]{1,0:T(8,128)S(1)}, f32[24,128]{1,0:T(8,128)S(1)}, u32[]{:S(2)}, u32[]{:S(2)}) collective-permute-start(f32[24,128]{1,0:T(8,128)S(1)} %convert_reduce_fusion.total), channel_id=1, source_target_pairs={{0,2},{2,0},{4,6},{6,4},{8,10},{10,8},{12,14},{14,12},{16,18},{18,... | collective-permute-start | bytes 36872 | tf_op jit(solution)/shard_map/ppermute | solution.py:483
  101.1 0.0 collective-permute-done.10.crossed
  101.1 0.8 collective-permute-done.9.near
  101.9 0.6 shard_map.123
  (7 shorter events, 0.1 us)
Async XLA Ops:
  0.6 16.8 %copy-start = (bf16[1,64,3072]{2,1,0:T(8,128)(2,1)S(1)}, bf16[1,64,3072]{2,1,0:T(8,128)(2,1)}, u32[]{:S(2)}) copy-start(bf16[1,64,3072]{2,1,0:T(8,128)(2,1)} %param.16) | copy-start | bytes 1179652
  0.6 4.6 %collective-permute-start = (bf16[48,2304]{1,0:T(8,128)(2,1)}, bf16[48,2304]{1,0:T(8,128)(2,1)S(1)}, u32[]{:S(2)}, u32[]{:S(2)}) collective-permute-start(bf16[48,2304]{1,0:T(8,128)(2,1)} %bitcast.19), channel_id=1, source_target_pairs={{0,2},{2,0},{4,6},{6,4},{8,10},{10,8},{12,14},{14,12},{16,18},{18,... | collective-permute-start | bytes 663560 | tf_op jit(solution)/shard_map/ppermute | solution.py:483
  4.0 0.9 copy-start.1
  4.9 12.0 %copy-start.4 = (bf16[1,1,128,64]{2,3,1,0:T(8,128)(2,1)S(1)}, bf16[1,1,128,64]{2,3,1,0:T(8,128)(2,1)}, u32[]{:S(2)}) copy-start(bf16[1,1,128,64]{2,3,1,0:T(8,128)(2,1)} %param.10) | copy-start | bytes 49156
  4.9 12.1 %copy-start.5 = (bf16[1,1,128,64]{2,3,1,0:T(8,128)(2,1)S(1)}, bf16[1,1,128,64]{2,3,1,0:T(8,128)(2,1)}, u32[]{:S(2)}) copy-start(bf16[1,1,128,64]{2,3,1,0:T(8,128)(2,1)} %param.11) | copy-start | bytes 49156
  4.9 12.2 %copy-start.6 = (bf16[1,1,128,64]{2,3,1,0:T(8,128)(2,1)S(1)}, bf16[1,1,128,64]{2,3,1,0:T(8,128)(2,1)}, u32[]{:S(2)}) copy-start(bf16[1,1,128,64]{2,3,1,0:T(8,128)(2,1)} %param.13) | copy-start | bytes 49156
  4.9 12.4 %copy-start.7 = (bf16[1,1,128,64]{2,3,1,0:T(8,128)(2,1)S(1)}, bf16[1,1,128,64]{2,3,1,0:T(8,128)(2,1)}, u32[]{:S(2)}) copy-start(bf16[1,1,128,64]{2,3,1,0:T(8,128)(2,1)} %param.15) | copy-start | bytes 49156
  4.9 12.5 %copy-start.2 = (f32[1,2,2,3072]{3,2,1,0:T(2,128)S(1)}, f32[1,2,2,3072]{3,2,1,0:T(2,128)}, u32[]{:S(2)}) copy-start(f32[1,2,2,3072]{3,2,1,0:T(2,128)} %param.19) | copy-start | bytes 147460
  6.3 19.0 %all-to-all-start = ((bf16[32,32,128]{2,1,0:T(8,128)(2,1)}), bf16[32,32,128]{2,1,0:T(8,128)(2,1)S(1)}, u32[]{:S(2)}, u32[]{:S(2)}) async-start(bf16[32,32,128]{2,1,0:T(8,128)(2,1)} %shard_map.114.after), calls=%async_computation | async-start | bytes 524288 | tf_op jit(solution)/shard_map/all_to_all | solution.py:493
  25.3 12.2 %copy-start.3 = (bf16[1,768,64]{1,2,0:T(8,128)(2,1)S(1)}, bf16[1,768,64]{1,2,0:T(8,128)(2,1)}, u32[]{:S(2)}) copy-start(bf16[1,768,64]{1,2,0:T(8,128)(2,1)} %param.18) | copy-start | bytes 294916
  26.9 19.0 %all-to-all-start.1 = ((bf16[32,56,128]{2,1,0:T(8,128)(2,1)}), bf16[32,56,128]{2,1,0:T(8,128)(2,1)S(1)}, u32[]{:S(2)}, u32[]{:S(2)}) async-start(bf16[32,56,128]{2,1,0:T(8,128)(2,1)} %get-tuple-element.20), calls=%async_computation.1 | async-start | bytes 917504 | tf_op jit(solution)/shard_map/all_to_all | solution.py:493
  33.6 2.4 %collective-permute-start.1 = (bf16[128,384]{1,0:T(8,128)(2,1)S(1)}, bf16[128,384]{1,0:T(8,128)(2,1)S(1)}, u32[]{:S(2)}, u32[]{:S(2)}) collective-permute-start(bf16[128,384]{1,0:T(8,128)(2,1)S(1)} %get-tuple-element.21.own), channel_id=1, source_target_pairs={{0,2},{2,0},{4,6},{6,4},{8,10},{10,8},{12,14},{14,12},{16,18},{18,... | collective-permute-start | bytes 294920 | tf_op jit(solution)/shard_map/ppermute | solution.py:483
  36.1 6.2 %collective-permute-start.2 = (bf16[2,128,384]{2,1,0:T(8,128)(2,1)S(1)}, bf16[2,128,384]{2,1,0:T(8,128)(2,1)S(1)}, u32[]{:S(2)}, u32[]{:S(2)}) collective-permute-start(bf16[2,128,384]{2,1,0:T(8,128)(2,1)S(1)} %pad_maximum_fusion.here), channel_id=1, source_target_pairs={{0,1},{1,0},{2,3},{3,2},{4,5},{5,4},{6,7},{7,6},{8,9},{9,8},{10,11... | collective-permute-start | bytes 589832 | tf_op jit(solution)/shard_map/ppermute | solution.py:487
  48.3 5.5 %collective-permute-start.3 = (f32[256,128]{1,0:T(8,128)S(1)}, f32[256,128]{1,0:T(8,128)S(1)}, u32[]{:S(2)}, u32[]{:S(2)}) collective-permute-start(f32[256,128]{1,0:T(8,128)S(1)} %get-tuple-element.26), channel_id=1, source_target_pairs={{0,2},{2,0},{4,6},{6,4},{8,10},{10,8},{12,14},{14,12},{16,18},{18,... | collective-permute-start | bytes 393224 | tf_op jit(solution)/shard_map/ppermute | solution.py:483
  53.7 4.8 %collective-permute-start.4 = (f32[256,128]{1,0:T(8,128)S(1)}, f32[256,128]{1,0:T(8,128)S(1)}, u32[]{:S(2)}, u32[]{:S(2)}) collective-permute-start(f32[256,128]{1,0:T(8,128)S(1)} %add.9.after.vel_here.b_here), channel_id=1, source_target_pairs={{0,1},{1,0},{2,3},{3,2},{4,5},{5,4},{6,7},{7,6},{8,9},{9,8},{10,11... | collective-permute-start | bytes 393224 | tf_op jit(solution)/shard_map/ppermute | solution.py:487
  61.6 14.5 %all-to-all-start.2 = ((bf16[32,24,128]{2,1,0:T(8,128)(2,1)}), bf16[32,24,128]{2,1,0:T(8,128)(2,1)S(1)}, u32[]{:S(2)}, u32[]{:S(2)}) async-start(bf16[32,24,128]{2,1,0:T(8,128)(2,1)} %shard_map.119), calls=%async_computation.2 | async-start | bytes 393216 | tf_op jit(solution)/shard_map/all_to_all | solution.py:493
  66.8 2.5 %collective-permute-start.5 = (f32[256,128]{1,0:T(8,128)S(1)}, f32[256,128]{1,0:T(8,128)S(1)}, u32[]{:S(2)}, u32[]{:S(2)}) collective-permute-start(f32[256,128]{1,0:T(8,128)S(1)} %get-tuple-element.31), channel_id=1, source_target_pairs={{0,2},{2,0},{4,6},{6,4},{8,10},{10,8},{12,14},{14,12},{16,18},{18,... | collective-permute-start | bytes 393224 | tf_op jit(solution)/shard_map/ppermute | solution.py:483
  69.3 3.5 %collective-permute-start.6 = (f32[128,64]{1,0:T(8,128)S(1)}, f32[128,64]{1,0:T(8,128)S(1)}, u32[]{:S(2)}, u32[]{:S(2)}) collective-permute-start(f32[128,64]{1,0:T(8,128)S(1)} %slice.14), channel_id=1, source_target_pairs={{0,1},{1,0},{2,3},{3,2},{4,5},{5,4},{6,7},{7,6},{8,9},{9,8},{10,11... | collective-permute-start | bytes 98312 | tf_op jit(solution)/shard_map/ppermute | solution.py:487
  76.7 3.9 %collective-permute-start.7 = (f32[24,128]{1,0:T(8,128)S(1)}, f32[24,128]{1,0:T(8,128)S(1)}, u32[]{:S(2)}, u32[]{:S(2)}) collective-permute-start(f32[24,128]{1,0:T(8,128)S(1)} %get-tuple-element.33), channel_id=1, source_target_pairs={{0,2},{2,0},{4,6},{6,4},{8,10},{10,8},{12,14},{14,12},{16,18},{18,... | collective-permute-start | bytes 36872 | tf_op jit(solution)/shard_map/ppermute | solution.py:483
  80.6 2.5 %collective-permute-start.8 = (f32[24,128]{1,0:T(8,128)S(1)}, f32[24,128]{1,0:T(8,128)S(1)}, u32[]{:S(2)}, u32[]{:S(2)}) collective-permute-start(f32[24,128]{1,0:T(8,128)S(1)} %add.11.total), channel_id=1, source_target_pairs={{0,1},{1,0},{2,3},{3,2},{4,5},{5,4},{6,7},{7,6},{8,9},{9,8},{10,11... | collective-permute-start | bytes 36872 | tf_op jit(solution)/shard_map/ppermute | solution.py:487
  83.9 14.0 %all-to-all-start.3 = ((bf16[32,24,128]{2,1,0:T(8,128)(2,1)}), bf16[32,24,128]{2,1,0:T(8,128)(2,1)S(1)}, u32[]{:S(2)}, u32[]{:S(2)}) async-start(bf16[32,24,128]{2,1,0:T(8,128)(2,1)} %shard_map.122), calls=%async_computation.3 | async-start | bytes 393216 | tf_op jit(solution)/shard_map/all_to_all | solution.py:493
  88.4 12.6 %collective-permute-start.10 = (bf16[64,128]{1,0:T(8,128)(2,1)S(1)}, bf16[64,128]{1,0:T(8,128)(2,1)S(1)}, u32[]{:S(2)}, u32[]{:S(2)}) collective-permute-start(bf16[64,128]{1,0:T(8,128)(2,1)S(1)} %shard_map.120.after), channel_id=1, source_target_pairs={{0,128},{128,0},{1,129},{129,1},{2,130},{130,2},{3,131},{131,3},{4... | collective-permute-start | bytes 49160 | tf_op jit(solution)/shard_map/ppermute | solution.py:609
  97.9 4.0 %collective-permute-start.9 = (f32[24,128]{1,0:T(8,128)S(1)}, f32[24,128]{1,0:T(8,128)S(1)}, u32[]{:S(2)}, u32[]{:S(2)}) collective-permute-start(f32[24,128]{1,0:T(8,128)S(1)} %convert_reduce_fusion.total), channel_id=1, source_target_pairs={{0,2},{2,0},{4,6},{6,4},{8,10},{10,8},{12,14},{14,12},{16,18},{18,... | collective-permute-start | bytes 36872 | tf_op jit(solution)/shard_map/ppermute | solution.py:483

commit v7 on v6

--- a/solution.py
+++ b/solution.py
@@ -51,23 +51,24 @@
     return lax.axis_index("role") == 1
 
 
-def pack_kernel(noise_levels, replay_levels, base, noise, replay, cotangent, embed, modulation, after, pack, stack):
-    critic = on_critic()
+def stack_kernel(embed, modulation, after, stack):
     modulation_a = modulation[0]
-    modulation_b = jnp.where(critic, modulation[1], modulation_a)
+    modulation_b = jnp.where(on_critic(), modulation[1], modulation_a)
     embed_f = embed[...].astype(F32)
-    scaled_b = (embed_f * modulation_b[0:1, :]).astype(BF16)
     stack[0:64, :] = embed[...]
     stack[64:128, :] = (embed_f * modulation_a[0:1, :]).astype(BF16)
-    stack[128:192, :] = scaled_b
-    stack[192:256, :] = scaled_b
+    stack[128:192, :] = (embed_f * modulation_b[0:1, :]).astype(BF16)
     shifts = []
     for pair in (modulation_a, modulation_b):
         shift = pair[1:2, :]
         high = rounded(shift)
         shifts += [high, shift - high]
-    shifts.append(jnp.zeros((12, embed.shape[1]), F32))
-    stack[256:272, :] = jnp.concatenate(shifts, axis=0).astype(BF16)
+    shifts.append(jnp.zeros((60, embed.shape[1]), F32))
+    stack[192:256, :] = jnp.concatenate(shifts, axis=0).astype(BF16)
+
+
+def pack_kernel(noise_levels, replay_levels, base, noise, replay, cotangent, embed, after, pack):
+    critic = on_critic()
     level = noise_levels[0, 0]
     level_two = jnp.where(critic, level, replay_levels[0, 0])
     base_f = base[...].astype(F32)
@@ -117,7 +118,7 @@
     out[...] = turn_rows(half_columns(weight, second), out.shape[1], second)
 
 
-def weight_kernel(chips, own, received, out, turned, blocks, copied):
+def weight_kernel(chips, own, received, out, turned):
     second = on_second_core()
     columns, padded = own.shape
     turned[0:columns, :] = own[...] + turn_rows(half_columns(received, second), padded, jnp.logical_not(second))
@@ -125,24 +126,16 @@
     height = out.shape[1]
     spare = padded // 4
     upper_lanes = lane_index((16, padded)) >= padded - spare
-    group = 8
-    copies = []
     for chip in range(chips):
         piece = turned[chip * block : chip * block + height, :]
         last = turned[chip * block + height : (chip + 1) * block, :]
         lines = [pltpu.roll(last, padded - spare * (part + 1), 1) for part in range(3)]
         lines.append(jnp.zeros_like(last))
         top = jnp.where(upper_lanes, jnp.concatenate(lines, axis=0), piece[0:16])
-        blocks[chip] = jnp.concatenate([top, piece[16:]], axis=0).astype(BF16)
-        if chip % group == group - 1:
-            span = pl.ds(chip + 1 - group, group)
-            copies.append(pltpu.make_async_copy(blocks.at[span], out.at[span], copied.at[len(copies)]))
-            copies[-1].start()
-    for copy in copies:
-        copy.wait()
-
-
-def product_kernel(block, taken, stack, out, columns_out):
+        out[chip] = jnp.concatenate([top, piece[16:]], axis=0).astype(BF16)
+
+
+def product_kernel(block, taken, stack, after, out, columns_out):
     chips, height, padded = taken.shape
     half = block // 2
     width = stack.shape[1]
@@ -165,16 +158,17 @@
         span = slice(start * depth, (start + group) * depth)
         columns_out[:, span] = joined.astype(BF16)
     weight = columns_out[...]
-    products = dot(weight, stack[0:256, :], NT)
+    products = dot(weight, stack[...], NT)
     first, second = products[:, 0:128], products[:, 128:256]
-    offsets = dot(stack[256:272, :], weight, NT)
+    tall = jnp.concatenate([second, jnp.zeros((128 - second.shape[0], 128), F32)], axis=0).T
     lines = []
     gap = jnp.zeros((1, CHANNELS - block), F32)
-    for offset in (offsets[0:1, 0:block] + offsets[1:2, 0:block], offsets[2:3, 0:block] + offsets[3:4, 0:block]):
+    for at in (CHANNELS, CHANNELS + 2):
+        offset = tall[at : at + 1, 0:block] + tall[at + 1 : at + 2, 0:block]
         high = rounded(offset)
         lines.append(jnp.concatenate([high, gap, offset - high, gap], axis=1))
     low_lanes = lane_index((half, 128)) < CHANNELS
-    folded = jnp.where(low_lanes, second[0:half], second[half:block])
+    folded = jnp.where(low_lanes, second[0:half], pltpu.roll(second, CHANNELS, 1)[half:block])
     spare = out.shape[1] - block - half - 2
     parts = [first[0:block], folded] + lines
     if spare:
@@ -194,48 +188,44 @@
     return tail[:, at : at + 1] + tail[:, at + 1 : at + 2] + tail[:, at + 2 : at + 3]
 
 
-def forward(which, packs, matrices, offsets, output_turned, keep, keep_turned, probs_out, velocity):
-    heads = output_turned.shape[1] // HEAD_DIM
+def scaled_rows(which, packs):
     low_lanes = lane_index((1, 128)) < CHANNELS
-    rows, scales, levels, turned_scales = [], [], [], []
+    rows, scales, levels = [], [], []
     for sample in range(2):
         inputs = token_rows(packs, sample, 0, 128).astype(F32)
         turned = pltpu.roll(inputs, CHANNELS, 1)
         level = tail_column(packs, sample, 2 + which)
         plain, scaled = (turned, inputs) if which else (inputs, turned)
         rows.append(jnp.where(low_lanes, plain, scaled * level))
-        scale = tail_column(packs, sample, which)
-        scales.append(scale)
+        scales.append(tail_column(packs, sample, which))
         levels.append(level[0:1])
-        turned_scales.append(jnp.broadcast_to(scale, (scale.shape[0], 128)).T[0:1])
-    tokens = rows[0].shape[0]
-    inputs = jnp.concatenate(rows, axis=0)
+    return jnp.concatenate(rows, axis=0), scales, levels
+
+
+def forward(which, packs, matrices, offsets, output_turned, keys_out, probs_out, velocity, crossing):
+    heads = output_turned.shape[1] // HEAD_DIM
+    inputs, scales, levels = scaled_rows(which, packs)
+    tokens = inputs.shape[0] // 2
+    turned_scales = [jnp.broadcast_to(scale, (tokens, 128)).T[0:1] for scale in scales]
     turned = inputs.T.astype(BF16)
     inputs = inputs.astype(BF16)
     offset = offsets[which : which + 1, :]
-    columns = offset.shape[1]
-    offset_turned = jnp.broadcast_to(offset, (128, columns)).T[:, 0:1]
+    offset_turned = jnp.broadcast_to(offset, (128, offset.shape[1])).T[:, 0:1]
     units = []
     for head in range(heads):
         at = head * 3 * HEAD_DIM
         span = slice(at, at + 3 * HEAD_DIM)
         matrix = matrices[span, :]
-        if keep is None:
-            product = dot(inputs, matrix[HEAD_DIM : 2 * HEAD_DIM], NT)
-        else:
-            product = dot(inputs, matrix, NT)
+        product = dot(inputs, matrix[HEAD_DIM : 2 * HEAD_DIM], NT)
         product_turned = dot(matrix, turned)
+        line = offset[:, at + HEAD_DIM : at + 2 * HEAD_DIM]
         for sample in range(2):
             own = slice(sample * tokens, (sample + 1) * tokens)
-            line = offset[:, span] if keep is not None else offset[:, at + HEAD_DIM : at + 2 * HEAD_DIM]
-            qkv = (product[own] * scales[sample] + line * levels[sample]).astype(BF16)
+            key = (product[own] * scales[sample] + line * levels[sample]).astype(BF16)
             flipped = product_turned[:, own] * turned_scales[sample] + offset_turned[span] * levels[sample]
             flipped = flipped.astype(BF16)
-            key = qkv
-            if keep is not None:
-                keep[sample, :, span] = qkv
-                keep_turned[2 * head + sample] = flipped[HEAD_DIM : 2 * HEAD_DIM]
-                key = qkv[:, HEAD_DIM : 2 * HEAD_DIM]
+            if keys_out is not None:
+                keys_out[2 * head + sample] = flipped[HEAD_DIM : 2 * HEAD_DIM]
             units.append((key, flipped[0:HEAD_DIM], flipped[2 * HEAD_DIM :]))
     totals = [None, None]
     scores = [dot(key, query) * (HEAD_DIM**-0.5) for key, query, _ in units]
@@ -249,24 +239,13 @@
         term = dot(output_turned[:, head * HEAD_DIM : (head + 1) * HEAD_DIM], mixed)
         before = totals[unit % 2]
         totals[unit % 2] = term if before is None else before + term
-    velocity[...] = jnp.concatenate(totals, axis=0).T
+    whole = jnp.concatenate(totals, axis=0).T
+    velocity[...] = whole
+    crossing[...] = pltpu.roll(whole, CHANNELS, 1)
 
 
 def second_pass_kernel(
-    block,
-    taken,
-    here,
-    there,
-    output_turned,
-    matrices,
-    offsets,
-    keep,
-    keep_turned,
-    probs,
-    velocity,
-    crossing,
-    stacked,
-    stacked_two,
+    block, taken, here, there, output_turned, matrices, offsets, keys_turned, probs, velocity, crossing, stacked
 ):
     chips = taken.shape[0]
     half = block // 2
@@ -275,25 +254,45 @@
     for chip in range(chips):
         piece = taken[chip].astype(F32)
         at = chip * block
-        stacked[at : at + block, :] = piece[0:block]
         folded = piece[block : block + half]
         turned = pltpu.roll(folded, CHANNELS, 1)
-        stacked_two[at : at + half, :] = jnp.where(low_lanes, piece[0:half], turned)
-        stacked_two[at + half : at + block, :] = jnp.where(low_lanes, piece[half:block], folded)
+        stacked[at : at + half, :] = jnp.where(low_lanes, piece[0:half], turned)
+        stacked[at + half : at + block, :] = jnp.where(low_lanes, piece[half:block], folded)
         for which in range(2):
             line = piece[block + half + which : block + half + which + 1]
             lines[which].append((line + pltpu.roll(line, CHANNELS, 1))[:, 0:block])
-    matrices[...] = stacked[...].astype(BF16)
     joined = [jnp.concatenate(line, axis=1) for line in lines]
     offsets[...] = jnp.concatenate(joined + [jnp.zeros((6, offsets.shape[1]), F32)], axis=0)
-    both = stacked_two[...].astype(BF16)
-    forward(1, (here, there), both, offsets, output_turned, keep, keep_turned, probs, velocity)
-    crossing[...] = pltpu.roll(velocity[...], CHANNELS, 1)
-
-
-def first_pass_kernel(matrices, offsets, here, there, output_turned, after, velocity, crossing):
-    forward(0, (here, there), matrices, offsets, output_turned, None, None, None, velocity)
-    crossing[...] = pltpu.roll(velocity[...], CHANNELS, 1)
+    matrices[...] = stacked[...].astype(BF16)
+    forward(1, (here, there), matrices[...], offsets, output_turned, keys_turned, probs, velocity, crossing)
+
+
+def first_pass_kernel(
+    block, taken, matrices, offsets, here, there, output_turned, after, velocity, crossing, kept, scaled_out, rows_out, stacked
+):
+    packs = (here, there)
+    for chip in range(taken.shape[0]):
+        stacked[chip * block : (chip + 1) * block, :] = taken[chip].astype(F32)[0:block]
+    forward(0, packs, stacked[...].astype(BF16), offsets, output_turned, None, None, velocity, crossing)
+    inputs, scales, levels = scaled_rows(1, packs)
+    tokens = inputs.shape[0] // 2
+    low_lanes = lane_index((1, 128)) < CHANNELS
+    for sample in range(2):
+        plain = inputs[sample * tokens : (sample + 1) * tokens]
+        plain = jnp.where(low_lanes, plain, pltpu.roll(plain, CHANNELS, 1))
+        scaled = plain * (scales[sample] * levels[sample])
+        scaled_out[sample] = scaled.astype(BF16)
+        rows_out[sample] = scaled.T.astype(BF16)
+    inputs = inputs.astype(BF16)
+    for head in range(output_turned.shape[1] // HEAD_DIM):
+        for place, part in enumerate((0, 2)):
+            at = (3 * head + part) * HEAD_DIM
+            to = (2 * head + place) * HEAD_DIM
+            product = dot(inputs, matrices[at : at + HEAD_DIM, :], NT)
+            line = offsets[1:2, at : at + HEAD_DIM]
+            for sample in range(2):
+                own = product[sample * tokens : (sample + 1) * tokens]
+                kept[sample, :, to : to + HEAD_DIM] = (own * scales[sample] + line * levels[sample]).astype(BF16)
 
 
 def swap_tokens(value):
@@ -304,6 +303,8 @@
 def backward_kernel(
     block,
     kept,
+    scaled,
+    rows,
     keys_turned,
     probs_turned,
     here,
@@ -311,35 +312,23 @@
     vel_here,
     vel_there,
     output_turned,
-    after,
     out,
     gathered,
     summed,
-    blocks,
-    copied,
 ):
     critic = on_critic()
     packs = (here, there)
     heads = output_turned.shape[1] // HEAD_DIM
-    velocity = vel_here[...] + swap_tokens(vel_there[...])
-    lane = lane_index((1, 128))
-    known = []
+    velocity = vel_here[...] + swap_tokens(vel_there[...].astype(F32))
+    known, levels = [], []
     for sample in range(2):
         part = token_rows(packs, sample, 128, 256).astype(F32)
         known.append(part[:, 0:CHANNELS] + part[:, CHANNELS:])
+        levels.append(tail_column((here,), sample, 3)[0:1])
     known = jnp.concatenate(known, axis=1)
     grad_velocity = jnp.where(critic, velocity - known, known)
     grads_turned = grad_velocity.T.astype(BF16)
     grads = grad_velocity.astype(BF16)
-    inputs, rows, levels = [], [], []
-    for sample in range(2):
-        packed = token_rows(packs, sample, 0, 128).astype(F32)
-        packed = jnp.where(lane < CHANNELS, pltpu.roll(packed, CHANNELS, 1), packed)
-        level = tail_column(packs, sample, 3)
-        levels.append(level[0:1])
-        scaled = packed * (tail_column(packs, sample, 1) * level)
-        inputs.append(scaled.astype(BF16))
-        rows.append(scaled.T.astype(BF16))
     grad_mixed, grad_probs = [], []
     for unit in range(2 * heads):
         head, sample = unit // 2, unit % 2
@@ -347,7 +336,7 @@
         lanes = slice(sample * CHANNELS, (sample + 1) * CHANNELS)
         grad_mixed.append(dot(grads[:, lanes], weight).astype(BF16))
         turned = dot(weight, grads_turned[lanes], TN).astype(BF16)
-        value = kept[sample, :, head * 3 * HEAD_DIM + 2 * HEAD_DIM : (head + 1) * 3 * HEAD_DIM]
+        value = kept[sample, :, (2 * head + 1) * HEAD_DIM : (2 * head + 2) * HEAD_DIM]
         grad_probs.append(dot(value, turned))
     columns = heads * 3 * HEAD_DIM
     gathered[columns:, :] = jnp.zeros((gathered.shape[0] - columns, 128), F32)
@@ -356,7 +345,6 @@
     row = row_index((height, 128))
     low_lanes = lane_index((height, 128)) < CHANNELS
     pad = jnp.zeros((1, 128 - block), F32) if block < 128 else None
-    copies = []
     for head in range(heads):
         at = head * 3 * HEAD_DIM
         query_total, rest_total = None, None
@@ -368,10 +356,10 @@
             inner = jnp.sum(grad * probs, axis=0, keepdims=True)
             grad_scores = (probs * (grad - inner) * (HEAD_DIM**-0.5)).astype(BF16)
             grad_value = dot(probs.astype(BF16), grad_mixed[unit])
-            grad_key = dot(grad_scores, kept[sample, :, at : at + HEAD_DIM])
+            grad_key = dot(grad_scores, kept[sample, :, 2 * head * HEAD_DIM : (2 * head + 1) * HEAD_DIM])
             grad_query = dot(keys_turned[unit], grad_scores).astype(BF16)
             rest = jnp.concatenate([grad_key, grad_value], axis=1).astype(BF16)
-            query_term = dot(grad_query, inputs[sample])
+            query_term = dot(grad_query, scaled[sample])
             rest_term = dot(rows[sample], rest)
             query_total = query_term if query_total is None else query_total + query_term
             rest_total = rest_term if rest_total is None else rest_total + rest_term
@@ -393,12 +381,7 @@
             if pad is not None:
                 pair = [jnp.concatenate([part, pad], axis=1) for part in pair]
             tail = jnp.where(row == half, pair[0], jnp.where(row == half + 1, pair[1], 0.0))
-            blocks[chip] = jnp.where(row < half, piece, tail).astype(BF16)
-        span = pl.ds(start, stop - start)
-        copies.append(pltpu.make_async_copy(blocks.at[span], out.at[span], copied.at[head]))
-        copies[-1].start()
-    for copy in copies:
-        copy.wait()
+            out[chip] = jnp.where(row < half, piece, tail).astype(BF16)
 
 
 def closing_kernel(block, factor, taken, weight, embed, after, kept, sent):
@@ -432,10 +415,10 @@
     sent[...] = jnp.where(second, sides[0], sides[1])
 
 
-def payload_kernel(noise_levels, own, a_here, a_there, b_here, b_there, out):
+def payload_kernel(noise_levels, own, a_here, b_here, there, out):
     tokens = own.shape[0]
-    own_a = a_here[0:tokens, 0:CHANNELS] + a_there[...]
-    own_b = b_here[0:tokens, 0:CHANNELS] + b_there[tokens:, 0:CHANNELS]
+    own_a = a_here[0:tokens, 0:CHANNELS] + there[:, 0:CHANNELS]
+    own_b = b_here[0:tokens, 0:CHANNELS] + there[:, CHANNELS:]
     sample = own[:, 0:CHANNELS].astype(F32) - noise_levels[0, 0] * own_a
     out[...] = jnp.where(on_critic(), own_b - own_a, sample).T.astype(BF16)
 
@@ -459,16 +442,15 @@
                 out[which : which + 1, at : at + 128] = half[which * count + i : which * count + i + 1, :]
 
 
-def call(kernel, out_shapes, inputs, scalars=0, scratch=(), flops=0, after=(), far_out=False):
+def call(kernel, out_shapes, inputs, scalars=0, scratch=(), flops=0, after=()):
     specs = [pl.BlockSpec(memory_space=pltpu.SMEM)] * scalars
     specs += [pl.BlockSpec(memory_space=pltpu.VMEM)] * (len(inputs) - scalars)
     specs += [pl.BlockSpec(memory_space=pl.ANY)] * len(after)
-    space = pl.ANY if far_out else pltpu.VMEM
     return pl.pallas_call(
         kernel,
         out_shape=out_shapes,
         in_specs=specs,
-        out_specs=jax.tree.map(lambda _: pl.BlockSpec(memory_space=space), out_shapes),
+        out_specs=jax.tree.map(lambda _: pl.BlockSpec(memory_space=pltpu.VMEM), out_shapes),
         scratch_shapes=list(scratch),
         compiler_params=pltpu.CompilerParams(vmem_limit_bytes=28 * 2**20),
         cost_estimate=pl.CostEstimate(flops=flops, bytes_accessed=0, transcendentals=0),
@@ -529,18 +511,14 @@
         functools.partial(weight_kernel, chips),
         struct((chips, height, padded), BF16),
         (own_turned, received),
-        scratch=[
-            pltpu.VMEM((columns, padded), F32),
-            pltpu.VMEM((chips, height, padded), BF16),
-            pltpu.SemaphoreType.DMA((chips // 8,)),
-        ],
-        far_out=True,
+        scratch=[pltpu.VMEM((columns, padded), F32)],
     )
     taken = between_chips(turned)
-
-    own, stack = call(
+    stack = call(stack_kernel, struct((256, width), BF16), (embed, modulation[0]), after=(turned,))
+
+    own = call(
         pack_kernel,
-        (struct((tokens, 384), BF16), struct((272, width), BF16)),
+        struct((tokens, 384), BF16),
         (
             noise_levels,
             replay_levels,
@@ -549,61 +527,62 @@
             replay_latents[0, 0],
             cotangent[0, 0],
             embed,
-            modulation[0],
         ),
         scalars=2,
         after=(turned,),
     )
-    here = jnp.stack([own, other_core(own)])
-    there = other_half(here)
-
     matrices, own_columns = call(
         functools.partial(product_kernel, block),
         (struct((chips, packed, 128), BF16), struct((height + 8, width), BF16)),
         (taken, stack),
-    )
-    whole, offsets, kept, keys_turned, probs, vel_b, vel_crossing = call(
+        after=(own,),
+    )
+    here = jnp.stack([own, other_core(own)])
+    there = other_half(here)
+
+    taken = between_chips(matrices)
+    whole, offsets, keys_turned, probs, vel_b, vel_crossing = call(
         functools.partial(second_pass_kernel, block),
         (
             struct((columns, 2 * CHANNELS), BF16),
             struct((8, columns), F32),
-            struct((2, 2 * tokens, columns), BF16),
             struct((2 * heads, HEAD_DIM, 2 * tokens), BF16),
             struct((2 * heads, 2 * tokens, 2 * tokens), F32),
             struct((2 * tokens, 2 * CHANNELS), F32),
             struct((2 * tokens, 2 * CHANNELS), F32),
         ),
-        (between_chips(matrices), here, there, output_turned),
-        scratch=[pltpu.VMEM((columns, 2 * CHANNELS), F32), pltpu.VMEM((columns, 2 * CHANNELS), F32)],
+        (taken, here, there, output_turned),
+        scratch=[pltpu.VMEM((columns, 2 * CHANNELS), F32)],
     )
     vel_here = vel_b + other_core(vel_crossing)
-    vel_there = other_half(vel_here)
-    vel_a, vel_a_crossing = call(
-        first_pass_kernel,
-        (struct((2 * tokens, 2 * CHANNELS), F32), struct((2 * tokens, 2 * CHANNELS), F32)),
-        (whole, offsets, here, there, output_turned),
+    vel_there = other_half(vel_here.astype(BF16))
+    vel_a, vel_a_crossing, kept, scaled, rows = call(
+        functools.partial(first_pass_kernel, block),
+        (
+            struct((2 * tokens, 2 * CHANNELS), F32),
+            struct((2 * tokens, 2 * CHANNELS), F32),
+            struct((2, 2 * tokens, 2 * heads * HEAD_DIM), BF16),
+            struct((2, 2 * tokens, 2 * CHANNELS), BF16),
+            struct((2, 2 * CHANNELS, 2 * tokens), BF16),
+        ),
+        (taken, whole, offsets, here, there, output_turned),
+        scratch=[pltpu.VMEM((columns, 2 * CHANNELS), F32)],
         flops=4 * 10**9,
         after=(vel_here,),
     )
-    vel_a_here = vel_a + other_core(vel_a_crossing)
     products = call(
         functools.partial(backward_kernel, block),
         struct((chips, folded, 128), BF16),
-        (kept, keys_turned, probs, here, there, vel_here, vel_there, output_turned),
-        scratch=[
-            pltpu.VMEM((columns + 2 * folded, 128), F32),
-            pltpu.VMEM((1, columns), F32),
-            pltpu.VMEM((chips, folded, 128), BF16),
-            pltpu.SemaphoreType.DMA((heads,)),
-        ],
-        after=(vel_a,),
-        far_out=True,
-    )
-
+        (kept, scaled, rows, keys_turned, probs, here, there, vel_here, vel_there, output_turned),
+        scratch=[pltpu.VMEM((columns + 2 * folded, 128), F32), pltpu.VMEM((1, columns), F32)],
+    )
+
+    vel_a_here = vel_a + other_core(vel_a_crossing)
+    both_there = other_half(jnp.concatenate([vel_a_here[tokens:, :CHANNELS], vel_here[tokens:, :CHANNELS]], axis=1))
     payload = call(
         payload_kernel,
         struct((CHANNELS, tokens), BF16),
-        (noise_levels, own, vel_a_here, other_half(vel_a_here[tokens:, :CHANNELS]), vel_here, vel_there),
+        (noise_levels, own, vel_a_here, vel_here, both_there),
         scalars=1,
     )
     crossed = lax.ppermute(payload, "role", [(0, 1), (1, 0)])

time: 103 us -> 102 us (level)
  waiting for transfers between devices: 34.5 us -> 33.2 us
    ppermute x4, waiting for transfers between devices: 9.74 us -> 8.38 us  [other_half(): return lax.ppermute(value, 'seq', [(0, 1), (1, 0)])]
    pallas_call x11 -> x12, Pallas kernels: 13.1 us -> 13.2 us  [call(): pl.pallas_call(kernel, out_shape=out_shapes, in_specs=specs, out_specs=ja...]
  transfers between devices with their start and end apart: 15 -> 15, of which waited for: 14 -> 13; matrix products, arithmetic and copies ran while one was open for 1% -> 1% of each run, Pallas kernels for 3% -> 3%
where the time goes in v7:
time: 102 us; the launch traced here: 101 us
  starting transfers between devices  50.9 us (50%)
  waiting for transfers between devices  33.2 us (33%)
  Pallas kernels  13.2 us (13%)
  between operations  2.15 us (2%)
  local copies, waits for them, and re-layouts  1.43 us (1%)
    all_to_all x4, starting transfers between devices, between_chips(): lax.all_to_all(value, 'fsdp', 0, 0, tiled=True, axis_index_groups=groups)  25.8 us
    all_to_all x4, waiting for transfers between devices, between_chips(): lax.all_to_all(value, 'fsdp', 0, 0, tiled=True, axis_index_groups=groups)  20.1 us
    ppermute x6, starting transfers between devices, other_core(): lax.ppermute(value, 'fsdp', [(i, i ^ 1) for i in range(lax.axis_size('fsd...  16.9 us
    pallas_call x12, Pallas kernels, call(): pl.pallas_call(kernel, out_shape=out_shapes, in_specs=specs, out_specs=ja...  13.2 us
    ppermute x4, waiting for transfers between devices, other_half(): return lax.ppermute(value, 'seq', [(0, 1), (1, 0)])  8.38 us
    ppermute x4, starting transfers between devices, other_half(): return lax.ppermute(value, 'seq', [(0, 1), (1, 0)])  5.25 us
    ppermute x6, waiting for transfers between devices, other_core(): lax.ppermute(value, 'fsdp', [(i, i ^ 1) for i in range(lax.axis_size('fsd...  4.75 us
    ppermute x1, starting transfers between devices, per_device(): crossed = lax.ppermute(payload, 'role', [(0, 1), (1, 0)])  3 us
  transfers between devices with their start and end apart: 15, of which 13 were waited for; matrix products, arithmetic and copies ran while one was open for 1% of the time, Pallas kernels for 3%

profile of v7, /device:TPU:1, one launch (start us, length us, event | category | flops | bytes accessed | tf_op | source)
XLA Modules:
  0.0 101.1 jit_solution(17203139634182812974)
XLA Ops:
  0.6 0.0 copy-start
  0.6 3.3 %collective-permute-start = (bf16[48,2304]{1,0:T(8,128)(2,1)}, bf16[48,2304]{1,0:T(8,128)(2,1)S(1)}, u32[]{:S(2)}, u32[]{:S(2)}) collective-permute-start(bf16[48,2304]{1,0:T(8,128)(2,1)} %bitcast.20), channel_id=1, source_target_pairs={{0,2},{2,0},{4,6},{6,4},{8,10},{10,8},{12,14},{14,12},{16,18},{18,... | collective-permute-start | bytes 663560 | tf_op jit(solution)/shard_map/ppermute | solution.py:465
  4.0 0.0 copy-start.1
  4.0 0.9 copy-done.1
  4.9 0.0 copy-start.4
  4.9 0.0 copy-start.5
  4.9 0.0 copy-start.6
  4.9 0.0 copy-start.7
  4.9 0.0 copy-start.2
  4.9 0.2 shard_map.113.own
  5.1 0.2 collective-permute-done.received
  5.3 1.0 shard_map.114.after
  6.3 9.3 %all-to-all-start = ((bf16[32,32,128]{2,1,0:T(8,128)(2,1)}), bf16[32,32,128]{2,1,0:T(8,128)(2,1)S(1)}, u32[]{:S(2)}, u32[]{:S(2)}) async-start(bf16[32,32,128]{2,1,0:T(8,128)(2,1)} %shard_map.114.after), calls=%async_computation | async-start | bytes 524288 | tf_op jit(solution)/shard_map/all_to_all | solution.py:475
  16.2 0.0 copy-done.4
  16.3 0.1 copy.12
  16.4 0.0 copy-done.5
  16.4 0.1 copy.13
  16.5 0.0 copy-done.6
  16.5 0.1 copy.14
  16.6 0.0 copy-done.7
  16.6 0.1 copy.15
  17.4 0.0 copy-done
  17.4 0.0 copy-done.2
  17.4 0.3 shard_map.115.stack
  17.7 0.7 shard_map.116.after.own
  18.4 0.0 copy-start.3
  18.4 6.9 %all-to-all-done.taken = bf16[32,32,128]{2,1,0:T(8,128)(2,1)S(1)} async-done(((bf16[32,32,128]{2,1,0:T(8,128)(2,1)}), bf16[32,32,128]{2,1,0:T(8,128)(2,1)S(1)}, u32[]{:S(2)}, u32[]{:S(2)}) %all-to-all-start) | async-done | bytes 262176 | tf_op jit(solution)/shard_map/all_to_all | solution.py:475
  25.3 1.6 %shard_map.117 = (bf16[32,56,128]{2,1,0:T(8,128)(2,1)}, bf16[40,3072]{1,0:T(8,128)(2,1)S(1)}) custom-call(bf16[32,32,128]{2,1,0:T(8,128)(2,1)S(1)} %all-to-all-done.taken, bf16[256,3072]{1,0:T(8,128)(2,1)S(1)} %shard_map.115.stack, bf16[128,384]{1,0:T(8,128)(2,1)S(1)} %shard_map.116.after.own), custom_call_target="tpu_custom_call" | custom-call | tf_op jit(solution)/shard_map/pallas_call | solution.py:449
  26.9 6.7 %all-to-all-start.1 = ((bf16[32,56,128]{2,1,0:T(8,128)(2,1)}), bf16[32,56,128]{2,1,0:T(8,128)(2,1)S(1)}, u32[]{:S(2)}, u32[]{:S(2)}) async-start(bf16[32,56,128]{2,1,0:T(8,128)(2,1)} %get-tuple-element.19), calls=%async_computation.1 | async-start | bytes 917504 | tf_op jit(solution)/shard_map/all_to_all | solution.py:475
  33.6 1.5 %collective-permute-start.1 = (bf16[128,384]{1,0:T(8,128)(2,1)S(1)}, bf16[128,384]{1,0:T(8,128)(2,1)S(1)}, u32[]{:S(2)}, u32[]{:S(2)}) collective-permute-start(bf16[128,384]{1,0:T(8,128)(2,1)S(1)} %shard_map.116.after.own), channel_id=1, source_target_pairs={{0,2},{2,0},{4,6},{6,4},{8,10},{10,8},{12,14},{14,12},{16,18},{18,... | collective-permute-start | bytes 294920 | tf_op jit(solution)/shard_map/ppermute | solution.py:465
  35.1 0.9 collective-permute-done.1
  36.1 1.4 %collective-permute-start.2 = (bf16[2,128,384]{2,1,0:T(8,128)(2,1)S(1)}, bf16[2,128,384]{2,1,0:T(8,128)(2,1)S(1)}, u32[]{:S(2)}, u32[]{:S(2)}) collective-permute-start(bf16[2,128,384]{2,1,0:T(8,128)(2,1)S(1)} %pad_maximum_fusion.here), channel_id=1, source_target_pairs={{0,1},{1,0},{2,3},{3,2},{4,5},{5,4},{6,7},{7,6},{8,9},{9,8},{10,11... | collective-permute-start | bytes 589832 | tf_op jit(solution)/shard_map/ppermute | solution.py:469
  37.4 0.0 copy-done.3
  37.5 4.8 %collective-permute-done.2.there = bf16[2,128,384]{2,1,0:T(8,128)(2,1)S(1)} collective-permute-done((bf16[2,128,384]{2,1,0:T(8,128)(2,1)S(1)}, bf16[2,128,384]{2,1,0:T(8,128)(2,1)S(1)}, u32[]{:S(2)}, u32[]{:S(2)}) %collective-permute-start.2) | collective-permute-done | bytes 196640 | tf_op jit(solution)/shard_map/ppermute | solution.py:469
  42.3 3.5 %all-to-all-done.1.taken = bf16[32,56,128]{2,1,0:T(8,128)(2,1)S(1)} async-done(((bf16[32,56,128]{2,1,0:T(8,128)(2,1)}), bf16[32,56,128]{2,1,0:T(8,128)(2,1)S(1)}, u32[]{:S(2)}, u32[]{:S(2)}) %all-to-all-start.1) | async-done | bytes 458784 | tf_op jit(solution)/shard_map/all_to_all | solution.py:475
  45.8 2.3 %shard_map.118 = (bf16[1152,128]{1,0:T(8,128)(2,1)S(1)}, f32[8,1152]{1,0:T(8,128)S(1)}, bf16[6,128,256]{2,1,0:T(8,128)(2,1)S(1)}, f32[6,256,256]{2,1,0:T(8,128)S...) custom-call(bf16[32,56,128]{2,1,0:T(8,128)(2,1)S(1)} %all-to-all-done.1.taken, ...), custom_call_target="tpu_custom_call" | custom-call | tf_op jit(solution)/shard_map/pallas_call | solution.py:449
  48.1 4.5 %collective-permute-start.3 = (f32[256,128]{1,0:T(8,128)S(1)}, f32[256,128]{1,0:T(8,128)S(1)}, u32[]{:S(2)}, u32[]{:S(2)}) collective-permute-start(f32[256,128]{1,0:T(8,128)S(1)} %get-tuple-element.23), channel_id=1, source_target_pairs={{0,2},{2,0},{4,6},{6,4},{8,10},{10,8},{12,14},{14,12},{16,18},{18,... | collective-permute-start | bytes 393224 | tf_op jit(solution)/shard_map/ppermute | solution.py:465
  52.6 1.0 collective-permute-done.3
  53.6 1.4 %collective-permute-start.4 = (bf16[256,128]{1,0:T(8,128)(2,1)S(1)}, bf16[256,128]{1,0:T(8,128)(2,1)S(1)}, u32[]{:S(2)}, u32[]{:S(2)}) collective-permute-start(bf16[256,128]{1,0:T(8,128)(2,1)S(1)} %get-tuple-element.36), channel_id=1, source_target_pairs={{0,1},{1,0},{2,3},{3,2},{4,5},{5,4},{6,7},{7,6},{8,9},{9,8},{10,11... | collective-permute-start | bytes 196616 | tf_op jit(solution)/shard_map/ppermute | solution.py:469
  55.0 2.2 %shard_map.119 = (f32[256,128]{1,0:T(8,128)S(1)}, f32[256,128]{1,0:T(8,128)S(1)}, bf16[2,256,768]{2,1,0:T(8,128)(2,1)S(1)}, bf16[2,256,128]{2,1,0:T(8,128)(2,1)S(1)}, bf16[2,128,256]{2,1,0:T(8,128)(2,1)S(1)}) custom-call(bf16[32,56,128]{2,1,0:T(8,128)(2,1)S(1)} %all-to-all-done.1.taken, bf16[1152,128]{1,0:T(8,128)(2,1)S(1)} %get-tuple-element.20.matrices, ...), custom_call_target="tpu_custom_call" | custom-call | flops 4000000000 | tf_op jit(solution)/shard_map/pallas_call | solution.py:449
  57.2 0.0 collective-permute-done.4.vel_there
  57.2 2.9 %shard_map.120 = bf16[32,24,128]{2,1,0:T(8,128)(2,1)} custom-call(bf16[2,256,768]{2,1,0:T(8,128)(2,1)S(1)} %get-tuple-element.24.kept, bf16[2,256,128]{2,1,0:T(8,128)(2,1)S(1)} %get-tuple-element.25.scaled, bf16[2,128,256]{2,1,0:T(8,128)(2,1)S(1)} %get-tuple-element.26.rows, bf16[6,128,256]{2,1,0:T(8,128)(2,1)S(1)} %get-tuple-element.27.keys_turned, ...), custom_call_target="tpu_custom_call" | custom-call | tf_op jit(solution)/shard_map/pallas_call | solution.py:449
  60.2 5.1 %all-to-all-start.2 = ((bf16[32,24,128]{2,1,0:T(8,128)(2,1)}), bf16[32,24,128]{2,1,0:T(8,128)(2,1)S(1)}, u32[]{:S(2)}, u32[]{:S(2)}) async-start(bf16[32,24,128]{2,1,0:T(8,128)(2,1)} %shard_map.120), calls=%async_computation.2 | async-start | bytes 393216 | tf_op jit(solution)/shard_map/all_to_all | solution.py:475
  65.3 1.4 %collective-permute-start.5 = (f32[256,128]{1,0:T(8,128)S(1)}, f32[256,128]{1,0:T(8,128)S(1)}, u32[]{:S(2)}, u32[]{:S(2)}) collective-permute-start(f32[256,128]{1,0:T(8,128)S(1)} %get-tuple-element.31), channel_id=1, source_target_pairs={{0,2},{2,0},{4,6},{6,4},{8,10},{10,8},{12,14},{14,12},{16,18},{18,... | collective-permute-start | bytes 393224 | tf_op jit(solution)/shard_map/ppermute | solution.py:465
  66.7 1.0 collective-permute-done.5
  67.7 0.1 pad_maximum_fusion.1
  67.8 1.4 %collective-permute-start.6 = (f32[128,128]{1,0:T(8,128)S(1)}, f32[128,128]{1,0:T(8,128)S(1)}, u32[]{:S(2)}, u32[]{:S(2)}) collective-permute-start(f32[128,128]{1,0:T(8,128)S(1)} %pad_maximum_fusion.1), channel_id=1, source_target_pairs={{0,1},{1,0},{2,3},{3,2},{4,5},{5,4},{6,7},{7,6},{8,9},{9,8},{10,11... | collective-permute-start | bytes 196616 | tf_op jit(solution)/shard_map/ppermute | solution.py:469
  69.2 2.1 %collective-permute-done.6.there = f32[128,128]{1,0:T(8,128)S(1)} collective-permute-done((f32[128,128]{1,0:T(8,128)S(1)}, f32[128,128]{1,0:T(8,128)S(1)}, u32[]{:S(2)}, u32[]{:S(2)}) %collective-permute-start.6) | collective-permute-done | bytes 65568 | tf_op jit(solution)/shard_map/ppermute | solution.py:469
  71.3 0.1 shard_map.121.after
  71.5 3.2 %all-to-all-done.2.taken = bf16[32,24,128]{2,1,0:T(8,128)(2,1)S(1)} async-done(((bf16[32,24,128]{2,1,0:T(8,128)(2,1)}), bf16[32,24,128]{2,1,0:T(8,128)(2,1)S(1)}, u32[]{:S(2)}, u32[]{:S(2)}) %all-to-all-start.2) | async-done | bytes 196640 | tf_op jit(solution)/shard_map/all_to_all | solution.py:475
  74.7 0.6 shard_map.122
  75.3 2.9 %collective-permute-start.7 = (f32[24,128]{1,0:T(8,128)S(1)}, f32[24,128]{1,0:T(8,128)S(1)}, u32[]{:S(2)}, u32[]{:S(2)}) collective-permute-start(f32[24,128]{1,0:T(8,128)S(1)} %get-tuple-element.33), channel_id=1, source_target_pairs={{0,2},{2,0},{4,6},{6,4},{8,10},{10,8},{12,14},{14,12},{16,18},{18,... | collective-permute-start | bytes 36872 | tf_op jit(solution)/shard_map/ppermute | solution.py:465
  78.2 0.8 collective-permute-done.7
  79.1 1.1 %collective-permute-start.8 = (f32[24,128]{1,0:T(8,128)S(1)}, f32[24,128]{1,0:T(8,128)S(1)}, u32[]{:S(2)}, u32[]{:S(2)}) collective-permute-start(f32[24,128]{1,0:T(8,128)S(1)} %add.11.total), channel_id=1, source_target_pairs={{0,1},{1,0},{2,3},{3,2},{4,5},{5,4},{6,7},{7,6},{8,9},{9,8},{10,11... | collective-permute-start | bytes 36872 | tf_op jit(solution)/shard_map/ppermute | solution.py:469
  80.2 1.4 %collective-permute-done.8.other = f32[24,128]{1,0:T(8,128)S(1)} collective-permute-done((f32[24,128]{1,0:T(8,128)S(1)}, f32[24,128]{1,0:T(8,128)S(1)}, u32[]{:S(2)}, u32[]{:S(2)}) %collective-permute-start.8) | collective-permute-done | bytes 12320 | tf_op jit(solution)/shard_map/ppermute | solution.py:469
  81.6 0.7 shard_map.123
  82.3 4.6 %all-to-all-start.3 = ((bf16[32,24,128]{2,1,0:T(8,128)(2,1)}), bf16[32,24,128]{2,1,0:T(8,128)(2,1)S(1)}, u32[]{:S(2)}, u32[]{:S(2)}) async-start(bf16[32,24,128]{2,1,0:T(8,128)(2,1)} %shard_map.123), calls=%async_computation.3 | async-start | bytes 393216 | tf_op jit(solution)/shard_map/all_to_all | solution.py:475
  87.0 3.0 %collective-permute-start.10 = (bf16[64,128]{1,0:T(8,128)(2,1)S(1)}, bf16[64,128]{1,0:T(8,128)(2,1)S(1)}, u32[]{:S(2)}, u32[]{:S(2)}) collective-permute-start(bf16[64,128]{1,0:T(8,128)(2,1)S(1)} %shard_map.121.after), channel_id=1, source_target_pairs={{0,128},{128,0},{1,129},{129,1},{2,130},{130,2},{3,131},{131,3},{4... | collective-permute-start | bytes 49160 | tf_op jit(solution)/shard_map/ppermute | solution.py:588
  90.0 6.4 %all-to-all-done.3 = bf16[32,24,128]{2,1,0:T(8,128)(2,1)S(1)} async-done(((bf16[32,24,128]{2,1,0:T(8,128)(2,1)}), bf16[32,24,128]{2,1,0:T(8,128)(2,1)S(1)}, u32[]{:S(2)}, u32[]{:S(2)}) %all-to-all-start.3) | async-done | bytes 196640 | tf_op jit(solution)/shard_map/all_to_all | solution.py:475
  96.4 3.2 %collective-permute-start.9 = (f32[24,128]{1,0:T(8,128)S(1)}, f32[24,128]{1,0:T(8,128)S(1)}, u32[]{:S(2)}, u32[]{:S(2)}) collective-permute-start(f32[24,128]{1,0:T(8,128)S(1)} %convert_reduce_fusion.total), channel_id=1, source_target_pairs={{0,2},{2,0},{4,6},{6,4},{8,10},{10,8},{12,14},{14,12},{16,18},{18,... | collective-permute-start | bytes 36872 | tf_op jit(solution)/shard_map/ppermute | solution.py:465
  99.6 0.0 collective-permute-done.10.crossed
  99.6 0.8 collective-permute-done.9.near
  100.4 0.6 shard_map.124
  (8 shorter events, 0.1 us)
Async XLA Ops:
  0.6 16.8 %copy-start = (bf16[1,64,3072]{2,1,0:T(8,128)(2,1)S(1)}, bf16[1,64,3072]{2,1,0:T(8,128)(2,1)}, u32[]{:S(2)}) copy-start(bf16[1,64,3072]{2,1,0:T(8,128)(2,1)} %param.16) | copy-start | bytes 1179652
  0.6 4.6 %collective-permute-start = (bf16[48,2304]{1,0:T(8,128)(2,1)}, bf16[48,2304]{1,0:T(8,128)(2,1)S(1)}, u32[]{:S(2)}, u32[]{:S(2)}) collective-permute-start(bf16[48,2304]{1,0:T(8,128)(2,1)} %bitcast.20), channel_id=1, source_target_pairs={{0,2},{2,0},{4,6},{6,4},{8,10},{10,8},{12,14},{14,12},{16,18},{18,... | collective-permute-start | bytes 663560 | tf_op jit(solution)/shard_map/ppermute | solution.py:465
  4.0 0.9 copy-start.1
  4.9 11.3 %copy-start.4 = (bf16[1,1,128,64]{2,3,1,0:T(8,128)(2,1)S(1)}, bf16[1,1,128,64]{2,3,1,0:T(8,128)(2,1)}, u32[]{:S(2)}) copy-start(bf16[1,1,128,64]{2,3,1,0:T(8,128)(2,1)} %param.10) | copy-start | bytes 49156
  4.9 11.5 %copy-start.5 = (bf16[1,1,128,64]{2,3,1,0:T(8,128)(2,1)S(1)}, bf16[1,1,128,64]{2,3,1,0:T(8,128)(2,1)}, u32[]{:S(2)}) copy-start(bf16[1,1,128,64]{2,3,1,0:T(8,128)(2,1)} %param.11) | copy-start | bytes 49156
  4.9 11.6 %copy-start.6 = (bf16[1,1,128,64]{2,3,1,0:T(8,128)(2,1)S(1)}, bf16[1,1,128,64]{2,3,1,0:T(8,128)(2,1)}, u32[]{:S(2)}) copy-start(bf16[1,1,128,64]{2,3,1,0:T(8,128)(2,1)} %param.13) | copy-start | bytes 49156
  4.9 11.7 %copy-start.7 = (bf16[1,1,128,64]{2,3,1,0:T(8,128)(2,1)S(1)}, bf16[1,1,128,64]{2,3,1,0:T(8,128)(2,1)}, u32[]{:S(2)}) copy-start(bf16[1,1,128,64]{2,3,1,0:T(8,128)(2,1)} %param.15) | copy-start | bytes 49156
  4.9 12.5 %copy-start.2 = (f32[1,2,2,3072]{3,2,1,0:T(2,128)S(1)}, f32[1,2,2,3072]{3,2,1,0:T(2,128)}, u32[]{:S(2)}) copy-start(f32[1,2,2,3072]{3,2,1,0:T(2,128)} %param.19) | copy-start | bytes 147460
  6.3 19.0 %all-to-all-start = ((bf16[32,32,128]{2,1,0:T(8,128)(2,1)}), bf16[32,32,128]{2,1,0:T(8,128)(2,1)S(1)}, u32[]{:S(2)}, u32[]{:S(2)}) async-start(bf16[32,32,128]{2,1,0:T(8,128)(2,1)} %shard_map.114.after), calls=%async_computation | async-start | bytes 524288 | tf_op jit(solution)/shard_map/all_to_all | solution.py:475
  18.4 19.1 %copy-start.3 = (bf16[1,768,64]{1,2,0:T(8,128)(2,1)S(1)}, bf16[1,768,64]{1,2,0:T(8,128)(2,1)}, u32[]{:S(2)}) copy-start(bf16[1,768,64]{1,2,0:T(8,128)(2,1)} %param.18) | copy-start | bytes 294916
  26.9 19.0 %all-to-all-start.1 = ((bf16[32,56,128]{2,1,0:T(8,128)(2,1)}), bf16[32,56,128]{2,1,0:T(8,128)(2,1)S(1)}, u32[]{:S(2)}, u32[]{:S(2)}) async-start(bf16[32,56,128]{2,1,0:T(8,128)(2,1)} %get-tuple-element.19), calls=%async_computation.1 | async-start | bytes 917504 | tf_op jit(solution)/shard_map/all_to_all | solution.py:475
  33.6 2.4 %collective-permute-start.1 = (bf16[128,384]{1,0:T(8,128)(2,1)S(1)}, bf16[128,384]{1,0:T(8,128)(2,1)S(1)}, u32[]{:S(2)}, u32[]{:S(2)}) collective-permute-start(bf16[128,384]{1,0:T(8,128)(2,1)S(1)} %shard_map.116.after.own), channel_id=1, source_target_pairs={{0,2},{2,0},{4,6},{6,4},{8,10},{10,8},{12,14},{14,12},{16,18},{18,... | collective-permute-start | bytes 294920 | tf_op jit(solution)/shard_map/ppermute | solution.py:465
  36.1 6.2 %collective-permute-start.2 = (bf16[2,128,384]{2,1,0:T(8,128)(2,1)S(1)}, bf16[2,128,384]{2,1,0:T(8,128)(2,1)S(1)}, u32[]{:S(2)}, u32[]{:S(2)}) collective-permute-start(bf16[2,128,384]{2,1,0:T(8,128)(2,1)S(1)} %pad_maximum_fusion.here), channel_id=1, source_target_pairs={{0,1},{1,0},{2,3},{3,2},{4,5},{5,4},{6,7},{7,6},{8,9},{9,8},{10,11... | collective-permute-start | bytes 589832 | tf_op jit(solution)/shard_map/ppermute | solution.py:469
  48.1 5.5 %collective-permute-start.3 = (f32[256,128]{1,0:T(8,128)S(1)}, f32[256,128]{1,0:T(8,128)S(1)}, u32[]{:S(2)}, u32[]{:S(2)}) collective-permute-start(f32[256,128]{1,0:T(8,128)S(1)} %get-tuple-element.23), channel_id=1, source_target_pairs={{0,2},{2,0},{4,6},{6,4},{8,10},{10,8},{12,14},{14,12},{16,18},{18,... | collective-permute-start | bytes 393224 | tf_op jit(solution)/shard_map/ppermute | solution.py:465
  53.6 3.6 %collective-permute-start.4 = (bf16[256,128]{1,0:T(8,128)(2,1)S(1)}, bf16[256,128]{1,0:T(8,128)(2,1)S(1)}, u32[]{:S(2)}, u32[]{:S(2)}) collective-permute-start(bf16[256,128]{1,0:T(8,128)(2,1)S(1)} %get-tuple-element.36), channel_id=1, source_target_pairs={{0,1},{1,0},{2,3},{3,2},{4,5},{5,4},{6,7},{7,6},{8,9},{9,8},{10,11... | collective-permute-start | bytes 196616 | tf_op jit(solution)/shard_map/ppermute | solution.py:469
  60.2 14.5 %all-to-all-start.2 = ((bf16[32,24,128]{2,1,0:T(8,128)(2,1)}), bf16[32,24,128]{2,1,0:T(8,128)(2,1)S(1)}, u32[]{:S(2)}, u32[]{:S(2)}) async-start(bf16[32,24,128]{2,1,0:T(8,128)(2,1)} %shard_map.120), calls=%async_computation.2 | async-start | bytes 393216 | tf_op jit(solution)/shard_map/all_to_all | solution.py:475
  65.3 2.4 %collective-permute-start.5 = (f32[256,128]{1,0:T(8,128)S(1)}, f32[256,128]{1,0:T(8,128)S(1)}, u32[]{:S(2)}, u32[]{:S(2)}) collective-permute-start(f32[256,128]{1,0:T(8,128)S(1)} %get-tuple-element.31), channel_id=1, source_target_pairs={{0,2},{2,0},{4,6},{6,4},{8,10},{10,8},{12,14},{14,12},{16,18},{18,... | collective-permute-start | bytes 393224 | tf_op jit(solution)/shard_map/ppermute | solution.py:465
  67.8 3.5 %collective-permute-start.6 = (f32[128,128]{1,0:T(8,128)S(1)}, f32[128,128]{1,0:T(8,128)S(1)}, u32[]{:S(2)}, u32[]{:S(2)}) collective-permute-start(f32[128,128]{1,0:T(8,128)S(1)} %pad_maximum_fusion.1), channel_id=1, source_target_pairs={{0,1},{1,0},{2,3},{3,2},{4,5},{5,4},{6,7},{7,6},{8,9},{9,8},{10,11... | collective-permute-start | bytes 196616 | tf_op jit(solution)/shard_map/ppermute | solution.py:469
  75.3 3.8 %collective-permute-start.7 = (f32[24,128]{1,0:T(8,128)S(1)}, f32[24,128]{1,0:T(8,128)S(1)}, u32[]{:S(2)}, u32[]{:S(2)}) collective-permute-start(f32[24,128]{1,0:T(8,128)S(1)} %get-tuple-element.33), channel_id=1, source_target_pairs={{0,2},{2,0},{4,6},{6,4},{8,10},{10,8},{12,14},{14,12},{16,18},{18,... | collective-permute-start | bytes 36872 | tf_op jit(solution)/shard_map/ppermute | solution.py:465
  79.1 2.5 %collective-permute-start.8 = (f32[24,128]{1,0:T(8,128)S(1)}, f32[24,128]{1,0:T(8,128)S(1)}, u32[]{:S(2)}, u32[]{:S(2)}) collective-permute-start(f32[24,128]{1,0:T(8,128)S(1)} %add.11.total), channel_id=1, source_target_pairs={{0,1},{1,0},{2,3},{3,2},{4,5},{5,4},{6,7},{7,6},{8,9},{9,8},{10,11... | collective-permute-start | bytes 36872 | tf_op jit(solution)/shard_map/ppermute | solution.py:469
  82.3 14.0 %all-to-all-start.3 = ((bf16[32,24,128]{2,1,0:T(8,128)(2,1)}), bf16[32,24,128]{2,1,0:T(8,128)(2,1)S(1)}, u32[]{:S(2)}, u32[]{:S(2)}) async-start(bf16[32,24,128]{2,1,0:T(8,128)(2,1)} %shard_map.123), calls=%async_computation.3 | async-start | bytes 393216 | tf_op jit(solution)/shard_map/all_to_all | solution.py:475
  87.0 12.6 %collective-permute-start.10 = (bf16[64,128]{1,0:T(8,128)(2,1)S(1)}, bf16[64,128]{1,0:T(8,128)(2,1)S(1)}, u32[]{:S(2)}, u32[]{:S(2)}) collective-permute-start(bf16[64,128]{1,0:T(8,128)(2,1)S(1)} %shard_map.121.after), channel_id=1, source_target_pairs={{0,128},{128,0},{1,129},{129,1},{2,130},{130,2},{3,131},{131,3},{4... | collective-permute-start | bytes 49160 | tf_op jit(solution)/shard_map/ppermute | solution.py:588
  96.4 4.0 %collective-permute-start.9 = (f32[24,128]{1,0:T(8,128)S(1)}, f32[24,128]{1,0:T(8,128)S(1)}, u32[]{:S(2)}, u32[]{:S(2)}) collective-permute-start(f32[24,128]{1,0:T(8,128)S(1)} %convert_reduce_fusion.total), channel_id=1, source_target_pairs={{0,2},{2,0},{4,6},{6,4},{8,10},{10,8},{12,14},{14,12},{16,18},{18,... | collective-permute-start | bytes 36872 | tf_op jit(solution)/shard_map/ppermute | solution.py:465

commit v8 on v7

--- a/solution.py
+++ b/solution.py
@@ -188,27 +188,52 @@
     return tail[:, at : at + 1] + tail[:, at + 1 : at + 2] + tail[:, at + 2 : at + 3]
 
 
-def scaled_rows(which, packs):
+def fill_rows(which, packs, rows, turned, scale, lines):
     low_lanes = lane_index((1, 128)) < CHANNELS
-    rows, scales, levels = [], [], []
+    lines[...] = jnp.zeros_like(lines)
     for sample in range(2):
         inputs = token_rows(packs, sample, 0, 128).astype(F32)
-        turned = pltpu.roll(inputs, CHANNELS, 1)
-        level = tail_column(packs, sample, 2 + which)
-        plain, scaled = (turned, inputs) if which else (inputs, turned)
-        rows.append(jnp.where(low_lanes, plain, scaled * level))
-        scales.append(tail_column(packs, sample, which))
-        levels.append(level[0:1])
-    return jnp.concatenate(rows, axis=0), scales, levels
-
-
-def forward(which, packs, matrices, offsets, output_turned, keys_out, probs_out, velocity, crossing):
+        tokens = inputs.shape[0]
+        own = slice(sample * tokens, (sample + 1) * tokens)
+        flipped = pltpu.roll(inputs, CHANNELS, 1)
+        level = jnp.broadcast_to(tail_column(packs, sample, 2 + which), inputs.shape)
+        norm = jnp.broadcast_to(tail_column(packs, sample, which), inputs.shape)
+        plain, scaled_part = (flipped, inputs) if which else (inputs, flipped)
+        both = jnp.where(low_lanes, plain, scaled_part * level)
+        rows[own, :] = both.astype(BF16)
+        turned[:, own] = both.T.astype(BF16)
+        scale[own, :] = norm
+        lines[0:1, own] = norm.T[0:1]
+        lines[1:2, own] = level.T[0:1]
+
+
+def tokens_kernel(here, there, rows, turned, scale, lines, known, scaled, scaled_turned):
+    packs = (here, there)
+    fill_rows(1, packs, rows, turned, scale, lines)
+    low_lanes = lane_index((1, 128)) < CHANNELS
+    parts = []
+    for sample in range(2):
+        inputs = token_rows(packs, sample, 0, 128).astype(F32)
+        whole = jnp.where(low_lanes, pltpu.roll(inputs, CHANNELS, 1), inputs)
+        whole = whole * (tail_column(packs, sample, 1) * tail_column(packs, sample, 3))
+        scaled[sample] = whole.astype(BF16)
+        scaled_turned[sample] = whole.T.astype(BF16)
+        part = token_rows(packs, sample, 128, 256).astype(F32)
+        parts.append(part[:, 0:CHANNELS] + part[:, CHANNELS:])
+    known[...] = jnp.concatenate(parts, axis=1)
+
+
+def sample_level(lines, sample):
+    at = sample * (lines.shape[1] // 2)
+    return lines[1:2, at : at + 1]
+
+
+def forward(which, rows, turned, scale, lines, matrices, offsets, output_turned, keys_out, probs_out, velocity, crossing):
     heads = output_turned.shape[1] // HEAD_DIM
-    inputs, scales, levels = scaled_rows(which, packs)
-    tokens = inputs.shape[0] // 2
-    turned_scales = [jnp.broadcast_to(scale, (tokens, 128)).T[0:1] for scale in scales]
-    turned = inputs.T.astype(BF16)
-    inputs = inputs.astype(BF16)
+    tokens = rows.shape[0] // 2
+    inputs = rows[...]
+    inputs_turned = turned[...]
+    levels = [sample_level(lines, sample) for sample in range(2)]
     offset = offsets[which : which + 1, :]
     offset_turned = jnp.broadcast_to(offset, (128, offset.shape[1])).T[:, 0:1]
     units = []
@@ -217,12 +242,13 @@
         span = slice(at, at + 3 * HEAD_DIM)
         matrix = matrices[span, :]
         product = dot(inputs, matrix[HEAD_DIM : 2 * HEAD_DIM], NT)
-        product_turned = dot(matrix, turned)
+        product_turned = dot(matrix, inputs_turned)
         line = offset[:, at + HEAD_DIM : at + 2 * HEAD_DIM]
         for sample in range(2):
             own = slice(sample * tokens, (sample + 1) * tokens)
-            key = (product[own] * scales[sample] + line * levels[sample]).astype(BF16)
-            flipped = product_turned[:, own] * turned_scales[sample] + offset_turned[span] * levels[sample]
+            key = (product[own] * scale[own, :] + line * levels[sample]).astype(BF16)
+            norms = lines[0:1, own]
+            flipped = product_turned[:, own] * norms + offset_turned[span] * levels[sample]
             flipped = flipped.astype(BF16)
             if keys_out is not None:
                 keys_out[2 * head + sample] = flipped[HEAD_DIM : 2 * HEAD_DIM]
@@ -241,11 +267,25 @@
         totals[unit % 2] = term if before is None else before + term
     whole = jnp.concatenate(totals, axis=0).T
     velocity[...] = whole
-    crossing[...] = pltpu.roll(whole, CHANNELS, 1)
+    if crossing is not None:
+        crossing[...] = pltpu.roll(whole, CHANNELS, 1)
 
 
 def second_pass_kernel(
-    block, taken, here, there, output_turned, matrices, offsets, keys_turned, probs, velocity, crossing, stacked
+    block,
+    taken,
+    rows,
+    turned,
+    scale,
+    lines_in,
+    output_turned,
+    matrices,
+    offsets,
+    keys_turned,
+    probs,
+    velocity,
+    crossing,
+    stacked,
 ):
     chips = taken.shape[0]
     half = block // 2
@@ -255,8 +295,8 @@
         piece = taken[chip].astype(F32)
         at = chip * block
         folded = piece[block : block + half]
-        turned = pltpu.roll(folded, CHANNELS, 1)
-        stacked[at : at + half, :] = jnp.where(low_lanes, piece[0:half], turned)
+        moved = pltpu.roll(folded, CHANNELS, 1)
+        stacked[at : at + half, :] = jnp.where(low_lanes, piece[0:half], moved)
         stacked[at + half : at + block, :] = jnp.where(low_lanes, piece[half:block], folded)
         for which in range(2):
             line = piece[block + half + which : block + half + which + 1]
@@ -264,26 +304,61 @@
     joined = [jnp.concatenate(line, axis=1) for line in lines]
     offsets[...] = jnp.concatenate(joined + [jnp.zeros((6, offsets.shape[1]), F32)], axis=0)
     matrices[...] = stacked[...].astype(BF16)
-    forward(1, (here, there), matrices[...], offsets, output_turned, keys_turned, probs, velocity, crossing)
+    forward(
+        1,
+        rows,
+        turned,
+        scale,
+        lines_in,
+        matrices[...],
+        offsets,
+        output_turned,
+        keys_turned,
+        probs,
+        velocity,
+        crossing,
+    )
 
 
 def first_pass_kernel(
-    block, taken, matrices, offsets, here, there, output_turned, after, velocity, crossing, kept, scaled_out, rows_out, stacked
+    block,
+    taken,
+    matrices,
+    offsets,
+    here,
+    there,
+    rows_b,
+    scale_b,
+    lines,
+    output_turned,
+    after,
+    velocity,
+    kept,
+    stacked,
+    rows,
+    turned,
+    scale,
+    lines_a,
 ):
-    packs = (here, there)
+    fill_rows(0, (here, there), rows, turned, scale, lines_a)
     for chip in range(taken.shape[0]):
         stacked[chip * block : (chip + 1) * block, :] = taken[chip].astype(F32)[0:block]
-    forward(0, packs, stacked[...].astype(BF16), offsets, output_turned, None, None, velocity, crossing)
-    inputs, scales, levels = scaled_rows(1, packs)
+    forward(
+        0,
+        rows,
+        turned,
+        scale,
+        lines_a,
+        stacked[...].astype(BF16),
+        offsets,
+        output_turned,
+        None,
+        None,
+        velocity,
+        None,
+    )
+    inputs = rows_b[...]
     tokens = inputs.shape[0] // 2
-    low_lanes = lane_index((1, 128)) < CHANNELS
-    for sample in range(2):
-        plain = inputs[sample * tokens : (sample + 1) * tokens]
-        plain = jnp.where(low_lanes, plain, pltpu.roll(plain, CHANNELS, 1))
-        scaled = plain * (scales[sample] * levels[sample])
-        scaled_out[sample] = scaled.astype(BF16)
-        rows_out[sample] = scaled.T.astype(BF16)
-    inputs = inputs.astype(BF16)
     for head in range(output_turned.shape[1] // HEAD_DIM):
         for place, part in enumerate((0, 2)):
             at = (3 * head + part) * HEAD_DIM
@@ -291,8 +366,9 @@
             product = dot(inputs, matrices[at : at + HEAD_DIM, :], NT)
             line = offsets[1:2, at : at + HEAD_DIM]
             for sample in range(2):
-                own = product[sample * tokens : (sample + 1) * tokens]
-                kept[sample, :, to : to + HEAD_DIM] = (own * scales[sample] + line * levels[sample]).astype(BF16)
+                own = slice(sample * tokens, (sample + 1) * tokens)
+                value = product[own] * scale_b[own, :] + line * sample_level(lines, sample)
+                kept[sample, :, to : to + HEAD_DIM] = value.astype(BF16)
 
 
 def swap_tokens(value):
@@ -307,25 +383,30 @@
     rows,
     keys_turned,
     probs_turned,
-    here,
-    there,
+    lines,
+    known,
     vel_here,
     vel_there,
     output_turned,
+    vel_a,
     out,
+    first,
+    crossing,
     gathered,
     summed,
 ):
     critic = on_critic()
-    packs = (here, there)
+    first[...] = vel_a[...]
+    crossing[...] = pltpu.roll(vel_a[...], CHANNELS, 1)
     heads = output_turned.shape[1] // HEAD_DIM
     velocity = vel_here[...] + swap_tokens(vel_there[...].astype(F32))
-    known, levels = [], []
+    level_rows = []
     for sample in range(2):
-        part = token_rows(packs, sample, 128, 256).astype(F32)
-        known.append(part[:, 0:CHANNELS] + part[:, CHANNELS:])
-        levels.append(tail_column((here,), sample, 3)[0:1])
-    known = jnp.concatenate(known, axis=1)
+        tokens = lines.shape[1] // 2
+        level = lines[1:2, sample * tokens : (sample + 1) * tokens]
+        high = rounded(level)
+        level_rows.append(jnp.concatenate([high, level - high, jnp.zeros((14, tokens), F32)], axis=0).astype(BF16))
+    known = known[...]
     grad_velocity = jnp.where(critic, velocity - known, known)
     grads_turned = grad_velocity.T.astype(BF16)
     grads = grad_velocity.astype(BF16)
@@ -360,16 +441,14 @@
             grad_query = dot(keys_turned[unit], grad_scores).astype(BF16)
             rest = jnp.concatenate([grad_key, grad_value], axis=1).astype(BF16)
             query_term = dot(grad_query, scaled[sample])
-            rest_term = dot(rows[sample], rest)
+            rest_term = dot(jnp.concatenate([rows[sample], level_rows[sample]], axis=0), rest)
             query_total = query_term if query_total is None else query_total + query_term
             rest_total = rest_term if rest_total is None else rest_total + rest_term
-            turned_sum = jnp.sum(grad_query.astype(F32), axis=1, keepdims=True)
-            turned_sum = jnp.broadcast_to(turned_sum, (HEAD_DIM, 128)).T[0:1]
-            rest_sum = jnp.sum(rest.astype(F32), axis=0, keepdims=True)
-            ends.append(jnp.concatenate([turned_sum, rest_sum], axis=1) * levels[sample])
+            ends.append(dot(level_rows[sample], grad_query, NT))
+        ends = jnp.concatenate([ends[0] + ends[1], rest_total[128:]], axis=1)
         gathered[at : at + HEAD_DIM, :] = query_total
-        gathered[at + HEAD_DIM : at + 3 * HEAD_DIM, :] = rest_total.T
-        summed[:, at : at + 3 * HEAD_DIM] = ends[0] + ends[1]
+        gathered[at + HEAD_DIM : at + 3 * HEAD_DIM, :] = rest_total[0:128].T
+        summed[:, at : at + 3 * HEAD_DIM] = ends[0:1] + ends[1:2]
         start = columns * head // heads // block
         stop = columns * (head + 1) // heads // block
         for chip in range(start, stop):
@@ -540,6 +619,19 @@
     here = jnp.stack([own, other_core(own)])
     there = other_half(here)
 
+    rows, rows_turned, scale, lines, known, scaled, scaled_turned = call(
+        tokens_kernel,
+        (
+            struct((4 * tokens, 2 * CHANNELS), BF16),
+            struct((2 * CHANNELS, 4 * tokens), BF16),
+            struct((4 * tokens, 2 * CHANNELS), F32),
+            struct((8, 4 * tokens), F32),
+            struct((2 * tokens, 2 * CHANNELS), F32),
+            struct((2, 2 * tokens, 2 * CHANNELS), BF16),
+            struct((2, 2 * CHANNELS, 2 * tokens), BF16),
+        ),
+        (here, there),
+    )
     taken = between_chips(matrices)
     whole, offsets, keys_turned, probs, vel_b, vel_crossing = call(
         functools.partial(second_pass_kernel, block),
@@ -551,33 +643,37 @@
             struct((2 * tokens, 2 * CHANNELS), F32),
             struct((2 * tokens, 2 * CHANNELS), F32),
         ),
-        (taken, here, there, output_turned),
+        (taken, rows, rows_turned, scale, lines, output_turned),
         scratch=[pltpu.VMEM((columns, 2 * CHANNELS), F32)],
     )
     vel_here = vel_b + other_core(vel_crossing)
     vel_there = other_half(vel_here.astype(BF16))
-    vel_a, vel_a_crossing, kept, scaled, rows = call(
+    vel_a, kept = call(
         functools.partial(first_pass_kernel, block),
+        (struct((2 * tokens, 2 * CHANNELS), F32), struct((2, 2 * tokens, 2 * heads * HEAD_DIM), BF16)),
+        (taken, whole, offsets, here, there, rows, scale, lines, output_turned),
+        scratch=[
+            pltpu.VMEM((columns, 2 * CHANNELS), F32),
+            pltpu.VMEM((4 * tokens, 2 * CHANNELS), BF16),
+            pltpu.VMEM((2 * CHANNELS, 4 * tokens), BF16),
+            pltpu.VMEM((4 * tokens, 2 * CHANNELS), F32),
+            pltpu.VMEM((8, 4 * tokens), F32),
+        ],
+        flops=4 * 10**9,
+        after=(vel_here,),
+    )
+    products, vel_a, vel_crossing = call(
+        functools.partial(backward_kernel, block),
         (
+            struct((chips, folded, 128), BF16),
             struct((2 * tokens, 2 * CHANNELS), F32),
             struct((2 * tokens, 2 * CHANNELS), F32),
-            struct((2, 2 * tokens, 2 * heads * HEAD_DIM), BF16),
-            struct((2, 2 * tokens, 2 * CHANNELS), BF16),
-            struct((2, 2 * CHANNELS, 2 * tokens), BF16),
         ),
-        (taken, whole, offsets, here, there, output_turned),
-        scratch=[pltpu.VMEM((columns, 2 * CHANNELS), F32)],
-        flops=4 * 10**9,
-        after=(vel_here,),
-    )
-    products = call(
-        functools.partial(backward_kernel, block),
-        struct((chips, folded, 128), BF16),
-        (kept, scaled, rows, keys_turned, probs, here, there, vel_here, vel_there, output_turned),
+        (kept, scaled, scaled_turned, keys_turned, probs, lines, known, vel_here, vel_there, output_turned, vel_a),
         scratch=[pltpu.VMEM((columns + 2 * folded, 128), F32), pltpu.VMEM((1, columns), F32)],
     )
 
-    vel_a_here = vel_a + other_core(vel_a_crossing)
+    vel_a_here = vel_a + other_core(vel_crossing)
     both_there = other_half(jnp.concatenate([vel_a_here[tokens:, :CHANNELS], vel_here[tokens:, :CHANNELS]], axis=1))
     payload = call(
         payload_kernel,
@@ -588,15 +684,15 @@
     crossed = lax.ppermute(payload, "role", [(0, 1), (1, 0)])
 
     samples = devices * base_latents.shape[1]
-    lines = width // 128
+    height = width // 128
     kept_half, sent_half = call(
         functools.partial(closing_kernel, block, 1.0 / (samples * 2 * tokens)),
-        (struct((lines, 128), F32), struct((lines, 128), F32)),
+        (struct((height, 128), F32), struct((height, 128), F32)),
         (between_chips(products), own_columns, embed),
         after=(payload,),
     )
     total = kept_half + other_core(sent_half)
-    spread = call(spread_kernel, struct((chips, lines, 128), BF16), (total, other_half(total)))
+    spread = call(spread_kernel, struct((chips, height, 128), BF16), (total, other_half(total)))
     total = jnp.sum(between_chips(spread).astype(F32), axis=0)
     mod_grads, crossed = call(
         join_kernel,

time: 102 us -> 101 us (level)
  waiting for transfers between devices: 33.2 us -> 31.8 us
    all_to_all x4, waiting for transfers between devices: 20.1 us -> 18.7 us  [between_chips(): lax.all_to_all(value, 'fsdp', 0, 0, tiled=True, axis_index_groups=groups)]
    pallas_call x12 -> x13, Pallas kernels: 13.2 us -> 14.2 us  [call(): pl.pallas_call(kernel, out_shape=out_shapes, in_specs=specs, out_specs=ja...]
  transfers between devices with their start and end apart: 15 -> 15, of which waited for: 13 -> 13; matrix products, arithmetic and copies ran while one was open for 1% -> 1% of each run, Pallas kernels for 3% -> 5%
where the time goes in v8:
time: 101 us
  starting transfers between devices  51 us (50%)
  waiting for transfers between devices  31.8 us (31%)
  Pallas kernels  14.2 us (14%)
  between operations  2.14 us (2%)
  local copies, waits for them, and re-layouts  1.43 us (1%)
    all_to_all x4, starting transfers between devices, between_chips(): lax.all_to_all(value, 'fsdp', 0, 0, tiled=True, axis_index_groups=groups)  25.8 us
    all_to_all x4, waiting for transfers between devices, between_chips(): lax.all_to_all(value, 'fsdp', 0, 0, tiled=True, axis_index_groups=groups)  18.7 us
    ppermute x6, starting transfers between devices, other_core(): lax.ppermute(value, 'fsdp', [(i, i ^ 1) for i in range(lax.axis_size('fsd...  16.9 us
    pallas_call x13, Pallas kernels, call(): pl.pallas_call(kernel, out_shape=out_shapes, in_specs=specs, out_specs=ja...  14.2 us
    ppermute x4, waiting for transfers between devices, other_half(): return lax.ppermute(value, 'seq', [(0, 1), (1, 0)])  8.38 us
    ppermute x4, starting transfers between devices, other_half(): return lax.ppermute(value, 'seq', [(0, 1), (1, 0)])  5.43 us
    ppermute x6, waiting for transfers between devices, other_core(): lax.ppermute(value, 'fsdp', [(i, i ^ 1) for i in range(lax.axis_size('fsd...  4.75 us
    ppermute x1, starting transfers between devices, per_device(): crossed = lax.ppermute(payload, 'role', [(0, 1), (1, 0)])  3 us
  transfers between devices with their start and end apart: 15, of which 13 were waited for; matrix products, arithmetic and copies ran while one was open for 1% of the time, Pallas kernels for 5%

profile of v8, /device:TPU:1, one launch (start us, length us, event | category | flops | bytes accessed | tf_op | source)
XLA Modules:
  0.0 100.8 jit_solution(16475077150986292222)
XLA Ops:
  0.6 0.0 copy-start
  0.6 3.3 %collective-permute-start = (bf16[48,2304]{1,0:T(8,128)(2,1)}, bf16[48,2304]{1,0:T(8,128)(2,1)S(1)}, u32[]{:S(2)}, u32[]{:S(2)}) collective-permute-start(bf16[48,2304]{1,0:T(8,128)(2,1)} %bitcast.20), channel_id=1, source_target_pairs={{0,2},{2,0},{4,6},{6,4},{8,10},{10,8},{12,14},{14,12},{16,18},{18,... | collective-permute-start | bytes 663560 | tf_op jit(solution)/shard_map/ppermute | solution.py:544
  4.0 0.0 copy-start.1
  4.0 0.9 copy-done.1
  4.9 0.0 copy-start.4
  4.9 0.0 copy-start.5
  4.9 0.0 copy-start.6
  4.9 0.0 copy-start.7
  4.9 0.0 copy-start.2
  4.9 0.2 shard_map.113.own
  5.1 0.2 collective-permute-done.received
  5.3 1.0 shard_map.114.after
  6.3 9.3 %all-to-all-start = ((bf16[32,32,128]{2,1,0:T(8,128)(2,1)}), bf16[32,32,128]{2,1,0:T(8,128)(2,1)S(1)}, u32[]{:S(2)}, u32[]{:S(2)}) async-start(bf16[32,32,128]{2,1,0:T(8,128)(2,1)} %shard_map.114.after), calls=%async_computation | async-start | bytes 524288 | tf_op jit(solution)/shard_map/all_to_all | solution.py:554
  16.9 0.0 copy-done.4
  16.9 0.1 copy.12
  17.0 0.0 copy-done.5
  17.0 0.1 copy.13
  17.1 0.0 copy-done.6
  17.1 0.1 copy.14
  17.3 0.0 copy-done.7
  17.3 0.1 copy.15
  17.4 0.0 copy-done
  17.4 0.0 copy-done.2
  17.4 0.3 shard_map.115.stack
  17.7 0.7 shard_map.116.after.own
  18.4 0.0 copy-start.3
  18.4 6.9 %all-to-all-done.taken = bf16[32,32,128]{2,1,0:T(8,128)(2,1)S(1)} async-done(((bf16[32,32,128]{2,1,0:T(8,128)(2,1)}), bf16[32,32,128]{2,1,0:T(8,128)(2,1)S(1)}, u32[]{:S(2)}, u32[]{:S(2)}) %all-to-all-start) | async-done | bytes 262176 | tf_op jit(solution)/shard_map/all_to_all | solution.py:554
  25.3 1.6 %shard_map.117 = (bf16[32,56,128]{2,1,0:T(8,128)(2,1)}, bf16[40,3072]{1,0:T(8,128)(2,1)S(1)}) custom-call(bf16[32,32,128]{2,1,0:T(8,128)(2,1)S(1)} %all-to-all-done.taken, bf16[256,3072]{1,0:T(8,128)(2,1)S(1)} %shard_map.115.stack, bf16[128,384]{1,0:T(8,128)(2,1)S(1)} %shard_map.116.after.own), custom_call_target="tpu_custom_call" | custom-call | tf_op jit(solution)/shard_map/pallas_call | solution.py:528
  26.9 6.7 %all-to-all-start.1 = ((bf16[32,56,128]{2,1,0:T(8,128)(2,1)}), bf16[32,56,128]{2,1,0:T(8,128)(2,1)S(1)}, u32[]{:S(2)}, u32[]{:S(2)}) async-start(bf16[32,56,128]{2,1,0:T(8,128)(2,1)} %get-tuple-element.26), calls=%async_computation.1 | async-start | bytes 917504 | tf_op jit(solution)/shard_map/all_to_all | solution.py:554
  33.6 1.5 %collective-permute-start.1 = (bf16[128,384]{1,0:T(8,128)(2,1)S(1)}, bf16[128,384]{1,0:T(8,128)(2,1)S(1)}, u32[]{:S(2)}, u32[]{:S(2)}) collective-permute-start(bf16[128,384]{1,0:T(8,128)(2,1)S(1)} %shard_map.116.after.own), channel_id=1, source_target_pairs={{0,2},{2,0},{4,6},{6,4},{8,10},{10,8},{12,14},{14,12},{16,18},{18,... | collective-permute-start | bytes 294920 | tf_op jit(solution)/shard_map/ppermute | solution.py:544
  35.1 0.9 collective-permute-done.1
  36.1 1.4 %collective-permute-start.2 = (bf16[2,128,384]{2,1,0:T(8,128)(2,1)S(1)}, bf16[2,128,384]{2,1,0:T(8,128)(2,1)S(1)}, u32[]{:S(2)}, u32[]{:S(2)}) collective-permute-start(bf16[2,128,384]{2,1,0:T(8,128)(2,1)S(1)} %pad_maximum_fusion.here), channel_id=1, source_target_pairs={{0,1},{1,0},{2,3},{3,2},{4,5},{5,4},{6,7},{7,6},{8,9},{9,8},{10,11... | collective-permute-start | bytes 589832 | tf_op jit(solution)/shard_map/ppermute | solution.py:548
  37.4 0.0 copy-done.3
  37.5 4.8 %collective-permute-done.2.there = bf16[2,128,384]{2,1,0:T(8,128)(2,1)S(1)} collective-permute-done((bf16[2,128,384]{2,1,0:T(8,128)(2,1)S(1)}, bf16[2,128,384]{2,1,0:T(8,128)(2,1)S(1)}, u32[]{:S(2)}, u32[]{:S(2)}) %collective-permute-start.2) | collective-permute-done | bytes 196640 | tf_op jit(solution)/shard_map/ppermute | solution.py:548
  42.3 1.4 %shard_map.118 = (bf16[512,128]{1,0:T(8,128)(2,1)S(1)}, bf16[128,512]{1,0:T(8,128)(2,1)S(1)}, f32[512,128]{1,0:T(8,128)S(1)}, f32[8,512]{1,0:T(8,128)S(1)}, f32[...) custom-call(bf16[2,128,384]{2,1,0:T(8,128)(2,1)S(1)} %pad_maximum_fusion.here, ...), custom_call_target="tpu_custom_call" | custom-call | tf_op jit(solution)/shard_map/pallas_call | solution.py:528
  43.7 2.1 %all-to-all-done.1.taken = bf16[32,56,128]{2,1,0:T(8,128)(2,1)S(1)} async-done(((bf16[32,56,128]{2,1,0:T(8,128)(2,1)}), bf16[32,56,128]{2,1,0:T(8,128)(2,1)S(1)}, u32[]{:S(2)}, u32[]{:S(2)}) %all-to-all-start.1) | async-done | bytes 458784 | tf_op jit(solution)/shard_map/all_to_all | solution.py:554
  45.8 1.9 %shard_map.119 = (bf16[1152,128]{1,0:T(8,128)(2,1)S(1)}, f32[8,1152]{1,0:T(8,128)S(1)}, bf16[6,128,256]{2,1,0:T(8,128)(2,1)S(1)}, f32[6,256,256]{2,1,0:T(8,128)S...) custom-call(bf16[32,56,128]{2,1,0:T(8,128)(2,1)S(1)} %all-to-all-done.1.taken, ...), custom_call_target="tpu_custom_call" | custom-call | tf_op jit(solution)/shard_map/pallas_call | solution.py:528
  47.7 4.5 %collective-permute-start.3 = (f32[256,128]{1,0:T(8,128)S(1)}, f32[256,128]{1,0:T(8,128)S(1)}, u32[]{:S(2)}, u32[]{:S(2)}) collective-permute-start(f32[256,128]{1,0:T(8,128)S(1)} %get-tuple-element.34), channel_id=1, source_target_pairs={{0,2},{2,0},{4,6},{6,4},{8,10},{10,8},{12,14},{14,12},{16,18},{18,... | collective-permute-start | bytes 393224 | tf_op jit(solution)/shard_map/ppermute | solution.py:544
  52.2 1.0 collective-permute-done.3
  53.2 1.6 %collective-permute-start.4 = (bf16[256,128]{1,0:T(8,128)(2,1)S(1)}, bf16[256,128]{1,0:T(8,128)(2,1)S(1)}, u32[]{:S(2)}, u32[]{:S(2)}) collective-permute-start(bf16[256,128]{1,0:T(8,128)(2,1)S(1)} %get-tuple-element.50), channel_id=1, source_target_pairs={{0,1},{1,0},{2,3},{3,2},{4,5},{5,4},{6,7},{7,6},{8,9},{9,8},{10,11... | collective-permute-start | bytes 196616 | tf_op jit(solution)/shard_map/ppermute | solution.py:548
  54.8 2.3 %shard_map.120 = (f32[256,128]{1,0:T(8,128)S(1)}, bf16[2,256,768]{2,1,0:T(8,128)(2,1)S(1)}) custom-call(bf16[32,56,128]{2,1,0:T(8,128)(2,1)S(1)} %all-to-all-done.1.taken, bf16[1152,128]{1,0:T(8,128)(2,1)S(1)} %get-tuple-element.31.matrices, f32[8,1152]{1,0:T(8,128)S(1)} %get-tuple-element.32.offsets, bf16[2,128,384]{2,1,0:T(8,128)(2,1)S(1)} %pad_maximum_fusion.here, ...), custom_call_target="tpu_custom_call" | custom-call | flops 4000000000 | tf_op jit(solution)/shard_map/pallas_call | solution.py:528
  57.0 0.0 collective-permute-done.4.vel_there
  57.1 2.9 %shard_map.121 = (bf16[32,24,128]{2,1,0:T(8,128)(2,1)}, f32[256,128]{1,0:T(8,128)S(1)}, f32[256,128]{1,0:T(8,128)S(1)}) custom-call(bf16[2,256,768]{2,1,0:T(8,128)(2,1)S(1)} %get-tuple-element.35.kept, bf16[2,256,128]{2,1,0:T(8,128)(2,1)S(1)} %get-tuple-element.36.scaled, bf16[2,128,256]{2,1,0:T(8,128)(2,1)S(1)} %get-tuple-element.37.rows, ...), custom_call_target="tpu_custom_call" | custom-call | tf_op jit(solution)/shard_map/pallas_call | solution.py:528
  59.9 5.1 %all-to-all-start.2 = ((bf16[32,24,128]{2,1,0:T(8,128)(2,1)}), bf16[32,24,128]{2,1,0:T(8,128)(2,1)S(1)}, u32[]{:S(2)}, u32[]{:S(2)}) async-start(bf16[32,24,128]{2,1,0:T(8,128)(2,1)} %get-tuple-element.42), calls=%async_computation.2 | async-start | bytes 393216 | tf_op jit(solution)/shard_map/all_to_all | solution.py:554
  65.0 1.4 %collective-permute-start.5 = (f32[256,128]{1,0:T(8,128)S(1)}, f32[256,128]{1,0:T(8,128)S(1)}, u32[]{:S(2)}, u32[]{:S(2)}) collective-permute-start(f32[256,128]{1,0:T(8,128)S(1)} %get-tuple-element.45), channel_id=1, source_target_pairs={{0,2},{2,0},{4,6},{6,4},{8,10},{10,8},{12,14},{14,12},{16,18},{18,... | collective-permute-start | bytes 393224 | tf_op jit(solution)/shard_map/ppermute | solution.py:544
  66.4 1.0 collective-permute-done.5
  67.5 0.1 pad_maximum_fusion.1
  67.5 1.4 %collective-permute-start.6 = (f32[128,128]{1,0:T(8,128)S(1)}, f32[128,128]{1,0:T(8,128)S(1)}, u32[]{:S(2)}, u32[]{:S(2)}) collective-permute-start(f32[128,128]{1,0:T(8,128)S(1)} %pad_maximum_fusion.1), channel_id=1, source_target_pairs={{0,1},{1,0},{2,3},{3,2},{4,5},{5,4},{6,7},{7,6},{8,9},{9,8},{10,11... | collective-permute-start | bytes 196616 | tf_op jit(solution)/shard_map/ppermute | solution.py:548
  68.9 2.1 %collective-permute-done.6.there = f32[128,128]{1,0:T(8,128)S(1)} collective-permute-done((f32[128,128]{1,0:T(8,128)S(1)}, f32[128,128]{1,0:T(8,128)S(1)}, u32[]{:S(2)}, u32[]{:S(2)}) %collective-permute-start.6) | collective-permute-done | bytes 65568 | tf_op jit(solution)/shard_map/ppermute | solution.py:548
  71.0 0.1 shard_map.122.after
  71.2 3.3 %all-to-all-done.2.taken = bf16[32,24,128]{2,1,0:T(8,128)(2,1)S(1)} async-done(((bf16[32,24,128]{2,1,0:T(8,128)(2,1)}), bf16[32,24,128]{2,1,0:T(8,128)(2,1)S(1)}, u32[]{:S(2)}, u32[]{:S(2)}) %all-to-all-start.2) | async-done | bytes 196640 | tf_op jit(solution)/shard_map/all_to_all | solution.py:554
  74.4 0.6 shard_map.123
  75.0 2.9 %collective-permute-start.7 = (f32[24,128]{1,0:T(8,128)S(1)}, f32[24,128]{1,0:T(8,128)S(1)}, u32[]{:S(2)}, u32[]{:S(2)}) collective-permute-start(f32[24,128]{1,0:T(8,128)S(1)} %get-tuple-element.47), channel_id=1, source_target_pairs={{0,2},{2,0},{4,6},{6,4},{8,10},{10,8},{12,14},{14,12},{16,18},{18,... | collective-permute-start | bytes 36872 | tf_op jit(solution)/shard_map/ppermute | solution.py:544
  78.0 0.8 collective-permute-done.7
  78.8 1.1 %collective-permute-start.8 = (f32[24,128]{1,0:T(8,128)S(1)}, f32[24,128]{1,0:T(8,128)S(1)}, u32[]{:S(2)}, u32[]{:S(2)}) collective-permute-start(f32[24,128]{1,0:T(8,128)S(1)} %add.11.total), channel_id=1, source_target_pairs={{0,1},{1,0},{2,3},{3,2},{4,5},{5,4},{6,7},{7,6},{8,9},{9,8},{10,11... | collective-permute-start | bytes 36872 | tf_op jit(solution)/shard_map/ppermute | solution.py:548
  79.9 1.5 %collective-permute-done.8.other = f32[24,128]{1,0:T(8,128)S(1)} collective-permute-done((f32[24,128]{1,0:T(8,128)S(1)}, f32[24,128]{1,0:T(8,128)S(1)}, u32[]{:S(2)}, u32[]{:S(2)}) %collective-permute-start.8) | collective-permute-done | bytes 12320 | tf_op jit(solution)/shard_map/ppermute | solution.py:548
  81.3 0.7 shard_map.124
  82.0 4.6 %all-to-all-start.3 = ((bf16[32,24,128]{2,1,0:T(8,128)(2,1)}), bf16[32,24,128]{2,1,0:T(8,128)(2,1)S(1)}, u32[]{:S(2)}, u32[]{:S(2)}) async-start(bf16[32,24,128]{2,1,0:T(8,128)(2,1)} %shard_map.124), calls=%async_computation.3 | async-start | bytes 393216 | tf_op jit(solution)/shard_map/all_to_all | solution.py:554
  86.7 3.0 %collective-permute-start.10 = (bf16[64,128]{1,0:T(8,128)(2,1)S(1)}, bf16[64,128]{1,0:T(8,128)(2,1)S(1)}, u32[]{:S(2)}, u32[]{:S(2)}) collective-permute-start(bf16[64,128]{1,0:T(8,128)(2,1)S(1)} %shard_map.122.after), channel_id=1, source_target_pairs={{0,128},{128,0},{1,129},{129,1},{2,130},{130,2},{3,131},{131,3},{4... | collective-permute-start | bytes 49160 | tf_op jit(solution)/shard_map/ppermute | solution.py:684
  89.7 6.4 %all-to-all-done.3 = bf16[32,24,128]{2,1,0:T(8,128)(2,1)S(1)} async-done(((bf16[32,24,128]{2,1,0:T(8,128)(2,1)}), bf16[32,24,128]{2,1,0:T(8,128)(2,1)S(1)}, u32[]{:S(2)}, u32[]{:S(2)}) %all-to-all-start.3) | async-done | bytes 196640 | tf_op jit(solution)/shard_map/all_to_all | solution.py:554
  96.1 3.2 %collective-permute-start.9 = (f32[24,128]{1,0:T(8,128)S(1)}, f32[24,128]{1,0:T(8,128)S(1)}, u32[]{:S(2)}, u32[]{:S(2)}) collective-permute-start(f32[24,128]{1,0:T(8,128)S(1)} %convert_reduce_fusion.total), channel_id=1, source_target_pairs={{0,2},{2,0},{4,6},{6,4},{8,10},{10,8},{12,14},{14,12},{16,18},{18,... | collective-permute-start | bytes 36872 | tf_op jit(solution)/shard_map/ppermute | solution.py:544
  99.3 0.0 collective-permute-done.10.crossed
  99.3 0.8 collective-permute-done.9.near
  100.2 0.6 shard_map.125
  (8 shorter events, 0.1 us)
Async XLA Ops:
  0.6 16.8 %copy-start = (bf16[1,64,3072]{2,1,0:T(8,128)(2,1)S(1)}, bf16[1,64,3072]{2,1,0:T(8,128)(2,1)}, u32[]{:S(2)}) copy-start(bf16[1,64,3072]{2,1,0:T(8,128)(2,1)} %param.16) | copy-start | bytes 1179652
  0.6 4.6 %collective-permute-start = (bf16[48,2304]{1,0:T(8,128)(2,1)}, bf16[48,2304]{1,0:T(8,128)(2,1)S(1)}, u32[]{:S(2)}, u32[]{:S(2)}) collective-permute-start(bf16[48,2304]{1,0:T(8,128)(2,1)} %bitcast.20), channel_id=1, source_target_pairs={{0,2},{2,0},{4,6},{6,4},{8,10},{10,8},{12,14},{14,12},{16,18},{18,... | collective-permute-start | bytes 663560 | tf_op jit(solution)/shard_map/ppermute | solution.py:544
  4.0 0.9 copy-start.1
  4.9 12.0 %copy-start.4 = (bf16[1,1,128,64]{2,3,1,0:T(8,128)(2,1)S(1)}, bf16[1,1,128,64]{2,3,1,0:T(8,128)(2,1)}, u32[]{:S(2)}) copy-start(bf16[1,1,128,64]{2,3,1,0:T(8,128)(2,1)} %param.10) | copy-start | bytes 49156
  4.9 12.1 %copy-start.5 = (bf16[1,1,128,64]{2,3,1,0:T(8,128)(2,1)S(1)}, bf16[1,1,128,64]{2,3,1,0:T(8,128)(2,1)}, u32[]{:S(2)}) copy-start(bf16[1,1,128,64]{2,3,1,0:T(8,128)(2,1)} %param.11) | copy-start | bytes 49156
  4.9 12.2 %copy-start.6 = (bf16[1,1,128,64]{2,3,1,0:T(8,128)(2,1)S(1)}, bf16[1,1,128,64]{2,3,1,0:T(8,128)(2,1)}, u32[]{:S(2)}) copy-start(bf16[1,1,128,64]{2,3,1,0:T(8,128)(2,1)} %param.13) | copy-start | bytes 49156
  4.9 12.4 %copy-start.7 = (bf16[1,1,128,64]{2,3,1,0:T(8,128)(2,1)S(1)}, bf16[1,1,128,64]{2,3,1,0:T(8,128)(2,1)}, u32[]{:S(2)}) copy-start(bf16[1,1,128,64]{2,3,1,0:T(8,128)(2,1)} %param.15) | copy-start | bytes 49156
  4.9 12.5 %copy-start.2 = (f32[1,2,2,3072]{3,2,1,0:T(2,128)S(1)}, f32[1,2,2,3072]{3,2,1,0:T(2,128)}, u32[]{:S(2)}) copy-start(f32[1,2,2,3072]{3,2,1,0:T(2,128)} %param.19) | copy-start | bytes 147460
  6.3 19.0 %all-to-all-start = ((bf16[32,32,128]{2,1,0:T(8,128)(2,1)}), bf16[32,32,128]{2,1,0:T(8,128)(2,1)S(1)}, u32[]{:S(2)}, u32[]{:S(2)}) async-start(bf16[32,32,128]{2,1,0:T(8,128)(2,1)} %shard_map.114.after), calls=%async_computation | async-start | bytes 524288 | tf_op jit(solution)/shard_map/all_to_all | solution.py:554
  18.4 19.1 %copy-start.3 = (bf16[1,768,64]{1,2,0:T(8,128)(2,1)S(1)}, bf16[1,768,64]{1,2,0:T(8,128)(2,1)}, u32[]{:S(2)}) copy-start(bf16[1,768,64]{1,2,0:T(8,128)(2,1)} %param.18) | copy-start | bytes 294916
  26.9 19.0 %all-to-all-start.1 = ((bf16[32,56,128]{2,1,0:T(8,128)(2,1)}), bf16[32,56,128]{2,1,0:T(8,128)(2,1)S(1)}, u32[]{:S(2)}, u32[]{:S(2)}) async-start(bf16[32,56,128]{2,1,0:T(8,128)(2,1)} %get-tuple-element.26), calls=%async_computation.1 | async-start | bytes 917504 | tf_op jit(solution)/shard_map/all_to_all | solution.py:554
  33.6 2.4 %collective-permute-start.1 = (bf16[128,384]{1,0:T(8,128)(2,1)S(1)}, bf16[128,384]{1,0:T(8,128)(2,1)S(1)}, u32[]{:S(2)}, u32[]{:S(2)}) collective-permute-start(bf16[128,384]{1,0:T(8,128)(2,1)S(1)} %shard_map.116.after.own), channel_id=1, source_target_pairs={{0,2},{2,0},{4,6},{6,4},{8,10},{10,8},{12,14},{14,12},{16,18},{18,... | collective-permute-start | bytes 294920 | tf_op jit(solution)/shard_map/ppermute | solution.py:544
  36.1 6.2 %collective-permute-start.2 = (bf16[2,128,384]{2,1,0:T(8,128)(2,1)S(1)}, bf16[2,128,384]{2,1,0:T(8,128)(2,1)S(1)}, u32[]{:S(2)}, u32[]{:S(2)}) collective-permute-start(bf16[2,128,384]{2,1,0:T(8,128)(2,1)S(1)} %pad_maximum_fusion.here), channel_id=1, source_target_pairs={{0,1},{1,0},{2,3},{3,2},{4,5},{5,4},{6,7},{7,6},{8,9},{9,8},{10,11... | collective-permute-start | bytes 589832 | tf_op jit(solution)/shard_map/ppermute | solution.py:548
  47.7 5.5 %collective-permute-start.3 = (f32[256,128]{1,0:T(8,128)S(1)}, f32[256,128]{1,0:T(8,128)S(1)}, u32[]{:S(2)}, u32[]{:S(2)}) collective-permute-start(f32[256,128]{1,0:T(8,128)S(1)} %get-tuple-element.34), channel_id=1, source_target_pairs={{0,2},{2,0},{4,6},{6,4},{8,10},{10,8},{12,14},{14,12},{16,18},{18,... | collective-permute-start | bytes 393224 | tf_op jit(solution)/shard_map/ppermute | solution.py:544
  53.2 3.8 %collective-permute-start.4 = (bf16[256,128]{1,0:T(8,128)(2,1)S(1)}, bf16[256,128]{1,0:T(8,128)(2,1)S(1)}, u32[]{:S(2)}, u32[]{:S(2)}) collective-permute-start(bf16[256,128]{1,0:T(8,128)(2,1)S(1)} %get-tuple-element.50), channel_id=1, source_target_pairs={{0,1},{1,0},{2,3},{3,2},{4,5},{5,4},{6,7},{7,6},{8,9},{9,8},{10,11... | collective-permute-start | bytes 196616 | tf_op jit(solution)/shard_map/ppermute | solution.py:548
  59.9 14.5 %all-to-all-start.2 = ((bf16[32,24,128]{2,1,0:T(8,128)(2,1)}), bf16[32,24,128]{2,1,0:T(8,128)(2,1)S(1)}, u32[]{:S(2)}, u32[]{:S(2)}) async-start(bf16[32,24,128]{2,1,0:T(8,128)(2,1)} %get-tuple-element.42), calls=%async_computation.2 | async-start | bytes 393216 | tf_op jit(solution)/shard_map/all_to_all | solution.py:554
  65.0 2.4 %collective-permute-start.5 = (f32[256,128]{1,0:T(8,128)S(1)}, f32[256,128]{1,0:T(8,128)S(1)}, u32[]{:S(2)}, u32[]{:S(2)}) collective-permute-start(f32[256,128]{1,0:T(8,128)S(1)} %get-tuple-element.45), channel_id=1, source_target_pairs={{0,2},{2,0},{4,6},{6,4},{8,10},{10,8},{12,14},{14,12},{16,18},{18,... | collective-permute-start | bytes 393224 | tf_op jit(solution)/shard_map/ppermute | solution.py:544
  67.5 3.5 %collective-permute-start.6 = (f32[128,128]{1,0:T(8,128)S(1)}, f32[128,128]{1,0:T(8,128)S(1)}, u32[]{:S(2)}, u32[]{:S(2)}) collective-permute-start(f32[128,128]{1,0:T(8,128)S(1)} %pad_maximum_fusion.1), channel_id=1, source_target_pairs={{0,1},{1,0},{2,3},{3,2},{4,5},{5,4},{6,7},{7,6},{8,9},{9,8},{10,11... | collective-permute-start | bytes 196616 | tf_op jit(solution)/shard_map/ppermute | solution.py:548
  75.0 3.8 %collective-permute-start.7 = (f32[24,128]{1,0:T(8,128)S(1)}, f32[24,128]{1,0:T(8,128)S(1)}, u32[]{:S(2)}, u32[]{:S(2)}) collective-permute-start(f32[24,128]{1,0:T(8,128)S(1)} %get-tuple-element.47), channel_id=1, source_target_pairs={{0,2},{2,0},{4,6},{6,4},{8,10},{10,8},{12,14},{14,12},{16,18},{18,... | collective-permute-start | bytes 36872 | tf_op jit(solution)/shard_map/ppermute | solution.py:544
  78.8 2.5 %collective-permute-start.8 = (f32[24,128]{1,0:T(8,128)S(1)}, f32[24,128]{1,0:T(8,128)S(1)}, u32[]{:S(2)}, u32[]{:S(2)}) collective-permute-start(f32[24,128]{1,0:T(8,128)S(1)} %add.11.total), channel_id=1, source_target_pairs={{0,1},{1,0},{2,3},{3,2},{4,5},{5,4},{6,7},{7,6},{8,9},{9,8},{10,11... | collective-permute-start | bytes 36872 | tf_op jit(solution)/shard_map/ppermute | solution.py:548
  82.0 14.0 %all-to-all-start.3 = ((bf16[32,24,128]{2,1,0:T(8,128)(2,1)}), bf16[32,24,128]{2,1,0:T(8,128)(2,1)S(1)}, u32[]{:S(2)}, u32[]{:S(2)}) async-start(bf16[32,24,128]{2,1,0:T(8,128)(2,1)} %shard_map.124), calls=%async_computation.3 | async-start | bytes 393216 | tf_op jit(solution)/shard_map/all_to_all | solution.py:554
  86.7 12.6 %collective-permute-start.10 = (bf16[64,128]{1,0:T(8,128)(2,1)S(1)}, bf16[64,128]{1,0:T(8,128)(2,1)S(1)}, u32[]{:S(2)}, u32[]{:S(2)}) collective-permute-start(bf16[64,128]{1,0:T(8,128)(2,1)S(1)} %shard_map.122.after), channel_id=1, source_target_pairs={{0,128},{128,0},{1,129},{129,1},{2,130},{130,2},{3,131},{131,3},{4... | collective-permute-start | bytes 49160 | tf_op jit(solution)/shard_map/ppermute | solution.py:684
  96.1 4.0 %collective-permute-start.9 = (f32[24,128]{1,0:T(8,128)S(1)}, f32[24,128]{1,0:T(8,128)S(1)}, u32[]{:S(2)}, u32[]{:S(2)}) collective-permute-start(f32[24,128]{1,0:T(8,128)S(1)} %convert_reduce_fusion.total), channel_id=1, source_target_pairs={{0,2},{2,0},{4,6},{6,4},{8,10},{10,8},{12,14},{14,12},{16,18},{18,... | collective-permute-start | bytes 36872 | tf_op jit(solution)/shard_map/ppermute | solution.py:544

commit v9 on v8

--- a/solution.py
+++ b/solution.py
@@ -463,7 +463,7 @@
             out[chip] = jnp.where(row < half, piece, tail).astype(BF16)
 
 
-def closing_kernel(block, factor, taken, weight, embed, after, kept, sent):
+def closing_kernel(block, factor, taken, weight, embed, kept, sent):
     second = on_second_core()
     total = taken[0].astype(F32)
     for chip in range(1, taken.shape[0]):
@@ -494,12 +494,13 @@
     sent[...] = jnp.where(second, sides[0], sides[1])
 
 
-def payload_kernel(noise_levels, own, a_here, b_here, there, out):
+def payload_kernel(noise_levels, own, vel_a, vel_b, here, there):
     tokens = own.shape[0]
-    own_a = a_here[0:tokens, 0:CHANNELS] + there[:, 0:CHANNELS]
-    own_b = b_here[0:tokens, 0:CHANNELS] + there[:, CHANNELS:]
-    sample = own[:, 0:CHANNELS].astype(F32) - noise_levels[0, 0] * own_a
-    out[...] = jnp.where(on_critic(), own_b - own_a, sample).T.astype(BF16)
+    velocity = vel_a[:, 0:CHANNELS]
+    part = jnp.where(on_critic(), vel_b[:, 0:CHANNELS] - velocity, -noise_levels[0, 0] * velocity)
+    sample = jnp.where(on_critic(), 0.0, own[:, 0:CHANNELS].astype(F32))
+    here[...] = (sample + part[0:tokens]).T
+    there[...] = part[tokens:].T
 
 
 def spread_kernel(total, other, out):
@@ -508,8 +509,8 @@
         out[chip] = line
 
 
-def join_kernel(total, near, crossed, out, crossed_out):
-    crossed_out[...] = crossed[...]
+def join_kernel(total, near, crossed_here, crossed_there, out, crossed):
+    crossed[...] = (crossed_here[...] + crossed_there[...]).astype(BF16)
     second = on_second_core()
     count = total.shape[0] // 2
     left = jnp.where(second, near[...], total[...])
@@ -674,14 +675,14 @@
     )
 
     vel_a_here = vel_a + other_core(vel_crossing)
-    both_there = other_half(jnp.concatenate([vel_a_here[tokens:, :CHANNELS], vel_here[tokens:, :CHANNELS]], axis=1))
-    payload = call(
+    part_here, part_there = call(
         payload_kernel,
-        struct((CHANNELS, tokens), BF16),
-        (noise_levels, own, vel_a_here, vel_here, both_there),
+        (struct((CHANNELS, tokens), F32), struct((CHANNELS, tokens), F32)),
+        (noise_levels, own, vel_a_here, vel_here),
         scalars=1,
     )
-    crossed = lax.ppermute(payload, "role", [(0, 1), (1, 0)])
+    crossed_here = lax.ppermute(part_here, "role", [(0, 1), (1, 0)])
+    crossed_there = lax.ppermute(part_there, ("role", "seq"), [(i, i ^ 3) for i in range(4)])
 
     samples = devices * base_latents.shape[1]
     height = width // 128
@@ -689,15 +690,14 @@
         functools.partial(closing_kernel, block, 1.0 / (samples * 2 * tokens)),
         (struct((height, 128), F32), struct((height, 128), F32)),
         (between_chips(products), own_columns, embed),
-        after=(payload,),
     )
     total = kept_half + other_core(sent_half)
     spread = call(spread_kernel, struct((chips, height, 128), BF16), (total, other_half(total)))
     total = jnp.sum(between_chips(spread).astype(F32), axis=0)
     mod_grads, crossed = call(
         join_kernel,
-        (struct((2, width), F32), struct(crossed.shape, BF16)),
-        (total, other_core(total), crossed),
+        (struct((2, width), F32), struct((CHANNELS, tokens), BF16)),
+        (total, other_core(total), crossed_here, crossed_there),
     )
     return (crossed.T[None, None], mod_grads[None])
 

time: 101 us -> 99.6 us (0.986)
  blocking collectives: 0 us -> 14.3 us
  waiting for transfers between devices: 31.8 us -> 23 us
  starting transfers between devices: 51 us -> 44.7 us
    all_to_all x0 -> x1, blocking collectives: none -> 14.3 us  [between_chips(): lax.all_to_all(value, 'fsdp', 0, 0, tiled=True, axis_index_groups=groups)]
    all_to_all x4 -> x3, waiting for transfers between devices: 18.7 us -> 12 us  [between_chips(): lax.all_to_all(value, 'fsdp', 0, 0, tiled=True, axis_index_groups=groups)]
    all_to_all x4 -> x3, starting transfers between devices: 25.8 us -> 19.9 us  [between_chips(): lax.all_to_all(value, 'fsdp', 0, 0, tiled=True, axis_index_groups=groups)]
    ppermute x4 -> x3, waiting for transfers between devices: 8.38 us -> 6.28 us  [other_half(): return lax.ppermute(value, 'seq', [(0, 1), (1, 0)])]
    ppermute x4 -> x3, starting transfers between devices: 5.43 us -> 4.04 us  [other_half(): return lax.ppermute(value, 'seq', [(0, 1), (1, 0)])]
    ppermute x1 -> x2, starting transfers between devices: 3 us -> 3.46 us  [the longest x1 2.71 us: per_device(): crossed_here = lax.ppermute(part_here, 'role', [(0, 1), (1, 0)])]
  transfers between devices with their start and end apart: 15 -> 14, of which waited for: 13 -> 11; matrix products, arithmetic and copies ran while one was open for 1% -> 1% of each run, Pallas kernels for 5% -> 5%
where the time goes in v9:
time: 99.6 us; the launch traced here: 99.1 us
  starting transfers between devices  44.7 us (45%)
  waiting for transfers between devices  23 us (23%)
  blocking collectives  14.3 us (14%)
  Pallas kernels  13.4 us (13%)
  between operations  2.13 us (2%)
  local copies, waits for them, and re-layouts  1.42 us (1%)
    all_to_all x3, starting transfers between devices, between_chips(): lax.all_to_all(value, 'fsdp', 0, 0, tiled=True, axis_index_groups=groups)  19.9 us
    ppermute x6, starting transfers between devices, other_core(): lax.ppermute(value, 'fsdp', [(i, i ^ 1) for i in range(lax.axis_size('fsd...  17.3 us
    all_to_all x1, blocking collectives, between_chips(): lax.all_to_all(value, 'fsdp', 0, 0, tiled=True, axis_index_groups=groups)  14.3 us
    pallas_call x13, Pallas kernels, call(): pl.pallas_call(kernel, out_shape=out_shapes, in_specs=specs, out_specs=ja...  13.4 us
    all_to_all x3, waiting for transfers between devices, between_chips(): lax.all_to_all(value, 'fsdp', 0, 0, tiled=True, axis_index_groups=groups)  12 us
    ppermute x3, waiting for transfers between devices, other_half(): return lax.ppermute(value, 'seq', [(0, 1), (1, 0)])  6.28 us
    ppermute x6, waiting for transfers between devices, other_core(): lax.ppermute(value, 'fsdp', [(i, i ^ 1) for i in range(lax.axis_size('fsd...  4.75 us
    ppermute x3, starting transfers between devices, other_half(): return lax.ppermute(value, 'seq', [(0, 1), (1, 0)])  4.04 us
  transfers between devices with their start and end apart: 14, of which 11 were waited for; matrix products, arithmetic and copies ran while one was open for 1% of the time, Pallas kernels for 5%

profile of v9, /device:TPU:1, one launch (start us, length us, event | category | flops | bytes accessed | tf_op | source)
XLA Modules:
  0.0 99.1 jit_solution(14738687676501779098)
XLA Ops:
  0.6 0.0 copy-start
  0.6 3.3 %collective-permute-start = (bf16[48,2304]{1,0:T(8,128)(2,1)}, bf16[48,2304]{1,0:T(8,128)(2,1)S(1)}, u32[]{:S(2)}, u32[]{:S(2)}) collective-permute-start(bf16[48,2304]{1,0:T(8,128)(2,1)} %bitcast.20), channel_id=1, source_target_pairs={{0,2},{2,0},{4,6},{6,4},{8,10},{10,8},{12,14},{14,12},{16,18},{18,... | collective-permute-start | bytes 663560 | tf_op jit(solution)/shard_map/ppermute | solution.py:545
  4.0 0.0 copy-start.1
  4.0 0.9 copy-done.1
  4.9 0.0 copy-start.4
  4.9 0.0 copy-start.5
  4.9 0.0 copy-start.6
  4.9 0.0 copy-start.7
  4.9 0.0 copy-start.2
  4.9 0.2 shard_map.113.own
  5.1 0.2 collective-permute-done.received
  5.3 1.0 %shard_map.114.after = bf16[32,32,128]{2,1,0:T(8,128)(2,1)} custom-call(f32[1152,128]{1,0:T(8,128)S(1)} %shard_map.113.own, bf16[48,2304]{1,0:T(8,128)(2,1)S(1)} %collective-permute-done.received), custom_call_target="tpu_custom_call" | custom-call | tf_op jit(solution)/shard_map/pallas_call | solution.py:529
  6.3 9.3 %all-to-all-start = ((bf16[32,32,128]{2,1,0:T(8,128)(2,1)}), bf16[32,32,128]{2,1,0:T(8,128)(2,1)S(1)}, u32[]{:S(2)}, u32[]{:S(2)}) async-start(bf16[32,32,128]{2,1,0:T(8,128)(2,1)} %shard_map.114.after), calls=%async_computation | async-start | bytes 524288 | tf_op jit(solution)/shard_map/all_to_all | solution.py:555
  16.9 0.0 copy-done.4
  16.9 0.1 copy.12
  17.0 0.0 copy-done.5
  17.0 0.1 copy.13
  17.1 0.0 copy-done.6
  17.2 0.1 copy.14
  17.3 0.0 copy-done.7
  17.3 0.1 copy.15
  17.4 0.0 copy-done
  17.4 0.0 copy-done.2
  17.4 0.3 shard_map.115.stack
  17.7 0.7 shard_map.116.after.own
  18.4 0.0 copy-start.3
  18.4 6.9 %all-to-all-done.taken = bf16[32,32,128]{2,1,0:T(8,128)(2,1)S(1)} async-done(((bf16[32,32,128]{2,1,0:T(8,128)(2,1)}), bf16[32,32,128]{2,1,0:T(8,128)(2,1)S(1)}, u32[]{:S(2)}, u32[]{:S(2)}) %all-to-all-start) | async-done | bytes 262176 | tf_op jit(solution)/shard_map/all_to_all | solution.py:555
  25.3 1.6 %shard_map.117 = (bf16[32,56,128]{2,1,0:T(8,128)(2,1)}, bf16[40,3072]{1,0:T(8,128)(2,1)S(1)}) custom-call(bf16[32,32,128]{2,1,0:T(8,128)(2,1)S(1)} %all-to-all-done.taken, bf16[256,3072]{1,0:T(8,128)(2,1)S(1)} %shard_map.115.stack, bf16[128,384]{1,0:T(8,128)(2,1)S(1)} %shard_map.116.after.own), custom_call_target="tpu_custom_call" | custom-call | tf_op jit(solution)/shard_map/pallas_call | solution.py:529
  26.9 6.7 %all-to-all-start.1 = ((bf16[32,56,128]{2,1,0:T(8,128)(2,1)}), bf16[32,56,128]{2,1,0:T(8,128)(2,1)S(1)}, u32[]{:S(2)}, u32[]{:S(2)}) async-start(bf16[32,56,128]{2,1,0:T(8,128)(2,1)} %get-tuple-element.28), calls=%async_computation.1 | async-start | bytes 917504 | tf_op jit(solution)/shard_map/all_to_all | solution.py:555
  33.6 1.5 %collective-permute-start.1 = (bf16[128,384]{1,0:T(8,128)(2,1)S(1)}, bf16[128,384]{1,0:T(8,128)(2,1)S(1)}, u32[]{:S(2)}, u32[]{:S(2)}) collective-permute-start(bf16[128,384]{1,0:T(8,128)(2,1)S(1)} %shard_map.116.after.own), channel_id=1, source_target_pairs={{0,2},{2,0},{4,6},{6,4},{8,10},{10,8},{12,14},{14,12},{16,18},{18,... | collective-permute-start | bytes 294920 | tf_op jit(solution)/shard_map/ppermute | solution.py:545
  35.1 0.9 collective-permute-done.1
  36.1 1.4 %collective-permute-start.2 = (bf16[2,128,384]{2,1,0:T(8,128)(2,1)S(1)}, bf16[2,128,384]{2,1,0:T(8,128)(2,1)S(1)}, u32[]{:S(2)}, u32[]{:S(2)}) collective-permute-start(bf16[2,128,384]{2,1,0:T(8,128)(2,1)S(1)} %pad_maximum_fusion.here), channel_id=1, source_target_pairs={{0,1},{1,0},{2,3},{3,2},{4,5},{5,4},{6,7},{7,6},{8,9},{9,8},{10,11... | collective-permute-start | bytes 589832 | tf_op jit(solution)/shard_map/ppermute | solution.py:549
  37.4 0.0 copy-done.3
  37.5 4.8 %collective-permute-done.2.there = bf16[2,128,384]{2,1,0:T(8,128)(2,1)S(1)} collective-permute-done((bf16[2,128,384]{2,1,0:T(8,128)(2,1)S(1)}, bf16[2,128,384]{2,1,0:T(8,128)(2,1)S(1)}, u32[]{:S(2)}, u32[]{:S(2)}) %collective-permute-start.2) | collective-permute-done | bytes 196640 | tf_op jit(solution)/shard_map/ppermute | solution.py:549
  42.3 1.4 %shard_map.118 = (bf16[512,128]{1,0:T(8,128)(2,1)S(1)}, bf16[128,512]{1,0:T(8,128)(2,1)S(1)}, f32[512,128]{1,0:T(8,128)S(1)}, f32[8,512]{1,0:T(8,128)S(1)}, f32[...) custom-call(bf16[2,128,384]{2,1,0:T(8,128)(2,1)S(1)} %pad_maximum_fusion.here, ...), custom_call_target="tpu_custom_call" | custom-call | tf_op jit(solution)/shard_map/pallas_call | solution.py:529
  43.7 2.1 %all-to-all-done.1.taken = bf16[32,56,128]{2,1,0:T(8,128)(2,1)S(1)} async-done(((bf16[32,56,128]{2,1,0:T(8,128)(2,1)}), bf16[32,56,128]{2,1,0:T(8,128)(2,1)S(1)}, u32[]{:S(2)}, u32[]{:S(2)}) %all-to-all-start.1) | async-done | bytes 458784 | tf_op jit(solution)/shard_map/all_to_all | solution.py:555
  45.8 1.9 %shard_map.119 = (bf16[1152,128]{1,0:T(8,128)(2,1)S(1)}, f32[8,1152]{1,0:T(8,128)S(1)}, bf16[6,128,256]{2,1,0:T(8,128)(2,1)S(1)}, f32[6,256,256]{2,1,0:T(8,128)S...) custom-call(bf16[32,56,128]{2,1,0:T(8,128)(2,1)S(1)} %all-to-all-done.1.taken, ...), custom_call_target="tpu_custom_call" | custom-call | tf_op jit(solution)/shard_map/pallas_call | solution.py:529
  47.7 4.5 %collective-permute-start.3 = (f32[256,128]{1,0:T(8,128)S(1)}, f32[256,128]{1,0:T(8,128)S(1)}, u32[]{:S(2)}, u32[]{:S(2)}) collective-permute-start(f32[256,128]{1,0:T(8,128)S(1)} %get-tuple-element.36), channel_id=1, source_target_pairs={{0,2},{2,0},{4,6},{6,4},{8,10},{10,8},{12,14},{14,12},{16,18},{18,... | collective-permute-start | bytes 393224 | tf_op jit(solution)/shard_map/ppermute | solution.py:545
  52.2 1.0 collective-permute-done.3
  53.2 1.6 %collective-permute-start.4 = (bf16[256,128]{1,0:T(8,128)(2,1)S(1)}, bf16[256,128]{1,0:T(8,128)(2,1)S(1)}, u32[]{:S(2)}, u32[]{:S(2)}) collective-permute-start(bf16[256,128]{1,0:T(8,128)(2,1)S(1)} %get-tuple-element.54), channel_id=1, source_target_pairs={{0,1},{1,0},{2,3},{3,2},{4,5},{5,4},{6,7},{7,6},{8,9},{9,8},{10,11... | collective-permute-start | bytes 196616 | tf_op jit(solution)/shard_map/ppermute | solution.py:549
  54.8 2.3 %shard_map.120 = (f32[256,128]{1,0:T(8,128)S(1)}, bf16[2,256,768]{2,1,0:T(8,128)(2,1)S(1)}) custom-call(bf16[32,56,128]{2,1,0:T(8,128)(2,1)S(1)} %all-to-all-done.1.taken, bf16[1152,128]{1,0:T(8,128)(2,1)S(1)} %get-tuple-element.33.matrices, f32[8,1152]{1,0:T(8,128)S(1)} %get-tuple-element.34.offsets, bf16[2,128,384]{2,1,0:T(8,128)(2,1)S(1)} %pad_maximum_fusion.here, ...), custom_call_target="tpu_custom_call" | custom-call | flops 4000000000 | tf_op jit(solution)/shard_map/pallas_call | solution.py:529
  57.1 0.0 collective-permute-done.4.vel_there
  57.1 2.2 %shard_map.121 = (bf16[32,24,128]{2,1,0:T(8,128)(2,1)S(1)}, f32[256,128]{1,0:T(8,128)S(1)}, f32[256,128]{1,0:T(8,128)S(1)}) custom-call(bf16[2,256,768]{2,1,0:T(8,128)(2,1)S(1)} %get-tuple-element.37.kept, bf16[2,256,128]{2,1,0:T(8,128)(2,1)S(1)} %get-tuple-element.38.scaled, bf16[2,128,256]{2,1,0:T(8,128)(2,1)S(1)} %get-tuple-element.39.rows, ...), custom_call_target="tpu_custom_call" | custom-call | tf_op jit(solution)/shard_map/pallas_call | solution.py:529
  59.2 14.3 %all_to_all.20.taken = bf16[32,24,128]{2,1,0:T(8,128)(2,1)S(1)} all-to-all(bf16[32,24,128]{2,1,0:T(8,128)(2,1)S(1)} %get-tuple-element.44), channel_id=1, replica_groups={{0,4,8,12,16,20,24,28,32,36,40,44,48,52,56,60,64,68,72,76,80,84,88,92,9..., dimensions={0} | all-to-all | bytes 393216 | tf_op jit(solution)/shard_map/all_to_all | solution.py:555
  73.6 0.6 shard_map.122
  74.2 2.9 %collective-permute-start.5 = (f32[24,128]{1,0:T(8,128)S(1)}, f32[24,128]{1,0:T(8,128)S(1)}, u32[]{:S(2)}, u32[]{:S(2)}) collective-permute-start(f32[24,128]{1,0:T(8,128)S(1)} %get-tuple-element.47), channel_id=1, source_target_pairs={{0,2},{2,0},{4,6},{6,4},{8,10},{10,8},{12,14},{14,12},{16,18},{18,... | collective-permute-start | bytes 36872 | tf_op jit(solution)/shard_map/ppermute | solution.py:545
  77.1 0.8 collective-permute-done.5
  77.9 1.1 %collective-permute-start.6 = (f32[24,128]{1,0:T(8,128)S(1)}, f32[24,128]{1,0:T(8,128)S(1)}, u32[]{:S(2)}, u32[]{:S(2)}) collective-permute-start(f32[24,128]{1,0:T(8,128)S(1)} %add.10.total), channel_id=1, source_target_pairs={{0,1},{1,0},{2,3},{3,2},{4,5},{5,4},{6,7},{7,6},{8,9},{9,8},{10,11... | collective-permute-start | bytes 36872 | tf_op jit(solution)/shard_map/ppermute | solution.py:549
  79.0 1.5 %collective-permute-done.6.other = f32[24,128]{1,0:T(8,128)S(1)} collective-permute-done((f32[24,128]{1,0:T(8,128)S(1)}, f32[24,128]{1,0:T(8,128)S(1)}, u32[]{:S(2)}, u32[]{:S(2)}) %collective-permute-start.6) | collective-permute-done | bytes 12320 | tf_op jit(solution)/shard_map/ppermute | solution.py:549
  80.5 0.7 shard_map.123
  81.2 3.9 %all-to-all-start.3 = ((bf16[32,24,128]{2,1,0:T(8,128)(2,1)}), bf16[32,24,128]{2,1,0:T(8,128)(2,1)S(1)}, u32[]{:S(2)}, u32[]{:S(2)}) async-start(bf16[32,24,128]{2,1,0:T(8,128)(2,1)} %shard_map.123), calls=%async_computation.3 | async-start | bytes 393216 | tf_op jit(solution)/shard_map/all_to_all | solution.py:555
  85.0 1.9 %collective-permute-start.8 = (f32[256,128]{1,0:T(8,128)S(1)}, f32[256,128]{1,0:T(8,128)S(1)}, u32[]{:S(2)}, u32[]{:S(2)}) collective-permute-start(f32[256,128]{1,0:T(8,128)S(1)} %get-tuple-element.49), channel_id=1, source_target_pairs={{0,2},{2,0},{4,6},{6,4},{8,10},{10,8},{12,14},{14,12},{16,18},{18,... | collective-permute-start | bytes 393224 | tf_op jit(solution)/shard_map/ppermute | solution.py:545
  86.9 1.0 collective-permute-done.8
  87.9 0.1 shard_map.124
  88.0 2.7 %collective-permute-start.9 = (f32[64,128]{1,0:T(8,128)S(1)}, f32[64,128]{1,0:T(8,128)S(1)}, u32[]{:S(2)}, u32[]{:S(2)}) collective-permute-start(f32[64,128]{1,0:T(8,128)S(1)} %get-tuple-element.50), channel_id=1, source_target_pairs={{0,128},{128,0},{1,129},{129,1},{2,130},{130,2},{3,131},{131,3},{4... | collective-permute-start | bytes 98312 | tf_op jit(solution)/shard_map/ppermute | solution.py:684
  90.7 0.7 collective-permute-start.10
  91.5 3.0 %all-to-all-done.3 = bf16[32,24,128]{2,1,0:T(8,128)(2,1)S(1)} async-done(((bf16[32,24,128]{2,1,0:T(8,128)(2,1)}), bf16[32,24,128]{2,1,0:T(8,128)(2,1)S(1)}, u32[]{:S(2)}, u32[]{:S(2)}) %all-to-all-start.3) | async-done | bytes 196640 | tf_op jit(solution)/shard_map/all_to_all | solution.py:555
  94.5 3.2 %collective-permute-start.7 = (f32[24,128]{1,0:T(8,128)S(1)}, f32[24,128]{1,0:T(8,128)S(1)}, u32[]{:S(2)}, u32[]{:S(2)}) collective-permute-start(f32[24,128]{1,0:T(8,128)S(1)} %convert_reduce_fusion.total), channel_id=1, source_target_pairs={{0,2},{2,0},{4,6},{6,4},{8,10},{10,8},{12,14},{14,12},{16,18},{18,... | collective-permute-start | bytes 36872 | tf_op jit(solution)/shard_map/ppermute | solution.py:545
  97.7 0.0 collective-permute-done.9.crossed_here
  97.7 0.0 collective-permute-done.10.crossed_there
  97.7 0.8 collective-permute-done.7.near
  98.5 0.6 shard_map.125
  (6 shorter events, 0.1 us)
Async XLA Ops:
  0.6 16.8 %copy-start = (bf16[1,64,3072]{2,1,0:T(8,128)(2,1)S(1)}, bf16[1,64,3072]{2,1,0:T(8,128)(2,1)}, u32[]{:S(2)}) copy-start(bf16[1,64,3072]{2,1,0:T(8,128)(2,1)} %param.16) | copy-start | bytes 1179652
  0.6 4.6 %collective-permute-start = (bf16[48,2304]{1,0:T(8,128)(2,1)}, bf16[48,2304]{1,0:T(8,128)(2,1)S(1)}, u32[]{:S(2)}, u32[]{:S(2)}) collective-permute-start(bf16[48,2304]{1,0:T(8,128)(2,1)} %bitcast.20), channel_id=1, source_target_pairs={{0,2},{2,0},{4,6},{6,4},{8,10},{10,8},{12,14},{14,12},{16,18},{18,... | collective-permute-start | bytes 663560 | tf_op jit(solution)/shard_map/ppermute | solution.py:545
  4.0 0.9 copy-start.1
  4.9 12.0 %copy-start.4 = (bf16[1,1,128,64]{2,3,1,0:T(8,128)(2,1)S(1)}, bf16[1,1,128,64]{2,3,1,0:T(8,128)(2,1)}, u32[]{:S(2)}) copy-start(bf16[1,1,128,64]{2,3,1,0:T(8,128)(2,1)} %param.10) | copy-start | bytes 49156
  4.9 12.1 %copy-start.5 = (bf16[1,1,128,64]{2,3,1,0:T(8,128)(2,1)S(1)}, bf16[1,1,128,64]{2,3,1,0:T(8,128)(2,1)}, u32[]{:S(2)}) copy-start(bf16[1,1,128,64]{2,3,1,0:T(8,128)(2,1)} %param.11) | copy-start | bytes 49156
  4.9 12.2 %copy-start.6 = (bf16[1,1,128,64]{2,3,1,0:T(8,128)(2,1)S(1)}, bf16[1,1,128,64]{2,3,1,0:T(8,128)(2,1)}, u32[]{:S(2)}) copy-start(bf16[1,1,128,64]{2,3,1,0:T(8,128)(2,1)} %param.13) | copy-start | bytes 49156
  4.9 12.4 %copy-start.7 = (bf16[1,1,128,64]{2,3,1,0:T(8,128)(2,1)S(1)}, bf16[1,1,128,64]{2,3,1,0:T(8,128)(2,1)}, u32[]{:S(2)}) copy-start(bf16[1,1,128,64]{2,3,1,0:T(8,128)(2,1)} %param.15) | copy-start | bytes 49156
  4.9 12.5 %copy-start.2 = (f32[1,2,2,3072]{3,2,1,0:T(2,128)S(1)}, f32[1,2,2,3072]{3,2,1,0:T(2,128)}, u32[]{:S(2)}) copy-start(f32[1,2,2,3072]{3,2,1,0:T(2,128)} %param.19) | copy-start | bytes 147460
  6.3 19.0 %all-to-all-start = ((bf16[32,32,128]{2,1,0:T(8,128)(2,1)}), bf16[32,32,128]{2,1,0:T(8,128)(2,1)S(1)}, u32[]{:S(2)}, u32[]{:S(2)}) async-start(bf16[32,32,128]{2,1,0:T(8,128)(2,1)} %shard_map.114.after), calls=%async_computation | async-start | bytes 524288 | tf_op jit(solution)/shard_map/all_to_all | solution.py:555
  18.4 19.1 %copy-start.3 = (bf16[1,768,64]{1,2,0:T(8,128)(2,1)S(1)}, bf16[1,768,64]{1,2,0:T(8,128)(2,1)}, u32[]{:S(2)}) copy-start(bf16[1,768,64]{1,2,0:T(8,128)(2,1)} %param.18) | copy-start | bytes 294916
  26.9 19.0 %all-to-all-start.1 = ((bf16[32,56,128]{2,1,0:T(8,128)(2,1)}), bf16[32,56,128]{2,1,0:T(8,128)(2,1)S(1)}, u32[]{:S(2)}, u32[]{:S(2)}) async-start(bf16[32,56,128]{2,1,0:T(8,128)(2,1)} %get-tuple-element.28), calls=%async_computation.1 | async-start | bytes 917504 | tf_op jit(solution)/shard_map/all_to_all | solution.py:555
  33.6 2.4 %collective-permute-start.1 = (bf16[128,384]{1,0:T(8,128)(2,1)S(1)}, bf16[128,384]{1,0:T(8,128)(2,1)S(1)}, u32[]{:S(2)}, u32[]{:S(2)}) collective-permute-start(bf16[128,384]{1,0:T(8,128)(2,1)S(1)} %shard_map.116.after.own), channel_id=1, source_target_pairs={{0,2},{2,0},{4,6},{6,4},{8,10},{10,8},{12,14},{14,12},{16,18},{18,... | collective-permute-start | bytes 294920 | tf_op jit(solution)/shard_map/ppermute | solution.py:545
  36.1 6.2 %collective-permute-start.2 = (bf16[2,128,384]{2,1,0:T(8,128)(2,1)S(1)}, bf16[2,128,384]{2,1,0:T(8,128)(2,1)S(1)}, u32[]{:S(2)}, u32[]{:S(2)}) collective-permute-start(bf16[2,128,384]{2,1,0:T(8,128)(2,1)S(1)} %pad_maximum_fusion.here), channel_id=1, source_target_pairs={{0,1},{1,0},{2,3},{3,2},{4,5},{5,4},{6,7},{7,6},{8,9},{9,8},{10,11... | collective-permute-start | bytes 589832 | tf_op jit(solution)/shard_map/ppermute | solution.py:549
  47.7 5.5 %collective-permute-start.3 = (f32[256,128]{1,0:T(8,128)S(1)}, f32[256,128]{1,0:T(8,128)S(1)}, u32[]{:S(2)}, u32[]{:S(2)}) collective-permute-start(f32[256,128]{1,0:T(8,128)S(1)} %get-tuple-element.36), channel_id=1, source_target_pairs={{0,2},{2,0},{4,6},{6,4},{8,10},{10,8},{12,14},{14,12},{16,18},{18,... | collective-permute-start | bytes 393224 | tf_op jit(solution)/shard_map/ppermute | solution.py:545
  53.2 3.8 %collective-permute-start.4 = (bf16[256,128]{1,0:T(8,128)(2,1)S(1)}, bf16[256,128]{1,0:T(8,128)(2,1)S(1)}, u32[]{:S(2)}, u32[]{:S(2)}) collective-permute-start(bf16[256,128]{1,0:T(8,128)(2,1)S(1)} %get-tuple-element.54), channel_id=1, source_target_pairs={{0,1},{1,0},{2,3},{3,2},{4,5},{5,4},{6,7},{7,6},{8,9},{9,8},{10,11... | collective-permute-start | bytes 196616 | tf_op jit(solution)/shard_map/ppermute | solution.py:549
  74.2 3.8 %collective-permute-start.5 = (f32[24,128]{1,0:T(8,128)S(1)}, f32[24,128]{1,0:T(8,128)S(1)}, u32[]{:S(2)}, u32[]{:S(2)}) collective-permute-start(f32[24,128]{1,0:T(8,128)S(1)} %get-tuple-element.47), channel_id=1, source_target_pairs={{0,2},{2,0},{4,6},{6,4},{8,10},{10,8},{12,14},{14,12},{16,18},{18,... | collective-permute-start | bytes 36872 | tf_op jit(solution)/shard_map/ppermute | solution.py:545
  77.9 2.5 %collective-permute-start.6 = (f32[24,128]{1,0:T(8,128)S(1)}, f32[24,128]{1,0:T(8,128)S(1)}, u32[]{:S(2)}, u32[]{:S(2)}) collective-permute-start(f32[24,128]{1,0:T(8,128)S(1)} %add.10.total), channel_id=1, source_target_pairs={{0,1},{1,0},{2,3},{3,2},{4,5},{5,4},{6,7},{7,6},{8,9},{9,8},{10,11... | collective-permute-start | bytes 36872 | tf_op jit(solution)/shard_map/ppermute | solution.py:549
  81.2 13.3 %all-to-all-start.3 = ((bf16[32,24,128]{2,1,0:T(8,128)(2,1)}), bf16[32,24,128]{2,1,0:T(8,128)(2,1)S(1)}, u32[]{:S(2)}, u32[]{:S(2)}) async-start(bf16[32,24,128]{2,1,0:T(8,128)(2,1)} %shard_map.123), calls=%async_computation.3 | async-start | bytes 393216 | tf_op jit(solution)/shard_map/all_to_all | solution.py:555
  85.0 2.8 %collective-permute-start.8 = (f32[256,128]{1,0:T(8,128)S(1)}, f32[256,128]{1,0:T(8,128)S(1)}, u32[]{:S(2)}, u32[]{:S(2)}) collective-permute-start(f32[256,128]{1,0:T(8,128)S(1)} %get-tuple-element.49), channel_id=1, source_target_pairs={{0,2},{2,0},{4,6},{6,4},{8,10},{10,8},{12,14},{14,12},{16,18},{18,... | collective-permute-start | bytes 393224 | tf_op jit(solution)/shard_map/ppermute | solution.py:545
  88.0 9.7 %collective-permute-start.9 = (f32[64,128]{1,0:T(8,128)S(1)}, f32[64,128]{1,0:T(8,128)S(1)}, u32[]{:S(2)}, u32[]{:S(2)}) collective-permute-start(f32[64,128]{1,0:T(8,128)S(1)} %get-tuple-element.50), channel_id=1, source_target_pairs={{0,128},{128,0},{1,129},{129,1},{2,130},{130,2},{3,131},{131,3},{4... | collective-permute-start | bytes 98312 | tf_op jit(solution)/shard_map/ppermute | solution.py:684
  90.7 7.0 %collective-permute-start.10 = (f32[64,128]{1,0:T(8,128)S(1)}, f32[64,128]{1,0:T(8,128)S(1)}, u32[]{:S(2)}, u32[]{:S(2)}) collective-permute-start(f32[64,128]{1,0:T(8,128)S(1)} %get-tuple-element.51), channel_id=1, source_target_pairs={{0,129},{1,128},{128,1},{129,0},{2,131},{3,130},{130,3},{131,2},{4... | collective-permute-start | bytes 98312 | tf_op jit(solution)/shard_map/ppermute | solution.py:685
  94.5 4.0 %collective-permute-start.7 = (f32[24,128]{1,0:T(8,128)S(1)}, f32[24,128]{1,0:T(8,128)S(1)}, u32[]{:S(2)}, u32[]{:S(2)}) collective-permute-start(f32[24,128]{1,0:T(8,128)S(1)} %convert_reduce_fusion.total), channel_id=1, source_target_pairs={{0,2},{2,0},{4,6},{6,4},{8,10},{10,8},{12,14},{14,12},{16,18},{18,... | collective-permute-start | bytes 36872 | tf_op jit(solution)/shard_map/ppermute | solution.py:545

commit v10 on v9

--- a/solution.py
+++ b/solution.py
@@ -71,11 +71,11 @@
     critic = on_critic()
     level = noise_levels[0, 0]
     level_two = jnp.where(critic, level, replay_levels[0, 0])
-    base_f = base[...].astype(F32)
-    noise_f = noise[...].astype(F32)
+    base_f = base[...].astype(F32).T
+    noise_f = noise[...].astype(F32).T
     input_a = rounded((1.0 - level) * base_f + level * noise_f)
-    input_b = jnp.where(critic, input_a, replay[...].astype(F32))
-    known = jnp.where(critic, noise_f - base_f, cotangent[...].astype(F32))
+    input_b = jnp.where(critic, input_a, replay[...].astype(F32).T)
+    known = jnp.where(critic, noise_f - base_f, cotangent[...].astype(F32).T)
     known_high = rounded(known)
     tokens = input_a.shape[0]
     rows = jnp.concatenate([input_a, input_b], axis=0).astype(BF16)
@@ -85,17 +85,16 @@
         embedded = dot(rows, embed[:, start : start + 512])
         total = total + jnp.sum(embedded * embedded, axis=-1, keepdims=True)
     scale = lax.rsqrt(total / width + EPSILON)
-    lane = lane_index((tokens, 128))
-    tail = jnp.zeros((tokens, 128), F32)
+    lane = lane_index((tokens, CHANNELS))
+    tail = jnp.zeros((tokens, CHANNELS), F32)
     ones = jnp.ones((tokens, 1), F32)
     for which, column in enumerate((scale[:tokens], scale[tokens:], ones * level, ones * level_two)):
         for part, value in enumerate(three_parts(column)):
             tail = jnp.where(lane == which * 3 + part, value, tail)
     pack[:, 0:64] = input_a.astype(BF16)
-    pack[:, 64:128] = input_b.astype(BF16)
+    pack[:, 64:128] = jnp.where(critic, known - known_high, input_b).astype(BF16)
     pack[:, 128:192] = known_high.astype(BF16)
-    pack[:, 192:256] = (known - known_high).astype(BF16)
-    pack[:, 256:384] = tail.astype(BF16)
+    pack[:, 192:256] = tail.astype(BF16)
 
 
 def turn_rows(rows, padded, second):
@@ -135,7 +134,7 @@
         out[chip] = jnp.concatenate([top, piece[16:]], axis=0).astype(BF16)
 
 
-def product_kernel(block, taken, stack, after, out, columns_out):
+def product_kernel(block, taken, stack, out, columns_out):
     chips, height, padded = taken.shape
     half = block // 2
     width = stack.shape[1]
@@ -183,16 +182,23 @@
 
 
 def tail_column(packs, sample, which):
-    tail = token_rows(packs, sample, 256, 384).astype(F32)
-    at = 3 * which
+    tail = token_rows(packs, sample, 128, 256).astype(F32)
+    at = CHANNELS + 3 * which
     return tail[:, at : at + 1] + tail[:, at + 1 : at + 2] + tail[:, at + 2 : at + 3]
+
+
+def both_inputs(packs, sample):
+    inputs = token_rows(packs, sample, 0, 128).astype(F32)
+    low_lanes = lane_index((1, 128)) < CHANNELS
+    same = jnp.where(low_lanes, inputs, pltpu.roll(inputs, CHANNELS, 1))
+    return jnp.where(on_critic(), same, inputs)
 
 
 def fill_rows(which, packs, rows, turned, scale, lines):
     low_lanes = lane_index((1, 128)) < CHANNELS
     lines[...] = jnp.zeros_like(lines)
     for sample in range(2):
-        inputs = token_rows(packs, sample, 0, 128).astype(F32)
+        inputs = both_inputs(packs, sample)
         tokens = inputs.shape[0]
         own = slice(sample * tokens, (sample + 1) * tokens)
         flipped = pltpu.roll(inputs, CHANNELS, 1)
@@ -213,13 +219,14 @@
     low_lanes = lane_index((1, 128)) < CHANNELS
     parts = []
     for sample in range(2):
-        inputs = token_rows(packs, sample, 0, 128).astype(F32)
+        inputs = both_inputs(packs, sample)
         whole = jnp.where(low_lanes, pltpu.roll(inputs, CHANNELS, 1), inputs)
         whole = whole * (tail_column(packs, sample, 1) * tail_column(packs, sample, 3))
         scaled[sample] = whole.astype(BF16)
         scaled_turned[sample] = whole.T.astype(BF16)
-        part = token_rows(packs, sample, 128, 256).astype(F32)
-        parts.append(part[:, 0:CHANNELS] + part[:, CHANNELS:])
+        high = token_rows(packs, sample, 128, 256).astype(F32)[:, 0:CHANNELS]
+        low = token_rows(packs, sample, 0, 128).astype(F32)[:, CHANNELS:]
+        parts.append(high + jnp.where(on_critic(), low, 0.0))
     known[...] = jnp.concatenate(parts, axis=1)
 
 
@@ -594,28 +601,27 @@
         scratch=[pltpu.VMEM((columns, padded), F32)],
     )
     taken = between_chips(turned)
-    stack = call(stack_kernel, struct((256, width), BF16), (embed, modulation[0]), after=(turned,))
-
-    own = call(
-        pack_kernel,
-        struct((tokens, 384), BF16),
-        (
-            noise_levels,
-            replay_levels,
-            base_latents[0, 0],
-            noise_latents[0, 0],
-            replay_latents[0, 0],
-            cotangent[0, 0],
-            embed,
-        ),
-        scalars=2,
-        after=(turned,),
-    )
+    stack = call(stack_kernel, struct((256, width), BF16), (embed, modulation[0]), after=(taken,))
+
     matrices, own_columns = call(
         functools.partial(product_kernel, block),
         (struct((chips, packed, 128), BF16), struct((height + 8, width), BF16)),
         (taken, stack),
-        after=(own,),
+    )
+    own = call(
+        pack_kernel,
+        struct((tokens, 256), BF16),
+        (
+            noise_levels,
+            replay_levels,
+            base_latents[0, 0].T,
+            noise_latents[0, 0].T,
+            replay_latents[0, 0].T,
+            cotangent[0, 0].T,
+            embed,
+        ),
+        scalars=2,
+        after=(matrices,),
     )
     here = jnp.stack([own, other_core(own)])
     there = other_half(here)

time: 99.6 us -> 98.9 us (level)
  blocking collectives: 14.3 us -> 33.1 us
  starting transfers between devices: 44.7 us -> 35.3 us
  waiting for transfers between devices: 23 us -> 13.8 us
    all_to_all x1 -> x2, blocking collectives: 14.3 us -> 33.1 us  [between_chips(): lax.all_to_all(value, 'fsdp', 0, 0, tiled=True, axis_index_groups=groups)]
    all_to_all x3 -> x2, starting transfers between devices: 19.9 us -> 10.6 us  [between_chips(): lax.all_to_all(value, 'fsdp', 0, 0, tiled=True, axis_index_groups=groups)]
    all_to_all x3 -> x2, waiting for transfers between devices: 12 us -> 4.22 us  [between_chips(): lax.all_to_all(value, 'fsdp', 0, 0, tiled=True, axis_index_groups=groups)]
    ppermute x3, waiting for transfers between devices: 6.28 us -> 4.88 us  [other_half(): return lax.ppermute(value, 'seq', [(0, 1), (1, 0)])]
  transfers between devices with their start and end apart: 14 -> 13, of which waited for: 11 -> 10; matrix products, arithmetic and copies ran while one was open for 1% -> 0% of each run, Pallas kernels for 5% -> 5%
where the time goes in v10:
time: 98.9 us; the launch traced here: 98.6 us
  starting transfers between devices  35.3 us (36%)
  blocking collectives  33.1 us (33%)
  waiting for transfers between devices  13.8 us (14%)
  Pallas kernels  13.1 us (13%)
  between operations  2.11 us (2%)
    all_to_all x2, blocking collectives, between_chips(): lax.all_to_all(value, 'fsdp', 0, 0, tiled=True, axis_index_groups=groups)  33.1 us
    ppermute x6, starting transfers between devices, other_core(): lax.ppermute(value, 'fsdp', [(i, i ^ 1) for i in range(lax.axis_size('fsd...  17.3 us
    pallas_call x13, Pallas kernels, call(): pl.pallas_call(kernel, out_shape=out_shapes, in_specs=specs, out_specs=ja...  13.1 us
    all_to_all x2, starting transfers between devices, between_chips(): lax.all_to_all(value, 'fsdp', 0, 0, tiled=True, axis_index_groups=groups)  10.6 us
    ppermute x3, waiting for transfers between devices, other_half(): return lax.ppermute(value, 'seq', [(0, 1), (1, 0)])  4.88 us
    ppermute x6, waiting for transfers between devices, other_core(): lax.ppermute(value, 'fsdp', [(i, i ^ 1) for i in range(lax.axis_size('fsd...  4.74 us
    all_to_all x2, waiting for transfers between devices, between_chips(): lax.all_to_all(value, 'fsdp', 0, 0, tiled=True, axis_index_groups=groups)  4.22 us
    ppermute x3, starting transfers between devices, other_half(): return lax.ppermute(value, 'seq', [(0, 1), (1, 0)])  4.03 us
  transfers between devices with their start and end apart: 13, of which 10 were waited for; matrix products, arithmetic and copies ran while one was open for 0% of the time, Pallas kernels for 5%

profile of v10, /device:TPU:1, one launch (start us, length us, event | category | flops | bytes accessed | tf_op | source)
XLA Modules:
  0.0 98.6 jit_solution(6050178754458205061)
XLA Ops:
  0.6 0.0 copy-start
  0.6 3.3 %collective-permute-start = (bf16[48,2304]{1,0:T(8,128)(2,1)}, bf16[48,2304]{1,0:T(8,128)(2,1)S(1)}, u32[]{:S(2)}, u32[]{:S(2)}) collective-permute-start(bf16[48,2304]{1,0:T(8,128)(2,1)} %bitcast.28), channel_id=1, source_target_pairs={{0,2},{2,0},{4,6},{6,4},{8,10},{10,8},{12,14},{14,12},{16,18},{18,... | collective-permute-start | bytes 663560 | tf_op jit(solution)/shard_map/ppermute | solution.py:552
  4.0 0.0 copy-start.1
  4.0 0.9 copy-done.1
  4.9 0.0 copy-start.2
  4.9 0.2 shard_map.113.own
  5.1 0.2 collective-permute-done.received
  5.3 0.3 shard_map.114
  5.6 18.8 %all_to_all.20.after.taken = bf16[32,32,128]{2,1,0:T(8,128)(2,1)S(1)} all-to-all(bf16[32,32,128]{2,1,0:T(8,128)(2,1)S(1)} %shard_map.114), channel_id=1, replica_groups={{0,4,8,12,16,20,24,28,32,36,40,44,48,52,56,60,64,68,72,76,80,84,88,92,9..., dimensions={0} | all-to-all | bytes 524288 | tf_op jit(solution)/shard_map/all_to_all | solution.py:562
  24.4 0.0 copy-done
  24.4 0.0 copy-done.2
  24.4 0.3 shard_map.115.stack
  24.6 0.0 copy-start.3
  24.6 0.0 copy-start.4
  24.6 0.0 copy-start.5
  24.7 0.0 copy-start.6
  24.7 0.0 copy-start.7
  24.7 1.6 %shard_map.116 = (bf16[32,56,128]{2,1,0:T(8,128)(2,1)}, bf16[40,3072]{1,0:T(8,128)(2,1)S(1)}) custom-call(bf16[32,32,128]{2,1,0:T(8,128)(2,1)S(1)} %all_to_all.20.after.taken, bf16[256,3072]{1,0:T(8,128)(2,1)S(1)} %shard_map.115.stack), custom_call_target="tpu_custom_call" | custom-call | tf_op jit(solution)/shard_map/pallas_call | solution.py:536
  26.3 6.7 %all-to-all-start.1 = ((bf16[32,56,128]{2,1,0:T(8,128)(2,1)}), bf16[32,56,128]{2,1,0:T(8,128)(2,1)S(1)}, u32[]{:S(2)}, u32[]{:S(2)}) async-start(bf16[32,56,128]{2,1,0:T(8,128)(2,1)} %get-tuple-element.28.after), calls=%async_computation.1 | async-start | bytes 917504 | tf_op jit(solution)/shard_map/all_to_all | solution.py:562
  34.3 0.0 copy-done.3
  34.3 0.0 copy-done.4
  34.3 0.0 copy-done.5
  34.3 0.0 copy-done.6
  34.3 0.8 shard_map.117.own
  35.1 1.5 %collective-permute-start.1 = (bf16[128,256]{1,0:T(8,128)(2,1)S(1)}, bf16[128,256]{1,0:T(8,128)(2,1)S(1)}, u32[]{:S(2)}, u32[]{:S(2)}) collective-permute-start(bf16[128,256]{1,0:T(8,128)(2,1)S(1)} %shard_map.117.own), channel_id=1, source_target_pairs={{0,2},{2,0},{4,6},{6,4},{8,10},{10,8},{12,14},{14,12},{16,18},{18,... | collective-permute-start | bytes 196616 | tf_op jit(solution)/shard_map/ppermute | solution.py:552
  36.6 0.9 collective-permute-done.1
  37.6 1.4 %collective-permute-start.2 = (bf16[2,128,256]{2,1,0:T(8,128)(2,1)S(1)}, bf16[2,128,256]{2,1,0:T(8,128)(2,1)S(1)}, u32[]{:S(2)}, u32[]{:S(2)}) collective-permute-start(bf16[2,128,256]{2,1,0:T(8,128)(2,1)S(1)} %pad_maximum_fusion.here), channel_id=1, source_target_pairs={{0,1},{1,0},{2,3},{3,2},{4,5},{5,4},{6,7},{7,6},{8,9},{9,8},{10,11... | collective-permute-start | bytes 393224 | tf_op jit(solution)/shard_map/ppermute | solution.py:556
  38.9 0.0 copy-done.7
  39.0 3.4 %collective-permute-done.2.there = bf16[2,128,256]{2,1,0:T(8,128)(2,1)S(1)} collective-permute-done((bf16[2,128,256]{2,1,0:T(8,128)(2,1)S(1)}, bf16[2,128,256]{2,1,0:T(8,128)(2,1)S(1)}, u32[]{:S(2)}, u32[]{:S(2)}) %collective-permute-start.2) | collective-permute-done | bytes 131104 | tf_op jit(solution)/shard_map/ppermute | solution.py:556
  42.4 1.6 %shard_map.118 = (bf16[512,128]{1,0:T(8,128)(2,1)S(1)}, bf16[128,512]{1,0:T(8,128)(2,1)S(1)}, f32[512,128]{1,0:T(8,128)S(1)}, f32[8,512]{1,0:T(8,128)S(1)}, f32[...) custom-call(bf16[2,128,256]{2,1,0:T(8,128)(2,1)S(1)} %pad_maximum_fusion.here, ...), custom_call_target="tpu_custom_call" | custom-call | tf_op jit(solution)/shard_map/pallas_call | solution.py:536
  44.0 1.2 %all-to-all-done.1.taken = bf16[32,56,128]{2,1,0:T(8,128)(2,1)S(1)} async-done(((bf16[32,56,128]{2,1,0:T(8,128)(2,1)}), bf16[32,56,128]{2,1,0:T(8,128)(2,1)S(1)}, u32[]{:S(2)}, u32[]{:S(2)}) %all-to-all-start.1) | async-done | bytes 458784 | tf_op jit(solution)/shard_map/all_to_all | solution.py:562
  45.2 1.9 %shard_map.119 = (bf16[1152,128]{1,0:T(8,128)(2,1)S(1)}, f32[8,1152]{1,0:T(8,128)S(1)}, bf16[6,128,256]{2,1,0:T(8,128)(2,1)S(1)}, f32[6,256,256]{2,1,0:T(8,128)S...) custom-call(bf16[32,56,128]{2,1,0:T(8,128)(2,1)S(1)} %all-to-all-done.1.taken, ...), custom_call_target="tpu_custom_call" | custom-call | tf_op jit(solution)/shard_map/pallas_call | solution.py:536
  47.1 4.5 %collective-permute-start.3 = (f32[256,128]{1,0:T(8,128)S(1)}, f32[256,128]{1,0:T(8,128)S(1)}, u32[]{:S(2)}, u32[]{:S(2)}) collective-permute-start(f32[256,128]{1,0:T(8,128)S(1)} %get-tuple-element.36), channel_id=1, source_target_pairs={{0,2},{2,0},{4,6},{6,4},{8,10},{10,8},{12,14},{14,12},{16,18},{18,... | collective-permute-start | bytes 393224 | tf_op jit(solution)/shard_map/ppermute | solution.py:552
  51.6 1.0 %collective-permute-done.3 = f32[256,128]{1,0:T(8,128)S(1)} collective-permute-done((f32[256,128]{1,0:T(8,128)S(1)}, f32[256,128]{1,0:T(8,128)S(1)}, u32[]{:S(2)}, u32[]{:S(2)}) %collective-permute-start.3) | collective-permute-done | bytes 131104 | tf_op jit(solution)/shard_map/ppermute | solution.py:552
  52.6 1.6 %collective-permute-start.4 = (bf16[256,128]{1,0:T(8,128)(2,1)S(1)}, bf16[256,128]{1,0:T(8,128)(2,1)S(1)}, u32[]{:S(2)}, u32[]{:S(2)}) collective-permute-start(bf16[256,128]{1,0:T(8,128)(2,1)S(1)} %get-tuple-element.54), channel_id=1, source_target_pairs={{0,1},{1,0},{2,3},{3,2},{4,5},{5,4},{6,7},{7,6},{8,9},{9,8},{10,11... | collective-permute-start | bytes 196616 | tf_op jit(solution)/shard_map/ppermute | solution.py:556
  54.2 2.3 %shard_map.120 = (f32[256,128]{1,0:T(8,128)S(1)}, bf16[2,256,768]{2,1,0:T(8,128)(2,1)S(1)}) custom-call(bf16[32,56,128]{2,1,0:T(8,128)(2,1)S(1)} %all-to-all-done.1.taken, bf16[1152,128]{1,0:T(8,128)(2,1)S(1)} %get-tuple-element.33.matrices, f32[8,1152]{1,0:T(8,128)S(1)} %get-tuple-element.34.offsets, bf16[2,128,256]{2,1,0:T(8,128)(2,1)S(1)} %pad_maximum_fusion.here, ...), custom_call_target="tpu_custom_call" | custom-call | flops 4000000000 | tf_op jit(solution)/shard_map/pallas_call | solution.py:536
  56.5 0.0 collective-permute-done.4.vel_there
  56.5 2.2 %shard_map.121 = (bf16[32,24,128]{2,1,0:T(8,128)(2,1)S(1)}, f32[256,128]{1,0:T(8,128)S(1)}, f32[256,128]{1,0:T(8,128)S(1)}) custom-call(bf16[2,256,768]{2,1,0:T(8,128)(2,1)S(1)} %get-tuple-element.37.kept, bf16[2,256,128]{2,1,0:T(8,128)(2,1)S(1)} %get-tuple-element.38.scaled, bf16[2,128,256]{2,1,0:T(8,128)(2,1)S(1)} %get-tuple-element.39.rows, ...), custom_call_target="tpu_custom_call" | custom-call | tf_op jit(solution)/shard_map/pallas_call | solution.py:536
  58.6 14.3 %all_to_all.21.taken = bf16[32,24,128]{2,1,0:T(8,128)(2,1)S(1)} all-to-all(bf16[32,24,128]{2,1,0:T(8,128)(2,1)S(1)} %get-tuple-element.44), channel_id=1, replica_groups={{0,4,8,12,16,20,24,28,32,36,40,44,48,52,56,60,64,68,72,76,80,84,88,92,9..., dimensions={0} | all-to-all | bytes 393216 | tf_op jit(solution)/shard_map/all_to_all | solution.py:562
  73.0 0.6 shard_map.122
  73.6 2.9 %collective-permute-start.5 = (f32[24,128]{1,0:T(8,128)S(1)}, f32[24,128]{1,0:T(8,128)S(1)}, u32[]{:S(2)}, u32[]{:S(2)}) collective-permute-start(f32[24,128]{1,0:T(8,128)S(1)} %get-tuple-element.47), channel_id=1, source_target_pairs={{0,2},{2,0},{4,6},{6,4},{8,10},{10,8},{12,14},{14,12},{16,18},{18,... | collective-permute-start | bytes 36872 | tf_op jit(solution)/shard_map/ppermute | solution.py:552
  76.5 0.8 collective-permute-done.5
  77.3 1.1 %collective-permute-start.6 = (f32[24,128]{1,0:T(8,128)S(1)}, f32[24,128]{1,0:T(8,128)S(1)}, u32[]{:S(2)}, u32[]{:S(2)}) collective-permute-start(f32[24,128]{1,0:T(8,128)S(1)} %add.10.total), channel_id=1, source_target_pairs={{0,1},{1,0},{2,3},{3,2},{4,5},{5,4},{6,7},{7,6},{8,9},{9,8},{10,11... | collective-permute-start | bytes 36872 | tf_op jit(solution)/shard_map/ppermute | solution.py:556
  78.4 1.5 %collective-permute-done.6.other = f32[24,128]{1,0:T(8,128)S(1)} collective-permute-done((f32[24,128]{1,0:T(8,128)S(1)}, f32[24,128]{1,0:T(8,128)S(1)}, u32[]{:S(2)}, u32[]{:S(2)}) %collective-permute-start.6) | collective-permute-done | bytes 12320 | tf_op jit(solution)/shard_map/ppermute | solution.py:556
  79.9 0.7 shard_map.123
  80.6 3.9 %all-to-all-start.3 = ((bf16[32,24,128]{2,1,0:T(8,128)(2,1)}), bf16[32,24,128]{2,1,0:T(8,128)(2,1)S(1)}, u32[]{:S(2)}, u32[]{:S(2)}) async-start(bf16[32,24,128]{2,1,0:T(8,128)(2,1)} %shard_map.123), calls=%async_computation.3 | async-start | bytes 393216 | tf_op jit(solution)/shard_map/all_to_all | solution.py:562
  84.5 1.9 %collective-permute-start.8 = (f32[256,128]{1,0:T(8,128)S(1)}, f32[256,128]{1,0:T(8,128)S(1)}, u32[]{:S(2)}, u32[]{:S(2)}) collective-permute-start(f32[256,128]{1,0:T(8,128)S(1)} %get-tuple-element.49), channel_id=1, source_target_pairs={{0,2},{2,0},{4,6},{6,4},{8,10},{10,8},{12,14},{14,12},{16,18},{18,... | collective-permute-start | bytes 393224 | tf_op jit(solution)/shard_map/ppermute | solution.py:552
  86.3 1.0 %collective-permute-done.8 = f32[256,128]{1,0:T(8,128)S(1)} collective-permute-done((f32[256,128]{1,0:T(8,128)S(1)}, f32[256,128]{1,0:T(8,128)S(1)}, u32[]{:S(2)}, u32[]{:S(2)}) %collective-permute-start.8) | collective-permute-done | bytes 131104 | tf_op jit(solution)/shard_map/ppermute | solution.py:552
  87.3 0.1 shard_map.124
  87.4 2.7 %collective-permute-start.9 = (f32[64,128]{1,0:T(8,128)S(1)}, f32[64,128]{1,0:T(8,128)S(1)}, u32[]{:S(2)}, u32[]{:S(2)}) collective-permute-start(f32[64,128]{1,0:T(8,128)S(1)} %get-tuple-element.50), channel_id=1, source_target_pairs={{0,128},{128,0},{1,129},{129,1},{2,130},{130,2},{3,131},{131,3},{4... | collective-permute-start | bytes 98312 | tf_op jit(solution)/shard_map/ppermute | solution.py:690
  90.1 0.8 collective-permute-start.10
  90.9 3.0 %all-to-all-done.3 = bf16[32,24,128]{2,1,0:T(8,128)(2,1)S(1)} async-done(((bf16[32,24,128]{2,1,0:T(8,128)(2,1)}), bf16[32,24,128]{2,1,0:T(8,128)(2,1)S(1)}, u32[]{:S(2)}, u32[]{:S(2)}) %all-to-all-start.3) | async-done | bytes 196640 | tf_op jit(solution)/shard_map/all_to_all | solution.py:562
  93.9 3.2 %collective-permute-start.7 = (f32[24,128]{1,0:T(8,128)S(1)}, f32[24,128]{1,0:T(8,128)S(1)}, u32[]{:S(2)}, u32[]{:S(2)}) collective-permute-start(f32[24,128]{1,0:T(8,128)S(1)} %convert_reduce_fusion.total), channel_id=1, source_target_pairs={{0,2},{2,0},{4,6},{6,4},{8,10},{10,8},{12,14},{14,12},{16,18},{18,... | collective-permute-start | bytes 36872 | tf_op jit(solution)/shard_map/ppermute | solution.py:552
  97.1 0.0 collective-permute-done.9.crossed_here
  97.1 0.0 collective-permute-done.10.crossed_there
  97.1 0.8 collective-permute-done.7.near
  97.9 0.6 shard_map.125
  (6 shorter events, 0.1 us)
Async XLA Ops:
  0.6 23.7 %copy-start = (bf16[1,64,3072]{2,1,0:T(8,128)(2,1)S(1)}, bf16[1,64,3072]{2,1,0:T(8,128)(2,1)}, u32[]{:S(2)}) copy-start(bf16[1,64,3072]{2,1,0:T(8,128)(2,1)} %param.16) | copy-start | bytes 1179652
  0.6 4.6 %collective-permute-start = (bf16[48,2304]{1,0:T(8,128)(2,1)}, bf16[48,2304]{1,0:T(8,128)(2,1)S(1)}, u32[]{:S(2)}, u32[]{:S(2)}) collective-permute-start(bf16[48,2304]{1,0:T(8,128)(2,1)} %bitcast.28), channel_id=1, source_target_pairs={{0,2},{2,0},{4,6},{6,4},{8,10},{10,8},{12,14},{14,12},{16,18},{18,... | collective-permute-start | bytes 663560 | tf_op jit(solution)/shard_map/ppermute | solution.py:552
  4.0 0.9 copy-start.1
  4.9 19.5 %copy-start.2 = (f32[1,2,2,3072]{3,2,1,0:T(2,128)S(1)}, f32[1,2,2,3072]{3,2,1,0:T(2,128)}, u32[]{:S(2)}) copy-start(f32[1,2,2,3072]{3,2,1,0:T(2,128)} %param.19) | copy-start | bytes 147460
  24.6 9.7 %copy-start.3 = (bf16[1,1,128,64]{2,3,1,0:T(8,128)(2,1)S(1)}, bf16[1,1,128,64]{2,3,1,0:T(8,128)(2,1)}, u32[]{:S(2)}) copy-start(bf16[1,1,128,64]{2,3,1,0:T(8,128)(2,1)} %param.10) | copy-start | bytes 49156
  24.6 9.7 %copy-start.4 = (bf16[1,1,128,64]{2,3,1,0:T(8,128)(2,1)S(1)}, bf16[1,1,128,64]{2,3,1,0:T(8,128)(2,1)}, u32[]{:S(2)}) copy-start(bf16[1,1,128,64]{2,3,1,0:T(8,128)(2,1)} %param.11) | copy-start | bytes 49156
  24.6 9.7 %copy-start.5 = (bf16[1,1,128,64]{2,3,1,0:T(8,128)(2,1)S(1)}, bf16[1,1,128,64]{2,3,1,0:T(8,128)(2,1)}, u32[]{:S(2)}) copy-start(bf16[1,1,128,64]{2,3,1,0:T(8,128)(2,1)} %param.13) | copy-start | bytes 49156
  24.7 9.7 %copy-start.6 = (bf16[1,1,128,64]{2,3,1,0:T(8,128)(2,1)S(1)}, bf16[1,1,128,64]{2,3,1,0:T(8,128)(2,1)}, u32[]{:S(2)}) copy-start(bf16[1,1,128,64]{2,3,1,0:T(8,128)(2,1)} %param.15) | copy-start | bytes 49156
  24.7 14.3 %copy-start.7 = (bf16[1,768,64]{1,2,0:T(8,128)(2,1)S(1)}, bf16[1,768,64]{1,2,0:T(8,128)(2,1)}, u32[]{:S(2)}) copy-start(bf16[1,768,64]{1,2,0:T(8,128)(2,1)} %param.18) | copy-start | bytes 294916
  26.3 19.0 %all-to-all-start.1 = ((bf16[32,56,128]{2,1,0:T(8,128)(2,1)}), bf16[32,56,128]{2,1,0:T(8,128)(2,1)S(1)}, u32[]{:S(2)}, u32[]{:S(2)}) async-start(bf16[32,56,128]{2,1,0:T(8,128)(2,1)} %get-tuple-element.28.after), calls=%async_computation.1 | async-start | bytes 917504 | tf_op jit(solution)/shard_map/all_to_all | solution.py:562
  35.1 2.4 %collective-permute-start.1 = (bf16[128,256]{1,0:T(8,128)(2,1)S(1)}, bf16[128,256]{1,0:T(8,128)(2,1)S(1)}, u32[]{:S(2)}, u32[]{:S(2)}) collective-permute-start(bf16[128,256]{1,0:T(8,128)(2,1)S(1)} %shard_map.117.own), channel_id=1, source_target_pairs={{0,2},{2,0},{4,6},{6,4},{8,10},{10,8},{12,14},{14,12},{16,18},{18,... | collective-permute-start | bytes 196616 | tf_op jit(solution)/shard_map/ppermute | solution.py:552
  37.6 4.8 %collective-permute-start.2 = (bf16[2,128,256]{2,1,0:T(8,128)(2,1)S(1)}, bf16[2,128,256]{2,1,0:T(8,128)(2,1)S(1)}, u32[]{:S(2)}, u32[]{:S(2)}) collective-permute-start(bf16[2,128,256]{2,1,0:T(8,128)(2,1)S(1)} %pad_maximum_fusion.here), channel_id=1, source_target_pairs={{0,1},{1,0},{2,3},{3,2},{4,5},{5,4},{6,7},{7,6},{8,9},{9,8},{10,11... | collective-permute-start | bytes 393224 | tf_op jit(solution)/shard_map/ppermute | solution.py:556
  47.1 5.5 %collective-permute-start.3 = (f32[256,128]{1,0:T(8,128)S(1)}, f32[256,128]{1,0:T(8,128)S(1)}, u32[]{:S(2)}, u32[]{:S(2)}) collective-permute-start(f32[256,128]{1,0:T(8,128)S(1)} %get-tuple-element.36), channel_id=1, source_target_pairs={{0,2},{2,0},{4,6},{6,4},{8,10},{10,8},{12,14},{14,12},{16,18},{18,... | collective-permute-start | bytes 393224 | tf_op jit(solution)/shard_map/ppermute | solution.py:552
  52.6 3.8 %collective-permute-start.4 = (bf16[256,128]{1,0:T(8,128)(2,1)S(1)}, bf16[256,128]{1,0:T(8,128)(2,1)S(1)}, u32[]{:S(2)}, u32[]{:S(2)}) collective-permute-start(bf16[256,128]{1,0:T(8,128)(2,1)S(1)} %get-tuple-element.54), channel_id=1, source_target_pairs={{0,1},{1,0},{2,3},{3,2},{4,5},{5,4},{6,7},{7,6},{8,9},{9,8},{10,11... | collective-permute-start | bytes 196616 | tf_op jit(solution)/shard_map/ppermute | solution.py:556
  73.6 3.8 %collective-permute-start.5 = (f32[24,128]{1,0:T(8,128)S(1)}, f32[24,128]{1,0:T(8,128)S(1)}, u32[]{:S(2)}, u32[]{:S(2)}) collective-permute-start(f32[24,128]{1,0:T(8,128)S(1)} %get-tuple-element.47), channel_id=1, source_target_pairs={{0,2},{2,0},{4,6},{6,4},{8,10},{10,8},{12,14},{14,12},{16,18},{18,... | collective-permute-start | bytes 36872 | tf_op jit(solution)/shard_map/ppermute | solution.py:552
  77.3 2.5 %collective-permute-start.6 = (f32[24,128]{1,0:T(8,128)S(1)}, f32[24,128]{1,0:T(8,128)S(1)}, u32[]{:S(2)}, u32[]{:S(2)}) collective-permute-start(f32[24,128]{1,0:T(8,128)S(1)} %add.10.total), channel_id=1, source_target_pairs={{0,1},{1,0},{2,3},{3,2},{4,5},{5,4},{6,7},{7,6},{8,9},{9,8},{10,11... | collective-permute-start | bytes 36872 | tf_op jit(solution)/shard_map/ppermute | solution.py:556
  80.6 13.3 %all-to-all-start.3 = ((bf16[32,24,128]{2,1,0:T(8,128)(2,1)}), bf16[32,24,128]{2,1,0:T(8,128)(2,1)S(1)}, u32[]{:S(2)}, u32[]{:S(2)}) async-start(bf16[32,24,128]{2,1,0:T(8,128)(2,1)} %shard_map.123), calls=%async_computation.3 | async-start | bytes 393216 | tf_op jit(solution)/shard_map/all_to_all | solution.py:562
  84.5 2.8 %collective-permute-start.8 = (f32[256,128]{1,0:T(8,128)S(1)}, f32[256,128]{1,0:T(8,128)S(1)}, u32[]{:S(2)}, u32[]{:S(2)}) collective-permute-start(f32[256,128]{1,0:T(8,128)S(1)} %get-tuple-element.49), channel_id=1, source_target_pairs={{0,2},{2,0},{4,6},{6,4},{8,10},{10,8},{12,14},{14,12},{16,18},{18,... | collective-permute-start | bytes 393224 | tf_op jit(solution)/shard_map/ppermute | solution.py:552
  87.4 9.7 %collective-permute-start.9 = (f32[64,128]{1,0:T(8,128)S(1)}, f32[64,128]{1,0:T(8,128)S(1)}, u32[]{:S(2)}, u32[]{:S(2)}) collective-permute-start(f32[64,128]{1,0:T(8,128)S(1)} %get-tuple-element.50), channel_id=1, source_target_pairs={{0,128},{128,0},{1,129},{129,1},{2,130},{130,2},{3,131},{131,3},{4... | collective-permute-start | bytes 98312 | tf_op jit(solution)/shard_map/ppermute | solution.py:690
  90.1 7.0 %collective-permute-start.10 = (f32[64,128]{1,0:T(8,128)S(1)}, f32[64,128]{1,0:T(8,128)S(1)}, u32[]{:S(2)}, u32[]{:S(2)}) collective-permute-start(f32[64,128]{1,0:T(8,128)S(1)} %get-tuple-element.51), channel_id=1, source_target_pairs={{0,129},{1,128},{128,1},{129,0},{2,131},{3,130},{130,3},{131,2},{4... | collective-permute-start | bytes 98312 | tf_op jit(solution)/shard_map/ppermute | solution.py:691
  93.9 4.0 %collective-permute-start.7 = (f32[24,128]{1,0:T(8,128)S(1)}, f32[24,128]{1,0:T(8,128)S(1)}, u32[]{:S(2)}, u32[]{:S(2)}) collective-permute-start(f32[24,128]{1,0:T(8,128)S(1)} %convert_reduce_fusion.total), channel_id=1, source_target_pairs={{0,2},{2,0},{4,6},{6,4},{8,10},{10,8},{12,14},{14,12},{16,18},{18,... | collective-permute-start | bytes 36872 | tf_op jit(solution)/shard_map/ppermute | solution.py:552

commit v11 on v10

--- a/solution.py
+++ b/solution.py
@@ -213,9 +213,11 @@
         lines[1:2, own] = level.T[0:1]
 
 
-def tokens_kernel(here, there, rows, turned, scale, lines, known, scaled, scaled_turned):
-    packs = (here, there)
-    fill_rows(1, packs, rows, turned, scale, lines)
+def tokens_kernel(here, there, rows, turned, scale, lines):
+    fill_rows(1, (here, there), rows, turned, scale, lines)
+
+
+def fill_backward(packs, known, scaled, scaled_turned):
     low_lanes = lane_index((1, 128)) < CHANNELS
     parts = []
     for sample in range(2):
@@ -341,6 +343,9 @@
     after,
     velocity,
     kept,
+    known,
+    scaled,
+    scaled_turned,
     stacked,
     rows,
     turned,
@@ -348,6 +353,7 @@
     lines_a,
 ):
     fill_rows(0, (here, there), rows, turned, scale, lines_a)
+    fill_backward((here, there), known, scaled, scaled_turned)
     for chip in range(taken.shape[0]):
         stacked[chip * block : (chip + 1) * block, :] = taken[chip].astype(F32)[0:block]
     forward(
@@ -626,16 +632,13 @@
     here = jnp.stack([own, other_core(own)])
     there = other_half(here)
 
-    rows, rows_turned, scale, lines, known, scaled, scaled_turned = call(
+    rows, rows_turned, scale, lines = call(
         tokens_kernel,
         (
             struct((4 * tokens, 2 * CHANNELS), BF16),
             struct((2 * CHANNELS, 4 * tokens), BF16),
             struct((4 * tokens, 2 * CHANNELS), F32),
             struct((8, 4 * tokens), F32),
-            struct((2 * tokens, 2 * CHANNELS), F32),
-            struct((2, 2 * tokens, 2 * CHANNELS), BF16),
-            struct((2, 2 * CHANNELS, 2 * tokens), BF16),
         ),
         (here, there),
     )
@@ -655,9 +658,15 @@
     )
     vel_here = vel_b + other_core(vel_crossing)
     vel_there = other_half(vel_here.astype(BF16))
-    vel_a, kept = call(
+    vel_a, kept, known, scaled, scaled_turned = call(
         functools.partial(first_pass_kernel, block),
-        (struct((2 * tokens, 2 * CHANNELS), F32), struct((2, 2 * tokens, 2 * heads * HEAD_DIM), BF16)),
+        (
+            struct((2 * tokens, 2 * CHANNELS), F32),
+            struct((2, 2 * tokens, 2 * heads * HEAD_DIM), BF16),
+            struct((2 * tokens, 2 * CHANNELS), F32),
+            struct((2, 2 * tokens, 2 * CHANNELS), BF16),
+            struct((2, 2 * CHANNELS, 2 * tokens), BF16),
+        ),
         (taken, whole, offsets, here, there, rows, scale, lines, output_turned),
         scratch=[
             pltpu.VMEM((columns, 2 * CHANNELS), F32),

time: 98.9 us -> 99.5 us (level)
  waiting for transfers between devices: 13.8 us -> 15.8 us
  starting transfers between devices: 35.3 us -> 34.3 us
    all_to_all x2, waiting for transfers between devices: 4.22 us -> 5.65 us  [between_chips(): lax.all_to_all(value, 'fsdp', 0, 0, tiled=True, axis_index_groups=groups)]
where the time goes in v11:
time: 99.5 us; the launch traced here: 99.1 us
  starting transfers between devices  34.3 us (34%)
  blocking collectives  33.1 us (33%)
  waiting for transfers between devices  15.8 us (16%)
  Pallas kernels  12.7 us (13%)
  between operations  2.1 us (2%)
    all_to_all x2, blocking collectives, between_chips(): lax.all_to_all(value, 'fsdp', 0, 0, tiled=True, axis_index_groups=groups)  33.1 us
    ppermute x6, starting transfers between devices, other_core(): lax.ppermute(value, 'fsdp', [(i, i ^ 1) for i in range(lax.axis_size('fsd...  17.3 us
    pallas_call x13, Pallas kernels, call(): pl.pallas_call(kernel, out_shape=out_shapes, in_specs=specs, out_specs=ja...  12.7 us
    all_to_all x2, starting transfers between devices, between_chips(): lax.all_to_all(value, 'fsdp', 0, 0, tiled=True, axis_index_groups=groups)  10.6 us
    all_to_all x2, waiting for transfers between devices, between_chips(): lax.all_to_all(value, 'fsdp', 0, 0, tiled=True, axis_index_groups=groups)  5.65 us
    ppermute x3, waiting for transfers between devices, other_half(): return lax.ppermute(value, 'seq', [(0, 1), (1, 0)])  5.38 us
    ppermute x6, waiting for transfers between devices, other_core(): lax.ppermute(value, 'fsdp', [(i, i ^ 1) for i in range(lax.axis_size('fsd...  4.74 us
    ppermute x3, starting transfers between devices, other_half(): return lax.ppermute(value, 'seq', [(0, 1), (1, 0)])  3.53 us
  transfers between devices with their start and end apart: 13, of which 10 were waited for; matrix products, arithmetic and copies ran while one was open for 0% of the time, Pallas kernels for 5%

profile of v11, /device:TPU:1, one launch (start us, length us, event | category | flops | bytes accessed | tf_op | source)
XLA Modules:
  0.0 99.1 jit_solution(5407546001304937010)
XLA Ops:
  0.6 0.0 copy-start
  0.6 3.3 %collective-permute-start = (bf16[48,2304]{1,0:T(8,128)(2,1)}, bf16[48,2304]{1,0:T(8,128)(2,1)S(1)}, u32[]{:S(2)}, u32[]{:S(2)}) collective-permute-start(bf16[48,2304]{1,0:T(8,128)(2,1)} %bitcast.28), channel_id=1, source_target_pairs={{0,2},{2,0},{4,6},{6,4},{8,10},{10,8},{12,14},{14,12},{16,18},{18,... | collective-permute-start | bytes 663560 | tf_op jit(solution)/shard_map/ppermute | solution.py:558
  4.0 0.0 copy-start.1
  4.0 0.9 copy-done.1
  4.9 0.0 copy-start.2
  4.9 0.2 shard_map.113.own
  5.1 0.2 collective-permute-done.received
  5.3 0.3 shard_map.114
  5.6 18.8 %all_to_all.20.after.taken = bf16[32,32,128]{2,1,0:T(8,128)(2,1)S(1)} all-to-all(bf16[32,32,128]{2,1,0:T(8,128)(2,1)S(1)} %shard_map.114), channel_id=1, replica_groups={{0,4,8,12,16,20,24,28,32,36,40,44,48,52,56,60,64,68,72,76,80,84,88,92,9..., dimensions={0} | all-to-all | bytes 524288 | tf_op jit(solution)/shard_map/all_to_all | solution.py:568
  24.4 0.0 copy-done
  24.4 0.0 copy-done.2
  24.4 0.3 shard_map.115.stack
  24.6 0.0 copy-start.3
  24.6 0.0 copy-start.4
  24.6 0.0 copy-start.5
  24.7 0.0 copy-start.6
  24.7 0.0 copy-start.7
  24.7 1.6 %shard_map.116 = (bf16[32,56,128]{2,1,0:T(8,128)(2,1)}, bf16[40,3072]{1,0:T(8,128)(2,1)S(1)}) custom-call(bf16[32,32,128]{2,1,0:T(8,128)(2,1)S(1)} %all_to_all.20.after.taken, bf16[256,3072]{1,0:T(8,128)(2,1)S(1)} %shard_map.115.stack), custom_call_target="tpu_custom_call" | custom-call | tf_op jit(solution)/shard_map/pallas_call | solution.py:542
  26.3 6.7 %all-to-all-start.1 = ((bf16[32,56,128]{2,1,0:T(8,128)(2,1)}), bf16[32,56,128]{2,1,0:T(8,128)(2,1)S(1)}, u32[]{:S(2)}, u32[]{:S(2)}) async-start(bf16[32,56,128]{2,1,0:T(8,128)(2,1)} %get-tuple-element.28.after), calls=%async_computation.1 | async-start | bytes 917504 | tf_op jit(solution)/shard_map/all_to_all | solution.py:568
  34.3 0.0 copy-done.3
  34.3 0.0 copy-done.4
  34.3 0.0 copy-done.5
  34.3 0.0 copy-done.6
  34.3 0.8 shard_map.117.own
  35.1 1.5 %collective-permute-start.1 = (bf16[128,256]{1,0:T(8,128)(2,1)S(1)}, bf16[128,256]{1,0:T(8,128)(2,1)S(1)}, u32[]{:S(2)}, u32[]{:S(2)}) collective-permute-start(bf16[128,256]{1,0:T(8,128)(2,1)S(1)} %shard_map.117.own), channel_id=1, source_target_pairs={{0,2},{2,0},{4,6},{6,4},{8,10},{10,8},{12,14},{14,12},{16,18},{18,... | collective-permute-start | bytes 196616 | tf_op jit(solution)/shard_map/ppermute | solution.py:558
  36.6 0.9 collective-permute-done.1
  37.6 1.4 %collective-permute-start.2 = (bf16[2,128,256]{2,1,0:T(8,128)(2,1)S(1)}, bf16[2,128,256]{2,1,0:T(8,128)(2,1)S(1)}, u32[]{:S(2)}, u32[]{:S(2)}) collective-permute-start(bf16[2,128,256]{2,1,0:T(8,128)(2,1)S(1)} %pad_maximum_fusion.here), channel_id=1, source_target_pairs={{0,1},{1,0},{2,3},{3,2},{4,5},{5,4},{6,7},{7,6},{8,9},{9,8},{10,11... | collective-permute-start | bytes 393224 | tf_op jit(solution)/shard_map/ppermute | solution.py:562
  38.9 0.0 copy-done.7
  39.0 3.4 %collective-permute-done.2.there = bf16[2,128,256]{2,1,0:T(8,128)(2,1)S(1)} collective-permute-done((bf16[2,128,256]{2,1,0:T(8,128)(2,1)S(1)}, bf16[2,128,256]{2,1,0:T(8,128)(2,1)S(1)}, u32[]{:S(2)}, u32[]{:S(2)}) %collective-permute-start.2) | collective-permute-done | bytes 131104 | tf_op jit(solution)/shard_map/ppermute | solution.py:562
  42.4 0.7 shard_map.118
  43.1 2.2 %all-to-all-done.1.taken = bf16[32,56,128]{2,1,0:T(8,128)(2,1)S(1)} async-done(((bf16[32,56,128]{2,1,0:T(8,128)(2,1)}), bf16[32,56,128]{2,1,0:T(8,128)(2,1)S(1)}, u32[]{:S(2)}, u32[]{:S(2)}) %all-to-all-start.1) | async-done | bytes 458784 | tf_op jit(solution)/shard_map/all_to_all | solution.py:568
  45.2 1.9 %shard_map.119 = (bf16[1152,128]{1,0:T(8,128)(2,1)S(1)}, f32[8,1152]{1,0:T(8,128)S(1)}, bf16[6,128,256]{2,1,0:T(8,128)(2,1)S(1)}, f32[6,256,256]{2,1,0:T(8,128)S...) custom-call(bf16[32,56,128]{2,1,0:T(8,128)(2,1)S(1)} %all-to-all-done.1.taken, ...), custom_call_target="tpu_custom_call" | custom-call | tf_op jit(solution)/shard_map/pallas_call | solution.py:542
  47.1 4.5 %collective-permute-start.3 = (f32[256,128]{1,0:T(8,128)S(1)}, f32[256,128]{1,0:T(8,128)S(1)}, u32[]{:S(2)}, u32[]{:S(2)}) collective-permute-start(f32[256,128]{1,0:T(8,128)S(1)} %get-tuple-element.36), channel_id=1, source_target_pairs={{0,2},{2,0},{4,6},{6,4},{8,10},{10,8},{12,14},{14,12},{16,18},{18,... | collective-permute-start | bytes 393224 | tf_op jit(solution)/shard_map/ppermute | solution.py:558
  51.6 1.0 collective-permute-done.3
  52.6 1.6 %collective-permute-start.4 = (bf16[256,128]{1,0:T(8,128)(2,1)S(1)}, bf16[256,128]{1,0:T(8,128)(2,1)S(1)}, u32[]{:S(2)}, u32[]{:S(2)}) collective-permute-start(bf16[256,128]{1,0:T(8,128)(2,1)S(1)} %get-tuple-element.54), channel_id=1, source_target_pairs={{0,1},{1,0},{2,3},{3,2},{4,5},{5,4},{6,7},{7,6},{8,9},{9,8},{10,11... | collective-permute-start | bytes 196616 | tf_op jit(solution)/shard_map/ppermute | solution.py:562
  54.2 2.8 %shard_map.120 = (f32[256,128]{1,0:T(8,128)S(1)}, bf16[2,256,768]{2,1,0:T(8,128)(2,1)S(1)}, f32[256,128]{1,0:T(8,128)S(1)}, bf16[2,256,128]{2,1,0:T(8,128)(2,1)S(1)}, bf16[2,128,256]{2,1,0:T(8,128)(2,1)S(1)}) custom-call(bf16[32,56,128]{2,1,0:T(8,128)(2,1)S(1)} %all-to-all-done.1.taken, bf16[1152,128]{1,0:T(8,128)(2,1)S(1)} %get-tuple-element.33.matrices, ...), custom_call_target="tpu_custom_call" | custom-call | flops 4000000000 | tf_op jit(solution)/shard_map/pallas_call | solution.py:542
  57.0 0.0 collective-permute-done.4.vel_there
  57.0 2.2 %shard_map.121 = (bf16[32,24,128]{2,1,0:T(8,128)(2,1)S(1)}, f32[256,128]{1,0:T(8,128)S(1)}, f32[256,128]{1,0:T(8,128)S(1)}) custom-call(bf16[2,256,768]{2,1,0:T(8,128)(2,1)S(1)} %get-tuple-element.37.kept, bf16[2,256,128]{2,1,0:T(8,128)(2,1)S(1)} %get-tuple-element.38.scaled, bf16[2,128,256]{2,1,0:T(8,128)(2,1)S(1)} %get-tuple-element.39.rows, ...), custom_call_target="tpu_custom_call" | custom-call | tf_op jit(solution)/shard_map/pallas_call | solution.py:542
  59.2 14.3 %all_to_all.21.taken = bf16[32,24,128]{2,1,0:T(8,128)(2,1)S(1)} all-to-all(bf16[32,24,128]{2,1,0:T(8,128)(2,1)S(1)} %get-tuple-element.44), channel_id=1, replica_groups={{0,4,8,12,16,20,24,28,32,36,40,44,48,52,56,60,64,68,72,76,80,84,88,92,9..., dimensions={0} | all-to-all | bytes 393216 | tf_op jit(solution)/shard_map/all_to_all | solution.py:568
  73.5 0.6 shard_map.122
  74.1 2.9 %collective-permute-start.5 = (f32[24,128]{1,0:T(8,128)S(1)}, f32[24,128]{1,0:T(8,128)S(1)}, u32[]{:S(2)}, u32[]{:S(2)}) collective-permute-start(f32[24,128]{1,0:T(8,128)S(1)} %get-tuple-element.47), channel_id=1, source_target_pairs={{0,2},{2,0},{4,6},{6,4},{8,10},{10,8},{12,14},{14,12},{16,18},{18,... | collective-permute-start | bytes 36872 | tf_op jit(solution)/shard_map/ppermute | solution.py:558
  77.0 0.8 collective-permute-done.5
  77.8 0.6 collective-permute-start.6
  78.4 2.0 %collective-permute-done.6.other = f32[24,128]{1,0:T(8,128)S(1)} collective-permute-done((f32[24,128]{1,0:T(8,128)S(1)}, f32[24,128]{1,0:T(8,128)S(1)}, u32[]{:S(2)}, u32[]{:S(2)}) %collective-permute-start.6) | collective-permute-done | bytes 12320 | tf_op jit(solution)/shard_map/ppermute | solution.py:562
  80.4 0.7 shard_map.123
  81.1 3.9 %all-to-all-start.3 = ((bf16[32,24,128]{2,1,0:T(8,128)(2,1)}), bf16[32,24,128]{2,1,0:T(8,128)(2,1)S(1)}, u32[]{:S(2)}, u32[]{:S(2)}) async-start(bf16[32,24,128]{2,1,0:T(8,128)(2,1)} %shard_map.123), calls=%async_computation.3 | async-start | bytes 393216 | tf_op jit(solution)/shard_map/all_to_all | solution.py:568
  85.0 1.9 %collective-permute-start.8 = (f32[256,128]{1,0:T(8,128)S(1)}, f32[256,128]{1,0:T(8,128)S(1)}, u32[]{:S(2)}, u32[]{:S(2)}) collective-permute-start(f32[256,128]{1,0:T(8,128)S(1)} %get-tuple-element.49), channel_id=1, source_target_pairs={{0,2},{2,0},{4,6},{6,4},{8,10},{10,8},{12,14},{14,12},{16,18},{18,... | collective-permute-start | bytes 393224 | tf_op jit(solution)/shard_map/ppermute | solution.py:558
  86.8 1.0 collective-permute-done.8
  87.8 0.1 shard_map.124
  87.9 2.7 %collective-permute-start.9 = (f32[64,128]{1,0:T(8,128)S(1)}, f32[64,128]{1,0:T(8,128)S(1)}, u32[]{:S(2)}, u32[]{:S(2)}) collective-permute-start(f32[64,128]{1,0:T(8,128)S(1)} %get-tuple-element.50), channel_id=1, source_target_pairs={{0,128},{128,0},{1,129},{129,1},{2,130},{130,2},{3,131},{131,3},{4... | collective-permute-start | bytes 98312 | tf_op jit(solution)/shard_map/ppermute | solution.py:699
  90.6 0.2 collective-permute-start.10
  90.9 3.5 %all-to-all-done.3 = bf16[32,24,128]{2,1,0:T(8,128)(2,1)S(1)} async-done(((bf16[32,24,128]{2,1,0:T(8,128)(2,1)}), bf16[32,24,128]{2,1,0:T(8,128)(2,1)S(1)}, u32[]{:S(2)}, u32[]{:S(2)}) %all-to-all-start.3) | async-done | bytes 196640 | tf_op jit(solution)/shard_map/all_to_all | solution.py:568
  94.4 3.2 %collective-permute-start.7 = (f32[24,128]{1,0:T(8,128)S(1)}, f32[24,128]{1,0:T(8,128)S(1)}, u32[]{:S(2)}, u32[]{:S(2)}) collective-permute-start(f32[24,128]{1,0:T(8,128)S(1)} %convert_reduce_fusion.total), channel_id=1, source_target_pairs={{0,2},{2,0},{4,6},{6,4},{8,10},{10,8},{12,14},{14,12},{16,18},{18,... | collective-permute-start | bytes 36872 | tf_op jit(solution)/shard_map/ppermute | solution.py:558
  97.6 0.0 collective-permute-done.9.crossed_here
  97.6 0.0 collective-permute-done.10.crossed_there
  97.6 0.8 collective-permute-done.7.near
  98.4 0.6 shard_map.125
  (6 shorter events, 0.1 us)
Async XLA Ops:
  0.6 23.7 %copy-start = (bf16[1,64,3072]{2,1,0:T(8,128)(2,1)S(1)}, bf16[1,64,3072]{2,1,0:T(8,128)(2,1)}, u32[]{:S(2)}) copy-start(bf16[1,64,3072]{2,1,0:T(8,128)(2,1)} %param.16) | copy-start | bytes 1179652
  0.6 4.6 %collective-permute-start = (bf16[48,2304]{1,0:T(8,128)(2,1)}, bf16[48,2304]{1,0:T(8,128)(2,1)S(1)}, u32[]{:S(2)}, u32[]{:S(2)}) collective-permute-start(bf16[48,2304]{1,0:T(8,128)(2,1)} %bitcast.28), channel_id=1, source_target_pairs={{0,2},{2,0},{4,6},{6,4},{8,10},{10,8},{12,14},{14,12},{16,18},{18,... | collective-permute-start | bytes 663560 | tf_op jit(solution)/shard_map/ppermute | solution.py:558
  4.0 0.9 copy-start.1
  4.9 19.5 %copy-start.2 = (f32[1,2,2,3072]{3,2,1,0:T(2,128)S(1)}, f32[1,2,2,3072]{3,2,1,0:T(2,128)}, u32[]{:S(2)}) copy-start(f32[1,2,2,3072]{3,2,1,0:T(2,128)} %param.19) | copy-start | bytes 147460
  24.6 9.7 %copy-start.3 = (bf16[1,1,128,64]{2,3,1,0:T(8,128)(2,1)S(1)}, bf16[1,1,128,64]{2,3,1,0:T(8,128)(2,1)}, u32[]{:S(2)}) copy-start(bf16[1,1,128,64]{2,3,1,0:T(8,128)(2,1)} %param.10) | copy-start | bytes 49156
  24.6 9.7 %copy-start.4 = (bf16[1,1,128,64]{2,3,1,0:T(8,128)(2,1)S(1)}, bf16[1,1,128,64]{2,3,1,0:T(8,128)(2,1)}, u32[]{:S(2)}) copy-start(bf16[1,1,128,64]{2,3,1,0:T(8,128)(2,1)} %param.11) | copy-start | bytes 49156
  24.6 9.7 %copy-start.5 = (bf16[1,1,128,64]{2,3,1,0:T(8,128)(2,1)S(1)}, bf16[1,1,128,64]{2,3,1,0:T(8,128)(2,1)}, u32[]{:S(2)}) copy-start(bf16[1,1,128,64]{2,3,1,0:T(8,128)(2,1)} %param.13) | copy-start | bytes 49156
  24.7 9.7 %copy-start.6 = (bf16[1,1,128,64]{2,3,1,0:T(8,128)(2,1)S(1)}, bf16[1,1,128,64]{2,3,1,0:T(8,128)(2,1)}, u32[]{:S(2)}) copy-start(bf16[1,1,128,64]{2,3,1,0:T(8,128)(2,1)} %param.15) | copy-start | bytes 49156
  24.7 14.3 %copy-start.7 = (bf16[1,768,64]{1,2,0:T(8,128)(2,1)S(1)}, bf16[1,768,64]{1,2,0:T(8,128)(2,1)}, u32[]{:S(2)}) copy-start(bf16[1,768,64]{1,2,0:T(8,128)(2,1)} %param.18) | copy-start | bytes 294916
  26.3 19.0 %all-to-all-start.1 = ((bf16[32,56,128]{2,1,0:T(8,128)(2,1)}), bf16[32,56,128]{2,1,0:T(8,128)(2,1)S(1)}, u32[]{:S(2)}, u32[]{:S(2)}) async-start(bf16[32,56,128]{2,1,0:T(8,128)(2,1)} %get-tuple-element.28.after), calls=%async_computation.1 | async-start | bytes 917504 | tf_op jit(solution)/shard_map/all_to_all | solution.py:568
  35.1 2.4 %collective-permute-start.1 = (bf16[128,256]{1,0:T(8,128)(2,1)S(1)}, bf16[128,256]{1,0:T(8,128)(2,1)S(1)}, u32[]{:S(2)}, u32[]{:S(2)}) collective-permute-start(bf16[128,256]{1,0:T(8,128)(2,1)S(1)} %shard_map.117.own), channel_id=1, source_target_pairs={{0,2},{2,0},{4,6},{6,4},{8,10},{10,8},{12,14},{14,12},{16,18},{18,... | collective-permute-start | bytes 196616 | tf_op jit(solution)/shard_map/ppermute | solution.py:558
  37.6 4.8 %collective-permute-start.2 = (bf16[2,128,256]{2,1,0:T(8,128)(2,1)S(1)}, bf16[2,128,256]{2,1,0:T(8,128)(2,1)S(1)}, u32[]{:S(2)}, u32[]{:S(2)}) collective-permute-start(bf16[2,128,256]{2,1,0:T(8,128)(2,1)S(1)} %pad_maximum_fusion.here), channel_id=1, source_target_pairs={{0,1},{1,0},{2,3},{3,2},{4,5},{5,4},{6,7},{7,6},{8,9},{9,8},{10,11... | collective-permute-start | bytes 393224 | tf_op jit(solution)/shard_map/ppermute | solution.py:562
  47.1 5.5 %collective-permute-start.3 = (f32[256,128]{1,0:T(8,128)S(1)}, f32[256,128]{1,0:T(8,128)S(1)}, u32[]{:S(2)}, u32[]{:S(2)}) collective-permute-start(f32[256,128]{1,0:T(8,128)S(1)} %get-tuple-element.36), channel_id=1, source_target_pairs={{0,2},{2,0},{4,6},{6,4},{8,10},{10,8},{12,14},{14,12},{16,18},{18,... | collective-permute-start | bytes 393224 | tf_op jit(solution)/shard_map/ppermute | solution.py:558
  52.6 4.4 %collective-permute-start.4 = (bf16[256,128]{1,0:T(8,128)(2,1)S(1)}, bf16[256,128]{1,0:T(8,128)(2,1)S(1)}, u32[]{:S(2)}, u32[]{:S(2)}) collective-permute-start(bf16[256,128]{1,0:T(8,128)(2,1)S(1)} %get-tuple-element.54), channel_id=1, source_target_pairs={{0,1},{1,0},{2,3},{3,2},{4,5},{5,4},{6,7},{7,6},{8,9},{9,8},{10,11... | collective-permute-start | bytes 196616 | tf_op jit(solution)/shard_map/ppermute | solution.py:562
  74.1 3.8 %collective-permute-start.5 = (f32[24,128]{1,0:T(8,128)S(1)}, f32[24,128]{1,0:T(8,128)S(1)}, u32[]{:S(2)}, u32[]{:S(2)}) collective-permute-start(f32[24,128]{1,0:T(8,128)S(1)} %get-tuple-element.47), channel_id=1, source_target_pairs={{0,2},{2,0},{4,6},{6,4},{8,10},{10,8},{12,14},{14,12},{16,18},{18,... | collective-permute-start | bytes 36872 | tf_op jit(solution)/shard_map/ppermute | solution.py:558
  77.8 2.5 %collective-permute-start.6 = (f32[24,128]{1,0:T(8,128)S(1)}, f32[24,128]{1,0:T(8,128)S(1)}, u32[]{:S(2)}, u32[]{:S(2)}) collective-permute-start(f32[24,128]{1,0:T(8,128)S(1)} %add.10.total), channel_id=1, source_target_pairs={{0,1},{1,0},{2,3},{3,2},{4,5},{5,4},{6,7},{7,6},{8,9},{9,8},{10,11... | collective-permute-start | bytes 36872 | tf_op jit(solution)/shard_map/ppermute | solution.py:562
  81.1 13.3 %all-to-all-start.3 = ((bf16[32,24,128]{2,1,0:T(8,128)(2,1)}), bf16[32,24,128]{2,1,0:T(8,128)(2,1)S(1)}, u32[]{:S(2)}, u32[]{:S(2)}) async-start(bf16[32,24,128]{2,1,0:T(8,128)(2,1)} %shard_map.123), calls=%async_computation.3 | async-start | bytes 393216 | tf_op jit(solution)/shard_map/all_to_all | solution.py:568
  85.0 2.8 %collective-permute-start.8 = (f32[256,128]{1,0:T(8,128)S(1)}, f32[256,128]{1,0:T(8,128)S(1)}, u32[]{:S(2)}, u32[]{:S(2)}) collective-permute-start(f32[256,128]{1,0:T(8,128)S(1)} %get-tuple-element.49), channel_id=1, source_target_pairs={{0,2},{2,0},{4,6},{6,4},{8,10},{10,8},{12,14},{14,12},{16,18},{18,... | collective-permute-start | bytes 393224 | tf_op jit(solution)/shard_map/ppermute | solution.py:558
  87.9 9.7 %collective-permute-start.9 = (f32[64,128]{1,0:T(8,128)S(1)}, f32[64,128]{1,0:T(8,128)S(1)}, u32[]{:S(2)}, u32[]{:S(2)}) collective-permute-start(f32[64,128]{1,0:T(8,128)S(1)} %get-tuple-element.50), channel_id=1, source_target_pairs={{0,128},{128,0},{1,129},{129,1},{2,130},{130,2},{3,131},{131,3},{4... | collective-permute-start | bytes 98312 | tf_op jit(solution)/shard_map/ppermute | solution.py:699
  90.6 7.0 %collective-permute-start.10 = (f32[64,128]{1,0:T(8,128)S(1)}, f32[64,128]{1,0:T(8,128)S(1)}, u32[]{:S(2)}, u32[]{:S(2)}) collective-permute-start(f32[64,128]{1,0:T(8,128)S(1)} %get-tuple-element.51), channel_id=1, source_target_pairs={{0,129},{1,128},{128,1},{129,0},{2,131},{3,130},{130,3},{131,2},{4... | collective-permute-start | bytes 98312 | tf_op jit(solution)/shard_map/ppermute | solution.py:700
  94.4 4.0 %collective-permute-start.7 = (f32[24,128]{1,0:T(8,128)S(1)}, f32[24,128]{1,0:T(8,128)S(1)}, u32[]{:S(2)}, u32[]{:S(2)}) collective-permute-start(f32[24,128]{1,0:T(8,128)S(1)} %convert_reduce_fusion.total), channel_id=1, source_target_pairs={{0,2},{2,0},{4,6},{6,4},{8,10},{10,8},{12,14},{14,12},{16,18},{18,... | collective-permute-start | bytes 36872 | tf_op jit(solution)/shard_map/ppermute | solution.py:558
